TPU v7x, 128 devices: a whole 4x4x4 slice. The times are simulated.
128 devices in a mesh: seq: 16 (over y, z), exp: 8 (over x, core).
Axes of the slice: x: 4, y: 4, z: 4, core: 2. Of those that a mesh axis runs over, the one named last changes fastest.
Arguments:
- grad_out: bfloat16 [16384, 8192], P(('seq', 'exp')), may hold values from -6 to 6
- hidden: bfloat16 [16384, 8192], P(('seq', 'exp')), may hold values from -6 to 6
- norm_gain: float32 [8192], replicated, may hold values from 0.5 to 1.5
- router_logits: float32 [16384, 16], P(('seq', 'exp')), may hold values from -15 to 410
- router_weight: float32 [16, 8192], replicated, may hold values from -3 to 3
- expert_ids: int32 [16384, 2], P(('seq', 'exp')), may hold values from 0 to 15, as said below
- expert_grad: bfloat16 [16, 16, 192, 8192], P('seq', 'exp'), may hold values from -6 to 6
- expert_out: bfloat16 [16, 16, 192, 8192], P('seq', 'exp'), may hold values from -0.0625 to 0.0625
Outputs:
- grad_hidden: bfloat16 [16384, 8192], P(('seq', 'exp'))
- router_grad: float32 [16, 8192], replicated
Inputs may be any that keep to these rules, and one draw needn't show every extreme that they name: `expert_ids`: among the rows of one device, no expert is named by more than 24 entries, and some expert is named by exactly 24; the 2 experts of a row differ; every expert is named somewhere. Slots that no token uses hold values that no output reads.
All inputs are finite; a program needn't handle non-finite values.
Results may differ from a plain program's by a relative error of at most 0.0027.
Values may be sent and summed in bfloat16 or wider, within the bound.
No kernel may reach another device: no remote copies, remote signals or barrier semaphores. Data moves between devices by JAX's collectives and lax.ppermute only.
A program may use at most 128 MiB of HBM per device.

v0:
```python
import math

import jax
import jax.numpy as jnp
from jax import lax
from jax.sharding import PartitionSpec as P

D = 8192
EXPERTS = 16
TOP = 2


def body(
    grad_out, hidden, norm_gain, router_logits, router_weight, expert_ids, expert_grad, expert_out
):
    tok_rows = grad_out.shape[0]
    peers = lax.axis_size("exp")
    capacity = expert_grad.shape[2] // peers
    labels = jnp.arange(EXPERTS, dtype=jnp.int32)
    onehot = (expert_ids[:, :, None] == labels).astype(jnp.int32).reshape(tok_rows * TOP, EXPERTS)
    ranks = jnp.cumsum(onehot, axis=0) - onehot
    slot_index = jnp.sum(onehot * ranks, axis=1).reshape(tok_rows, TOP)
    counts = lax.psum(jnp.sum(onehot, axis=0), ("seq", "exp"))
    total_tokens = tok_rows * lax.axis_size(("seq", "exp"))
    row_index = (expert_ids * capacity + slot_index).reshape(-1)
    back_grad, back_out = (
        lax.all_to_all(expert_grad, "exp", split_axis=2, concat_axis=1, tiled=True),
        lax.all_to_all(expert_out, "exp", split_axis=2, concat_axis=1, tiled=True),
    )
    picked_out = jnp.take(back_out.reshape(EXPERTS * capacity, D), row_index, axis=0).reshape(
        tok_rows, TOP, D
    )
    gate_dots = jnp.einsum(
        "td,tkd->tk", grad_out, picked_out, preferred_element_type=jnp.float32
    ).astype(jnp.bfloat16)
    picked_grad = jnp.take(back_grad.reshape(EXPERTS * capacity, D), row_index, axis=0).reshape(
        tok_rows, TOP, D
    )
    dots_value = gate_dots.astype(jnp.float32)
    chosen = jnp.take_along_axis(router_logits, expert_ids, axis=1)
    gate_weights = jax.nn.softmax(chosen, axis=-1)
    combined = jnp.zeros((tok_rows, D), jnp.float32)
    for k in range(TOP):
        combined = combined + gate_weights[:, k : k + 1] * picked_grad[:, k].astype(jnp.float32)
    chosen_grad = gate_weights * (
        dots_value - jnp.sum(gate_weights * dots_value, axis=1, keepdims=True)
    )
    direct_grad = jnp.sum(
        chosen_grad[:, :, None] * (expert_ids[:, :, None] == labels).astype(jnp.float32), axis=1
    )
    router_probs = jax.nn.softmax(router_logits, axis=-1)
    expert_load = EXPERTS * counts.astype(jnp.float32) / (TOP * total_tokens)
    aux_grad = router_probs * (
        expert_load - jnp.sum(router_probs * expert_load, axis=1, keepdims=True)
    )
    logit_grad = direct_grad + aux_grad
    normed_grad = combined + jnp.dot(logit_grad, router_weight, precision=lax.Precision.HIGHEST)
    resid_f = hidden.astype(jnp.float32)
    inv_rms = lax.rsqrt(jnp.mean(resid_f * resid_f, axis=1, keepdims=True) + 1e-05)
    normed = resid_f * inv_rms
    scaled = norm_gain * normed_grad
    back = inv_rms * (scaled - normed * jnp.mean(normed * scaled, axis=1, keepdims=True))
    grad_hidden = (grad_out.astype(jnp.float32) + back).astype(jnp.bfloat16)
    routed_in = norm_gain * normed
    partial_router = lax.dot_general(
        logit_grad, routed_in, (((0,), (0,)), ((), ())), precision=lax.Precision.HIGHEST
    )
    totals = lax.psum(partial_router, ("seq", "exp"))
    router_grad = totals / math.sqrt(total_tokens)
    return (grad_hidden, router_grad)


def solution(mesh):
    in_specs = (
        P(("seq", "exp"), None),
        P(("seq", "exp"), None),
        P(),
        P(("seq", "exp"), None),
        P(),
        P(("seq", "exp"), None),
        P("seq", "exp", None, None),
        P("seq", "exp", None, None),
    )
    out_specs = (P(("seq", "exp"), None), P())
    return jax.shard_map(body, mesh=mesh, in_specs=in_specs, out_specs=out_specs, check_vma=False)
```

profile of v0, /device:TPU:0, one launch (start us, length us, event | category | flops | bytes accessed | tf_op | source)
XLA Modules:
  0.0 493.9 jit_solution(15552355234489630001)
XLA Ops:
  7.2 0.0 copy-start
  7.2 12.7 %copy.85 = bf16[1,2,192,8192]{3,1,0,2:T(2,128)(2,1)} copy(bf16[1,2,192,8192]{3,2,1,0:T(8,128)(2,1)} %param.16) | data formatting | bytes 12582912 | tf_op args[6]
  19.9 4.8 all-to-all-start
  24.6 12.6 %copy.89 = bf16[1,2,192,8192]{3,1,0,2:T(2,128)(2,1)} copy(bf16[1,2,192,8192]{3,2,1,0:T(8,128)(2,1)} %param.17) | data formatting | bytes 12582912 | tf_op args[7]
  37.3 0.0 copy-start.3
  37.3 0.0 copy-start.1
  37.3 59.5 %all-to-all-done = bf16[1,2,192,8192]{3,1,0,2:T(2,128)(2,1)} async-done(((bf16[1,2,192,8192]{3,1,0,2:T(2,128)(2,1)}), bf16[1,2,192,8192]{3,1,0,2:T(2,128)(2,1)}, u32[]{:S(2)}, u32[]{:S(2)}) %all-to-all-start) | async-done | bytes 6291488 | tf_op jit(solution)/shard_map/all_to_all | solution.py:27
  96.8 4.8 all-to-all-start.1
  101.6 0.0 all-reduce.2.cloned.1.call-start
  101.6 0.0 copy-done.3
  101.6 0.1 copy.80
  101.7 0.1 eq.43
  101.9 0.1 eq.39
  102.0 0.6 reduce-window.6
  102.6 0.2 slice_reduce_fusion
  102.9 0.1 convert_reduce_fusion
  103.0 127.4 %psum.14 = s32[16]{0:T(128)S(1)} all-reduce(s32[16]{0:T(128)S(1)} %get-tuple-element.3), channel_id=1, replica_groups=mesh['seq'=16,'exp'=8] {'seq','exp'}, use_global_device_ids=true, to_apply=%region_11.13 | all-reduce | flops 16 | bytes 128 | tf_op jit(solution)/shard_map/psum | solution.py:23
  230.4 0.1 reshape.84
  230.5 0.1 copy.83
  230.6 0.1 copy.84
  230.7 0.1 reshape.85
  230.9 0.1 copy.78
  231.0 0.1 reshape.107
  231.1 0.0 copy-done.1
  231.1 0.0 copy-start.2
  231.1 2.1 gather_fusion
  233.3 0.1 reshape.110
  233.4 0.1 copy.79
  233.6 0.1 multiply_reduce_fusion
  233.7 0.0 copy-done.2
  233.7 0.5 fusion.11
  234.2 9.7 %copy.86 = bf16[1,2,8,24,8192]{4,3,1,2,0:T(8,128)(2,1)} copy(bf16[1,2,8,24,8192]{4,1,3,2,0:T(2,128)(2,1)} %bitcast.3) | data formatting | bytes 12582912 | tf_op jit(solution)/shard_map/all_to_all | solution.py:27
  244.0 0.0 all-to-all-done.1
  244.0 9.7 %copy.90 = bf16[1,2,8,24,8192]{4,3,1,2,0:T(8,128)(2,1)} copy(bf16[1,2,8,24,8192]{4,1,3,2,0:T(2,128)(2,1)} %bitcast.9) | data formatting | bytes 12582912 | tf_op jit(solution)/shard_map/all_to_all | solution.py:28
  253.7 12.9 %gather_fusion.1 = bf16[256,8192]{1,0:T(8,128)(2,1)} fusion(bf16[384,8192]{1,0:T(8,128)(2,1)} %bitcast.46, s32[1024]{0:T(1024)S(1)} %pad_clamp_fusion), kind=kCustom, calls=%fused_computation.clone | custom fusion | bytes 8389632 | tf_op jit(solution)/shard_map/jit(_take)/gather | solution.py:36
  266.6 12.7 %gather_fusion.2 = bf16[256,8192]{1,0:T(8,128)(2,1)} fusion(bf16[384,8192]{1,0:T(8,128)(2,1)} %bitcast.47, s32[1024]{0:T(1024)S(1)} %pad_clamp_fusion), kind=kCustom, calls=%fused_computation.1.clone | custom fusion | bytes 8389632 | tf_op jit(solution)/shard_map/jit(_take)/gather | solution.py:30
  279.3 5.9 %broadcast_select_fusion = (bf16[256,8192]{1,0:T(8,128)(2,1)}, bf16[256,8192]{1,0:T(8,128)(2,1)}) fusion(bf16[256,8192]{1,0:T(8,128)(2,1)} %gather_fusion.2, pred[256]{0:T(512)(128)(4,1)S(1)} %compare_and_fusion, bf16[256,8192]{1,0:T(8,128)(2,1)} %gather_fusion.1), kind=kLoop, calls=%fused_computation.20 | loop fusion | flops 4194304 | bytes 16777472 | tf_op jit(solution)/shard_map/jit(_take)/select_n | solution.py:30
  285.2 7.6 %reshape.88 = bf16[128,2,8192]{2,1,0:T(2,128)(2,1)} reshape(bf16[256,8192]{1,0:T(8,128)(2,1)} %get-tuple-element.13) | data formatting | bytes 8388608 | tf_op jit(solution)/shard_map/reshape | solution.py:30
  292.8 10.7 %fusion.13 = bf16[128,1,2]{2,1,0:T(2,128)(2,1)S(1)} fusion(bf16[128,2,8192]{2,1,0:T(2,128)(2,1)} %reshape.88, bf16[128,8192,1]{1,0,2:T(8,128)(2,1)} %bitcast.48), kind=kOutput, calls=%fused_computation.22 | convolution fusion | flops 4194304 | bytes 6291968 | tf_op jit(solution)/shard_map/td,tkd->tk/dot_general | solution.py:33
  303.6 0.1 copy.92
  303.7 7.6 %reshape.86 = bf16[128,2,8192]{2,1,0:T(2,128)(2,1)} reshape(bf16[256,8192]{1,0:T(8,128)(2,1)} %get-tuple-element.14) | data formatting | bytes 8388608 | tf_op jit(solution)/shard_map/reshape | solution.py:36
  311.4 0.0 copy-start.4
  311.4 14.5 %fusion.28 = (bf16[128,1,8192]{2,1,0:T(2,128)(2,1)}, bf16[128,1,8192]{2,1,0:T(2,128)(2,1)}) fusion(bf16[128,2,8192]{2,1,0:T(2,128)(2,1)} %reshape.86), kind=kLoop, calls=%fused_computation.67 | loop fusion | bytes 8388608 | tf_op jit(solution)/shard_map/slice | solution.py:44
  325.8 0.0 copy-done.4
  325.8 3.3 fusion.9
  329.1 0.0 copy-done
  329.1 13.4 %fusion.4 = (f32[128]{0:T(128)S(1)}, f32[128,8192]{1,0:T(8,128)}) fusion(bf16[128,8192]{1,0:T(8,128)(2,1)S(1)} %copy-done.2, f32[128]{0:T(128)S(1)} %add_rsqrt_fusion, f32[16,8192]{1,0:T(8,128)S(1)} %copy-done, f32[128,16]{0,1:T(8,128)S(1)} %select_reduce_fusion, f32[128]{0:T(128)S(1)} %multiply_reduce_fusion, f32[16]{0:T(128)S(1)} %convert_multiply_fusion.5, ...), kind=kOutput, calls=%fused_computation.10 | convolution fusion | flops 212871040 | bytes 11062848 | tf_op jit(solution)/shard_map/dot_general | solution.py:57
  342.6 0.0 all-reduce.2.cloned.1.call-update
  342.6 5.3 %fusion.8 = bf16[128,8192]{1,0:T(8,128)(2,1)} fusion(f32[128,8192]{1,0:T(8,128)} %get-tuple-element.16, bf16[128,8192]{1,0:T(8,128)(2,1)S(1)} %copy-done.2, bf16[128,8192]{1,0:T(8,128)(2,1)} %param.10, f32[128]{0:T(128)S(1)} %broadcast_multiply_fusion.1, f32[128]{0:T(128)S(1)} %add_rsqrt_fusion), kind=kLoop, calls=%fused_computation.14 | loop fusion | flops 8388608 | bytes 10486784 | tf_op jit(solution)/shard_map/convert_element_type | solution.py:63
  347.9 137.1 %all-reduce.2.cloned.1.call-done = f32[16,8192]{1,0:T(8,128)} async-done(((f32[16,8192]{1,0:T(8,128)}), f32[16,8192]{1,0:T(8,128)}) %all-reduce.2.cloned.1.call-update) | async-done | bytes 524304 | tf_op jit(solution)/shard_map/psum | solution.py:68
  485.0 1.9 broadcast_multiply_fusion
  (19 shorter events, 0.2 us)
Async XLA Ops:
  7.2 322.0 %copy-start = (f32[16,8192]{1,0:T(8,128)S(1)}, f32[16,8192]{1,0:T(8,128)}, u32[]{:S(2)}) copy-start(f32[16,8192]{1,0:T(8,128)} %param.14) | copy-start | bytes 1572868
  19.9 76.9 %all-to-all-start = ((bf16[1,2,192,8192]{3,1,0,2:T(2,128)(2,1)}), bf16[1,2,192,8192]{3,1,0,2:T(2,128)(2,1)}, u32[]{:S(2)}, u32[]{:S(2)}) async-start(bf16[1,2,192,8192]{3,1,0,2:T(2,128)(2,1)} %copy.85), calls=%async_computation | async-start | bytes 12582912 | tf_op jit(solution)/shard_map/all_to_all | solution.py:27
  37.3 64.3 %copy-start.3 = (s32[128,2]{0,1:T(2,128)S(1)}, s32[128,2]{0,1:T(2,128)}, u32[]{:S(2)}) copy-start(s32[128,2]{0,1:T(2,128)} %param.15) | copy-start | bytes 3076
  37.3 193.8 %copy-start.1 = (f32[128,16]{0,1:T(8,128)S(1)}, f32[128,16]{0,1:T(8,128)}, u32[]{:S(2)}) copy-start(f32[128,16]{0,1:T(8,128)} %param.13) | copy-start | bytes 24580
  96.8 147.2 %all-to-all-start.1 = ((bf16[1,2,192,8192]{3,1,0,2:T(2,128)(2,1)}), bf16[1,2,192,8192]{3,1,0,2:T(2,128)(2,1)}, u32[]{:S(2)}, u32[]{:S(2)}) async-start(bf16[1,2,192,8192]{3,1,0,2:T(2,128)(2,1)} %copy.89), calls=%async_computation.1 | async-start | bytes 12582912 | tf_op jit(solution)/shard_map/all_to_all | solution.py:28
  101.6 383.4 %all-reduce.2.cloned.1.call-start = ((), (), s32[]{:S(2)}) async-start(), calls=%async_computation.2 | async-start | bytes 1048576 | tf_op jit(solution)/shard_map/psum | solution.py:68
  231.1 2.6 copy-start.2
  311.4 14.5 %copy-start.4 = (f32[8192]{0:T(1024)S(1)}, f32[8192]{0:T(1024)}, u32[]{:S(2)}) copy-start(f32[8192]{0:T(1024)} %param.12) | copy-start | bytes 98308
Sparse Core Ops, SparseCore 0:
  342.7 142.2 all-reduce.1
where the time goes:
time: 500 us; the launch traced here: 494 us
  waiting for transfers between devices  197 us (39%)
  blocking collectives  127 us (25%)
  local copies, waits for them, and re-layouts  104 us (21%)
  matrix products  27.5 us (6%)
  other arithmetic  14.6 us (3%)
  between operations  14.4 us (3%)
  starting transfers between devices  9.58 us (2%)
    psum x1, waiting for transfers between devices, body(): totals = lax.psum(partial_router, ('seq', 'exp'))  137 us
    psum x1, blocking collectives, body(): counts = lax.psum(jnp.sum(onehot, axis=0), ('seq', 'exp'))  127 us
    all_to_all x1, waiting for transfers between devices, body(): lax.all_to_all(expert_grad, 'exp', split_axis=2, concat_axis=1, tiled=True)  59.5 us
    unnamed x13, local copies, waits for them, and re-layouts  25.5 us
    slice x1, local copies, waits for them, and re-layouts, body(): picked_grad[:, k].astype(jnp.float32)  14.5 us
    dot_general x1, matrix products, body(): jnp.dot(logit_grad, router_weight, precision=lax.Precision.HIGHEST)  13.4 us
    gather x1, local copies, waits for them, and re-layouts, body(): jnp.take(back_grad.reshape(EXPERTS * capacity, D), row_index, axis=0)  12.9 us
    gather x1, local copies, waits for them, and re-layouts, body(): jnp.take(back_out.reshape(EXPERTS * capacity, D), row_index, axis=0)  12.7 us
  transfers between devices with their start and end apart: 3, of which 2 were waited for; matrix products, arithmetic and copies ran while one was open for 7% of the time, Pallas kernels for 0%

commit v1 on v0

v1 whole, which is shorter than its diff:
```python
import jax
import jax.numpy as jnp
from jax import lax
from jax.experimental import pallas as pl
from jax.experimental.pallas import tpu as pltpu
from jax.sharding import PartitionSpec as P

D = 8192
EXPERTS = 16
TOK = 128
CAP = 24
ROWS = 2 * CAP
TOKENS = 16384
AXES = ("seq", "exp")
WINDOW = 4
CHUNK = 1024
F32 = jnp.float32
BF16 = jnp.bfloat16
VMEM = pl.BlockSpec(memory_space=pltpu.VMEM)

ROUTES = ((0, 0), (1, 0), (3, 0), (2, 0), (1, 1), (3, 1), (2, 1), (0, 1))


def coords():
    s, e = lax.axis_index("seq"), lax.axis_index("exp")
    return {"y": s >> 2, "z": s & 3, "x": e >> 1, "c": e & 1}


STRIDE = {"y": 32, "z": 8, "x": 2, "c": 1}
SIZE = {"y": 4, "z": 4, "x": 4, "c": 2}


def shift_perm(axis, d):
    out = []
    for i in range(128):
        a = (i // STRIDE[axis]) % SIZE[axis]
        out.append((i, i + ((a + d) % SIZE[axis] - a) * STRIDE[axis]))
    return out


def xor_perm(axis, d):
    return [(i, i ^ (d * STRIDE[axis])) for i in range(128)]


def after(x, *deps):
    out = lax.optimization_barrier((x,) + deps)
    return out[0], out[1:]


def split3(v):
    a = v.astype(BF16)
    r = v - a.astype(F32)
    b = r.astype(BF16)
    c = (r - b.astype(F32)).astype(BF16)
    return a, b, c


def pre_kernel(ids_ref, logits_ref, hidden_ref, pack_ref, probs_ref, counts_ref):
    ids = ids_ref[...]
    logits = logits_ref[...]
    labels = lax.broadcasted_iota(jnp.int32, (TOK, EXPERTS), 1)
    oh = [(ids[:, k : k + 1] == labels).astype(F32) for k in range(2)]
    both = oh[0] + oh[1]
    row = lax.broadcasted_iota(jnp.int32, (TOK, TOK), 0)
    col = lax.broadcasted_iota(jnp.int32, (TOK, TOK), 1)
    before = (row > col).astype(F32).astype(BF16)
    ranks = jnp.dot(before, both.astype(BF16), preferred_element_type=F32)
    counts_ref[...] = jnp.broadcast_to(jnp.sum(both, axis=0, keepdims=True), (8, EXPERTS))
    index = [
        jnp.sum(oh[k] * (ranks + (CAP * labels).astype(F32)), axis=1, keepdims=True)
        for k in range(2)
    ]
    chosen = [jnp.sum(oh[k] * logits, axis=1, keepdims=True) for k in range(2)]
    top = jnp.maximum(chosen[0], chosen[1])
    w = [jnp.exp(c - top) for c in chosen]
    total = w[0] + w[1]
    e = jnp.exp(logits - jnp.max(logits, axis=1, keepdims=True))
    probs_ref[...] = e / jnp.sum(e, axis=1, keepdims=True)
    square = jnp.zeros((TOK, 128), F32)
    for c in range(D // CHUNK):
        h = hidden_ref[:, c * CHUNK : (c + 1) * CHUNK].astype(F32)
        h = h * h
        for j in range(CHUNK // 128):
            square = square + h[:, j * 128 : (j + 1) * 128]
    inv = lax.rsqrt(jnp.sum(square, axis=1, keepdims=True) / D + 1e-05)
    lane = lax.broadcasted_iota(jnp.int32, (TOK, 8), 1)
    pack = jnp.zeros((TOK, 8), F32)
    for i, v in enumerate((w[0] / total, w[1] / total, index[0], index[1], inv)):
        pack = jnp.where(lane == i, v, pack)
    pack_ref[...] = pack


def mid_kernel(
    slots_ref, pack_ref, ids_ref, probs_ref, counts_ref, gain_ref, hidden_ref, grad_ref, *refs
):
    blocks, (logit_ref, partial_ref) = refs[:8], refs[8:]
    pack = pack_ref[...]
    gate = [pack[:, 0:1], pack[:, 1:2]]
    inv = pack[:, 4:5]
    dots = jnp.zeros((TOK, 8 * ROWS), F32)
    for c in range(D // CHUNK):
        cols = slice(c * CHUNK, (c + 1) * CHUNK)
        picked = jnp.concatenate([b[:, cols] for b in blocks], axis=0)
        dots = dots + lax.dot_general(
            grad_ref[:, cols], picked, (((1,), (1,)), ((), ())), preferred_element_type=F32
        )
    slots = slots_ref[...]
    gate_dot = [
        jnp.sum(jnp.where(slots == pack[:, 2 + k : 3 + k], dots, 0.0), axis=1, keepdims=True)
        .astype(BF16)
        .astype(F32)
        for k in range(2)
    ]
    mean = gate[0] * gate_dot[0] + gate[1] * gate_dot[1]
    ids = ids_ref[...]
    labels = lax.broadcasted_iota(jnp.int32, (TOK, EXPERTS), 1)
    direct = jnp.zeros((TOK, EXPERTS), F32)
    for k in range(2):
        chosen = gate[k] * (gate_dot[k] - mean)
        direct = direct + jnp.where(ids[:, k : k + 1] == labels, chosen, 0.0)
    probs = probs_ref[...]
    load = counts_ref[0:1, :] * (EXPERTS / (2 * TOKENS))
    aux = probs * (load - jnp.sum(probs * load, axis=1, keepdims=True))
    logit = direct + aux
    logit_ref[...] = logit
    left = jnp.concatenate(split3(logit * inv), axis=1)
    for c in range(D // CHUNK):
        cols = slice(c * CHUNK, (c + 1) * CHUNK)
        p = lax.dot_general(
            left, hidden_ref[:, cols], (((0,), (0,)), ((), ())), preferred_element_type=F32
        )
        p = p[0:16] + p[16:32] + p[32:48]
        partial_ref[:, cols] = p * (gain_ref[:, cols] * (1.0 / 128.0))


def last_kernel(
    slots_ref, pack_ref, logit_ref, weight_ref, gain_ref, hidden_ref, grad_ref, *refs
):
    blocks, out_ref, scaled_ref = refs[:8], refs[8], refs[9]
    pack = pack_ref[...]
    inv = pack[:, 4:5]
    slots = slots_ref[...]
    w = jnp.where(slots == pack[:, 2:3], pack[:, 0:1], 0.0)
    w = w + jnp.where(slots == pack[:, 3:4], pack[:, 1:2], 0.0)
    w_hi, w_lo, _ = split3(w)
    l0, l1, l2 = split3(logit_ref[...])
    zero = jnp.zeros_like(l0)
    left = jnp.concatenate(
        [
            jnp.concatenate([w_hi, l0, l0, l0, l2], axis=1),
            jnp.concatenate([w_lo, l1, l1, zero, zero], axis=1),
        ],
        axis=0,
    )
    acc = jnp.zeros((TOK, 128), F32)
    for c in range(D // CHUNK):
        cols = slice(c * CHUNK, (c + 1) * CHUNK)
        r0, r1, r2 = split3(weight_ref[:, cols])
        right = jnp.concatenate([b[:, cols] for b in blocks] + [r0, r1, r2, r0], axis=0)
        both = jnp.dot(left, right, preferred_element_type=F32)
        scaled = (both[:TOK] + both[TOK:]) * gain_ref[:, cols]
        scaled_ref[:, cols] = scaled
        prod = scaled * hidden_ref[:, cols].astype(F32)
        for j in range(CHUNK // 128):
            acc = acc + prod[:, j * 128 : (j + 1) * 128]
    mean = jnp.sum(acc, axis=1, keepdims=True) * inv / D
    factor = inv * mean
    for c in range(D // CHUNK):
        cols = slice(c * CHUNK, (c + 1) * CHUNK)
        back = inv * (scaled_ref[:, cols] - hidden_ref[:, cols].astype(F32) * factor)
        out_ref[:, cols] = (grad_ref[:, cols].astype(F32) + back).astype(BF16)


def params(mib):
    return pltpu.CompilerParams(vmem_limit_bytes=mib * 1024 * 1024)


def reduce_all(v, at):
    v = v.reshape(1024, 128)
    for axis in ("y", "z"):
        v = v.reshape((4, v.shape[0] // 4, 128))
        me = at[axis]
        got = [
            lax.ppermute(
                lax.dynamic_index_in_dim(v, (me + d) & 3, 0, keepdims=False),
                AXES,
                shift_perm(axis, d),
            )
            for d in (1, 3, 2)
        ]
        v = lax.dynamic_index_in_dim(v, me, 0, keepdims=False) + got[0] + got[1] + got[2]
    for axis, d in (("c", 1), ("x", 1), ("x", 2)):
        v = v + lax.ppermute(v, AXES, xor_perm(axis, d))
    for axis in ("z", "y"):
        me = at[axis]
        parts = [v] + [lax.ppermute(v, AXES, shift_perm(axis, d)) for d in (1, 2, 3)]
        full = jnp.zeros((4,) + v.shape, F32)
        for d, part in enumerate(parts):
            full = lax.dynamic_update_index_in_dim(full, part, (me - d) & 3, 0)
        v = full.reshape(4 * v.shape[0], 128)
    return v.reshape(EXPERTS, D)


def body(
    grad_out, hidden, norm_gain, router_logits, router_weight, expert_ids, expert_grad, expert_out
):
    at = coords()
    gain = norm_gain.reshape(1, D)
    sources = [((at["x"] - s) & 3) * 2 + (at["c"] ^ m) for s, m in ROUTES]
    base = jnp.stack(sources).astype(F32) * ROWS
    slots = (base[:, None] + jnp.arange(ROWS, dtype=F32)[None, :]).reshape(1, 8 * ROWS)

    pack, probs, counts = pl.pallas_call(
        pre_kernel,
        out_shape=(
            jax.ShapeDtypeStruct((TOK, 8), F32),
            jax.ShapeDtypeStruct((TOK, EXPERTS), F32),
            jax.ShapeDtypeStruct((8, EXPERTS), F32),
        ),
        in_specs=[VMEM] * 3,
        out_specs=(VMEM,) * 3,
        compiler_params=params(16),
    )(expert_ids, router_logits, hidden)
    for axis, d in (("y", 1), ("y", 2), ("z", 1), ("z", 2), ("c", 1), ("x", 1), ("x", 2)):
        counts = counts + lax.ppermute(counts, AXES, xor_perm(axis, d))

    moved = []
    for array in (expert_out, expert_grad):
        for s, m in ROUTES[1:]:
            n = len(moved)
            if n >= WINDOW:
                array, (moved[n - WINDOW],) = after(array, moved[n - WINDOW])
            to = ((at["x"] + s) & 3) * 2 + (at["c"] ^ m)
            block = lax.dynamic_slice(array, (0, 0, to * CAP, 0), (1, 2, CAP, D))
            perm = [(i, ((i // 2 + s) % 4) * 2 + (i % 2 + m) % 2) for i in range(8)]
            moved.append(lax.ppermute(block.reshape(ROWS, D), "exp", perm))
    own = [
        lax.dynamic_slice(a, (0, 0, (at["x"] * 2 + at["c"]) * CAP, 0), (1, 2, CAP, D)).reshape(ROWS, D)
        for a in (expert_out, expert_grad)
    ]

    logit, partial = pl.pallas_call(
        mid_kernel,
        out_shape=(
            jax.ShapeDtypeStruct((TOK, EXPERTS), F32),
            jax.ShapeDtypeStruct((EXPERTS, D), F32),
        ),
        in_specs=[VMEM] * 16,
        out_specs=(VMEM,) * 2,
        compiler_params=params(24),
    )(slots, pack, expert_ids, probs, counts, gain, hidden, grad_out, own[0], *moved[:7])
    router_grad = reduce_all(partial, at)

    grad_hidden = pl.pallas_call(
        last_kernel,
        out_shape=jax.ShapeDtypeStruct((TOK, D), BF16),
        in_specs=[VMEM] * 15,
        out_specs=VMEM,
        scratch_shapes=[pltpu.VMEM((TOK, D), F32)],
        compiler_params=params(28),
    )(slots, pack, logit, router_weight, gain, hidden, grad_out, own[1], *moved[7:])
    return grad_hidden, router_grad


def solution(mesh):
    rows = P(("seq", "exp"), None)
    in_specs = (
        rows,
        rows,
        P(),
        rows,
        P(),
        rows,
        P("seq", "exp", None, None),
        P("seq", "exp", None, None),
    )
    return jax.shard_map(body, mesh=mesh, in_specs=in_specs, out_specs=(rows, P()), check_vma=False)
```

time: 500 us -> 220 us (0.44)
  blocking collectives: 127 us -> 0 us
  waiting for transfers between devices: 197 us -> 115 us
  local copies, waits for them, and re-layouts: 104 us -> 42.7 us
  starting transfers between devices: 9.58 us -> 44.5 us
  matrix products: 27.5 us -> 0 us
  other arithmetic: 14.6 us -> 1.14 us
  between operations: 14.4 us -> 0.95 us
  Pallas kernels: 0 us -> 13.4 us
    psum x1 -> x0, waiting for transfers between devices: 137 us -> none  [body(): totals = lax.psum(partial_router, ('seq', 'exp'))]
    psum x1 -> x0, blocking collectives: 127 us -> none  [body(): counts = lax.psum(jnp.sum(onehot, axis=0), ('seq', 'exp'))]
    ppermute x0 -> x36, waiting for transfers between devices: none -> 115 us  [the longest x14 71 us: body(): moved.append(lax.ppermute(block.reshape(ROWS, D), 'exp', perm))]
    all_to_all x2 -> x0, waiting for transfers between devices: 59.5 us -> none  [the longest x1 59.5 us: body(): lax.all_to_all(expert_grad, 'exp', split_axis=2, concat_axis=1, tiled=True)]
    ppermute x0 -> x36, starting transfers between devices: none -> 44.5 us  [the longest x14 11.5 us: body(): moved.append(lax.ppermute(block.reshape(ROWS, D), 'exp', perm))]
    gather x7 -> x0, local copies, waits for them, and re-layouts: 28.2 us -> none  [the longest x1 12.9 us: body(): jnp.take(back_grad.reshape(EXPERTS * capacity, D), row_index, axis=0)]
    dot_general x3 -> x0, matrix products: 27.5 us -> none  [the longest x1 13.4 us: body(): jnp.dot(logit_grad, router_weight, precision=lax.Precision.HIGHEST)]
    dynamic_slice x0 -> x12, local copies, waits for them, and re-layouts: none -> 23.5 us  [the longest x11 22.3 us: body(): block = lax.dynamic_slice(array, (0, 0, to * CAP, 0), (1, 2, CAP, D))]
  transfers between devices with their start and end apart: 3 -> 36, of which waited for: 2 -> 21; matrix products, arithmetic and copies ran while one was open for 7% -> 12% of each run, Pallas kernels for 0% -> 0%
where the time goes in v1:
time: 220 us; the launch traced here: 217 us
  waiting for transfers between devices  115 us (52%)
  starting transfers between devices  44.5 us (20%)
  local copies, waits for them, and re-layouts  42.7 us (19%)
  Pallas kernels  13.4 us (6%)
    ppermute x14, waiting for transfers between devices, body(): moved.append(lax.ppermute(block.reshape(ROWS, D), 'exp', perm))  71 us
    dynamic_slice x11, local copies, waits for them, and re-layouts, body(): block = lax.dynamic_slice(array, (0, 0, to * CAP, 0), (1, 2, CAP, D))  22.3 us
    ppermute x7, waiting for transfers between devices, body(): counts = counts + lax.ppermute(counts, AXES, xor_perm(axis, d))  16 us
    ppermute x6, waiting for transfers between devices, reduce_all(): lax.ppermute(v, AXES, shift_perm(axis, d))  13 us
    unnamed x40, local copies, waits for them, and re-layouts  12.6 us
    ppermute x14, starting transfers between devices, body(): moved.append(lax.ppermute(block.reshape(ROWS, D), 'exp', perm))  11.5 us
    ppermute x7, starting transfers between devices, body(): counts = counts + lax.ppermute(counts, AXES, xor_perm(axis, d))  11.5 us
    ppermute x6, starting transfers between devices, reduce_all(): lax.ppermute(lax.dynamic_index_in_dim(v, me + d & 3, 0, keepdims=False),...  10.8 us
  transfers between devices with their start and end apart: 36, of which 21 were waited for; matrix products, arithmetic and copies ran while one was open for 12% of the time, Pallas kernels for 0%

profile of v1, /device:TPU:0, one launch (start us, length us, event | category | flops | bytes accessed | tf_op | source)
XLA Modules:
  0.0 217.3 jit_solution(9296640467076448905)
XLA Ops:
  0.7 4.0 %constant_dynamic-slice_fusion.11 = (bf16[1,2,24,8192]{3,2,1,0:T(8,128)(2,1)}, bf16[1,2,24,8192]{3,2,1,0:T(8,128)(2,1)}, bf16[1,2,24,8192]{3,2,1,0:T(8,128)(2,1)...) fusion(bf16[1,2,192,8192]{3,2,1,0:T(8,128)(2,1)} %param.15, s32[]{:T(128)S(6)} %select_n.88, ...), kind=kLoop, calls=%fused_computation.31 | loop fusion | bytes 7864340 | tf_op jit(solution)/shard_map/dynamic_slice | solution.py:234
  4.7 1.6 collective-permute-start.7
  6.9 1.7 collective-permute-start.8
  8.6 1.5 collective-permute-start.9
  10.2 16.5 %collective-permute-done.7.refs_1_ = bf16[48,8192]{1,0:T(8,128)(2,1)} collective-permute-done((bf16[48,8192]{1,0:T(8,128)(2,1)}, bf16[48,8192]{1,0:T(8,128)(2,1)}, u32[]{:S(2)}, u32[]{:S(2)}) %collective-permute-start.7) | collective-permute-done | bytes 786464 | tf_op jit(solution)/shard_map/ppermute | solution.py:236
  26.6 2.1 constant_dynamic-slice_fusion.10
  28.7 15.0 %collective-permute-done.8.refs_2_ = bf16[48,8192]{1,0:T(8,128)(2,1)} collective-permute-done((bf16[48,8192]{1,0:T(8,128)(2,1)}, bf16[48,8192]{1,0:T(8,128)(2,1)}, u32[]{:S(2)}, u32[]{:S(2)}) %collective-permute-start.8) | collective-permute-done | bytes 786464 | tf_op jit(solution)/shard_map/ppermute | solution.py:236
  43.8 2.1 constant_dynamic-slice_fusion.9
  45.8 15.6 %collective-permute-done.9.refs_3_ = bf16[48,8192]{1,0:T(8,128)(2,1)} collective-permute-done((bf16[48,8192]{1,0:T(8,128)(2,1)}, bf16[48,8192]{1,0:T(8,128)(2,1)}, u32[]{:S(2)}, u32[]{:S(2)}) %collective-permute-start.9) | collective-permute-done | bytes 786464 | tf_op jit(solution)/shard_map/ppermute | solution.py:236
  61.4 2.2 constant_dynamic-slice_fusion.8
  64.4 1.7 collective-permute-start
  66.1 2.0 collective-permute-done
  68.1 3.2 %collective-permute-start.1 = (f32[8,16]{1,0:T(8,128)S(1)}, f32[8,16]{1,0:T(8,128)S(1)}, u32[]{:S(2)}, u32[]{:S(2)}) collective-permute-start(f32[8,16]{1,0:T(8,128)S(1)} %add.266), channel_id=1, source_target_pairs={{0,64},{1,65},{2,66},{3,67},{4,68},{5,69},{6,70},{7,71},{8,72},{9,... | collective-permute-start | bytes 1544 | tf_op jit(solution)/shard_map/ppermute | solution.py:225
  71.3 1.9 collective-permute-done.1
  73.2 1.9 collective-permute-start.2
  75.2 1.6 collective-permute-done.2
  76.9 3.9 %collective-permute-start.3 = (f32[8,16]{1,0:T(8,128)S(1)}, f32[8,16]{1,0:T(8,128)S(1)}, u32[]{:S(2)}, u32[]{:S(2)}) collective-permute-start(f32[8,16]{1,0:T(8,128)S(1)} %add.268), channel_id=1, source_target_pairs={{0,16},{1,17},{2,18},{3,19},{4,20},{5,21},{6,22},{7,23},{8,24},{9,... | collective-permute-start | bytes 1544 | tf_op jit(solution)/shard_map/ppermute | solution.py:225
  80.7 1.6 collective-permute-done.3
  82.4 1.1 collective-permute-done.4
  83.5 3.6 %collective-permute-done.5 = f32[8,16]{1,0:T(8,128)S(1)} collective-permute-done((f32[8,16]{1,0:T(8,128)S(1)}, f32[8,16]{1,0:T(8,128)S(1)}, u32[]{:S(2)}, u32[]{:S(2)}) %collective-permute-start.5) | collective-permute-done | bytes 544 | tf_op jit(solution)/shard_map/ppermute | solution.py:225
  88.0 4.2 %collective-permute-done.6 = f32[8,16]{1,0:T(8,128)S(1)} collective-permute-done((f32[8,16]{1,0:T(8,128)S(1)}, f32[8,16]{1,0:T(8,128)S(1)}, u32[]{:S(2)}, u32[]{:S(2)}) %collective-permute-start.6) | collective-permute-done | bytes 544 | tf_op jit(solution)/shard_map/ppermute | solution.py:225
  92.3 1.6 copy-done.1
  95.5 6.0 %shard_map.96 = (f32[128,16]{1,0:T(8,128)S(1)}, f32[16,8192]{1,0:T(8,128)S(1)}) custom-call(f32[1,384]{1,0:T(1,128)S(1)} %add.265.slots_ref, f32[128,8]{1,0:T(8,128)S(1)} %get-tuple-element.27.pack_ref, s32[128,2]{1,0:T(8,128)S(1)} %copy.10.ids_ref, f32[128,16]{1,0:T(8,128)S(1)} %copy-done.15, f32[8,16]{1,0:T(8,128)S(1)} %add.272.counts_ref, ...), custom_call_target="tpu_custom_call" | custom-call | tf_op jit(solution)/shard_map/pallas_call | solution.py:242
  103.0 1.6 collective-permute-start.21
  104.5 1.7 collective-permute-start.22
  106.2 2.0 collective-permute-start.23
  108.2 1.2 constant_dynamic-slice_fusion.7
  109.4 1.1 collective-permute-done.21
  110.5 2.3 %collective-permute-done.23 = f32[256,128]{1,0:T(8,128)} collective-permute-done((f32[256,128]{1,0:T(8,128)S(1)}, f32[256,128]{1,0:T(8,128)}, u32[]{:S(2)}, u32[]{:S(2)}) %collective-permute-start.23) | collective-permute-done | bytes 131104 | tf_op jit(solution)/shard_map/ppermute | solution.py:184
  112.8 1.0 fusion.1
  113.8 1.6 collective-permute-start.24
  115.4 2.2 %collective-permute-start.25 = (f32[64,128]{1,0:T(8,128)S(1)}, f32[64,128]{1,0:T(8,128)S(1)}, u32[]{:S(2)}, u32[]{:S(2)}) collective-permute-start(f32[64,128]{1,0:T(8,128)S(1)} %get-tuple-element.64), channel_id=1, source_target_pairs={{0,24},{1,25},{2,26},{3,27},{4,28},{5,29},{6,30},{7,31},{8,0},{9,1... | collective-permute-start | bytes 98312 | tf_op jit(solution)/shard_map/ppermute | solution.py:184
  117.7 1.8 collective-permute-start.26
  119.4 1.2 constant_dynamic-slice_fusion.6
  120.7 2.3 %collective-permute-done.26 = f32[64,128]{1,0:T(8,128)S(1)} collective-permute-done((f32[64,128]{1,0:T(8,128)S(1)}, f32[64,128]{1,0:T(8,128)S(1)}, u32[]{:S(2)}, u32[]{:S(2)}) %collective-permute-start.26) | collective-permute-done | bytes 32800 | tf_op jit(solution)/shard_map/ppermute | solution.py:184
  123.2 1.2 constant_dynamic-slice_fusion.5
  124.6 1.2 constant_dynamic-slice_fusion.4
  125.8 8.8 %collective-permute-done.28 = f32[64,128]{1,0:T(8,128)S(1)} collective-permute-done((f32[64,128]{1,0:T(8,128)S(1)}, f32[64,128]{1,0:T(8,128)S(1)}, u32[]{:S(2)}, u32[]{:S(2)}) %collective-permute-start.28) | collective-permute-done | bytes 32800 | tf_op jit(solution)/shard_map/ppermute | solution.py:193
  134.6 1.0 collective-permute-start.29
  135.6 2.1 constant_dynamic-slice_fusion.3
  138.5 4.2 %collective-permute-start.15 = (bf16[48,8192]{1,0:T(8,128)(2,1)S(1)}, bf16[48,8192]{1,0:T(8,128)(2,1)S(1)}, u32[]{:S(2)}, u32[]{:S(2)}) collective-permute-start(bf16[48,8192]{1,0:T(8,128)(2,1)S(1)} %bitcast.72), channel_id=1, source_target_pairs={{0,6},{1,7},{2,0},{3,1},{4,2},{5,3},{6,4},{7,5},{8,14},{9,15},{10,... | collective-permute-start | bytes 2359304 | tf_op jit(solution)/shard_map/ppermute | solution.py:236
  142.8 1.1 collective-permute-start.30
  143.8 2.1 constant_dynamic-slice_fusion.2
  145.9 1.7 collective-permute-start.17
  148.0 1.1 collective-permute-start.31
  149.0 4.4 %collective-permute-done.31 = f32[64,128]{1,0:T(8,128)S(1)} collective-permute-done((f32[64,128]{1,0:T(8,128)S(1)}, f32[64,128]{1,0:T(8,128)S(1)}, u32[]{:S(2)}, u32[]{:S(2)}) %collective-permute-start.31) | collective-permute-done | bytes 32800 | tf_op jit(solution)/shard_map/ppermute | solution.py:196
  153.4 1.9 collective-permute-start.32
  155.3 2.0 collective-permute-done.32
  157.9 19.7 %collective-permute-done.15.refs_2_ = bf16[48,8192]{1,0:T(8,128)(2,1)S(1)} collective-permute-done((bf16[48,8192]{1,0:T(8,128)(2,1)S(1)}, bf16[48,8192]{1,0:T(8,128)(2,1)S(1)}, u32[]{:S(2)}, u32[]{:S(2)}) %collective-permute-start.15) | collective-permute-done | bytes 786464 | tf_op jit(solution)/shard_map/ppermute | solution.py:236
  177.6 0.9 copy-done.5
  178.5 2.1 constant_dynamic-slice_fusion.1
  181.5 2.2 constant_dynamic-slice_fusion
  183.6 0.9 broadcast_in_dim.34
  185.2 3.1 %collective-permute-start.34 = (f32[256,128]{1,0:T(8,128)S(1)}, f32[256,128]{1,0:T(8,128)S(1)}, u32[]{:S(2)}, u32[]{:S(2)}) collective-permute-start(f32[256,128]{1,0:T(8,128)S(1)} %bitcast.79), channel_id=1, source_target_pairs={{0,64},{1,65},{2,66},{3,67},{4,68},{5,69},{6,70},{7,71},{8,72},{9,... | collective-permute-start | bytes 393224 | tf_op jit(solution)/shard_map/ppermute | solution.py:196
  189.0 3.6 %collective-permute-done.34 = f32[256,128]{1,0:T(8,128)S(1)} collective-permute-done((f32[256,128]{1,0:T(8,128)S(1)}, f32[256,128]{1,0:T(8,128)S(1)}, u32[]{:S(2)}, u32[]{:S(2)}) %collective-permute-start.34) | collective-permute-done | bytes 131104 | tf_op jit(solution)/shard_map/ppermute | solution.py:196
  192.6 1.8 collective-permute-start.35
  195.1 2.8 %collective-permute-done.35 = f32[256,128]{1,0:T(8,128)S(1)} collective-permute-done((f32[256,128]{1,0:T(8,128)S(1)}, f32[256,128]{1,0:T(8,128)S(1)}, u32[]{:S(2)}, u32[]{:S(2)}) %collective-permute-start.35) | collective-permute-done | bytes 131104 | tf_op jit(solution)/shard_map/ppermute | solution.py:196
  198.5 1.9 reshape_reshape.7
  200.5 4.2 %collective-permute-done.19.refs_6_ = bf16[48,8192]{1,0:T(8,128)(2,1)} collective-permute-done((bf16[48,8192]{1,0:T(8,128)(2,1)}, bf16[48,8192]{1,0:T(8,128)(2,1)}, u32[]{:S(2)}, u32[]{:S(2)}) %collective-permute-start.19) | collective-permute-done | bytes 786464 | tf_op jit(solution)/shard_map/ppermute | solution.py:236
  204.6 1.6 copy-done.2
  206.2 1.1 copy-done.4
  207.4 1.1 copy-done.6
  208.5 1.1 copy-done.8
  210.5 6.8 %shard_map.97 = bf16[128,8192]{1,0:T(8,128)(2,1)} custom-call(f32[1,384]{1,0:T(1,128)S(1)} %add.265.slots_ref, f32[128,8]{1,0:T(8,128)S(1)} %get-tuple-element.27.pack_ref, f32[128,16]{1,0:T(8,128)S(1)} %copy-done.13, f32[16,8192]{1,0:T(8,128)S(1)} %copy-done.9, f32[1,8192]{1,0:T(1,128)S(1)} %bitcast.71, bf16[128,8192]{1,0:T(8,128)(2,1)S(1)} %copy-done, ...), custom_call_target="tpu_custom_call" | custom-call | tf_op jit(solution)/shard_map/pallas_call | solution.py:254
  (92 shorter events, 12.2 us)
Async XLA Ops:
  0.7 62.9 %copy-start.18 = (s32[128,2]{0,1:T(2,128)S(1)}, s32[128,2]{0,1:T(2,128)}, u32[]{:S(2)}) copy-start(s32[128,2]{0,1:T(2,128)} %param.13) | copy-start | bytes 3076
  0.7 63.0 %copy-start.17 = (f32[128,16]{0,1:T(8,128)S(1)}, f32[128,16]{0,1:T(8,128)}, u32[]{:S(2)}) copy-start(f32[128,16]{0,1:T(8,128)} %param.11) | copy-start | bytes 24580
  0.7 63.1 %copy-start = (bf16[128,8192]{1,0:T(8,128)(2,1)S(1)}, bf16[128,8192]{1,0:T(8,128)(2,1)}, u32[]{:S(2)}) copy-start(bf16[128,8192]{1,0:T(8,128)(2,1)} %hidden_ref.5) | copy-start | bytes 6291460
  4.7 22.0 %collective-permute-start.7 = (bf16[48,8192]{1,0:T(8,128)(2,1)}, bf16[48,8192]{1,0:T(8,128)(2,1)}, u32[]{:S(2)}, u32[]{:S(2)}) collective-permute-start(bf16[48,8192]{1,0:T(8,128)(2,1)} %bitcast.10), channel_id=1, source_target_pairs={{0,2},{1,3},{2,4},{3,5},{4,6},{5,7},{6,0},{7,1},{8,10},{9,11},{10,... | collective-permute-start | bytes 2359304 | tf_op jit(solution)/shard_map/ppermute | solution.py:236
  6.2 86.0 %collective-permute-start.10 = (bf16[48,8192]{1,0:T(8,128)(2,1)}, bf16[48,8192]{1,0:T(8,128)(2,1)}, u32[]{:S(2)}, u32[]{:S(2)}) collective-permute-start(bf16[48,8192]{1,0:T(8,128)(2,1)} %bitcast.13), channel_id=1, source_target_pairs={{0,3},{1,2},{2,5},{3,4},{4,7},{5,6},{6,1},{7,0},{8,11},{9,10},{10,... | collective-permute-start | bytes 2359304 | tf_op jit(solution)/shard_map/ppermute | solution.py:236
  6.9 36.9 %collective-permute-start.8 = (bf16[48,8192]{1,0:T(8,128)(2,1)}, bf16[48,8192]{1,0:T(8,128)(2,1)}, u32[]{:S(2)}, u32[]{:S(2)}) collective-permute-start(bf16[48,8192]{1,0:T(8,128)(2,1)} %bitcast.11), channel_id=1, source_target_pairs={{0,6},{1,7},{2,0},{3,1},{4,2},{5,3},{6,4},{7,5},{8,14},{9,15},{10,... | collective-permute-start | bytes 2359304 | tf_op jit(solution)/shard_map/ppermute | solution.py:236
  8.6 52.8 %collective-permute-start.9 = (bf16[48,8192]{1,0:T(8,128)(2,1)}, bf16[48,8192]{1,0:T(8,128)(2,1)}, u32[]{:S(2)}, u32[]{:S(2)}) collective-permute-start(bf16[48,8192]{1,0:T(8,128)(2,1)} %bitcast.12), channel_id=1, source_target_pairs={{0,4},{1,5},{2,6},{3,7},{4,0},{5,1},{6,2},{7,3},{8,12},{9,13},{10,... | collective-permute-start | bytes 2359304 | tf_op jit(solution)/shard_map/ppermute | solution.py:236
  28.7 63.5 %collective-permute-start.11 = (bf16[48,8192]{1,0:T(8,128)(2,1)}, bf16[48,8192]{1,0:T(8,128)(2,1)}, u32[]{:S(2)}, u32[]{:S(2)}) collective-permute-start(bf16[48,8192]{1,0:T(8,128)(2,1)} %bitcast.14), channel_id=1, source_target_pairs={{0,7},{1,6},{2,1},{3,0},{4,3},{5,2},{6,5},{7,4},{8,15},{9,14},{10,... | collective-permute-start | bytes 2359304 | tf_op jit(solution)/shard_map/ppermute | solution.py:236
  45.8 46.4 %collective-permute-start.12 = (bf16[48,8192]{1,0:T(8,128)(2,1)}, bf16[48,8192]{1,0:T(8,128)(2,1)}, u32[]{:S(2)}, u32[]{:S(2)}) collective-permute-start(bf16[48,8192]{1,0:T(8,128)(2,1)} %bitcast.15), channel_id=1, source_target_pairs={{0,5},{1,4},{2,7},{3,6},{4,1},{5,0},{6,3},{7,2},{8,13},{9,12},{10,... | collective-permute-start | bytes 2359304 | tf_op jit(solution)/shard_map/ppermute | solution.py:236
  63.6 28.7 %collective-permute-start.13 = (bf16[48,8192]{1,0:T(8,128)(2,1)}, bf16[48,8192]{1,0:T(8,128)(2,1)}, u32[]{:S(2)}, u32[]{:S(2)}) collective-permute-start(bf16[48,8192]{1,0:T(8,128)(2,1)} %bitcast.16), channel_id=1, source_target_pairs={{0,1},{1,0},{2,3},{3,2},{4,5},{5,4},{6,7},{7,6},{8,9},{9,8},{10,11... | collective-permute-start | bytes 2359304 | tf_op jit(solution)/shard_map/ppermute | solution.py:236
  64.4 27.8 %copy-start.14 = (f32[128,16]{1,0:T(8,128)}, f32[128,16]{1,0:T(8,128)S(1)}, u32[]{:S(2)}) copy-start(f32[128,16]{1,0:T(8,128)S(1)} %get-tuple-element.28.probs_ref) | copy-start | bytes 24580
  64.4 3.7 %collective-permute-start = (f32[8,16]{1,0:T(8,128)S(1)}, f32[8,16]{1,0:T(8,128)S(1)}, u32[]{:S(2)}, u32[]{:S(2)}) collective-permute-start(f32[8,16]{1,0:T(8,128)S(1)} %get-tuple-element.29), channel_id=1, source_target_pairs={{0,32},{1,33},{2,34},{3,35},{4,36},{5,37},{6,38},{7,39},{8,40},{9,... | collective-permute-start | bytes 1544 | tf_op jit(solution)/shard_map/ppermute | solution.py:225
  68.1 5.1 %collective-permute-start.1 = (f32[8,16]{1,0:T(8,128)S(1)}, f32[8,16]{1,0:T(8,128)S(1)}, u32[]{:S(2)}, u32[]{:S(2)}) collective-permute-start(f32[8,16]{1,0:T(8,128)S(1)} %add.266), channel_id=1, source_target_pairs={{0,64},{1,65},{2,66},{3,67},{4,68},{5,69},{6,70},{7,71},{8,72},{9,... | collective-permute-start | bytes 1544 | tf_op jit(solution)/shard_map/ppermute | solution.py:225
  73.2 3.6 %collective-permute-start.2 = (f32[8,16]{1,0:T(8,128)S(1)}, f32[8,16]{1,0:T(8,128)S(1)}, u32[]{:S(2)}, u32[]{:S(2)}) collective-permute-start(f32[8,16]{1,0:T(8,128)S(1)} %add.267), channel_id=1, source_target_pairs={{0,8},{1,9},{2,10},{3,11},{4,12},{5,13},{6,14},{7,15},{8,0},{9,1},... | collective-permute-start | bytes 1544 | tf_op jit(solution)/shard_map/ppermute | solution.py:225
  76.9 5.5 %collective-permute-start.3 = (f32[8,16]{1,0:T(8,128)S(1)}, f32[8,16]{1,0:T(8,128)S(1)}, u32[]{:S(2)}, u32[]{:S(2)}) collective-permute-start(f32[8,16]{1,0:T(8,128)S(1)} %add.268), channel_id=1, source_target_pairs={{0,16},{1,17},{2,18},{3,19},{4,20},{5,21},{6,22},{7,23},{8,24},{9,... | collective-permute-start | bytes 1544 | tf_op jit(solution)/shard_map/ppermute | solution.py:225
  82.3 1.2 collective-permute-start.4
  83.5 3.6 %collective-permute-start.5 = (f32[8,16]{1,0:T(8,128)S(1)}, f32[8,16]{1,0:T(8,128)S(1)}, u32[]{:S(2)}, u32[]{:S(2)}) collective-permute-start(f32[8,16]{1,0:T(8,128)S(1)} %add.270), channel_id=1, source_target_pairs={{0,2},{1,3},{2,0},{3,1},{4,6},{5,7},{6,4},{7,5},{8,10},{9,11},{10,... | collective-permute-start | bytes 1544 | tf_op jit(solution)/shard_map/ppermute | solution.py:225
  87.1 5.1 %collective-permute-start.6 = (f32[8,16]{1,0:T(8,128)S(1)}, f32[8,16]{1,0:T(8,128)S(1)}, u32[]{:S(2)}, u32[]{:S(2)}) collective-permute-start(f32[8,16]{1,0:T(8,128)S(1)} %add.271), channel_id=1, source_target_pairs={{0,4},{1,5},{2,6},{3,7},{4,0},{5,1},{6,2},{7,3},{8,12},{9,13},{10,... | collective-permute-start | bytes 1544 | tf_op jit(solution)/shard_map/ppermute | solution.py:225
  92.3 1.6 copy-start.1
  93.9 0.8 copy-start.10
  94.6 0.8 copy-start.15
  101.4 0.6 copy-start.12
  102.2 4.0 %copy-start.16 = (f32[4,256,128]{2,1,0:T(8,128)}, f32[4,256,128]{2,1,0:T(8,128)S(1)}, u32[]{:S(2)}) copy-start(f32[4,256,128]{2,1,0:T(8,128)S(1)} %reshape_reshape.6) | copy-start | bytes 1572868
  103.0 7.5 %collective-permute-start.21 = (f32[256,128]{1,0:T(8,128)}, f32[256,128]{1,0:T(8,128)S(1)}, u32[]{:S(2)}, u32[]{:S(2)}) collective-permute-start(f32[256,128]{1,0:T(8,128)} %get-tuple-element.59), channel_id=1, source_target_pairs={{0,32},{1,33},{2,34},{3,35},{4,36},{5,37},{6,38},{7,39},{8,40},{9,... | collective-permute-start | bytes 393224 | tf_op jit(solution)/shard_map/ppermute | solution.py:184
  104.5 5.9 %collective-permute-start.22 = (f32[256,128]{1,0:T(8,128)S(1)}, f32[256,128]{1,0:T(8,128)S(1)}, u32[]{:S(2)}, u32[]{:S(2)}) collective-permute-start(f32[256,128]{1,0:T(8,128)S(1)} %get-tuple-element.61), channel_id=1, source_target_pairs={{0,96},{1,97},{2,98},{3,99},{4,100},{5,101},{6,102},{7,103},{8,104... | collective-permute-start | bytes 393224 | tf_op jit(solution)/shard_map/ppermute | solution.py:184
  106.2 6.6 %collective-permute-start.23 = (f32[256,128]{1,0:T(8,128)S(1)}, f32[256,128]{1,0:T(8,128)}, u32[]{:S(2)}, u32[]{:S(2)}) collective-permute-start(f32[256,128]{1,0:T(8,128)S(1)} %get-tuple-element.60), channel_id=1, source_target_pairs={{0,64},{1,65},{2,66},{3,67},{4,68},{5,69},{6,70},{7,71},{8,72},{9,... | collective-permute-start | bytes 393224 | tf_op jit(solution)/shard_map/ppermute | solution.py:184
  113.8 6.9 %collective-permute-start.24 = (f32[64,128]{1,0:T(8,128)S(1)}, f32[64,128]{1,0:T(8,128)S(1)}, u32[]{:S(2)}, u32[]{:S(2)}) collective-permute-start(f32[64,128]{1,0:T(8,128)S(1)} %get-tuple-element.62), channel_id=1, source_target_pairs={{0,8},{1,9},{2,10},{3,11},{4,12},{5,13},{6,14},{7,15},{8,16},{9,17... | collective-permute-start | bytes 98312 | tf_op jit(solution)/shard_map/ppermute | solution.py:184
  115.4 5.3 %collective-permute-start.25 = (f32[64,128]{1,0:T(8,128)S(1)}, f32[64,128]{1,0:T(8,128)S(1)}, u32[]{:S(2)}, u32[]{:S(2)}) collective-permute-start(f32[64,128]{1,0:T(8,128)S(1)} %get-tuple-element.64), channel_id=1, source_target_pairs={{0,24},{1,25},{2,26},{3,27},{4,28},{5,29},{6,30},{7,31},{8,0},{9,1... | collective-permute-start | bytes 98312 | tf_op jit(solution)/shard_map/ppermute | solution.py:184
  117.7 5.4 %collective-permute-start.26 = (f32[64,128]{1,0:T(8,128)S(1)}, f32[64,128]{1,0:T(8,128)S(1)}, u32[]{:S(2)}, u32[]{:S(2)}) collective-permute-start(f32[64,128]{1,0:T(8,128)S(1)} %get-tuple-element.63), channel_id=1, source_target_pairs={{0,16},{1,17},{2,18},{3,19},{4,20},{5,21},{6,22},{7,23},{8,24},{9,... | collective-permute-start | bytes 98312 | tf_op jit(solution)/shard_map/ppermute | solution.py:184
  120.6 17.0 %collective-permute-start.14 = (bf16[48,8192]{1,0:T(8,128)(2,1)S(1)}, bf16[48,8192]{1,0:T(8,128)(2,1)S(1)}, u32[]{:S(2)}, u32[]{:S(2)}) collective-permute-start(bf16[48,8192]{1,0:T(8,128)(2,1)S(1)} %bitcast.74), channel_id=1, source_target_pairs={{0,2},{1,3},{2,4},{3,5},{4,6},{5,7},{6,0},{7,1},{8,10},{9,11},{10,... | collective-permute-start | bytes 2359304 | tf_op jit(solution)/shard_map/ppermute | solution.py:236
  123.1 81.6 %copy-start.9 = (f32[16,8192]{1,0:T(8,128)S(1)}, f32[16,8192]{1,0:T(8,128)}, u32[]{:S(2)}) copy-start(f32[16,8192]{1,0:T(8,128)} %weight_ref.1) | copy-start | bytes 1572868
  123.1 81.5 %copy-start.11 = (f32[8192]{0:T(1024)S(1)}, f32[8192]{0:T(1024)}, u32[]{:S(2)}) copy-start(f32[8192]{0:T(1024)} %param.10) | copy-start | bytes 98308
  123.1 1.3 collective-permute-start.27
  124.5 10.1 %collective-permute-start.28 = (f32[64,128]{1,0:T(8,128)S(1)}, f32[64,128]{1,0:T(8,128)S(1)}, u32[]{:S(2)}, u32[]{:S(2)}) collective-permute-start(f32[64,128]{1,0:T(8,128)S(1)} %add.311), channel_id=1, source_target_pairs={{0,2},{1,3},{2,0},{3,1},{4,6},{5,7},{6,4},{7,5},{8,10},{9,11},{10,... | collective-permute-start | bytes 98312 | tf_op jit(solution)/shard_map/ppermute | solution.py:193
  134.6 8.1 %collective-permute-start.29 = (f32[64,128]{1,0:T(8,128)S(1)}, f32[64,128]{1,0:T(8,128)S(1)}, u32[]{:S(2)}, u32[]{:S(2)}) collective-permute-start(f32[64,128]{1,0:T(8,128)S(1)} %add.312), channel_id=1, source_target_pairs={{0,4},{1,5},{2,6},{3,7},{4,0},{5,1},{6,2},{7,3},{8,12},{9,13},{10,... | collective-permute-start | bytes 98312 | tf_op jit(solution)/shard_map/ppermute | solution.py:193
  137.6 0.9 copy-start.3
  138.5 39.1 %collective-permute-start.15 = (bf16[48,8192]{1,0:T(8,128)(2,1)S(1)}, bf16[48,8192]{1,0:T(8,128)(2,1)S(1)}, u32[]{:S(2)}, u32[]{:S(2)}) collective-permute-start(bf16[48,8192]{1,0:T(8,128)(2,1)S(1)} %bitcast.72), channel_id=1, source_target_pairs={{0,6},{1,7},{2,0},{3,1},{4,2},{5,3},{6,4},{7,5},{8,14},{9,15},{10,... | collective-permute-start | bytes 2359304 | tf_op jit(solution)/shard_map/ppermute | solution.py:236
  142.7 37.8 %collective-permute-start.16 = (bf16[48,8192]{1,0:T(8,128)(2,1)S(1)}, bf16[48,8192]{1,0:T(8,128)(2,1)S(1)}, u32[]{:S(2)}, u32[]{:S(2)}) collective-permute-start(bf16[48,8192]{1,0:T(8,128)(2,1)S(1)} %bitcast.73), channel_id=1, source_target_pairs={{0,4},{1,5},{2,6},{3,7},{4,0},{5,1},{6,2},{7,3},{8,12},{9,13},{10,... | collective-permute-start | bytes 2359304 | tf_op jit(solution)/shard_map/ppermute | solution.py:236
  142.8 5.2 %collective-permute-start.30 = (f32[64,128]{1,0:T(8,128)S(1)}, f32[64,128]{1,0:T(8,128)S(1)}, u32[]{:S(2)}, u32[]{:S(2)}) collective-permute-start(f32[64,128]{1,0:T(8,128)S(1)} %get-tuple-element.53), channel_id=1, source_target_pairs={{0,8},{1,9},{2,10},{3,11},{4,12},{5,13},{6,14},{7,15},{8,16},{9,17... | collective-permute-start | bytes 98312 | tf_op jit(solution)/shard_map/ppermute | solution.py:196
  145.9 54.5 %collective-permute-start.18 = (bf16[48,8192]{1,0:T(8,128)(2,1)}, bf16[48,8192]{1,0:T(8,128)(2,1)}, u32[]{:S(2)}, u32[]{:S(2)}) collective-permute-start(bf16[48,8192]{1,0:T(8,128)(2,1)} %bitcast.22), channel_id=1, source_target_pairs={{0,7},{1,6},{2,1},{3,0},{4,3},{5,2},{6,5},{7,4},{8,15},{9,14},{10,... | collective-permute-start | bytes 2359304 | tf_op jit(solution)/shard_map/ppermute | solution.py:236
  145.9 54.5 %collective-permute-start.17 = (bf16[48,8192]{1,0:T(8,128)(2,1)}, bf16[48,8192]{1,0:T(8,128)(2,1)}, u32[]{:S(2)}, u32[]{:S(2)}) collective-permute-start(bf16[48,8192]{1,0:T(8,128)(2,1)} %bitcast.21), channel_id=1, source_target_pairs={{0,3},{1,2},{2,5},{3,4},{4,7},{5,6},{6,1},{7,0},{8,11},{9,10},{10,... | collective-permute-start | bytes 2359304 | tf_op jit(solution)/shard_map/ppermute | solution.py:236
  148.0 5.4 %collective-permute-start.31 = (f32[64,128]{1,0:T(8,128)S(1)}, f32[64,128]{1,0:T(8,128)S(1)}, u32[]{:S(2)}, u32[]{:S(2)}) collective-permute-start(f32[64,128]{1,0:T(8,128)S(1)} %get-tuple-element.53), channel_id=1, source_target_pairs={{0,16},{1,17},{2,18},{3,19},{4,20},{5,21},{6,22},{7,23},{8,24},{9,... | collective-permute-start | bytes 98312 | tf_op jit(solution)/shard_map/ppermute | solution.py:196
  153.4 3.9 %collective-permute-start.32 = (f32[64,128]{1,0:T(8,128)S(1)}, f32[64,128]{1,0:T(8,128)S(1)}, u32[]{:S(2)}, u32[]{:S(2)}) collective-permute-start(f32[64,128]{1,0:T(8,128)S(1)} %get-tuple-element.53), channel_id=1, source_target_pairs={{0,24},{1,25},{2,26},{3,27},{4,28},{5,29},{6,30},{7,31},{8,0},{9,1... | collective-permute-start | bytes 98312 | tf_op jit(solution)/shard_map/ppermute | solution.py:196
  157.3 27.9 %collective-permute-start.33 = (f32[256,128]{1,0:T(8,128)S(1)}, f32[256,128]{1,0:T(8,128)S(1)}, u32[]{:S(2)}, u32[]{:S(2)}) collective-permute-start(f32[256,128]{1,0:T(8,128)S(1)} %bitcast.77), channel_id=1, source_target_pairs={{0,32},{1,33},{2,34},{3,35},{4,36},{5,37},{6,38},{7,39},{8,40},{9,... | collective-permute-start | bytes 393224 | tf_op jit(solution)/shard_map/ppermute | solution.py:196
  177.6 0.9 copy-start.5
  180.6 0.9 copy-start.7
  183.6 16.8 %collective-permute-start.20 = (bf16[48,8192]{1,0:T(8,128)(2,1)}, bf16[48,8192]{1,0:T(8,128)(2,1)}, u32[]{:S(2)}, u32[]{:S(2)}) collective-permute-start(bf16[48,8192]{1,0:T(8,128)(2,1)} %bitcast.24), channel_id=1, source_target_pairs={{0,1},{1,0},{2,3},{3,2},{4,5},{5,4},{6,7},{7,6},{8,9},{9,8},{10,11... | collective-permute-start | bytes 2359304 | tf_op jit(solution)/shard_map/ppermute | solution.py:236
  183.6 21.0 %collective-permute-start.19 = (bf16[48,8192]{1,0:T(8,128)(2,1)}, bf16[48,8192]{1,0:T(8,128)(2,1)}, u32[]{:S(2)}, u32[]{:S(2)}) collective-permute-start(bf16[48,8192]{1,0:T(8,128)(2,1)} %bitcast.23), channel_id=1, source_target_pairs={{0,5},{1,4},{2,7},{3,6},{4,1},{5,0},{6,3},{7,2},{8,13},{9,12},{10,... | collective-permute-start | bytes 2359304 | tf_op jit(solution)/shard_map/ppermute | solution.py:236
  185.2 7.4 %collective-permute-start.34 = (f32[256,128]{1,0:T(8,128)S(1)}, f32[256,128]{1,0:T(8,128)S(1)}, u32[]{:S(2)}, u32[]{:S(2)}) collective-permute-start(f32[256,128]{1,0:T(8,128)S(1)} %bitcast.79), channel_id=1, source_target_pairs={{0,64},{1,65},{2,66},{3,67},{4,68},{5,69},{6,70},{7,71},{8,72},{9,... | collective-permute-start | bytes 393224 | tf_op jit(solution)/shard_map/ppermute | solution.py:196
  192.6 5.2 %collective-permute-start.35 = (f32[256,128]{1,0:T(8,128)S(1)}, f32[256,128]{1,0:T(8,128)S(1)}, u32[]{:S(2)}, u32[]{:S(2)}) collective-permute-start(f32[256,128]{1,0:T(8,128)S(1)} %bitcast.80), channel_id=1, source_target_pairs={{0,96},{1,97},{2,98},{3,99},{4,100},{5,101},{6,102},{7,103},{8,104... | collective-permute-start | bytes 393224 | tf_op jit(solution)/shard_map/ppermute | solution.py:196
  204.6 1.6 copy-start.2
  206.2 1.1 copy-start.4
  207.4 1.1 copy-start.6
  208.5 1.1 copy-start.8
  209.6 0.8 copy-start.13

commit v2 on v1

--- a/solution.py
+++ b/solution.py
@@ -12,7 +12,6 @@
 ROWS = 2 * CAP
 TOKENS = 16384
 AXES = ("seq", "exp")
-WINDOW = 4
 CHUNK = 1024
 F32 = jnp.float32
 BF16 = jnp.bfloat16
@@ -42,9 +41,22 @@
     return [(i, i ^ (d * STRIDE[axis])) for i in range(128)]
 
 
-def after(x, *deps):
-    out = lax.optimization_barrier((x,) + deps)
-    return out[0], out[1:]
+def after(*xs):
+    return lax.optimization_barrier(xs)
+
+
+def ring_permute(v, s, m):
+    perm = [(i, (((i >> 1) + s) % 4) * 2 + ((i & 1) ^ m)) for i in range(8)]
+    return lax.ppermute(v, "exp", perm)
+
+
+def pick(v, axis, i):
+    return lax.dynamic_index_in_dim(v, i, axis, keepdims=False)
+
+
+def slot_numbers(sources):
+    base = jnp.stack(sources).astype(F32) * ROWS
+    return (base[:, None] + jnp.arange(ROWS, dtype=F32)[None, :]).reshape(1, 8 * ROWS)
 
 
 def split3(v):
@@ -136,7 +148,7 @@
 def last_kernel(
     slots_ref, pack_ref, logit_ref, weight_ref, gain_ref, hidden_ref, grad_ref, *refs
 ):
-    blocks, out_ref, scaled_ref = refs[:8], refs[8], refs[9]
+    blocks, out_ref, scaled_ref = refs[:-2], refs[-2], refs[-1]
     pack = pack_ref[...]
     inv = pack[:, 4:5]
     slots = slots_ref[...]
@@ -177,27 +189,19 @@
 
 def reduce_all(v, at):
     v = v.reshape(1024, 128)
-    for axis in ("y", "z"):
-        v = v.reshape((4, v.shape[0] // 4, 128))
-        me = at[axis]
-        got = [
-            lax.ppermute(
-                lax.dynamic_index_in_dim(v, (me + d) & 3, 0, keepdims=False),
-                AXES,
-                shift_perm(axis, d),
-            )
-            for d in (1, 3, 2)
-        ]
-        v = lax.dynamic_index_in_dim(v, me, 0, keepdims=False) + got[0] + got[1] + got[2]
+    steps = [(axis, d) for axis in ("y", "z") for d in (2, 1)]
+    for axis, d in steps:
+        half = v.shape[0] // 2
+        bit = (at[axis] & d) != 0
+        send = jnp.where(bit, v[:half], v[half:])
+        keep = jnp.where(bit, v[half:], v[:half])
+        v = keep + lax.ppermute(send, AXES, xor_perm(axis, d))
     for axis, d in (("c", 1), ("x", 1), ("x", 2)):
         v = v + lax.ppermute(v, AXES, xor_perm(axis, d))
-    for axis in ("z", "y"):
-        me = at[axis]
-        parts = [v] + [lax.ppermute(v, AXES, shift_perm(axis, d)) for d in (1, 2, 3)]
-        full = jnp.zeros((4,) + v.shape, F32)
-        for d, part in enumerate(parts):
-            full = lax.dynamic_update_index_in_dim(full, part, (me - d) & 3, 0)
-        v = full.reshape(4 * v.shape[0], 128)
+    for axis, d in reversed(steps):
+        bit = (at[axis] & d) != 0
+        got = lax.ppermute(v, AXES, xor_perm(axis, d))
+        v = jnp.concatenate([jnp.where(bit, got, v), jnp.where(bit, v, got)], axis=0)
     return v.reshape(EXPERTS, D)
 
 
@@ -207,8 +211,8 @@
     at = coords()
     gain = norm_gain.reshape(1, D)
     sources = [((at["x"] - s) & 3) * 2 + (at["c"] ^ m) for s, m in ROUTES]
-    base = jnp.stack(sources).astype(F32) * ROWS
-    slots = (base[:, None] + jnp.arange(ROWS, dtype=F32)[None, :]).reshape(1, 8 * ROWS)
+    slots = slot_numbers(sources)
+    grad_slots = slot_numbers([sources[i] for i in (0, 7, 1, 4, 2, 5, 3, 6)])
 
     pack, probs, counts = pl.pallas_call(
         pre_kernel,
@@ -221,23 +225,36 @@
         out_specs=(VMEM,) * 3,
         compiler_params=params(16),
     )(expert_ids, router_logits, hidden)
+    me = at["x"] * 2 + at["c"]
+    tally = [counts]
     for axis, d in (("y", 1), ("y", 2), ("z", 1), ("z", 2), ("c", 1), ("x", 1), ("x", 2)):
-        counts = counts + lax.ppermute(counts, AXES, xor_perm(axis, d))
-
-    moved = []
-    for array in (expert_out, expert_grad):
-        for s, m in ROUTES[1:]:
-            n = len(moved)
-            if n >= WINDOW:
-                array, (moved[n - WINDOW],) = after(array, moved[n - WINDOW])
-            to = ((at["x"] + s) & 3) * 2 + (at["c"] ^ m)
-            block = lax.dynamic_slice(array, (0, 0, to * CAP, 0), (1, 2, CAP, D))
-            perm = [(i, ((i // 2 + s) % 4) * 2 + (i % 2 + m) % 2) for i in range(8)]
-            moved.append(lax.ppermute(block.reshape(ROWS, D), "exp", perm))
-    own = [
-        lax.dynamic_slice(a, (0, 0, (at["x"] * 2 + at["c"]) * CAP, 0), (1, 2, CAP, D)).reshape(ROWS, D)
-        for a in (expert_out, expert_grad)
-    ]
+        tally.append(tally[-1] + lax.ppermute(tally[-1], AXES, xor_perm(axis, d)))
+
+    by_core = expert_grad.reshape(2, 4, 2, CAP, D)
+    swap = ring_permute(pick(by_core, 2, at["c"] ^ 1), 0, 1)
+    mine = pick(by_core, 2, at["c"])
+
+    outs = []
+    for n, (s, m) in enumerate(ROUTES[1:]):
+        array = expert_out
+        if n == 3:
+            array, swap = after(array, swap)
+        if n > 3:
+            array, outs[n - 4], tally[2 * n - 6] = after(array, outs[n - 4], tally[2 * n - 6])
+        to = ((at["x"] + s) & 3) * 2 + (at["c"] ^ m)
+        block = lax.dynamic_slice(array, (0, 0, to * CAP, 0), (1, 2, CAP, D))
+        outs.append(ring_permute(block.reshape(ROWS, D), s, m))
+    own_out = lax.dynamic_slice(expert_out, (0, 0, me * CAP, 0), (1, 2, CAP, D)).reshape(ROWS, D)
+
+    grads = [pick(mine, 1, at["x"]).reshape(ROWS, D), pick(swap, 1, at["x"]).reshape(ROWS, D)]
+    for n, s in enumerate((1, 3, 2)):
+        a, b = mine, swap
+        a, b, outs[n + 3] = after(a, b, outs[n + 3])
+        if n == 0:
+            a, tally[7] = after(a, tally[7])
+        to = (at["x"] + s) & 3
+        block = jnp.concatenate([pick(a, 1, to), pick(b, 1, to)], axis=0)
+        grads.append(ring_permute(block.reshape(2 * ROWS, D), s, 0))
 
     logit, partial = pl.pallas_call(
         mid_kernel,
@@ -248,17 +265,17 @@
         in_specs=[VMEM] * 16,
         out_specs=(VMEM,) * 2,
         compiler_params=params(24),
-    )(slots, pack, expert_ids, probs, counts, gain, hidden, grad_out, own[0], *moved[:7])
+    )(slots, pack, expert_ids, probs, tally[7], gain, hidden, grad_out, own_out, *outs)
     router_grad = reduce_all(partial, at)
 
     grad_hidden = pl.pallas_call(
         last_kernel,
         out_shape=jax.ShapeDtypeStruct((TOK, D), BF16),
-        in_specs=[VMEM] * 15,
+        in_specs=[VMEM] * 12,
         out_specs=VMEM,
         scratch_shapes=[pltpu.VMEM((TOK, D), F32)],
         compiler_params=params(28),
-    )(slots, pack, logit, router_weight, gain, hidden, grad_out, own[1], *moved[7:])
+    )(grad_slots, pack, logit, router_weight, gain, hidden, grad_out, *grads)
     return grad_hidden, router_grad
 
 

time: 220 us -> 227 us (1.032)
  starting transfers between devices: 44.5 us -> 79.9 us
  waiting for transfers between devices: 115 us -> 92.6 us
  local copies, waits for them, and re-layouts: 42.7 us -> 33.9 us
  other arithmetic: 1.14 us -> 5.21 us
    ppermute x33 -> x26, starting transfers between devices: 43.4 us -> 77.8 us  [the longest x11 43.1 us: ring_permute(): return lax.ppermute(v, 'exp', perm)]
    ppermute x33 -> x26, waiting for transfers between devices: 106 us -> 89.6 us  [the longest x7 49.8 us: body(): tally.append(tally[-1] + lax.ppermute(tally[-1], AXES, xor_perm(axis, d)))]
    dynamic_slice x11 -> x5, local copies, waits for them, and re-layouts: 22.3 us -> 11.8 us  [body(): block = lax.dynamic_slice(array, (0, 0, to * CAP, 0), (1, 2, CAP, D))]
    squeeze x2 -> x4, local copies, waits for them, and re-layouts: 0.81 us -> 10.5 us  [pick(): return lax.dynamic_index_in_dim(v, i, axis, keepdims=False)]
    unnamed x40 -> x24, local copies, waits for them, and re-layouts: 12.6 us -> 5.96 us
    ppermute x3, waiting for transfers between devices: 8.84 us -> 3.09 us  [reduce_all(): v = v + lax.ppermute(v, AXES, xor_perm(axis, d))]
    concatenate x0 -> x7, other arithmetic: none -> 4.8 us  [the longest x3 3.93 us: body(): block = jnp.concatenate([pick(a, 1, to), pick(b, 1, to)], axis=0)]
    dynamic_update_slice x7 -> x0, local copies, waits for them, and re-layouts: 2.68 us -> none  [reduce_all(): full = lax.dynamic_update_index_in_dim(full, part, me - d & 3, 0)]
  transfers between devices with their start and end apart: 36 -> 29, of which waited for: 21 -> 17; matrix products, arithmetic and copies ran while one was open for 12% -> 12% of each run, Pallas kernels for 0% -> 0%
where the time goes in v2:
time: 227 us; the launch traced here: 226 us
  waiting for transfers between devices  92.6 us (41%)
  starting transfers between devices  79.9 us (35%)
  local copies, waits for them, and re-layouts  33.9 us (15%)
  Pallas kernels  13.9 us (6%)
  other arithmetic  5.21 us (2%)
    ppermute x7, waiting for transfers between devices, body(): tally.append(tally[-1] + lax.ppermute(tally[-1], AXES, xor_perm(axis, d)))  49.8 us
    ppermute x11, starting transfers between devices, ring_permute(): return lax.ppermute(v, 'exp', perm)  43.1 us
    ppermute x11, waiting for transfers between devices, ring_permute(): return lax.ppermute(v, 'exp', perm)  22.7 us
    ppermute x7, starting transfers between devices, body(): tally.append(tally[-1] + lax.ppermute(tally[-1], AXES, xor_perm(axis, d)))  14.3 us
    ppermute x4, waiting for transfers between devices, reduce_all(): v = keep + lax.ppermute(send, AXES, xor_perm(axis, d))  12.2 us
    dynamic_slice x5, local copies, waits for them, and re-layouts, body(): block = lax.dynamic_slice(array, (0, 0, to * CAP, 0), (1, 2, CAP, D))  11.8 us
    ppermute x4, starting transfers between devices, reduce_all(): v = keep + lax.ppermute(send, AXES, xor_perm(axis, d))  10.5 us
    squeeze x4, local copies, waits for them, and re-layouts, pick(): return lax.dynamic_index_in_dim(v, i, axis, keepdims=False)  10.5 us
  transfers between devices with their start and end apart: 29, of which 17 were waited for; matrix products, arithmetic and copies ran while one was open for 12% of the time, Pallas kernels for 0%

profile of v2, /device:TPU:0, one launch (start us, length us, event | category | flops | bytes accessed | tf_op | source)
XLA Modules:
  0.0 226.4 jit_solution(2592053360624825537)
XLA Ops:
  0.6 6.4 %dynamic-slice_bitcast_fusion = (bf16[2,4,24,8192]{3,2,1,0:T(8,128)(2,1)}, bf16[2,4,24,8192]{3,2,1,0:T(8,128)(2,1)}) fusion(bf16[2,4,2,24,8192]{4,3,2,1,0:T(8,128)(2,1)} %bitcast.44, s32[]{:T(128)S(6)} %select_n.141, s32[]{:T(128)S(6)} %select_n.140), kind=kLoop, calls=%fused_computation | loop fusion | bytes 12582920 | tf_op jit(solution)/shard_map/jit(dynamic_index_in_dim)/squeeze | solution.py:54
  7.0 3.5 %constant_dynamic-slice_fusion.5 = (bf16[1,2,24,8192]{3,2,1,0:T(8,128)(2,1)}, bf16[1,2,24,8192]{3,2,1,0:T(8,128)(2,1)}, bf16[1,2,24,8192]{3,2,1,0:T(8,128)(2,1)}, bf16[1,2,24,8192]{3,2,1,0:T(8,128)(2,1)S(1)}) fusion(bf16[1,2,192,8192]{3,2,1,0:T(8,128)(2,1)} %param.15, s32[]{:T(128)S(6)} %select_n.146, s32[]{:T(128)S(6)} %select_n.145, s32[]{:T(128)S(6)} %select_n.144, ...), kind=kLoop, calls=%fused_computation.36 | loop fusion | bytes 6291472 | tf_op jit(solution)/shard_map/dynamic_slice | solution.py:245
  10.5 1.6 collective-permute-start.9
  12.1 1.7 collective-permute-start.10
  13.7 1.9 collective-permute-start.11
  15.8 0.6 shard_map.95
  16.5 1.7 collective-permute-start.2
  18.1 2.0 collective-permute-done.2
  20.2 3.2 %collective-permute-start.3 = (f32[8,16]{1,0:T(8,128)S(1)}, f32[8,16]{1,0:T(8,128)S(1)}, u32[]{:S(2)}, u32[]{:S(2)}) collective-permute-start(f32[8,16]{1,0:T(8,128)S(1)} %add.226), channel_id=1, source_target_pairs={{0,64},{1,65},{2,66},{3,67},{4,68},{5,69},{6,70},{7,71},{8,72},{9,... | collective-permute-start | bytes 1544 | tf_op jit(solution)/shard_map/ppermute | solution.py:231
  23.3 1.9 collective-permute-done.3
  25.3 1.9 collective-permute-start.4
  27.2 1.7 collective-permute-done.4
  28.9 3.9 %collective-permute-start.5 = (f32[8,16]{1,0:T(8,128)S(1)}, f32[8,16]{1,0:T(8,128)S(1)}, u32[]{:S(2)}, u32[]{:S(2)}) collective-permute-start(f32[8,16]{1,0:T(8,128)S(1)} %add.228), channel_id=1, source_target_pairs={{0,16},{1,17},{2,18},{3,19},{4,20},{5,21},{6,22},{7,23},{8,24},{9,... | collective-permute-start | bytes 1544 | tf_op jit(solution)/shard_map/ppermute | solution.py:231
  32.8 1.6 collective-permute-done.5
  34.3 1.2 collective-permute-done.6
  35.5 0.6 collective-permute-start.7
  36.1 12.8 %collective-permute-done.7 = f32[8,16]{1,0:T(8,128)S(1)} collective-permute-done((f32[8,16]{1,0:T(8,128)S(1)}, f32[8,16]{1,0:T(8,128)S(1)}, u32[]{:S(2)}, u32[]{:S(2)}) %collective-permute-start.7) | collective-permute-done | bytes 544 | tf_op jit(solution)/shard_map/ppermute | solution.py:231
  48.9 1.0 collective-permute-done.11.refs_3_
  49.9 2.1 constant_dynamic-slice_fusion.4
  52.0 0.7 collective-permute-start.12
  52.6 2.1 constant_dynamic-slice_fusion.3
  54.7 2.3 collective-permute-start.13
  57.0 2.1 constant_dynamic-slice_fusion.9
  59.1 2.2 constant_dynamic-slice_fusion.2
  61.4 3.1 %collective-permute-start.8 = (f32[8,16]{1,0:T(8,128)S(1)}, f32[8,16]{1,0:T(8,128)S(1)}, u32[]{:S(2)}, u32[]{:S(2)}) collective-permute-start(f32[8,16]{1,0:T(8,128)S(1)} %add.231), channel_id=1, source_target_pairs={{0,4},{1,5},{2,6},{3,7},{4,0},{5,1},{6,2},{7,3},{8,12},{9,13},{10,... | collective-permute-start | bytes 1544 | tf_op jit(solution)/shard_map/ppermute | solution.py:231
  64.6 28.7 %collective-permute-done.8 = f32[8,16]{1,0:T(8,128)S(1)} collective-permute-done((f32[8,16]{1,0:T(8,128)S(1)}, f32[8,16]{1,0:T(8,128)S(1)}, u32[]{:S(2)}, u32[]{:S(2)}) %collective-permute-start.8) | collective-permute-done | bytes 544 | tf_op jit(solution)/shard_map/ppermute | solution.py:231
  93.3 1.6 copy-done.1
  94.9 6.0 %shard_map.96 = (f32[128,16]{1,0:T(8,128)S(1)}, f32[16,8192]{1,0:T(8,128)S(1)}) custom-call(f32[1,384]{1,0:T(1,128)S(1)} %add.220.slots_ref, f32[128,8]{1,0:T(8,128)S(1)} %get-tuple-element.26.pack_ref, s32[128,2]{1,0:T(8,128)S(1)} %copy.18.ids_ref, f32[128,16]{1,0:T(8,128)S(1)} %get-tuple-element.27.probs_ref, f32[8,16]{1,0:T(8,128)S(1)} %add.232.counts_ref, ...), custom_call_target="tpu_custom_call" | custom-call | tf_op jit(solution)/shard_map/pallas_call | solution.py:259
  100.9 0.6 copy-done.6
  101.6 3.3 %collective-permute-start.18 = (f32[512,128]{1,0:T(8,128)S(1)}, f32[512,128]{1,0:T(8,128)S(1)}, u32[]{:S(2)}, u32[]{:S(2)}) collective-permute-start(f32[512,128]{1,0:T(8,128)S(1)} %select_n.164), channel_id=1, source_target_pairs={{0,64},{1,65},{2,66},{3,67},{4,68},{5,69},{6,70},{7,71},{8,72},{9,... | collective-permute-start | bytes 786440 | tf_op jit(solution)/shard_map/ppermute | solution.py:198
  104.9 6.5 %collective-permute-done.18 = f32[512,128]{1,0:T(8,128)S(1)} collective-permute-done((f32[512,128]{1,0:T(8,128)S(1)}, f32[512,128]{1,0:T(8,128)S(1)}, u32[]{:S(2)}, u32[]{:S(2)}) %collective-permute-start.18) | collective-permute-done | bytes 262176 | tf_op jit(solution)/shard_map/ppermute | solution.py:198
  111.5 1.7 collective-permute-start.19
  113.1 2.1 constant_dynamic-slice_fusion.1
  115.3 1.2 collective-permute-done.19
  116.6 4.0 %collective-permute-start.20 = (f32[128,128]{1,0:T(8,128)S(1)}, f32[128,128]{1,0:T(8,128)S(1)}, u32[]{:S(2)}, u32[]{:S(2)}) collective-permute-start(f32[128,128]{1,0:T(8,128)S(1)} %slice_select_fusion.3), channel_id=1, source_target_pairs={{0,16},{1,17},{2,18},{3,19},{4,20},{5,21},{6,22},{7,23},{8,24},{9,... | collective-permute-start | bytes 196616 | tf_op jit(solution)/shard_map/ppermute | solution.py:198
  120.5 2.2 collective-permute-done.20
  122.8 1.6 collective-permute-start.21
  124.6 2.2 collective-permute-done.21
  126.9 1.6 dynamic-slice_bitcast_fusion.4
  128.9 1.4 pad_maximum_fusion.1
  130.3 1.7 collective-permute-start.16
  132.0 0.5 collective-permute-done.23
  132.6 1.6 collective-permute-start.24
  134.2 1.2 dynamic-slice_bitcast_fusion.2
  135.4 2.6 %collective-permute-done.24 = f32[64,128]{1,0:T(8,128)S(1)} collective-permute-done((f32[64,128]{1,0:T(8,128)S(1)}, f32[64,128]{1,0:T(8,128)S(1)}, u32[]{:S(2)}, u32[]{:S(2)}) %collective-permute-start.24) | collective-permute-done | bytes 32800 | tf_op jit(solution)/shard_map/ppermute | solution.py:200
  138.0 1.6 collective-permute-start.25
  139.5 1.3 pad_maximum_fusion.2
  140.8 1.6 collective-permute-start.17
  142.5 3.7 %collective-permute-start.26 = (f32[128,128]{1,0:T(8,128)S(1)}, f32[128,128]{1,0:T(8,128)S(1)}, u32[]{:S(2)}, u32[]{:S(2)}) collective-permute-start(f32[128,128]{1,0:T(8,128)S(1)} %pad_maximum_fusion.6), channel_id=1, source_target_pairs={{0,16},{1,17},{2,18},{3,19},{4,20},{5,21},{6,22},{7,23},{8,24},{9,... | collective-permute-start | bytes 196616 | tf_op jit(solution)/shard_map/ppermute | solution.py:203
  146.2 1.2 dynamic-slice_bitcast_fusion.6
  147.4 1.0 collective-permute-done.26
  148.4 1.6 collective-permute-start.27
  150.1 1.3 pad_maximum_fusion
  151.4 31.6 %collective-permute-start.15 = (bf16[96,8192]{1,0:T(8,128)(2,1)}, bf16[96,8192]{1,0:T(8,128)(2,1)}, u32[]{:S(2)}, u32[]{:S(2)}) collective-permute-start(bf16[96,8192]{1,0:T(8,128)(2,1)} %bitcast.24), channel_id=1, source_target_pairs={{0,2},{1,3},{2,4},{3,5},{4,6},{5,7},{6,0},{7,1},{8,10},{9,11},{10,... | collective-permute-start | bytes 4718600 | tf_op jit(solution)/shard_map/ppermute | solution.py:50
  183.0 3.0 %collective-permute-start.28 = (f32[512,128]{1,0:T(8,128)S(1)}, f32[512,128]{1,0:T(8,128)S(1)}, u32[]{:S(2)}, u32[]{:S(2)}) collective-permute-start(f32[512,128]{1,0:T(8,128)S(1)} %pad_maximum_fusion.4), channel_id=1, source_target_pairs={{0,64},{1,65},{2,66},{3,67},{4,68},{5,69},{6,70},{7,71},{8,72},{9,... | collective-permute-start | bytes 786440 | tf_op jit(solution)/shard_map/ppermute | solution.py:203
  186.0 1.2 constant_dynamic-slice_fusion
  187.2 3.8 %collective-permute-done.28 = f32[512,128]{1,0:T(8,128)S(1)} collective-permute-done((f32[512,128]{1,0:T(8,128)S(1)}, f32[512,128]{1,0:T(8,128)S(1)}, u32[]{:S(2)}, u32[]{:S(2)}) %collective-permute-start.28) | collective-permute-done | bytes 262176 | tf_op jit(solution)/shard_map/ppermute | solution.py:203
  191.0 0.8 pad_maximum_fusion.3
  191.8 1.9 reshape.256
  193.8 21.7 %collective-permute-done.15.refs_2_ = bf16[96,8192]{1,0:T(8,128)(2,1)} collective-permute-done((bf16[96,8192]{1,0:T(8,128)(2,1)}, bf16[96,8192]{1,0:T(8,128)(2,1)}, u32[]{:S(2)}, u32[]{:S(2)}) %collective-permute-start.15) | collective-permute-done | bytes 1572896 | tf_op jit(solution)/shard_map/ppermute | solution.py:50
  215.5 1.6 copy-done.2
  217.1 1.1 copy-done.3
  218.2 0.8 copy-done.7
  219.1 7.3 %shard_map.97 = bf16[128,8192]{1,0:T(8,128)(2,1)} custom-call(f32[1,384]{1,0:T(1,128)S(1)} %add.216.slots_ref, f32[128,8]{1,0:T(8,128)S(1)} %get-tuple-element.26.pack_ref, f32[128,16]{1,0:T(8,128)S(1)} %copy-done.7, f32[16,8192]{1,0:T(8,128)S(1)} %copy-done.4, f32[1,8192]{1,0:T(1,128)S(1)} %bitcast.43, bf16[128,8192]{1,0:T(8,128)(2,1)S(1)} %copy-done, ...), custom_call_target="tpu_custom_call" | custom-call | tf_op jit(solution)/shard_map/pallas_call | solution.py:271
  (72 shorter events, 1.7 us)
Async XLA Ops:
  7.0 50.0 %collective-permute-start = (bf16[2,4,24,8192]{3,2,1,0:T(8,128)(2,1)}, bf16[2,4,24,8192]{3,2,1,0:T(8,128)(2,1)}, u32[]{:S(2)}, u32[]{:S(2)}) collective-permute-start(bf16[2,4,24,8192]{3,2,1,0:T(8,128)(2,1)} %get-tuple-element.54), channel_id=1, source_target_pairs={{0,1},{1,0},{2,3},{3,2},{4,5},{5,4},{6,7},{7,6},{8,9},{9,8},{10,11... | collective-permute-start | bytes 9437192 | tf_op jit(solution)/shard_map/ppermute | solution.py:50
  7.0 8.6 %copy-start.10 = (s32[128,2]{0,1:T(2,128)S(1)}, s32[128,2]{0,1:T(2,128)}, u32[]{:S(2)}) copy-start(s32[128,2]{0,1:T(2,128)} %param.13) | copy-start | bytes 3076
  7.0 8.7 %copy-start.9 = (f32[128,16]{0,1:T(8,128)S(1)}, f32[128,16]{0,1:T(8,128)}, u32[]{:S(2)}) copy-start(f32[128,16]{0,1:T(8,128)} %param.11) | copy-start | bytes 24580
  7.0 8.8 %copy-start = (bf16[128,8192]{1,0:T(8,128)(2,1)S(1)}, bf16[128,8192]{1,0:T(8,128)(2,1)}, u32[]{:S(2)}) copy-start(bf16[128,8192]{1,0:T(8,128)(2,1)} %hidden_ref.5) | copy-start | bytes 6291460
  10.5 38.4 %collective-permute-start.9 = (bf16[48,8192]{1,0:T(8,128)(2,1)}, bf16[48,8192]{1,0:T(8,128)(2,1)}, u32[]{:S(2)}, u32[]{:S(2)}) collective-permute-start(bf16[48,8192]{1,0:T(8,128)(2,1)} %bitcast.14), channel_id=1, source_target_pairs={{0,2},{1,3},{2,4},{3,5},{4,6},{5,7},{6,0},{7,1},{8,10},{9,11},{10,... | collective-permute-start | bytes 2359304 | tf_op jit(solution)/shard_map/ppermute | solution.py:50
  12.1 36.9 %collective-permute-start.10 = (bf16[48,8192]{1,0:T(8,128)(2,1)}, bf16[48,8192]{1,0:T(8,128)(2,1)}, u32[]{:S(2)}, u32[]{:S(2)}) collective-permute-start(bf16[48,8192]{1,0:T(8,128)(2,1)} %bitcast.15), channel_id=1, source_target_pairs={{0,6},{1,7},{2,0},{3,1},{4,2},{5,3},{6,4},{7,5},{8,14},{9,15},{10,... | collective-permute-start | bytes 2359304 | tf_op jit(solution)/shard_map/ppermute | solution.py:50
  13.7 36.2 %collective-permute-start.11 = (bf16[48,8192]{1,0:T(8,128)(2,1)}, bf16[48,8192]{1,0:T(8,128)(2,1)}, u32[]{:S(2)}, u32[]{:S(2)}) collective-permute-start(bf16[48,8192]{1,0:T(8,128)(2,1)} %bitcast.16), channel_id=1, source_target_pairs={{0,4},{1,5},{2,6},{3,7},{4,0},{5,1},{6,2},{7,3},{8,12},{9,13},{10,... | collective-permute-start | bytes 2359304 | tf_op jit(solution)/shard_map/ppermute | solution.py:50
  16.5 3.7 %collective-permute-start.2 = (f32[8,16]{1,0:T(8,128)S(1)}, f32[8,16]{1,0:T(8,128)S(1)}, u32[]{:S(2)}, u32[]{:S(2)}) collective-permute-start(f32[8,16]{1,0:T(8,128)S(1)} %get-tuple-element.31), channel_id=1, source_target_pairs={{0,32},{1,33},{2,34},{3,35},{4,36},{5,37},{6,38},{7,39},{8,40},{9,... | collective-permute-start | bytes 1544 | tf_op jit(solution)/shard_map/ppermute | solution.py:231
  20.2 5.1 %collective-permute-start.3 = (f32[8,16]{1,0:T(8,128)S(1)}, f32[8,16]{1,0:T(8,128)S(1)}, u32[]{:S(2)}, u32[]{:S(2)}) collective-permute-start(f32[8,16]{1,0:T(8,128)S(1)} %add.226), channel_id=1, source_target_pairs={{0,64},{1,65},{2,66},{3,67},{4,68},{5,69},{6,70},{7,71},{8,72},{9,... | collective-permute-start | bytes 1544 | tf_op jit(solution)/shard_map/ppermute | solution.py:231
  25.3 3.6 %collective-permute-start.4 = (f32[8,16]{1,0:T(8,128)S(1)}, f32[8,16]{1,0:T(8,128)S(1)}, u32[]{:S(2)}, u32[]{:S(2)}) collective-permute-start(f32[8,16]{1,0:T(8,128)S(1)} %add.227), channel_id=1, source_target_pairs={{0,8},{1,9},{2,10},{3,11},{4,12},{5,13},{6,14},{7,15},{8,0},{9,1},... | collective-permute-start | bytes 1544 | tf_op jit(solution)/shard_map/ppermute | solution.py:231
  28.9 5.5 %collective-permute-start.5 = (f32[8,16]{1,0:T(8,128)S(1)}, f32[8,16]{1,0:T(8,128)S(1)}, u32[]{:S(2)}, u32[]{:S(2)}) collective-permute-start(f32[8,16]{1,0:T(8,128)S(1)} %add.228), channel_id=1, source_target_pairs={{0,16},{1,17},{2,18},{3,19},{4,20},{5,21},{6,22},{7,23},{8,24},{9,... | collective-permute-start | bytes 1544 | tf_op jit(solution)/shard_map/ppermute | solution.py:231
  34.3 1.2 collective-permute-start.6
  35.5 13.4 %collective-permute-start.7 = (f32[8,16]{1,0:T(8,128)S(1)}, f32[8,16]{1,0:T(8,128)S(1)}, u32[]{:S(2)}, u32[]{:S(2)}) collective-permute-start(f32[8,16]{1,0:T(8,128)S(1)} %add.230), channel_id=1, source_target_pairs={{0,2},{1,3},{2,0},{3,1},{4,6},{5,7},{6,4},{7,5},{8,10},{9,11},{10,... | collective-permute-start | bytes 1544 | tf_op jit(solution)/shard_map/ppermute | solution.py:231
  48.9 44.4 %copy-start.5 = (f32[8192]{0:T(1024)S(1)}, f32[8192]{0:T(1024)}, u32[]{:S(2)}) copy-start(f32[8192]{0:T(1024)} %param.10) | copy-start | bytes 98308
  52.0 41.3 %collective-permute-start.12 = (bf16[48,8192]{1,0:T(8,128)(2,1)}, bf16[48,8192]{1,0:T(8,128)(2,1)}, u32[]{:S(2)}, u32[]{:S(2)}) collective-permute-start(bf16[48,8192]{1,0:T(8,128)(2,1)} %bitcast.17), channel_id=1, source_target_pairs={{0,7},{1,6},{2,1},{3,0},{4,3},{5,2},{6,5},{7,4},{8,15},{9,14},{10,... | collective-permute-start | bytes 2359304 | tf_op jit(solution)/shard_map/ppermute | solution.py:50
  54.7 38.6 %collective-permute-start.13 = (bf16[48,8192]{1,0:T(8,128)(2,1)}, bf16[48,8192]{1,0:T(8,128)(2,1)}, u32[]{:S(2)}, u32[]{:S(2)}) collective-permute-start(bf16[48,8192]{1,0:T(8,128)(2,1)} %bitcast.18), channel_id=1, source_target_pairs={{0,5},{1,4},{2,7},{3,6},{4,1},{5,0},{6,3},{7,2},{8,13},{9,12},{10,... | collective-permute-start | bytes 2359304 | tf_op jit(solution)/shard_map/ppermute | solution.py:50
  59.1 34.2 %collective-permute-start.1 = (bf16[48,8192]{1,0:T(8,128)(2,1)}, bf16[48,8192]{1,0:T(8,128)(2,1)}, u32[]{:S(2)}, u32[]{:S(2)}) collective-permute-start(bf16[48,8192]{1,0:T(8,128)(2,1)} %bitcast.11), channel_id=1, source_target_pairs={{0,3},{1,2},{2,5},{3,4},{4,7},{5,6},{6,1},{7,0},{8,11},{9,10},{10,... | collective-permute-start | bytes 2359304 | tf_op jit(solution)/shard_map/ppermute | solution.py:50
  61.2 32.1 %collective-permute-start.14 = (bf16[48,8192]{1,0:T(8,128)(2,1)}, bf16[48,8192]{1,0:T(8,128)(2,1)}, u32[]{:S(2)}, u32[]{:S(2)}) collective-permute-start(bf16[48,8192]{1,0:T(8,128)(2,1)} %bitcast.19), channel_id=1, source_target_pairs={{0,1},{1,0},{2,3},{3,2},{4,5},{5,4},{6,7},{7,6},{8,9},{9,8},{10,11... | collective-permute-start | bytes 2359304 | tf_op jit(solution)/shard_map/ppermute | solution.py:50
  61.4 31.9 %collective-permute-start.8 = (f32[8,16]{1,0:T(8,128)S(1)}, f32[8,16]{1,0:T(8,128)S(1)}, u32[]{:S(2)}, u32[]{:S(2)}) collective-permute-start(f32[8,16]{1,0:T(8,128)S(1)} %add.231), channel_id=1, source_target_pairs={{0,4},{1,5},{2,6},{3,7},{4,0},{5,1},{6,2},{7,3},{8,12},{9,13},{10,... | collective-permute-start | bytes 1544 | tf_op jit(solution)/shard_map/ppermute | solution.py:231
  93.3 1.6 copy-start.1
  100.9 0.6 copy-start.6
  101.6 9.8 %collective-permute-start.18 = (f32[512,128]{1,0:T(8,128)S(1)}, f32[512,128]{1,0:T(8,128)S(1)}, u32[]{:S(2)}, u32[]{:S(2)}) collective-permute-start(f32[512,128]{1,0:T(8,128)S(1)} %select_n.164), channel_id=1, source_target_pairs={{0,64},{1,65},{2,66},{3,67},{4,68},{5,69},{6,70},{7,71},{8,72},{9,... | collective-permute-start | bytes 786440 | tf_op jit(solution)/shard_map/ppermute | solution.py:198
  111.5 5.0 %collective-permute-start.19 = (f32[256,128]{1,0:T(8,128)S(1)}, f32[256,128]{1,0:T(8,128)S(1)}, u32[]{:S(2)}, u32[]{:S(2)}) collective-permute-start(f32[256,128]{1,0:T(8,128)S(1)} %slice_select_fusion.2), channel_id=1, source_target_pairs={{0,32},{1,33},{2,34},{3,35},{4,36},{5,37},{6,38},{7,39},{8,40},{9,... | collective-permute-start | bytes 393224 | tf_op jit(solution)/shard_map/ppermute | solution.py:198
  116.6 6.2 %collective-permute-start.20 = (f32[128,128]{1,0:T(8,128)S(1)}, f32[128,128]{1,0:T(8,128)S(1)}, u32[]{:S(2)}, u32[]{:S(2)}) collective-permute-start(f32[128,128]{1,0:T(8,128)S(1)} %slice_select_fusion.3), channel_id=1, source_target_pairs={{0,16},{1,17},{2,18},{3,19},{4,20},{5,21},{6,22},{7,23},{8,24},{9,... | collective-permute-start | bytes 196616 | tf_op jit(solution)/shard_map/ppermute | solution.py:198
  122.8 4.0 %collective-permute-start.21 = (f32[64,128]{1,0:T(8,128)S(1)}, f32[64,128]{1,0:T(8,128)S(1)}, u32[]{:S(2)}, u32[]{:S(2)}) collective-permute-start(f32[64,128]{1,0:T(8,128)S(1)} %slice_select_fusion.4), channel_id=1, source_target_pairs={{0,8},{1,9},{2,10},{3,11},{4,12},{5,13},{6,14},{7,15},{8,0},{9,1},... | collective-permute-start | bytes 98312 | tf_op jit(solution)/shard_map/ppermute | solution.py:198
  126.8 7.4 %copy-start.8 = (bf16[2,4,24,8192]{3,2,1,0:T(8,128)(2,1)S(1)}, bf16[2,4,24,8192]{3,2,1,0:T(8,128)(2,1)}, u32[]{:S(2)}) copy-start(bf16[2,4,24,8192]{3,2,1,0:T(8,128)(2,1)} %get-tuple-element.47) | copy-start | bytes 9437188
  126.8 1.7 collective-permute-start.22
  128.6 4.0 %collective-permute-start.23 = (f32[64,128]{1,0:T(8,128)S(1)}, f32[64,128]{1,0:T(8,128)S(1)}, u32[]{:S(2)}, u32[]{:S(2)}) collective-permute-start(f32[64,128]{1,0:T(8,128)S(1)} %add.256), channel_id=1, source_target_pairs={{0,2},{1,3},{2,0},{3,1},{4,6},{5,7},{6,4},{7,5},{8,10},{9,11},{10,... | collective-permute-start | bytes 98312 | tf_op jit(solution)/shard_map/ppermute | solution.py:200
  130.3 63.5 %collective-permute-start.16 = (bf16[96,8192]{1,0:T(8,128)(2,1)}, bf16[96,8192]{1,0:T(8,128)(2,1)}, u32[]{:S(2)}, u32[]{:S(2)}) collective-permute-start(bf16[96,8192]{1,0:T(8,128)(2,1)} %bitcast.27), channel_id=1, source_target_pairs={{0,6},{1,7},{2,0},{3,1},{4,2},{5,3},{6,4},{7,5},{8,14},{9,15},{10,... | collective-permute-start | bytes 4718600 | tf_op jit(solution)/shard_map/ppermute | solution.py:50
  132.6 5.4 %collective-permute-start.24 = (f32[64,128]{1,0:T(8,128)S(1)}, f32[64,128]{1,0:T(8,128)S(1)}, u32[]{:S(2)}, u32[]{:S(2)}) collective-permute-start(f32[64,128]{1,0:T(8,128)S(1)} %add.257), channel_id=1, source_target_pairs={{0,4},{1,5},{2,6},{3,7},{4,0},{5,1},{6,2},{7,3},{8,12},{9,13},{10,... | collective-permute-start | bytes 98312 | tf_op jit(solution)/shard_map/ppermute | solution.py:200
  138.0 4.5 %collective-permute-start.25 = (f32[64,128]{1,0:T(8,128)S(1)}, f32[64,128]{1,0:T(8,128)S(1)}, u32[]{:S(2)}, u32[]{:S(2)}) collective-permute-start(f32[64,128]{1,0:T(8,128)S(1)} %add.258), channel_id=1, source_target_pairs={{0,8},{1,9},{2,10},{3,11},{4,12},{5,13},{6,14},{7,15},{8,0},{9,1},... | collective-permute-start | bytes 98312 | tf_op jit(solution)/shard_map/ppermute | solution.py:203
  140.8 52.9 %collective-permute-start.17 = (bf16[96,8192]{1,0:T(8,128)(2,1)}, bf16[96,8192]{1,0:T(8,128)(2,1)}, u32[]{:S(2)}, u32[]{:S(2)}) collective-permute-start(bf16[96,8192]{1,0:T(8,128)(2,1)} %bitcast.30), channel_id=1, source_target_pairs={{0,4},{1,5},{2,6},{3,7},{4,0},{5,1},{6,2},{7,3},{8,12},{9,13},{10,... | collective-permute-start | bytes 4718600 | tf_op jit(solution)/shard_map/ppermute | solution.py:50
  142.5 5.9 %collective-permute-start.26 = (f32[128,128]{1,0:T(8,128)S(1)}, f32[128,128]{1,0:T(8,128)S(1)}, u32[]{:S(2)}, u32[]{:S(2)}) collective-permute-start(f32[128,128]{1,0:T(8,128)S(1)} %pad_maximum_fusion.6), channel_id=1, source_target_pairs={{0,16},{1,17},{2,18},{3,19},{4,20},{5,21},{6,22},{7,23},{8,24},{9,... | collective-permute-start | bytes 196616 | tf_op jit(solution)/shard_map/ppermute | solution.py:203
  148.4 34.5 %collective-permute-start.27 = (f32[256,128]{1,0:T(8,128)S(1)}, f32[256,128]{1,0:T(8,128)S(1)}, u32[]{:S(2)}, u32[]{:S(2)}) collective-permute-start(f32[256,128]{1,0:T(8,128)S(1)} %pad_maximum_fusion.5), channel_id=1, source_target_pairs={{0,32},{1,33},{2,34},{3,35},{4,36},{5,37},{6,38},{7,39},{8,40},{9,... | collective-permute-start | bytes 393224 | tf_op jit(solution)/shard_map/ppermute | solution.py:203
  151.4 64.1 %copy-start.4 = (f32[16,8192]{1,0:T(8,128)S(1)}, f32[16,8192]{1,0:T(8,128)}, u32[]{:S(2)}) copy-start(f32[16,8192]{1,0:T(8,128)} %weight_ref.1) | copy-start | bytes 1572868
  151.4 64.1 %collective-permute-start.15 = (bf16[96,8192]{1,0:T(8,128)(2,1)}, bf16[96,8192]{1,0:T(8,128)(2,1)}, u32[]{:S(2)}, u32[]{:S(2)}) collective-permute-start(bf16[96,8192]{1,0:T(8,128)(2,1)} %bitcast.24), channel_id=1, source_target_pairs={{0,2},{1,3},{2,4},{3,5},{4,6},{5,7},{6,0},{7,1},{8,10},{9,11},{10,... | collective-permute-start | bytes 4718600 | tf_op jit(solution)/shard_map/ppermute | solution.py:50
  183.0 8.0 %collective-permute-start.28 = (f32[512,128]{1,0:T(8,128)S(1)}, f32[512,128]{1,0:T(8,128)S(1)}, u32[]{:S(2)}, u32[]{:S(2)}) collective-permute-start(f32[512,128]{1,0:T(8,128)S(1)} %pad_maximum_fusion.4), channel_id=1, source_target_pairs={{0,64},{1,65},{2,66},{3,67},{4,68},{5,69},{6,70},{7,71},{8,72},{9,... | collective-permute-start | bytes 786440 | tf_op jit(solution)/shard_map/ppermute | solution.py:203
  215.5 1.6 copy-start.2
  217.1 1.1 copy-start.3
  218.2 0.8 copy-start.7

commit v3 on v2

v3 whole, which is shorter than its diff:
```python
import jax
import jax.numpy as jnp
from jax import lax
from jax.experimental import pallas as pl
from jax.experimental.pallas import tpu as pltpu
from jax.sharding import PartitionSpec as P

D = 8192
EXPERTS = 16
TOK = 128
CAP = 24
ROWS = 2 * CAP
TOKENS = 16384
AXES = ("seq", "exp")
CHUNK = 1024
F32 = jnp.float32
BF16 = jnp.bfloat16
VMEM = pl.BlockSpec(memory_space=pltpu.VMEM)

ROUTES = ((0, 0), (1, 0), (3, 0), (2, 0), (1, 1), (3, 1), (2, 1), (0, 1))


def coords():
    s, e = lax.axis_index("seq"), lax.axis_index("exp")
    return {"y": s >> 2, "z": s & 3, "x": e >> 1, "c": e & 1}


STRIDE = {"y": 32, "z": 8, "x": 2, "c": 1}
SIZE = {"y": 4, "z": 4, "x": 4, "c": 2}


def shift_perm(axis, d):
    out = []
    for i in range(128):
        a = (i // STRIDE[axis]) % SIZE[axis]
        out.append((i, i + ((a + d) % SIZE[axis] - a) * STRIDE[axis]))
    return out


def xor_perm(axis, d):
    return [(i, i ^ (d * STRIDE[axis])) for i in range(128)]


def after(*xs):
    return lax.optimization_barrier(xs)


def ring_permute(v, s, m):
    perm = [(i, (((i >> 1) + s) % 4) * 2 + ((i & 1) ^ m)) for i in range(8)]
    return lax.ppermute(v, "exp", perm)


def pick(v, axis, i):
    return lax.dynamic_index_in_dim(v, i, axis, keepdims=False)


def slot_numbers(sources):
    base = jnp.stack(sources).astype(F32) * ROWS
    return (base[:, None] + jnp.arange(ROWS, dtype=F32)[None, :]).reshape(1, 8 * ROWS)


def split3(v):
    a = v.astype(BF16)
    r = v - a.astype(F32)
    b = r.astype(BF16)
    c = (r - b.astype(F32)).astype(BF16)
    return a, b, c


def pre_kernel(ids_ref, logits_ref, hidden_ref, pack_ref, probs_ref, counts_ref):
    ids = ids_ref[...]
    logits = logits_ref[...]
    labels = lax.broadcasted_iota(jnp.int32, (TOK, EXPERTS), 1)
    oh = [(ids[:, k : k + 1] == labels).astype(F32) for k in range(2)]
    both = oh[0] + oh[1]
    row = lax.broadcasted_iota(jnp.int32, (TOK, TOK), 0)
    col = lax.broadcasted_iota(jnp.int32, (TOK, TOK), 1)
    before = (row > col).astype(F32).astype(BF16)
    ranks = jnp.dot(before, both.astype(BF16), preferred_element_type=F32)
    counts_ref[...] = jnp.broadcast_to(jnp.sum(both, axis=0, keepdims=True), (8, EXPERTS))
    index = [
        jnp.sum(oh[k] * (ranks + (CAP * labels).astype(F32)), axis=1, keepdims=True)
        for k in range(2)
    ]
    chosen = [jnp.sum(oh[k] * logits, axis=1, keepdims=True) for k in range(2)]
    top = jnp.maximum(chosen[0], chosen[1])
    w = [jnp.exp(c - top) for c in chosen]
    total = w[0] + w[1]
    e = jnp.exp(logits - jnp.max(logits, axis=1, keepdims=True))
    probs_ref[...] = e / jnp.sum(e, axis=1, keepdims=True)
    square = jnp.zeros((TOK, 128), F32)
    for c in range(D // CHUNK):
        h = hidden_ref[:, c * CHUNK : (c + 1) * CHUNK].astype(F32)
        h = h * h
        for j in range(CHUNK // 128):
            square = square + h[:, j * 128 : (j + 1) * 128]
    inv = lax.rsqrt(jnp.sum(square, axis=1, keepdims=True) / D + 1e-05)
    lane = lax.broadcasted_iota(jnp.int32, (TOK, 8), 1)
    pack = jnp.zeros((TOK, 8), F32)
    for i, v in enumerate((w[0] / total, w[1] / total, index[0], index[1], inv)):
        pack = jnp.where(lane == i, v, pack)
    pack_ref[...] = pack


def mid_kernel(
    slots_ref, pack_ref, ids_ref, probs_ref, counts_ref, gain_ref, hidden_ref, grad_ref, *refs
):
    blocks, (logit_ref, partial_ref, dots_ref, left_ref) = refs[:8], refs[8:]
    stage, c = pl.program_id(0), pl.program_id(1)

    @pl.when(stage == 0)
    def _():
        picked = jnp.concatenate([b[...] for b in blocks], axis=0)
        d = lax.dot_general(
            grad_ref[...], picked, (((1,), (1,)), ((), ())), preferred_element_type=F32
        )

        @pl.when(c == 0)
        def _():
            dots_ref[...] = d

        @pl.when(c > 0)
        def _():
            dots_ref[...] += d

    @pl.when((stage == 1) & (c == 0))
    def _():
        pack = pack_ref[...]
        gate = [pack[:, 0:1], pack[:, 1:2]]
        slots = slots_ref[...]
        dots = dots_ref[...]
        gate_dot = [
            jnp.sum(jnp.where(slots == pack[:, 2 + k : 3 + k], dots, 0.0), axis=1, keepdims=True)
            .astype(BF16)
            .astype(F32)
            for k in range(2)
        ]
        mean = gate[0] * gate_dot[0] + gate[1] * gate_dot[1]
        ids = ids_ref[...]
        labels = lax.broadcasted_iota(jnp.int32, (TOK, EXPERTS), 1)
        direct = jnp.zeros((TOK, EXPERTS), F32)
        for k in range(2):
            chosen = gate[k] * (gate_dot[k] - mean)
            direct = direct + jnp.where(ids[:, k : k + 1] == labels, chosen, 0.0)
        probs = probs_ref[...]
        load = counts_ref[0:1, :] * (EXPERTS / (2 * TOKENS))
        aux = probs * (load - jnp.sum(probs * load, axis=1, keepdims=True))
        logit = direct + aux
        logit_ref[...] = logit
        left_ref[...] = jnp.concatenate(split3(logit * pack[:, 4:5]), axis=1)

    @pl.when(stage == 1)
    def _():
        p = lax.dot_general(
            left_ref[...], hidden_ref[...], (((0,), (0,)), ((), ())), preferred_element_type=F32
        )
        p = (p[0:16] + p[16:32] + p[32:48]) * (gain_ref[...] * (1.0 / 128.0))
        for j in range(WIDE // 1024):
            partial_ref[:, c * (WIDE // 1024) + j, :] = p[:, j * 1024 : (j + 1) * 1024]


def last_kernel(
    slots_ref, pack_ref, logit_ref, weight_ref, gain_ref, hidden_ref, grad_ref, *refs
):
    blocks, (out_ref, scaled_ref, normed_ref, left_ref, acc_ref, factor_ref) = refs[:-6], refs[-6:]
    stage, c = pl.program_id(0), pl.program_id(1)
    cols = pl.ds(pl.multiple_of(c * WIDE, WIDE), WIDE)

    @pl.when((stage == 0) & (c == 0))
    def _():
        pack = pack_ref[...]
        slots = slots_ref[...]
        w = jnp.where(slots == pack[:, 2:3], pack[:, 0:1], 0.0)
        w = w + jnp.where(slots == pack[:, 3:4], pack[:, 1:2], 0.0)
        w_hi, w_lo, _ = split3(w)
        l0, l1, l2 = split3(logit_ref[...])
        zero = jnp.zeros_like(l0)
        left_ref[...] = jnp.concatenate(
            [
                jnp.concatenate([w_hi, l0, l0, l0, l2], axis=1),
                jnp.concatenate([w_lo, l1, l1, zero, zero], axis=1),
            ],
            axis=0,
        )
        acc_ref[...] = jnp.zeros_like(acc_ref)

    @pl.when(stage == 0)
    def _():
        r0, r1, r2 = split3(weight_ref[...])
        right = jnp.concatenate([b[...] for b in blocks] + [r0, r1, r2, r0], axis=0)
        both = jnp.dot(left_ref[...], right, preferred_element_type=F32)
        scaled = (both[:TOK] + both[TOK:]) * gain_ref[...]
        scaled_ref[:, cols] = scaled
        hidden = hidden_ref[...]
        normed_ref[:, cols] = hidden
        prod = scaled * hidden.astype(F32)
        acc = acc_ref[...]
        for j in range(WIDE // 128):
            acc = acc + prod[:, j * 128 : (j + 1) * 128]
        acc_ref[...] = acc

    @pl.when((stage == 1) & (c == 0))
    def _():
        inv = pack_ref[:, 4:5]
        mean = jnp.sum(acc_ref[...], axis=1, keepdims=True) * inv / D
        factor_ref[...] = jnp.broadcast_to(inv * mean, (TOK, 128))

    @pl.when(stage == 1)
    def _():
        inv = pack_ref[:, 4:5]
        factor = factor_ref[:, 0:1]
        back = inv * (scaled_ref[:, cols] - normed_ref[:, cols].astype(F32) * factor)
        out_ref[...] = (grad_ref[...].astype(F32) + back).astype(BF16)


STEPS = 4
WIDE = D // STEPS


def first(rows):
    return pl.BlockSpec((rows, WIDE), lambda p, c: (0, jnp.where(p == 0, c, STEPS - 1)))


def second(rows):
    return pl.BlockSpec((rows, WIDE), lambda p, c: (0, jnp.where(p == 0, 0, c)))


def params(mib):
    return pltpu.CompilerParams(vmem_limit_bytes=mib * 1024 * 1024)


def reduce_all(v):
    v = jnp.sum(lax.all_to_all(v, "seq", 0, 0, tiled=True), axis=0)
    for axis, d in (("c", 1), ("x", 1), ("x", 2)):
        v = v + lax.ppermute(v, AXES, xor_perm(axis, d))
    return lax.all_gather(v, "seq").reshape(EXPERTS, D)


def body(
    grad_out, hidden, norm_gain, router_logits, router_weight, expert_ids, expert_grad, expert_out
):
    at = coords()
    gain = norm_gain.reshape(1, D)
    sources = [((at["x"] - s) & 3) * 2 + (at["c"] ^ m) for s, m in ROUTES]
    slots = slot_numbers(sources)
    grad_slots = slot_numbers([sources[i] for i in (0, 7, 1, 4, 2, 5, 3, 6)])

    pack, probs, counts = pl.pallas_call(
        pre_kernel,
        out_shape=(
            jax.ShapeDtypeStruct((TOK, 8), F32),
            jax.ShapeDtypeStruct((TOK, EXPERTS), F32),
            jax.ShapeDtypeStruct((8, EXPERTS), F32),
        ),
        in_specs=[VMEM] * 3,
        out_specs=(VMEM,) * 3,
        compiler_params=params(16),
    )(expert_ids, router_logits, hidden)
    me = at["x"] * 2 + at["c"]
    tally = [counts]
    for axis, d in (("c", 1), ("x", 1), ("x", 2), ("y", 1), ("y", 2), ("z", 1), ("z", 2)):
        tally.append(tally[-1] + lax.ppermute(tally[-1], AXES, xor_perm(axis, d)))

    source, tally[2] = after(expert_grad, tally[2])
    by_core = source.reshape(2, 4, 2, CAP, D)
    swap = ring_permute(pick(by_core, 2, at["c"] ^ 1), 0, 1)
    mine = pick(by_core, 2, at["c"])

    outs = []
    for n, (s, m) in enumerate(ROUTES[1:]):
        array = expert_out
        if n > 3:
            array, outs[n - 4], tally[2 * n - 5] = after(array, outs[n - 4], tally[2 * n - 5])
        to = ((at["x"] + s) & 3) * 2 + (at["c"] ^ m)
        block = lax.dynamic_slice(array, (0, 0, to * CAP, 0), (1, 2, CAP, D))
        outs.append(ring_permute(block.reshape(ROWS, D), s, m))
    own_out = lax.dynamic_slice(expert_out, (0, 0, me * CAP, 0), (1, 2, CAP, D)).reshape(ROWS, D)

    grads = [pick(mine, 1, at["x"]).reshape(ROWS, D), pick(swap, 1, at["x"]).reshape(ROWS, D)]
    for n, s in enumerate((1, 3, 2)):
        a, b = mine, swap
        a, b, outs[n + 3] = after(a, b, outs[n + 3])
        to = (at["x"] + s) & 3
        block = jnp.concatenate([pick(a, 1, to), pick(b, 1, to)], axis=0)
        grads.append(ring_permute(block.reshape(2 * ROWS, D), s, 0))

    small = lambda *shape: pl.BlockSpec(shape, lambda p, c: (0,) * len(shape))
    logit, partial = pl.pallas_call(
        mid_kernel,
        grid=(2, STEPS),
        out_shape=(
            jax.ShapeDtypeStruct((TOK, EXPERTS), F32),
            jax.ShapeDtypeStruct((EXPERTS, 8, 1024), F32),
        ),
        in_specs=[
            small(1, 8 * ROWS),
            small(TOK, 8),
            small(TOK, 2),
            small(TOK, EXPERTS),
            small(8, EXPERTS),
            second(1),
            second(TOK),
            first(TOK),
        ]
        + [first(ROWS)] * 8,
        out_specs=(
            small(TOK, EXPERTS),
            small(EXPERTS, 8, 1024),
        ),
        scratch_shapes=[pltpu.VMEM((TOK, 8 * ROWS), F32), pltpu.VMEM((TOK, 3 * EXPERTS), BF16)],
        compiler_params=params(24),
    )(slots, pack, expert_ids, probs, tally[7], gain, hidden, grad_out, own_out, *outs)
    router_grad = reduce_all(partial)

    grad_hidden = pl.pallas_call(
        last_kernel,
        grid=(2, STEPS),
        out_shape=jax.ShapeDtypeStruct((TOK, D), BF16),
        in_specs=[
            small(1, 8 * ROWS),
            small(TOK, 8),
            small(TOK, EXPERTS),
            first(EXPERTS),
            first(1),
            first(TOK),
            second(TOK),
        ]
        + [first(g.shape[0]) for g in grads],
        out_specs=second(TOK),
        scratch_shapes=[
            pltpu.VMEM((TOK, D), F32),
            pltpu.VMEM((TOK, D), BF16),
            pltpu.VMEM((2 * TOK, 8 * ROWS + 4 * EXPERTS), BF16),
            pltpu.VMEM((TOK, 128), F32),
            pltpu.VMEM((TOK, 128), F32),
        ],
        compiler_params=params(28),
    )(grad_slots, pack, logit, router_weight, gain, hidden, grad_out, *grads)
    return grad_hidden, router_grad


def solution(mesh):
    rows = P(("seq", "exp"), None)
    in_specs = (
        rows,
        rows,
        P(),
        rows,
        P(),
        rows,
        P("seq", "exp", None, None),
        P("seq", "exp", None, None),
    )
    return jax.shard_map(body, mesh=mesh, in_specs=in_specs, out_specs=(rows, P()), check_vma=False)
```

time: 227 us -> 232 us (1.022)
  starting transfers between devices: 79.9 us -> 39.2 us
  blocking collectives: 0 us -> 27 us
  waiting for transfers between devices: 92.6 us -> 114 us
  local copies, waits for them, and re-layouts: 33.9 us -> 28.6 us
    ppermute x3, waiting for transfers between devices: 3.09 us -> 36.6 us  [reduce_all(): v = v + lax.ppermute(v, AXES, xor_perm(axis, d))]
    ppermute x11, starting transfers between devices: 43.1 us -> 14.8 us  [ring_permute(): return lax.ppermute(v, 'exp', perm)]
    all_gather x0 -> x1, blocking collectives: none -> 27 us  [reduce_all(): return lax.all_gather(v, 'seq').reshape(EXPERTS, D)]
    ppermute x8 -> x0, starting transfers between devices: 20.4 us -> none  [the longest x4 10.5 us: reduce_all(): v = keep + lax.ppermute(send, AXES, xor_perm(axis, d))]
    ppermute x8 -> x0, waiting for transfers between devices: 17 us -> none  [the longest x4 12.2 us: reduce_all(): v = keep + lax.ppermute(send, AXES, xor_perm(axis, d))]
    ppermute x7, waiting for transfers between devices: 49.8 us -> 37.5 us  [body(): tally.append(tally[-1] + lax.ppermute(tally[-1], AXES, xor_perm(axis, d)))]
    all_to_all x0 -> x1, waiting for transfers between devices: none -> 9.21 us  [reduce_all(): v = jnp.sum(lax.all_to_all(v, 'seq', 0, 0, tiled=True), axis=0)]
    ppermute x11, waiting for transfers between devices: 22.7 us -> 30.5 us  [ring_permute(): return lax.ppermute(v, 'exp', perm)]
  transfers between devices with their start and end apart: 29 -> 22, of which waited for: 17 -> 10; matrix products, arithmetic and copies ran while one was open for 12% -> 11% of each run, Pallas kernels for 0% -> 3%
where the time goes in v3:
time: 232 us; the launch traced here: 231 us
  waiting for transfers between devices  114 us (49%)
  starting transfers between devices  39.2 us (17%)
  local copies, waits for them, and re-layouts  28.6 us (12%)
  blocking collectives  27 us (12%)
  Pallas kernels  16.2 us (7%)
  other arithmetic  5.26 us (2%)
    ppermute x7, waiting for transfers between devices, body(): tally.append(tally[-1] + lax.ppermute(tally[-1], AXES, xor_perm(axis, d)))  37.5 us
    ppermute x3, waiting for transfers between devices, reduce_all(): v = v + lax.ppermute(v, AXES, xor_perm(axis, d))  36.6 us
    ppermute x11, waiting for transfers between devices, ring_permute(): return lax.ppermute(v, 'exp', perm)  30.5 us
    all_gather x1, blocking collectives, reduce_all(): return lax.all_gather(v, 'seq').reshape(EXPERTS, D)  27 us
    ppermute x11, starting transfers between devices, ring_permute(): return lax.ppermute(v, 'exp', perm)  14.8 us
    ppermute x7, starting transfers between devices, body(): tally.append(tally[-1] + lax.ppermute(tally[-1], AXES, xor_perm(axis, d)))  12.8 us
    squeeze x4, local copies, waits for them, and re-layouts, pick(): return lax.dynamic_index_in_dim(v, i, axis, keepdims=False)  11.1 us
    all_to_all x1, waiting for transfers between devices, reduce_all(): v = jnp.sum(lax.all_to_all(v, 'seq', 0, 0, tiled=True), axis=0)  9.21 us
  transfers between devices with their start and end apart: 22, of which 10 were waited for; matrix products, arithmetic and copies ran while one was open for 11% of the time, Pallas kernels for 3%

profile of v3, /device:TPU:0, one launch (start us, length us, event | category | flops | bytes accessed | tf_op | source)
XLA Modules:
  0.0 230.9 jit_solution(2250840911199208736)
XLA Ops:
  0.7 4.0 %constant_dynamic-slice_fusion.5 = (bf16[1,2,24,8192]{3,2,1,0:T(8,128)(2,1)}, bf16[1,2,24,8192]{3,2,1,0:T(8,128)(2,1)}, bf16[1,2,24,8192]{3,2,1,0:T(8,128)(2,1)}...) fusion(bf16[1,2,192,8192]{3,2,1,0:T(8,128)(2,1)} %param.15, s32[]{:T(128)S(6)} %select_n.58, ...), kind=kLoop, calls=%fused_computation.16 | loop fusion | bytes 7864340 | tf_op jit(solution)/shard_map/dynamic_slice | solution.py:275
  4.7 3.1 %collective-permute-start = (bf16[48,8192]{1,0:T(8,128)(2,1)}, bf16[48,8192]{1,0:T(8,128)(2,1)}, u32[]{:S(2)}, u32[]{:S(2)}) collective-permute-start(bf16[48,8192]{1,0:T(8,128)(2,1)} %bitcast.8), channel_id=1, source_target_pairs={{0,4},{1,5},{2,6},{3,7},{4,0},{5,1},{6,2},{7,3},{8,12},{9,13},{10,... | collective-permute-start | bytes 2359304 | tf_op jit(solution)/shard_map/ppermute | solution.py:50
  7.8 0.1 copy.18.ids_ref
  7.9 0.1 copy.19.logits_ref
  8.0 0.6 shard_map.95
  8.6 0.1 collective-permute-start.1
  8.7 0.7 collective-permute-start.8
  9.4 2.6 %collective-permute-start.9 = (bf16[48,8192]{1,0:T(8,128)(2,1)}, bf16[48,8192]{1,0:T(8,128)(2,1)}, u32[]{:S(2)}, u32[]{:S(2)}) collective-permute-start(bf16[48,8192]{1,0:T(8,128)(2,1)} %bitcast.47), channel_id=1, source_target_pairs={{0,6},{1,7},{2,0},{3,1},{4,2},{5,3},{6,4},{7,5},{8,14},{9,15},{10,... | collective-permute-start | bytes 2359304 | tf_op jit(solution)/shard_map/ppermute | solution.py:50
  12.0 0.1 stack.46
  12.1 0.0 collective-permute-done.1
  12.1 0.1 collective-permute-start.2
  12.2 0.1 iota_add_fusion.1
  12.3 0.1 stack.47
  12.4 30.5 %collective-permute-done.2 = f32[8,16]{1,0:T(8,128)S(1)} collective-permute-done((f32[8,16]{1,0:T(8,128)S(1)}, f32[8,16]{1,0:T(8,128)S(1)}, u32[]{:S(2)}, u32[]{:S(2)}) %collective-permute-start.2) | collective-permute-done | bytes 544 | tf_op jit(solution)/shard_map/ppermute | solution.py:262
  42.9 2.0 collective-permute-start.3
  44.9 6.3 %dynamic-slice_bitcast_fusion = (bf16[2,4,24,8192]{3,2,1,0:T(8,128)(2,1)}, bf16[2,4,24,8192]{3,2,1,0:T(8,128)(2,1)}) fusion(bf16[2,4,2,24,8192]{4,3,2,1,0:T(8,128)(2,1)} %bitcast.44, s32[]{:T(128)S(6)} %select_n.57, s32[]{:T(128)S(6)} %select_n.56), kind=kLoop, calls=%fused_computation | loop fusion | bytes 12582920 | tf_op jit(solution)/shard_map/jit(dynamic_index_in_dim)/squeeze | solution.py:54
  51.2 0.0 collective-permute-start.10
  51.2 1.7 collective-permute-start.4
  52.9 0.1 iota_add_fusion
  52.9 2.0 collective-permute-done.4
  54.9 3.2 %collective-permute-start.5 = (f32[8,16]{1,0:T(8,128)S(1)}, f32[8,16]{1,0:T(8,128)S(1)}, u32[]{:S(2)}, u32[]{:S(2)}) collective-permute-start(f32[8,16]{1,0:T(8,128)S(1)} %add.215), channel_id=1, source_target_pairs={{0,64},{1,65},{2,66},{3,67},{4,68},{5,69},{6,70},{7,71},{8,72},{9,... | collective-permute-start | bytes 1544 | tf_op jit(solution)/shard_map/ppermute | solution.py:262
  58.1 1.9 collective-permute-done.5
  60.0 1.9 collective-permute-start.6
  61.9 1.7 collective-permute-done.6
  63.6 3.9 %collective-permute-start.7 = (f32[8,16]{1,0:T(8,128)S(1)}, f32[8,16]{1,0:T(8,128)S(1)}, u32[]{:S(2)}, u32[]{:S(2)}) collective-permute-start(f32[8,16]{1,0:T(8,128)S(1)} %add.217), channel_id=1, source_target_pairs={{0,16},{1,17},{2,18},{3,19},{4,20},{5,21},{6,22},{7,23},{8,24},{9,... | collective-permute-start | bytes 1544 | tf_op jit(solution)/shard_map/ppermute | solution.py:262
  67.5 0.1 add.204.slots_ref
  67.6 0.1 add.208.slots_ref
  67.7 1.4 collective-permute-done.7
  69.1 0.0 collective-permute-start.11
  69.1 1.2 constant_dynamic-slice_fusion.4
  70.3 3.0 %collective-permute-start.12 = (bf16[48,8192]{1,0:T(8,128)(2,1)S(1)}, bf16[48,8192]{1,0:T(8,128)(2,1)S(1)}, u32[]{:S(2)}, u32[]{:S(2)}) collective-permute-start(bf16[48,8192]{1,0:T(8,128)(2,1)S(1)} %bitcast.50), channel_id=1, source_target_pairs={{0,7},{1,6},{2,1},{3,0},{4,3},{5,2},{6,5},{7,4},{8,15},{9,14},{10,... | collective-permute-start | bytes 2359304 | tf_op jit(solution)/shard_map/ppermute | solution.py:50
  73.3 1.2 constant_dynamic-slice_fusion.3
  74.5 0.4 collective-permute-start.13
  75.0 1.2 constant_dynamic-slice_fusion.2
  76.2 0.1 collective-permute-start.14
  76.3 30.3 %collective-permute-done.11.refs_4_ = bf16[48,8192]{1,0:T(8,128)(2,1)S(1)} collective-permute-done((bf16[48,8192]{1,0:T(8,128)(2,1)}, bf16[48,8192]{1,0:T(8,128)(2,1)S(1)}, u32[]{:S(2)}, u32[]{:S(2)}) %collective-permute-start.11) | collective-permute-done | bytes 786464 | tf_op jit(solution)/shard_map/ppermute | solution.py:50
  106.6 0.1 collective-permute-done.12.refs_5_
  106.7 1.2 dynamic-slice_bitcast_fusion.6
  108.0 1.3 pad_maximum_fusion
  109.3 1.2 collective-permute-start.15
  110.5 1.2 dynamic-slice_bitcast_fusion.4
  111.7 1.3 pad_maximum_fusion.1
  113.0 2.2 collective-permute-start.16
  115.2 7.4 %shard_map.96 = (f32[128,16]{1,0:T(8,128)S(1)}, f32[16,8,1024]{2,1,0:T(8,128)}) custom-call(f32[1,384]{1,0:T(1,128)S(1)} %add.208.slots_ref, f32[128,8]{1,0:T(8,128)S(1)} %get-tuple-element.24.pack_ref, s32[128,2]{1,0:T(8,128)S(1)} %copy.18.ids_ref, f32[128,16]{1,0:T(8,128)S(1)} %get-tuple-element.25.probs_ref, f32[8,16]{1,0:T(8,128)S(1)} %add.218.counts_ref, ...), custom_call_target="tpu_custom_call" | custom-call | tf_op jit(solution)/shard_map/pallas_call | solution.py:288
  122.6 0.6 copy-done.6
  123.2 7.7 %all-to-all-start = ((f32[16,8,1024]{2,1,0:T(8,128)}), f32[16,8,1024]{2,1,0:T(8,128)S(1)}, u32[]{:S(2)}, u32[]{:S(2)}) async-start(f32[16,8,1024]{2,1,0:T(8,128)} %get-tuple-element.45), calls=%async_computation | async-start | bytes 1048576 | tf_op jit(solution)/shard_map/all_to_all | solution.py:233
  130.9 2.4 %dynamic-slice_bitcast_fusion.2 = (bf16[2,24,8192]{2,1,0:T(8,128)(2,1)S(1)}, bf16[2,24,8192]{2,1,0:T(8,128)(2,1)}) fusion(bf16[2,4,24,8192]{3,2,1,0:T(8,128)(2,1)} %collective-permute-done.10, s32[]{:T(128)S(6)} %select_n.67, bf16[2,4,24,8192]{3,2,1,0:T(8,128)(2,1)} %get-tuple-element.43), kind=kLoop, calls=%fused_computation.5 | loop fusion | bytes 3145732 | tf_op jit(solution)/shard_map/jit(dynamic_index_in_dim)/squeeze | solution.py:54
  133.3 9.2 %all-to-all-done = f32[16,8,1024]{2,1,0:T(8,128)S(1)} async-done(((f32[16,8,1024]{2,1,0:T(8,128)}), f32[16,8,1024]{2,1,0:T(8,128)S(1)}, u32[]{:S(2)}, u32[]{:S(2)}) %all-to-all-start) | async-done | bytes 524320 | tf_op jit(solution)/shard_map/all_to_all | solution.py:233
  142.5 0.1 collective-permute-start.18
  142.6 2.5 %pad_maximum_fusion.2 = bf16[4,24,8192]{2,1,0:T(8,128)(2,1)} fusion(bf16[2,24,8192]{2,1,0:T(8,128)(2,1)S(1)} %get-tuple-element.57, bf16[2,24,8192]{2,1,0:T(8,128)(2,1)} %get-tuple-element.58), kind=kLoop, calls=%fused_computation.4 | loop fusion | flops 786432 | bytes 3145728 | tf_op jit(solution)/shard_map/concatenate | solution.py:284
  145.1 1.3 collective-permute-start.17
  146.4 1.2 collective-permute-start.19
  147.6 2.1 constant_dynamic-slice_fusion.1
  149.7 35.0 %collective-permute-done.19 = f32[8,1024]{1,0:T(8,128)S(1)} collective-permute-done((f32[8,1024]{1,0:T(8,128)S(1)}, f32[8,1024]{1,0:T(8,128)S(1)}, u32[]{:S(2)}, u32[]{:S(2)}) %collective-permute-start.19) | collective-permute-done | bytes 32800 | tf_op jit(solution)/shard_map/ppermute | solution.py:235
  184.7 2.7 %collective-permute-start.20 = (f32[8,1024]{1,0:T(8,128)S(1)}, f32[8,1024]{1,0:T(8,128)S(1)}, u32[]{:S(2)}, u32[]{:S(2)}) collective-permute-start(f32[8,1024]{1,0:T(8,128)S(1)} %add.241), channel_id=1, source_target_pairs={{0,4},{1,5},{2,6},{3,7},{4,0},{5,1},{6,2},{7,3},{8,12},{9,13},{10,... | collective-permute-start | bytes 98312 | tf_op jit(solution)/shard_map/ppermute | solution.py:235
  187.4 1.2 constant_dynamic-slice_fusion
  188.6 1.6 collective-permute-done.20
  190.1 27.0 %all-gather = f32[128,1024]{1,0:T(8,128)} all-gather(f32[8,1024]{1,0:T(8,128)S(1)} %add.242), channel_id=2, replica_groups=mesh['seq'=16,'exp'=8] {'seq'}, dimensions={0}, use_global_device_ids=true | all-gather | bytes 557056 | tf_op jit(solution)/shard_map/all_gather | solution.py:236
  217.2 1.9 reshape.249
  219.1 0.0 copy-start.2
  219.1 1.6 copy-done.2
  220.7 1.1 copy-done.3
  221.8 0.8 copy-done.7
  222.7 8.3 %shard_map.97 = bf16[128,8192]{1,0:T(8,128)(2,1)} custom-call(f32[1,384]{1,0:T(1,128)S(1)} %add.204.slots_ref, f32[128,8]{1,0:T(8,128)S(1)} %get-tuple-element.24.pack_ref, f32[128,16]{1,0:T(8,128)S(1)} %copy-done.7, f32[16,8192]{1,0:T(8,128)S(1)} %copy-done.4, f32[1,8192]{1,0:T(1,128)S(1)} %bitcast.43, bf16[128,8192]{1,0:T(8,128)(2,1)S(1)} %copy-done, ...), custom_call_target="tpu_custom_call" | custom-call | tf_op jit(solution)/shard_map/pallas_call | solution.py:315
  (41 shorter events, 0.1 us)
Async XLA Ops:
  0.7 7.1 %copy-start.10 = (s32[128,2]{0,1:T(2,128)S(1)}, s32[128,2]{0,1:T(2,128)}, u32[]{:S(2)}) copy-start(s32[128,2]{0,1:T(2,128)} %param.13) | copy-start | bytes 3076
  0.7 7.2 %copy-start.9 = (f32[128,16]{0,1:T(8,128)S(1)}, f32[128,16]{0,1:T(8,128)}, u32[]{:S(2)}) copy-start(f32[128,16]{0,1:T(8,128)} %param.11) | copy-start | bytes 24580
  0.7 7.3 %copy-start = (bf16[128,8192]{1,0:T(8,128)(2,1)S(1)}, bf16[128,8192]{1,0:T(8,128)(2,1)}, u32[]{:S(2)}) copy-start(bf16[128,8192]{1,0:T(8,128)(2,1)} %hidden_ref.5) | copy-start | bytes 6291460
  4.7 64.4 %collective-permute-start = (bf16[48,8192]{1,0:T(8,128)(2,1)}, bf16[48,8192]{1,0:T(8,128)(2,1)}, u32[]{:S(2)}, u32[]{:S(2)}) collective-permute-start(bf16[48,8192]{1,0:T(8,128)(2,1)} %bitcast.8), channel_id=1, source_target_pairs={{0,4},{1,5},{2,6},{3,7},{4,0},{5,1},{6,2},{7,3},{8,12},{9,13},{10,... | collective-permute-start | bytes 2359304 | tf_op jit(solution)/shard_map/ppermute | solution.py:50
  8.6 3.5 %collective-permute-start.1 = (f32[8,16]{1,0:T(8,128)S(1)}, f32[8,16]{1,0:T(8,128)S(1)}, u32[]{:S(2)}, u32[]{:S(2)}) collective-permute-start(f32[8,16]{1,0:T(8,128)S(1)} %get-tuple-element.26), channel_id=1, source_target_pairs={{0,1},{1,0},{2,3},{3,2},{4,5},{5,4},{6,7},{7,6},{8,9},{9,8},{10,11... | collective-permute-start | bytes 1544 | tf_op jit(solution)/shard_map/ppermute | solution.py:262
  8.7 60.4 %collective-permute-start.8 = (bf16[48,8192]{1,0:T(8,128)(2,1)}, bf16[48,8192]{1,0:T(8,128)(2,1)}, u32[]{:S(2)}, u32[]{:S(2)}) collective-permute-start(bf16[48,8192]{1,0:T(8,128)(2,1)} %bitcast.48), channel_id=1, source_target_pairs={{0,2},{1,3},{2,4},{3,5},{4,6},{5,7},{6,0},{7,1},{8,10},{9,11},{10,... | collective-permute-start | bytes 2359304 | tf_op jit(solution)/shard_map/ppermute | solution.py:50
  9.4 59.7 %collective-permute-start.9 = (bf16[48,8192]{1,0:T(8,128)(2,1)}, bf16[48,8192]{1,0:T(8,128)(2,1)}, u32[]{:S(2)}, u32[]{:S(2)}) collective-permute-start(bf16[48,8192]{1,0:T(8,128)(2,1)} %bitcast.47), channel_id=1, source_target_pairs={{0,6},{1,7},{2,0},{3,1},{4,2},{5,3},{6,4},{7,5},{8,14},{9,15},{10,... | collective-permute-start | bytes 2359304 | tf_op jit(solution)/shard_map/ppermute | solution.py:50
  12.1 30.7 %collective-permute-start.2 = (f32[8,16]{1,0:T(8,128)S(1)}, f32[8,16]{1,0:T(8,128)S(1)}, u32[]{:S(2)}, u32[]{:S(2)}) collective-permute-start(f32[8,16]{1,0:T(8,128)S(1)} %add.212), channel_id=1, source_target_pairs={{0,2},{1,3},{2,0},{3,1},{4,6},{5,7},{6,4},{7,5},{8,10},{9,11},{10,... | collective-permute-start | bytes 1544 | tf_op jit(solution)/shard_map/ppermute | solution.py:262
  42.9 8.3 %collective-permute-start.3 = (f32[8,16]{1,0:T(8,128)S(1)}, f32[8,16]{1,0:T(8,128)S(1)}, u32[]{:S(2)}, u32[]{:S(2)}) collective-permute-start(f32[8,16]{1,0:T(8,128)S(1)} %add.213), channel_id=1, source_target_pairs={{0,4},{1,5},{2,6},{3,7},{4,0},{5,1},{6,2},{7,3},{8,12},{9,13},{10,... | collective-permute-start | bytes 1544 | tf_op jit(solution)/shard_map/ppermute | solution.py:262
  51.2 55.5 %collective-permute-start.10 = (bf16[2,4,24,8192]{3,2,1,0:T(8,128)(2,1)}, bf16[2,4,24,8192]{3,2,1,0:T(8,128)(2,1)}, u32[]{:S(2)}, u32[]{:S(2)}) collective-permute-start(bf16[2,4,24,8192]{3,2,1,0:T(8,128)(2,1)} %get-tuple-element.51), channel_id=1, source_target_pairs={{0,1},{1,0},{2,3},{3,2},{4,5},{5,4},{6,7},{7,6},{8,9},{9,8},{10,11... | collective-permute-start | bytes 9437192 | tf_op jit(solution)/shard_map/ppermute | solution.py:50
  51.2 3.7 %collective-permute-start.4 = (f32[8,16]{1,0:T(8,128)S(1)}, f32[8,16]{1,0:T(8,128)S(1)}, u32[]{:S(2)}, u32[]{:S(2)}) collective-permute-start(f32[8,16]{1,0:T(8,128)S(1)} %add.214), channel_id=1, source_target_pairs={{0,32},{1,33},{2,34},{3,35},{4,36},{5,37},{6,38},{7,39},{8,40},{9,... | collective-permute-start | bytes 1544 | tf_op jit(solution)/shard_map/ppermute | solution.py:262
  54.9 5.1 %collective-permute-start.5 = (f32[8,16]{1,0:T(8,128)S(1)}, f32[8,16]{1,0:T(8,128)S(1)}, u32[]{:S(2)}, u32[]{:S(2)}) collective-permute-start(f32[8,16]{1,0:T(8,128)S(1)} %add.215), channel_id=1, source_target_pairs={{0,64},{1,65},{2,66},{3,67},{4,68},{5,69},{6,70},{7,71},{8,72},{9,... | collective-permute-start | bytes 1544 | tf_op jit(solution)/shard_map/ppermute | solution.py:262
  60.0 3.6 %collective-permute-start.6 = (f32[8,16]{1,0:T(8,128)S(1)}, f32[8,16]{1,0:T(8,128)S(1)}, u32[]{:S(2)}, u32[]{:S(2)}) collective-permute-start(f32[8,16]{1,0:T(8,128)S(1)} %add.216), channel_id=1, source_target_pairs={{0,8},{1,9},{2,10},{3,11},{4,12},{5,13},{6,14},{7,15},{8,0},{9,1},... | collective-permute-start | bytes 1544 | tf_op jit(solution)/shard_map/ppermute | solution.py:262
  63.6 5.5 %collective-permute-start.7 = (f32[8,16]{1,0:T(8,128)S(1)}, f32[8,16]{1,0:T(8,128)S(1)}, u32[]{:S(2)}, u32[]{:S(2)}) collective-permute-start(f32[8,16]{1,0:T(8,128)S(1)} %add.217), channel_id=1, source_target_pairs={{0,16},{1,17},{2,18},{3,19},{4,20},{5,21},{6,22},{7,23},{8,24},{9,... | collective-permute-start | bytes 1544 | tf_op jit(solution)/shard_map/ppermute | solution.py:262
  67.7 39.1 %copy-start.8 = (bf16[2,4,24,8192]{3,2,1,0:T(8,128)(2,1)S(1)}, bf16[2,4,24,8192]{3,2,1,0:T(8,128)(2,1)}, u32[]{:S(2)}) copy-start(bf16[2,4,24,8192]{3,2,1,0:T(8,128)(2,1)} %get-tuple-element.43) | copy-start | bytes 9437188
  69.1 37.6 %collective-permute-start.11 = (bf16[48,8192]{1,0:T(8,128)(2,1)}, bf16[48,8192]{1,0:T(8,128)(2,1)S(1)}, u32[]{:S(2)}, u32[]{:S(2)}) collective-permute-start(bf16[48,8192]{1,0:T(8,128)(2,1)} %bitcast.46), channel_id=1, source_target_pairs={{0,3},{1,2},{2,5},{3,4},{4,7},{5,6},{6,1},{7,0},{8,11},{9,10},{10,... | collective-permute-start | bytes 2359304 | tf_op jit(solution)/shard_map/ppermute | solution.py:50
  70.3 36.4 %collective-permute-start.12 = (bf16[48,8192]{1,0:T(8,128)(2,1)S(1)}, bf16[48,8192]{1,0:T(8,128)(2,1)S(1)}, u32[]{:S(2)}, u32[]{:S(2)}) collective-permute-start(bf16[48,8192]{1,0:T(8,128)(2,1)S(1)} %bitcast.50), channel_id=1, source_target_pairs={{0,7},{1,6},{2,1},{3,0},{4,3},{5,2},{6,5},{7,4},{8,15},{9,14},{10,... | collective-permute-start | bytes 2359304 | tf_op jit(solution)/shard_map/ppermute | solution.py:50
  74.5 32.2 %collective-permute-start.13 = (bf16[48,8192]{1,0:T(8,128)(2,1)S(1)}, bf16[48,8192]{1,0:T(8,128)(2,1)S(1)}, u32[]{:S(2)}, u32[]{:S(2)}) collective-permute-start(bf16[48,8192]{1,0:T(8,128)(2,1)S(1)} %bitcast.51), channel_id=1, source_target_pairs={{0,5},{1,4},{2,7},{3,6},{4,1},{5,0},{6,3},{7,2},{8,13},{9,12},{10,... | collective-permute-start | bytes 2359304 | tf_op jit(solution)/shard_map/ppermute | solution.py:50
  76.2 39.1 %collective-permute-start.14 = (bf16[48,8192]{1,0:T(8,128)(2,1)S(1)}, bf16[48,8192]{1,0:T(8,128)(2,1)S(1)}, u32[]{:S(2)}, u32[]{:S(2)}) collective-permute-start(bf16[48,8192]{1,0:T(8,128)(2,1)S(1)} %bitcast.49), channel_id=1, source_target_pairs={{0,1},{1,0},{2,3},{3,2},{4,5},{5,4},{6,7},{7,6},{8,9},{9,8},{10,11... | collective-permute-start | bytes 2359304 | tf_op jit(solution)/shard_map/ppermute | solution.py:50
  109.3 6.0 %copy-start.1 = (bf16[128,8192]{1,0:T(8,128)(2,1)S(1)}, bf16[128,8192]{1,0:T(8,128)(2,1)}, u32[]{:S(2)}) copy-start(bf16[128,8192]{1,0:T(8,128)(2,1)} %grad_ref.3) | copy-start | bytes 6291460
  109.3 6.0 %copy-start.5 = (f32[8192]{0:T(1024)S(1)}, f32[8192]{0:T(1024)}, u32[]{:S(2)}) copy-start(f32[8192]{0:T(1024)} %param.10) | copy-start | bytes 98308
  109.3 109.8 %collective-permute-start.15 = (bf16[96,8192]{1,0:T(8,128)(2,1)}, bf16[96,8192]{1,0:T(8,128)(2,1)}, u32[]{:S(2)}, u32[]{:S(2)}) collective-permute-start(bf16[96,8192]{1,0:T(8,128)(2,1)} %bitcast.24), channel_id=1, source_target_pairs={{0,2},{1,3},{2,4},{3,5},{4,6},{5,7},{6,0},{7,1},{8,10},{9,11},{10,... | collective-permute-start | bytes 4718600 | tf_op jit(solution)/shard_map/ppermute | solution.py:50
  113.0 106.1 %collective-permute-start.16 = (bf16[96,8192]{1,0:T(8,128)(2,1)}, bf16[96,8192]{1,0:T(8,128)(2,1)}, u32[]{:S(2)}, u32[]{:S(2)}) collective-permute-start(bf16[96,8192]{1,0:T(8,128)(2,1)} %bitcast.27), channel_id=1, source_target_pairs={{0,6},{1,7},{2,0},{3,1},{4,2},{5,3},{6,4},{7,5},{8,14},{9,15},{10,... | collective-permute-start | bytes 4718600 | tf_op jit(solution)/shard_map/ppermute | solution.py:50
  122.6 0.6 copy-start.6
  123.2 19.3 %all-to-all-start = ((f32[16,8,1024]{2,1,0:T(8,128)}), f32[16,8,1024]{2,1,0:T(8,128)S(1)}, u32[]{:S(2)}, u32[]{:S(2)}) async-start(f32[16,8,1024]{2,1,0:T(8,128)} %get-tuple-element.45), calls=%async_computation | async-start | bytes 1048576 | tf_op jit(solution)/shard_map/all_to_all | solution.py:233
  142.5 3.9 %collective-permute-start.18 = (f32[8,1024]{1,0:T(8,128)S(1)}, f32[8,1024]{1,0:T(8,128)S(1)}, u32[]{:S(2)}, u32[]{:S(2)}) collective-permute-start(f32[8,1024]{1,0:T(8,128)S(1)} %reduce_sum.9), channel_id=1, source_target_pairs={{0,1},{1,0},{2,3},{3,2},{4,5},{5,4},{6,7},{7,6},{8,9},{9,8},{10,11... | collective-permute-start | bytes 98312 | tf_op jit(solution)/shard_map/ppermute | solution.py:235
  145.1 74.0 %copy-start.4 = (f32[16,8192]{1,0:T(8,128)S(1)}, f32[16,8192]{1,0:T(8,128)}, u32[]{:S(2)}) copy-start(f32[16,8192]{1,0:T(8,128)} %weight_ref.1) | copy-start | bytes 1572868
  145.1 74.0 %collective-permute-start.17 = (bf16[96,8192]{1,0:T(8,128)(2,1)}, bf16[96,8192]{1,0:T(8,128)(2,1)}, u32[]{:S(2)}, u32[]{:S(2)}) collective-permute-start(bf16[96,8192]{1,0:T(8,128)(2,1)} %bitcast.30), channel_id=1, source_target_pairs={{0,4},{1,5},{2,6},{3,7},{4,0},{5,1},{6,2},{7,3},{8,12},{9,13},{10,... | collective-permute-start | bytes 4718600 | tf_op jit(solution)/shard_map/ppermute | solution.py:50
  146.4 38.3 %collective-permute-start.19 = (f32[8,1024]{1,0:T(8,128)S(1)}, f32[8,1024]{1,0:T(8,128)S(1)}, u32[]{:S(2)}, u32[]{:S(2)}) collective-permute-start(f32[8,1024]{1,0:T(8,128)S(1)} %add.240), channel_id=1, source_target_pairs={{0,2},{1,3},{2,0},{3,1},{4,6},{5,7},{6,4},{7,5},{8,10},{9,11},{10,... | collective-permute-start | bytes 98312 | tf_op jit(solution)/shard_map/ppermute | solution.py:235
  184.7 5.4 %collective-permute-start.20 = (f32[8,1024]{1,0:T(8,128)S(1)}, f32[8,1024]{1,0:T(8,128)S(1)}, u32[]{:S(2)}, u32[]{:S(2)}) collective-permute-start(f32[8,1024]{1,0:T(8,128)S(1)} %add.241), channel_id=1, source_target_pairs={{0,4},{1,5},{2,6},{3,7},{4,0},{5,1},{6,2},{7,3},{8,12},{9,13},{10,... | collective-permute-start | bytes 98312 | tf_op jit(solution)/shard_map/ppermute | solution.py:235
  219.1 1.6 copy-start.2
  220.7 1.1 copy-start.3
  221.8 0.8 copy-start.7

commit v4 on v3

--- a/solution.py
+++ b/solution.py
@@ -67,7 +67,7 @@
     return a, b, c
 
 
-def pre_kernel(ids_ref, logits_ref, hidden_ref, pack_ref, probs_ref, counts_ref):
+def pre_kernel(ids_ref, logits_ref, pack_ref, probs_ref, counts_ref):
     ids = ids_ref[...]
     logits = logits_ref[...]
     labels = lax.broadcasted_iota(jnp.int32, (TOK, EXPERTS), 1)
@@ -88,29 +88,31 @@
     total = w[0] + w[1]
     e = jnp.exp(logits - jnp.max(logits, axis=1, keepdims=True))
     probs_ref[...] = e / jnp.sum(e, axis=1, keepdims=True)
-    square = jnp.zeros((TOK, 128), F32)
-    for c in range(D // CHUNK):
-        h = hidden_ref[:, c * CHUNK : (c + 1) * CHUNK].astype(F32)
-        h = h * h
-        for j in range(CHUNK // 128):
-            square = square + h[:, j * 128 : (j + 1) * 128]
-    inv = lax.rsqrt(jnp.sum(square, axis=1, keepdims=True) / D + 1e-05)
     lane = lax.broadcasted_iota(jnp.int32, (TOK, 8), 1)
     pack = jnp.zeros((TOK, 8), F32)
-    for i, v in enumerate((w[0] / total, w[1] / total, index[0], index[1], inv)):
+    for i, v in enumerate((w[0] / total, w[1] / total, index[0], index[1])):
         pack = jnp.where(lane == i, v, pack)
     pack_ref[...] = pack
 
 
 def mid_kernel(
-    slots_ref, pack_ref, ids_ref, probs_ref, counts_ref, gain_ref, hidden_ref, grad_ref, *refs
+    slots_ref,
+    pack_ref,
+    inv_ref,
+    ids_ref,
+    probs_ref,
+    counts_ref,
+    gain_ref,
+    hidden_ref,
+    grad_ref,
+    *refs,
 ):
-    blocks, (logit_ref, partial_ref, dots_ref, left_ref) = refs[:8], refs[8:]
+    blocks, (logit_ref, partial_ref, dots_ref, left_ref, total_ref) = refs[:8], refs[8:]
     stage, c = pl.program_id(0), pl.program_id(1)
 
     @pl.when(stage == 0)
     def _():
-        picked = jnp.concatenate([b[...] for b in blocks], axis=0)
+        picked = jnp.concatenate([b[:ROWS] for b in blocks], axis=0)
         d = lax.dot_general(
             grad_ref[...], picked, (((1,), (1,)), ((), ())), preferred_element_type=F32
         )
@@ -118,6 +120,11 @@
         @pl.when(c == 0)
         def _():
             dots_ref[...] = d
+            total = counts_ref[...]
+            for b in blocks[4:7]:
+                other = b[ROWS : ROWS + 8, 0 : 2 * EXPERTS].astype(F32)
+                total = total + other[:, :EXPERTS] + other[:, EXPERTS:]
+            total_ref[...] = total
 
         @pl.when(c > 0)
         def _():
@@ -143,11 +150,11 @@
             chosen = gate[k] * (gate_dot[k] - mean)
             direct = direct + jnp.where(ids[:, k : k + 1] == labels, chosen, 0.0)
         probs = probs_ref[...]
-        load = counts_ref[0:1, :] * (EXPERTS / (2 * TOKENS))
+        load = total_ref[0:1, :] * (EXPERTS / (2 * TOKENS))
         aux = probs * (load - jnp.sum(probs * load, axis=1, keepdims=True))
         logit = direct + aux
         logit_ref[...] = logit
-        left_ref[...] = jnp.concatenate(split3(logit * pack[:, 4:5]), axis=1)
+        left_ref[...] = jnp.concatenate(split3(logit * inv_ref[...]), axis=1)
 
     @pl.when(stage == 1)
     def _():
@@ -160,7 +167,7 @@
 
 
 def last_kernel(
-    slots_ref, pack_ref, logit_ref, weight_ref, gain_ref, hidden_ref, grad_ref, *refs
+    slots_ref, pack_ref, inv_ref, logit_ref, weight_ref, gain_ref, hidden_ref, grad_ref, *refs
 ):
     blocks, (out_ref, scaled_ref, normed_ref, left_ref, acc_ref, factor_ref) = refs[:-6], refs[-6:]
     stage, c = pl.program_id(0), pl.program_id(1)
@@ -201,13 +208,13 @@
 
     @pl.when((stage == 1) & (c == 0))
     def _():
-        inv = pack_ref[:, 4:5]
+        inv = inv_ref[...]
         mean = jnp.sum(acc_ref[...], axis=1, keepdims=True) * inv / D
         factor_ref[...] = jnp.broadcast_to(inv * mean, (TOK, 128))
 
     @pl.when(stage == 1)
     def _():
-        inv = pack_ref[:, 4:5]
+        inv = inv_ref[...]
         factor = factor_ref[:, 0:1]
         back = inv * (scaled_ref[:, cols] - normed_ref[:, cols].astype(F32) * factor)
         out_ref[...] = (grad_ref[...].astype(F32) + back).astype(BF16)
@@ -229,11 +236,9 @@
     return pltpu.CompilerParams(vmem_limit_bytes=mib * 1024 * 1024)
 
 
-def reduce_all(v):
-    v = jnp.sum(lax.all_to_all(v, "seq", 0, 0, tiled=True), axis=0)
-    for axis, d in (("c", 1), ("x", 1), ("x", 2)):
-        v = v + lax.ppermute(v, AXES, xor_perm(axis, d))
-    return lax.all_gather(v, "seq").reshape(EXPERTS, D)
+def sum_x(v):
+    a, b, c = [lax.ppermute(v, AXES, xor_perm("x", d)) for d in (1, 2, 3)]
+    return (v + a) + (b + c)
 
 
 def body(
@@ -252,16 +257,21 @@
             jax.ShapeDtypeStruct((TOK, EXPERTS), F32),
             jax.ShapeDtypeStruct((8, EXPERTS), F32),
         ),
-        in_specs=[VMEM] * 3,
+        in_specs=[VMEM] * 2,
         out_specs=(VMEM,) * 3,
-        compiler_params=params(16),
-    )(expert_ids, router_logits, hidden)
+        compiler_params=params(8),
+    )(expert_ids, router_logits)
+    wide = hidden.astype(F32)
+    inv = lax.rsqrt(jnp.mean(wide * wide, axis=1, keepdims=True) + 1e-05)
     me = at["x"] * 2 + at["c"]
     tally = [counts]
-    for axis, d in (("c", 1), ("x", 1), ("x", 2), ("y", 1), ("y", 2), ("z", 1), ("z", 2)):
+    for axis, d in (("y", 1), ("y", 2), ("z", 1), ("z", 2), ("c", 1)):
         tally.append(tally[-1] + lax.ppermute(tally[-1], AXES, xor_perm(axis, d)))
-
-    source, tally[2] = after(expert_grad, tally[2])
+    share = tally[5][0:1].astype(BF16)
+    share = jnp.concatenate([share, (tally[5][0:1] - share.astype(F32)).astype(BF16)], axis=1)
+    share = jnp.pad(share, ((0, 7), (0, D - 2 * EXPERTS)))
+
+    source, tally[1] = after(expert_grad, tally[1])
     by_core = source.reshape(2, 4, 2, CAP, D)
     swap = ring_permute(pick(by_core, 2, at["c"] ^ 1), 0, 1)
     mine = pick(by_core, 2, at["c"])
@@ -269,20 +279,28 @@
     outs = []
     for n, (s, m) in enumerate(ROUTES[1:]):
         array = expert_out
+        if n == 3:
+            array, swap, share = after(array, swap, share)
         if n > 3:
-            array, outs[n - 4], tally[2 * n - 5] = after(array, outs[n - 4], tally[2 * n - 5])
+            array, outs[n - 4] = after(array, outs[n - 4])
         to = ((at["x"] + s) & 3) * 2 + (at["c"] ^ m)
         block = lax.dynamic_slice(array, (0, 0, to * CAP, 0), (1, 2, CAP, D))
-        outs.append(ring_permute(block.reshape(ROWS, D), s, m))
+        block = block.reshape(ROWS, D)
+        if 3 <= n <= 5:
+            block = jnp.concatenate([block, share], axis=0)
+        outs.append(ring_permute(block, s, m))
     own_out = lax.dynamic_slice(expert_out, (0, 0, me * CAP, 0), (1, 2, CAP, D)).reshape(ROWS, D)
 
-    grads = [pick(mine, 1, at["x"]).reshape(ROWS, D), pick(swap, 1, at["x"]).reshape(ROWS, D)]
-    for n, s in enumerate((1, 3, 2)):
-        a, b = mine, swap
-        a, b, outs[n + 3] = after(a, b, outs[n + 3])
+    def send_grad(s, *deps):
+        a, b, *deps = after(mine, swap, *deps)
         to = (at["x"] + s) & 3
         block = jnp.concatenate([pick(a, 1, to), pick(b, 1, to)], axis=0)
-        grads.append(ring_permute(block.reshape(2 * ROWS, D), s, 0))
+        return ring_permute(block.reshape(2 * ROWS, D), s, 0), *deps
+
+    grads = [pick(mine, 1, at["x"]).reshape(ROWS, D), pick(swap, 1, at["x"]).reshape(ROWS, D)]
+    for s, n in ((1, 3), (3, 4)):
+        moved, outs[n] = send_grad(s, outs[n])
+        grads.append(moved)
 
     small = lambda *shape: pl.BlockSpec(shape, lambda p, c: (0,) * len(shape))
     logit, partial = pl.pallas_call(
@@ -295,6 +313,7 @@
         in_specs=[
             small(1, 8 * ROWS),
             small(TOK, 8),
+            small(TOK, 1),
             small(TOK, 2),
             small(TOK, EXPERTS),
             small(8, EXPERTS),
@@ -302,15 +321,26 @@
             second(TOK),
             first(TOK),
         ]
-        + [first(ROWS)] * 8,
+        + [first(b.shape[0]) for b in (own_out, *outs)],
         out_specs=(
             small(TOK, EXPERTS),
             small(EXPERTS, 8, 1024),
         ),
-        scratch_shapes=[pltpu.VMEM((TOK, 8 * ROWS), F32), pltpu.VMEM((TOK, 3 * EXPERTS), BF16)],
-        compiler_params=params(24),
-    )(slots, pack, expert_ids, probs, tally[7], gain, hidden, grad_out, own_out, *outs)
-    router_grad = reduce_all(partial)
+        scratch_shapes=[
+            pltpu.VMEM((TOK, 8 * ROWS), F32),
+            pltpu.VMEM((TOK, 3 * EXPERTS), BF16),
+            pltpu.VMEM((8, EXPERTS), F32),
+        ],
+        cost_estimate=pl.CostEstimate(flops=20_000_000_000, bytes_accessed=60_000_000, transcendentals=0),
+        compiler_params=params(20),
+    )(slots, pack, inv, expert_ids, probs, tally[5], gain, hidden, grad_out, own_out, *outs)
+    partial = jnp.sum(lax.all_to_all(partial, "seq", 0, 0, tiled=True), axis=0)
+    partial = partial + lax.ppermute(partial, AXES, xor_perm("c", 1))
+    partial, grads[2], grads[3] = after(partial, grads[2], grads[3])
+    partial = sum_x(partial)
+    moved, partial = send_grad(2, partial)
+    grads.append(moved)
+    router_grad = lax.all_gather(partial, "seq").reshape(EXPERTS, D)
 
     grad_hidden = pl.pallas_call(
         last_kernel,
@@ -319,6 +349,7 @@
         in_specs=[
             small(1, 8 * ROWS),
             small(TOK, 8),
+            small(TOK, 1),
             small(TOK, EXPERTS),
             first(EXPERTS),
             first(1),
@@ -335,7 +366,7 @@
             pltpu.VMEM((TOK, 128), F32),
         ],
         compiler_params=params(28),
-    )(grad_slots, pack, logit, router_weight, gain, hidden, grad_out, *grads)
+    )(grad_slots, pack, inv, logit, router_weight, gain, hidden, grad_out, *grads)
     return grad_hidden, router_grad
 
 

time: 232 us -> 198 us (0.85)
  waiting for transfers between devices: 114 us -> 76.4 us
  local copies, waits for them, and re-layouts: 28.6 us -> 32.1 us
    ppermute x7 -> x5, waiting for transfers between devices: 37.5 us -> 4.89 us  [body(): tally.append(tally[-1] + lax.ppermute(tally[-1], AXES, xor_perm(axis, d)))]
    ppermute x3 -> x4, waiting for transfers between devices: 36.6 us -> 5.26 us  [the longest x3 4.08 us: sum_x(): a, b, c = [lax.ppermute(v, AXES, xor_perm('x', d)) for d in (1, 2, 3)]]
    ppermute x11, waiting for transfers between devices: 30.5 us -> 55 us  [ring_permute(): return lax.ppermute(v, 'exp', perm)]
    ppermute x7 -> x5, starting transfers between devices: 12.8 us -> 10.3 us  [body(): tally.append(tally[-1] + lax.ppermute(tally[-1], AXES, xor_perm(axis, d)))]
    unnamed x24 -> x20, local copies, waits for them, and re-layouts: 4.43 us -> 6.55 us
    dynamic_slice x4 -> x5, local copies, waits for them, and re-layouts: 7.55 us -> 8.22 us  [body(): block = lax.dynamic_slice(array, (0, 0, to * CAP, 0), (1, 2, CAP, D))]
    concatenate x3 -> x5, other arithmetic: 5.04 us -> 5.57 us  [the longest x3 3.86 us: send_grad(): block = jnp.concatenate([pick(a, 1, to), pick(b, 1, to)], axis=0)]
    squeeze x4 -> x5, local copies, waits for them, and re-layouts: 11.1 us -> 11.6 us  [pick(): return lax.dynamic_index_in_dim(v, i, axis, keepdims=False)]
  transfers between devices with their start and end apart: 22 -> 21, of which waited for: 10 -> 13; matrix products, arithmetic and copies ran while one was open for 11% -> 14% of each run, Pallas kernels for 3% -> 4%
where the time goes in v4:
time: 198 us; the launch traced here: 197 us
  waiting for transfers between devices  76.4 us (39%)
  starting transfers between devices  38.3 us (19%)
  local copies, waits for them, and re-layouts  32.1 us (16%)
  blocking collectives  27.1 us (14%)
  Pallas kernels  16.3 us (8%)
  other arithmetic  6.28 us (3%)
    ppermute x11, waiting for transfers between devices, ring_permute(): return lax.ppermute(v, 'exp', perm)  55 us
    all_gather x1, blocking collectives, body(): router_grad = lax.all_gather(partial, 'seq').reshape(EXPERTS, D)  27.1 us
    ppermute x11, starting transfers between devices, ring_permute(): return lax.ppermute(v, 'exp', perm)  15.6 us
    squeeze x5, local copies, waits for them, and re-layouts, pick(): return lax.dynamic_index_in_dim(v, i, axis, keepdims=False)  11.6 us
    all_to_all x1, waiting for transfers between devices, body(): partial = jnp.sum(lax.all_to_all(partial, 'seq', 0, 0, tiled=True), axis=0)  11.3 us
    ppermute x5, starting transfers between devices, body(): tally.append(tally[-1] + lax.ppermute(tally[-1], AXES, xor_perm(axis, d)))  10.3 us
    pallas_call x1, Pallas kernels, body(): pl.pallas_call(last_kernel, grid=(2, STEPS), out_shape=jax.ShapeDtypeStru...  8.27 us
    dynamic_slice x5, local copies, waits for them, and re-layouts, body(): block = lax.dynamic_slice(array, (0, 0, to * CAP, 0), (1, 2, CAP, D))  8.22 us
  transfers between devices with their start and end apart: 21, of which 13 were waited for; matrix products, arithmetic and copies ran while one was open for 14% of the time, Pallas kernels for 4%

profile of v4, /device:TPU:0, one launch (start us, length us, event | category | flops | bytes accessed | tf_op | source)
XLA Modules:
  0.0 197.3 jit_solution(12877837139642726786)
XLA Ops:
  0.6 0.8 copy.22.ids_ref
  1.4 0.8 copy.23.logits_ref
  2.2 0.3 shard_map.95
  2.6 1.7 collective-permute-start
  4.3 3.4 %constant_dynamic-slice_fusion.6 = (bf16[1,2,24,8192]{3,2,1,0:T(8,128)(2,1)}, bf16[1,2,24,8192]{3,2,1,0:T(8,128)(2,1)}, bf16[1,2,24,8192]{3,2,1,0:T(8,128)(2,1)}, bf16[1,2,24,8192]{3,2,1,0:T(8,128)(2,1)S(1)}) fusion(bf16[1,2,192,8192]{3,2,1,0:T(8,128)(2,1)} %param.15, s32[]{:T(128)S(6)} %select_n.55, s32[]{:T(128)S(6)} %select_n.54, s32[]{:T(128)S(6)} %select_n.53, ...), kind=kLoop, calls=%fused_computation.30 | loop fusion | bytes 6291472 | tf_op jit(solution)/shard_map/dynamic_slice | solution.py:287
  7.8 1.5 collective-permute-start.5
  9.3 1.7 collective-permute-start.6
  11.0 1.8 collective-permute-start.7
  12.8 0.5 multiply_reduce_fusion
  13.3 0.1 stack.47
  13.4 3.0 %collective-permute-start.1 = (f32[8,16]{1,0:T(8,128)S(1)}, f32[8,16]{1,0:T(8,128)S(1)}, u32[]{:S(2)}, u32[]{:S(2)}) collective-permute-start(f32[8,16]{1,0:T(8,128)S(1)} %add.225), channel_id=1, source_target_pairs={{0,64},{1,65},{2,66},{3,67},{4,68},{5,69},{6,70},{7,71},{8,72},{9,... | collective-permute-start | bytes 1544 | tf_op jit(solution)/shard_map/ppermute | solution.py:269
  16.4 2.2 %collective-permute-done.1 = f32[8,16]{1,0:T(8,128)S(1)} collective-permute-done((f32[8,16]{1,0:T(8,128)S(1)}, f32[8,16]{1,0:T(8,128)S(1)}, u32[]{:S(2)}, u32[]{:S(2)}) %collective-permute-start.1) | collective-permute-done | bytes 544 | tf_op jit(solution)/shard_map/ppermute | solution.py:269
  18.6 1.9 collective-permute-start.2
  20.5 6.3 %dynamic-slice_bitcast_fusion = (bf16[2,4,24,8192]{3,2,1,0:T(8,128)(2,1)}, bf16[2,4,24,8192]{3,2,1,0:T(8,128)(2,1)}) fusion(bf16[2,4,2,24,8192]{4,3,2,1,0:T(8,128)(2,1)} %bitcast.46, s32[]{:T(128)S(6)} %select_n.57, s32[]{:T(128)S(6)} %select_n.56), kind=kLoop, calls=%fused_computation.1 | loop fusion | bytes 12582920 | tf_op jit(solution)/shard_map/jit(dynamic_index_in_dim)/squeeze | solution.py:54
  26.8 3.7 %collective-permute-start.3 = (f32[8,16]{1,0:T(8,128)S(1)}, f32[8,16]{1,0:T(8,128)S(1)}, u32[]{:S(2)}, u32[]{:S(2)}) collective-permute-start(f32[8,16]{1,0:T(8,128)S(1)} %add.227), channel_id=1, source_target_pairs={{0,16},{1,17},{2,18},{3,19},{4,20},{5,21},{6,22},{7,23},{8,24},{9,... | collective-permute-start | bytes 1544 | tf_op jit(solution)/shard_map/ppermute | solution.py:269
  30.6 1.5 collective-permute-done.3
  32.1 1.2 collective-permute-done.4
  33.3 0.1 fusion.5
  33.4 11.1 %collective-permute-done.6.refs_2_ = bf16[48,8192]{1,0:T(8,128)(2,1)} collective-permute-done((bf16[48,8192]{1,0:T(8,128)(2,1)}, bf16[48,8192]{1,0:T(8,128)(2,1)}, u32[]{:S(2)}, u32[]{:S(2)}) %collective-permute-start.6) | collective-permute-done | bytes 786464 | tf_op jit(solution)/shard_map/ppermute | solution.py:50
  44.4 1.2 constant_dynamic-slice_fusion.3
  45.6 1.2 constant_dynamic-slice_fusion.4
  46.8 1.2 constant_dynamic-slice_fusion.5
  48.0 1.6 pad_maximum_fusion.3
  49.7 3.0 %collective-permute-start.10 = (bf16[56,8192]{1,0:T(8,128)(2,1)}, bf16[56,8192]{1,0:T(8,128)(2,1)}, u32[]{:S(2)}, u32[]{:S(2)}) collective-permute-start(bf16[56,8192]{1,0:T(8,128)(2,1)} %get-tuple-element.63), channel_id=1, source_target_pairs={{0,7},{1,6},{2,1},{3,0},{4,3},{5,2},{6,5},{7,4},{8,15},{9,14},{10,... | collective-permute-start | bytes 2752520 | tf_op jit(solution)/shard_map/ppermute | solution.py:50
  52.6 0.1 copy.26.inv_ref
  52.7 0.1 add.224.slots_ref
  52.8 1.2 constant_dynamic-slice_fusion.2
  54.0 0.9 collective-permute-start.12
  54.9 1.2 collective-permute-start.11
  56.1 36.4 %collective-permute-done.9.refs_4_ = bf16[56,8192]{1,0:T(8,128)(2,1)} collective-permute-done((bf16[56,8192]{1,0:T(8,128)(2,1)}, bf16[56,8192]{1,0:T(8,128)(2,1)}, u32[]{:S(2)}, u32[]{:S(2)}) %collective-permute-start.9) | collective-permute-done | bytes 917536 | tf_op jit(solution)/shard_map/ppermute | solution.py:50
  92.5 0.7 collective-permute-done.10.refs_5_
  93.2 1.5 dynamic-slice_bitcast_fusion.6
  94.7 1.3 pad_maximum_fusion
  96.0 1.5 dynamic-slice_bitcast_fusion.4
  97.5 1.3 pad_maximum_fusion.1
  98.8 3.8 %collective-permute-start.15 = (bf16[96,8192]{1,0:T(8,128)(2,1)}, bf16[96,8192]{1,0:T(8,128)(2,1)}, u32[]{:S(2)}, u32[]{:S(2)}) collective-permute-start(bf16[96,8192]{1,0:T(8,128)(2,1)} %bitcast.28), channel_id=1, source_target_pairs={{0,6},{1,7},{2,0},{3,1},{4,2},{5,3},{6,4},{7,5},{8,14},{9,15},{10,... | collective-permute-start | bytes 4718600 | tf_op jit(solution)/shard_map/ppermute | solution.py:50
  102.6 7.7 %shard_map.96 = (f32[128,16]{1,0:T(8,128)S(1)}, f32[16,8,1024]{2,1,0:T(8,128)}) custom-call(f32[1,384]{1,0:T(1,128)S(1)} %add.224.slots_ref, f32[128,8]{1,0:T(8,128)S(1)} %get-tuple-element.29.pack_ref, f32[128,1]{1,0:T(8,128)S(1)} %copy.26.inv_ref, s32[128,2]{1,0:T(8,128)S(1)} %copy.22.ids_ref, f32[128,16]{1,0:T(8,128)S(1)} %get-tuple-element.30.probs_ref, ...), custom_call_target="tpu_custom_call" | custom-call | flops 20000000000 | bytes 60000000 | tf_op jit(solution)/shard_map/pallas_call | solution.py:306
  110.3 0.6 copy-done.5
  111.0 7.8 %all-to-all-start = ((f32[16,8,1024]{2,1,0:T(8,128)}), f32[16,8,1024]{2,1,0:T(8,128)S(1)}, u32[]{:S(2)}, u32[]{:S(2)}) async-start(f32[16,8,1024]{2,1,0:T(8,128)} %get-tuple-element.45), calls=%async_computation | async-start | bytes 1048576 | tf_op jit(solution)/shard_map/all_to_all | solution.py:337
  118.7 0.1 stack.46
  118.8 11.3 %all-to-all-done = f32[16,8,1024]{2,1,0:T(8,128)S(1)} async-done(((f32[16,8,1024]{2,1,0:T(8,128)}), f32[16,8,1024]{2,1,0:T(8,128)S(1)}, u32[]{:S(2)}, u32[]{:S(2)}) %all-to-all-start) | async-done | bytes 524320 | tf_op jit(solution)/shard_map/all_to_all | solution.py:337
  130.1 0.1 collective-permute-start.13
  130.2 1.2 collective-permute-done.13
  131.4 3.2 %collective-permute-done.14.refs_2_ = bf16[96,8192]{1,0:T(8,128)(2,1)} collective-permute-done((bf16[96,8192]{1,0:T(8,128)(2,1)}, bf16[96,8192]{1,0:T(8,128)(2,1)}, u32[]{:S(2)}, u32[]{:S(2)}) %collective-permute-start.14) | collective-permute-done | bytes 1572896 | tf_op jit(solution)/shard_map/ppermute | solution.py:50
  134.6 2.1 %collective-permute-done.15.refs_3_ = bf16[96,8192]{1,0:T(8,128)(2,1)} collective-permute-done((bf16[96,8192]{1,0:T(8,128)(2,1)}, bf16[96,8192]{1,0:T(8,128)(2,1)}, u32[]{:S(2)}, u32[]{:S(2)}) %collective-permute-start.15) | collective-permute-done | bytes 1572896 | tf_op jit(solution)/shard_map/ppermute | solution.py:50
  136.7 3.7 %collective-permute-start.17 = (f32[8,1024]{1,0:T(8,128)S(1)}, f32[8,1024]{1,0:T(8,128)S(1)}, u32[]{:S(2)}, u32[]{:S(2)}) collective-permute-start(f32[8,1024]{1,0:T(8,128)S(1)} %add.251), channel_id=1, source_target_pairs={{0,4},{1,5},{2,6},{3,7},{4,0},{5,1},{6,2},{7,3},{8,12},{9,13},{10,... | collective-permute-start | bytes 98312 | tf_op jit(solution)/shard_map/ppermute | solution.py:240
  140.4 0.9 collective-permute-start.18
  141.3 0.1 add.218.slots_ref
  141.4 0.8 collective-permute-done.17
  142.3 3.2 %collective-permute-done.18 = f32[8,1024]{1,0:T(8,128)S(1)} collective-permute-done((f32[8,1024]{1,0:T(8,128)S(1)}, f32[8,1024]{1,0:T(8,128)S(1)}, u32[]{:S(2)}, u32[]{:S(2)}) %collective-permute-start.18) | collective-permute-done | bytes 32800 | tf_op jit(solution)/shard_map/ppermute | solution.py:240
  145.5 1.2 dynamic-slice_bitcast_fusion.2
  146.7 1.2 dynamic-slice_bitcast_fusion.3
  147.9 1.3 pad_maximum_fusion.2
  149.2 1.7 collective-permute-start.19
  150.9 2.1 %constant_dynamic-slice_fusion.1 = bf16[2,1,1,24,8192]{4,3,2,1,0:T(8,128)(2,1)} fusion(bf16[2,4,2,24,8192]{4,3,2,1,0:T(8,128)(2,1)} %bitcast.47, s32[]{:T(128)S(6)} %select_n.63, s32[]{:T(128)S(6)} %select_n.64), kind=kLoop, calls=%fused_computation.25 | loop fusion | bytes 1572872 | tf_op jit(solution)/shard_map/jit(dynamic_index_in_dim)/dynamic_slice | solution.py:54
  153.0 1.2 constant_dynamic-slice_fusion
  154.2 27.1 %all-gather = f32[128,1024]{1,0:T(8,128)} all-gather(f32[8,1024]{1,0:T(8,128)S(1)} %add_add_fusion), channel_id=2, replica_groups=mesh['seq'=16,'exp'=8] {'seq'}, dimensions={0}, use_global_device_ids=true | all-gather | bytes 557056 | tf_op jit(solution)/shard_map/all_gather | solution.py:343
  181.3 1.9 reshape.270
  183.2 1.5 collective-permute-done.19.refs_4_
  184.7 1.1 copy-done.1
  185.8 1.6 copy-done.3
  187.4 0.8 copy-done.6
  188.3 0.8 copy-done.8
  189.0 8.3 %shard_map.97 = bf16[128,8192]{1,0:T(8,128)(2,1)} custom-call(f32[1,384]{1,0:T(1,128)S(1)} %add.218.slots_ref, f32[128,8]{1,0:T(8,128)S(1)} %get-tuple-element.29.pack_ref, f32[128,1]{1,0:T(8,128)S(1)} %copy.26.inv_ref, f32[128,16]{1,0:T(8,128)S(1)} %copy-done.6, f32[16,8192]{1,0:T(8,128)S(1)} %copy-done.4, f32[1,8192]{1,0:T(1,128)S(1)} %bitcast.45, ...), custom_call_target="tpu_custom_call" | custom-call | tf_op jit(solution)/shard_map/pallas_call | solution.py:345
  (41 shorter events, 0.3 us)
Async XLA Ops:
  2.6 10.8 %collective-permute-start = (f32[8,16]{1,0:T(8,128)S(1)}, f32[8,16]{1,0:T(8,128)S(1)}, u32[]{:S(2)}, u32[]{:S(2)}) collective-permute-start(f32[8,16]{1,0:T(8,128)S(1)} %get-tuple-element.31), channel_id=1, source_target_pairs={{0,32},{1,33},{2,34},{3,35},{4,36},{5,37},{6,38},{7,39},{8,40},{9,... | collective-permute-start | bytes 1544 | tf_op jit(solution)/shard_map/ppermute | solution.py:269
  4.3 8.5 %copy-start = (bf16[128,8192]{1,0:T(8,128)(2,1)S(1)}, bf16[128,8192]{1,0:T(8,128)(2,1)}, u32[]{:S(2)}) copy-start(bf16[128,8192]{1,0:T(8,128)(2,1)} %hidden_ref.3) | copy-start | bytes 6291460
  7.8 25.6 %collective-permute-start.5 = (bf16[48,8192]{1,0:T(8,128)(2,1)}, bf16[48,8192]{1,0:T(8,128)(2,1)}, u32[]{:S(2)}, u32[]{:S(2)}) collective-permute-start(bf16[48,8192]{1,0:T(8,128)(2,1)} %bitcast.11), channel_id=1, source_target_pairs={{0,2},{1,3},{2,4},{3,5},{4,6},{5,7},{6,0},{7,1},{8,10},{9,11},{10,... | collective-permute-start | bytes 2359304 | tf_op jit(solution)/shard_map/ppermute | solution.py:50
  9.3 35.2 %collective-permute-start.6 = (bf16[48,8192]{1,0:T(8,128)(2,1)}, bf16[48,8192]{1,0:T(8,128)(2,1)}, u32[]{:S(2)}, u32[]{:S(2)}) collective-permute-start(bf16[48,8192]{1,0:T(8,128)(2,1)} %bitcast.12), channel_id=1, source_target_pairs={{0,6},{1,7},{2,0},{3,1},{4,2},{5,3},{6,4},{7,5},{8,14},{9,15},{10,... | collective-permute-start | bytes 2359304 | tf_op jit(solution)/shard_map/ppermute | solution.py:50
  11.0 41.8 %collective-permute-start.7 = (bf16[48,8192]{1,0:T(8,128)(2,1)}, bf16[48,8192]{1,0:T(8,128)(2,1)}, u32[]{:S(2)}, u32[]{:S(2)}) collective-permute-start(bf16[48,8192]{1,0:T(8,128)(2,1)} %bitcast.13), channel_id=1, source_target_pairs={{0,4},{1,5},{2,6},{3,7},{4,0},{5,1},{6,2},{7,3},{8,12},{9,13},{10,... | collective-permute-start | bytes 2359304 | tf_op jit(solution)/shard_map/ppermute | solution.py:50
  13.4 5.2 %collective-permute-start.1 = (f32[8,16]{1,0:T(8,128)S(1)}, f32[8,16]{1,0:T(8,128)S(1)}, u32[]{:S(2)}, u32[]{:S(2)}) collective-permute-start(f32[8,16]{1,0:T(8,128)S(1)} %add.225), channel_id=1, source_target_pairs={{0,64},{1,65},{2,66},{3,67},{4,68},{5,69},{6,70},{7,71},{8,72},{9,... | collective-permute-start | bytes 1544 | tf_op jit(solution)/shard_map/ppermute | solution.py:269
  18.6 8.2 %collective-permute-start.2 = (f32[8,16]{1,0:T(8,128)S(1)}, f32[8,16]{1,0:T(8,128)S(1)}, u32[]{:S(2)}, u32[]{:S(2)}) collective-permute-start(f32[8,16]{1,0:T(8,128)S(1)} %add.226), channel_id=1, source_target_pairs={{0,8},{1,9},{2,10},{3,11},{4,12},{5,13},{6,14},{7,15},{8,0},{9,1},... | collective-permute-start | bytes 1544 | tf_op jit(solution)/shard_map/ppermute | solution.py:269
  26.8 20.0 %collective-permute-start.8 = (bf16[2,4,24,8192]{3,2,1,0:T(8,128)(2,1)}, bf16[2,4,24,8192]{3,2,1,0:T(8,128)(2,1)}, u32[]{:S(2)}, u32[]{:S(2)}) collective-permute-start(bf16[2,4,24,8192]{3,2,1,0:T(8,128)(2,1)} %get-tuple-element.56), channel_id=1, source_target_pairs={{0,1},{1,0},{2,3},{3,2},{4,5},{5,4},{6,7},{7,6},{8,9},{9,8},{10,11... | collective-permute-start | bytes 9437192 | tf_op jit(solution)/shard_map/ppermute | solution.py:50
  26.8 5.2 %collective-permute-start.3 = (f32[8,16]{1,0:T(8,128)S(1)}, f32[8,16]{1,0:T(8,128)S(1)}, u32[]{:S(2)}, u32[]{:S(2)}) collective-permute-start(f32[8,16]{1,0:T(8,128)S(1)} %add.227), channel_id=1, source_target_pairs={{0,16},{1,17},{2,18},{3,19},{4,20},{5,21},{6,22},{7,23},{8,24},{9,... | collective-permute-start | bytes 1544 | tf_op jit(solution)/shard_map/ppermute | solution.py:269
  32.1 1.2 collective-permute-start.4
  49.7 42.8 %collective-permute-start.9 = (bf16[56,8192]{1,0:T(8,128)(2,1)}, bf16[56,8192]{1,0:T(8,128)(2,1)}, u32[]{:S(2)}, u32[]{:S(2)}) collective-permute-start(bf16[56,8192]{1,0:T(8,128)(2,1)} %get-tuple-element.64), channel_id=1, source_target_pairs={{0,3},{1,2},{2,5},{3,4},{4,7},{5,6},{6,1},{7,0},{8,11},{9,10},{10,... | collective-permute-start | bytes 2752520 | tf_op jit(solution)/shard_map/ppermute | solution.py:50
  49.7 43.5 %collective-permute-start.10 = (bf16[56,8192]{1,0:T(8,128)(2,1)}, bf16[56,8192]{1,0:T(8,128)(2,1)}, u32[]{:S(2)}, u32[]{:S(2)}) collective-permute-start(bf16[56,8192]{1,0:T(8,128)(2,1)} %get-tuple-element.63), channel_id=1, source_target_pairs={{0,7},{1,6},{2,1},{3,0},{4,3},{5,2},{6,5},{7,4},{8,15},{9,14},{10,... | collective-permute-start | bytes 2752520 | tf_op jit(solution)/shard_map/ppermute | solution.py:50
  54.0 48.6 %collective-permute-start.12 = (bf16[48,8192]{1,0:T(8,128)(2,1)S(1)}, bf16[48,8192]{1,0:T(8,128)(2,1)S(1)}, u32[]{:S(2)}, u32[]{:S(2)}) collective-permute-start(bf16[48,8192]{1,0:T(8,128)(2,1)S(1)} %bitcast.51), channel_id=1, source_target_pairs={{0,1},{1,0},{2,3},{3,2},{4,5},{5,4},{6,7},{7,6},{8,9},{9,8},{10,11... | collective-permute-start | bytes 2359304 | tf_op jit(solution)/shard_map/ppermute | solution.py:50
  54.9 47.7 %collective-permute-start.11 = (bf16[56,8192]{1,0:T(8,128)(2,1)}, bf16[56,8192]{1,0:T(8,128)(2,1)S(1)}, u32[]{:S(2)}, u32[]{:S(2)}) collective-permute-start(bf16[56,8192]{1,0:T(8,128)(2,1)} %get-tuple-element.62), channel_id=1, source_target_pairs={{0,5},{1,4},{2,7},{3,6},{4,1},{5,0},{6,3},{7,2},{8,13},{9,12},{10,... | collective-permute-start | bytes 2752520 | tf_op jit(solution)/shard_map/ppermute | solution.py:50
  96.0 38.7 %collective-permute-start.14 = (bf16[96,8192]{1,0:T(8,128)(2,1)}, bf16[96,8192]{1,0:T(8,128)(2,1)}, u32[]{:S(2)}, u32[]{:S(2)}) collective-permute-start(bf16[96,8192]{1,0:T(8,128)(2,1)} %bitcast.25), channel_id=1, source_target_pairs={{0,2},{1,3},{2,4},{3,5},{4,6},{5,7},{6,0},{7,1},{8,10},{9,11},{10,... | collective-permute-start | bytes 4718600 | tf_op jit(solution)/shard_map/ppermute | solution.py:50
  97.4 5.2 %copy-start.2 = (bf16[128,8192]{1,0:T(8,128)(2,1)S(1)}, bf16[128,8192]{1,0:T(8,128)(2,1)}, u32[]{:S(2)}) copy-start(bf16[128,8192]{1,0:T(8,128)(2,1)} %grad_ref.3) | copy-start | bytes 6291460
  97.5 5.2 %copy-start.7 = (f32[8192]{0:T(1024)S(1)}, f32[8192]{0:T(1024)}, u32[]{:S(2)}) copy-start(f32[8192]{0:T(1024)} %param.10) | copy-start | bytes 98308
  98.8 37.9 %collective-permute-start.15 = (bf16[96,8192]{1,0:T(8,128)(2,1)}, bf16[96,8192]{1,0:T(8,128)(2,1)}, u32[]{:S(2)}, u32[]{:S(2)}) collective-permute-start(bf16[96,8192]{1,0:T(8,128)(2,1)} %bitcast.28), channel_id=1, source_target_pairs={{0,6},{1,7},{2,0},{3,1},{4,2},{5,3},{6,4},{7,5},{8,14},{9,15},{10,... | collective-permute-start | bytes 4718600 | tf_op jit(solution)/shard_map/ppermute | solution.py:50
  110.3 0.6 copy-start.5
  111.0 19.1 %all-to-all-start = ((f32[16,8,1024]{2,1,0:T(8,128)}), f32[16,8,1024]{2,1,0:T(8,128)S(1)}, u32[]{:S(2)}, u32[]{:S(2)}) async-start(f32[16,8,1024]{2,1,0:T(8,128)} %get-tuple-element.45), calls=%async_computation | async-start | bytes 1048576 | tf_op jit(solution)/shard_map/all_to_all | solution.py:337
  130.1 1.3 collective-permute-start.13
  136.7 5.6 %collective-permute-start.17 = (f32[8,1024]{1,0:T(8,128)S(1)}, f32[8,1024]{1,0:T(8,128)S(1)}, u32[]{:S(2)}, u32[]{:S(2)}) collective-permute-start(f32[8,1024]{1,0:T(8,128)S(1)} %add.251), channel_id=1, source_target_pairs={{0,4},{1,5},{2,6},{3,7},{4,0},{5,1},{6,2},{7,3},{8,12},{9,13},{10,... | collective-permute-start | bytes 98312 | tf_op jit(solution)/shard_map/ppermute | solution.py:240
  140.4 5.1 %collective-permute-start.18 = (f32[8,1024]{1,0:T(8,128)S(1)}, f32[8,1024]{1,0:T(8,128)S(1)}, u32[]{:S(2)}, u32[]{:S(2)}) collective-permute-start(f32[8,1024]{1,0:T(8,128)S(1)} %add.251), channel_id=1, source_target_pairs={{0,6},{1,7},{2,4},{3,5},{4,2},{5,3},{6,0},{7,1},{8,14},{9,15},{10,... | collective-permute-start | bytes 98312 | tf_op jit(solution)/shard_map/ppermute | solution.py:240
  141.3 4.2 %collective-permute-start.16 = (f32[8,1024]{1,0:T(8,128)S(1)}, f32[8,1024]{1,0:T(8,128)S(1)}, u32[]{:S(2)}, u32[]{:S(2)}) collective-permute-start(f32[8,1024]{1,0:T(8,128)S(1)} %add.251), channel_id=1, source_target_pairs={{0,2},{1,3},{2,0},{3,1},{4,6},{5,7},{6,4},{7,5},{8,10},{9,11},{10,... | collective-permute-start | bytes 98312 | tf_op jit(solution)/shard_map/ppermute | solution.py:240
  149.2 35.5 %copy-start.4 = (f32[16,8192]{1,0:T(8,128)S(1)}, f32[16,8192]{1,0:T(8,128)}, u32[]{:S(2)}) copy-start(f32[16,8192]{1,0:T(8,128)} %weight_ref.1) | copy-start | bytes 1572868
  149.2 35.5 %collective-permute-start.19 = (bf16[96,8192]{1,0:T(8,128)(2,1)}, bf16[96,8192]{1,0:T(8,128)(2,1)}, u32[]{:S(2)}, u32[]{:S(2)}) collective-permute-start(bf16[96,8192]{1,0:T(8,128)(2,1)} %bitcast.31), channel_id=1, source_target_pairs={{0,4},{1,5},{2,6},{3,7},{4,0},{5,1},{6,2},{7,3},{8,12},{9,13},{10,... | collective-permute-start | bytes 4718600 | tf_op jit(solution)/shard_map/ppermute | solution.py:50
  184.7 1.1 copy-start.1
  185.8 1.6 copy-start.3
  187.4 0.8 copy-start.6
  188.3 0.8 copy-start.8

commit v5 on v4

--- a/solution.py
+++ b/solution.py
@@ -48,10 +48,6 @@
 def ring_permute(v, s, m):
     perm = [(i, (((i >> 1) + s) % 4) * 2 + ((i & 1) ^ m)) for i in range(8)]
     return lax.ppermute(v, "exp", perm)
-
-
-def pick(v, axis, i):
-    return lax.dynamic_index_in_dim(v, i, axis, keepdims=False)
 
 
 def slot_numbers(sources):
@@ -248,7 +244,14 @@
     gain = norm_gain.reshape(1, D)
     sources = [((at["x"] - s) & 3) * 2 + (at["c"] ^ m) for s, m in ROUTES]
     slots = slot_numbers(sources)
-    grad_slots = slot_numbers([sources[i] for i in (0, 7, 1, 4, 2, 5, 3, 6)])
+
+    def block(array, s, m):
+        to = ((at["x"] + s) & 3) * 2 + (at["c"] ^ m)
+        return lax.dynamic_slice(array, (0, 0, to * CAP, 0), (1, 2, CAP, D)).reshape(ROWS, D)
+
+    ready = [block(expert_out, s, m) for s, m in ROUTES[1:4]]
+    ids, *ready = after(expert_ids, *ready)
+    outs = [ring_permute(b, s, m) for b, (s, m) in zip(ready, ROUTES[1:4])]
 
     pack, probs, counts = pl.pallas_call(
         pre_kernel,
@@ -260,10 +263,9 @@
         in_specs=[VMEM] * 2,
         out_specs=(VMEM,) * 3,
         compiler_params=params(8),
-    )(expert_ids, router_logits)
+    )(ids, router_logits)
     wide = hidden.astype(F32)
     inv = lax.rsqrt(jnp.mean(wide * wide, axis=1, keepdims=True) + 1e-05)
-    me = at["x"] * 2 + at["c"]
     tally = [counts]
     for axis, d in (("y", 1), ("y", 2), ("z", 1), ("z", 2), ("c", 1)):
         tally.append(tally[-1] + lax.ppermute(tally[-1], AXES, xor_perm(axis, d)))
@@ -271,36 +273,22 @@
     share = jnp.concatenate([share, (tally[5][0:1] - share.astype(F32)).astype(BF16)], axis=1)
     share = jnp.pad(share, ((0, 7), (0, D - 2 * EXPERTS)))
 
-    source, tally[1] = after(expert_grad, tally[1])
-    by_core = source.reshape(2, 4, 2, CAP, D)
-    swap = ring_permute(pick(by_core, 2, at["c"] ^ 1), 0, 1)
-    mine = pick(by_core, 2, at["c"])
-
-    outs = []
-    for n, (s, m) in enumerate(ROUTES[1:]):
-        array = expert_out
-        if n == 3:
-            array, swap, share = after(array, swap, share)
-        if n > 3:
-            array, outs[n - 4] = after(array, outs[n - 4])
-        to = ((at["x"] + s) & 3) * 2 + (at["c"] ^ m)
-        block = lax.dynamic_slice(array, (0, 0, to * CAP, 0), (1, 2, CAP, D))
-        block = block.reshape(ROWS, D)
-        if 3 <= n <= 5:
-            block = jnp.concatenate([block, share], axis=0)
-        outs.append(ring_permute(block, s, m))
-    own_out = lax.dynamic_slice(expert_out, (0, 0, me * CAP, 0), (1, 2, CAP, D)).reshape(ROWS, D)
-
-    def send_grad(s, *deps):
-        a, b, *deps = after(mine, swap, *deps)
-        to = (at["x"] + s) & 3
-        block = jnp.concatenate([pick(a, 1, to), pick(b, 1, to)], axis=0)
-        return ring_permute(block.reshape(2 * ROWS, D), s, 0), *deps
-
-    grads = [pick(mine, 1, at["x"]).reshape(ROWS, D), pick(swap, 1, at["x"]).reshape(ROWS, D)]
-    for s, n in ((1, 3), (3, 4)):
-        moved, outs[n] = send_grad(s, outs[n])
-        grads.append(moved)
+    source, tally[1] = after(expert_out, tally[1])
+    ready = [block(source, s, m) for s, m in ROUTES[4:]]
+    ready = [jnp.concatenate([b, share], axis=0) for b in ready[:3]] + ready[3:]
+    for n, (b, (s, m)) in enumerate(zip(ready, ROUTES[4:])):
+        if n != 1:
+            b, outs[n % 3] = after(b, outs[n % 3])
+        outs.append(ring_permute(b, s, m))
+    own_out = block(expert_out, 0, 0)
+
+    source, tally[2] = after(expert_grad, tally[2])
+    grads = [block(source, 0, 0)]
+    for n, (s, m) in zip((3, 3, 4), ROUTES[1:4]):
+        b, outs[n] = after(block(source, s, m), outs[n])
+        grads.append(ring_permute(b, s, m))
+    source, tally[3] = after(expert_grad, tally[3])
+    rest = [block(source, s, m) for s, m in ROUTES[4:]]
 
     small = lambda *shape: pl.BlockSpec(shape, lambda p, c: (0,) * len(shape))
     logit, partial = pl.pallas_call(
@@ -336,10 +324,10 @@
     )(slots, pack, inv, expert_ids, probs, tally[5], gain, hidden, grad_out, own_out, *outs)
     partial = jnp.sum(lax.all_to_all(partial, "seq", 0, 0, tiled=True), axis=0)
     partial = partial + lax.ppermute(partial, AXES, xor_perm("c", 1))
-    partial, grads[2], grads[3] = after(partial, grads[2], grads[3])
+    partial, *grads[1:4] = after(partial, *grads[1:4])
     partial = sum_x(partial)
-    moved, partial = send_grad(2, partial)
-    grads.append(moved)
+    *rest, partial = after(*rest, partial)
+    grads += [ring_permute(b, s, m) for b, (s, m) in zip(rest, ROUTES[4:])]
     router_grad = lax.all_gather(partial, "seq").reshape(EXPERTS, D)
 
     grad_hidden = pl.pallas_call(
@@ -365,8 +353,8 @@
             pltpu.VMEM((TOK, 128), F32),
             pltpu.VMEM((TOK, 128), F32),
         ],
-        compiler_params=params(28),
-    )(grad_slots, pack, inv, logit, router_weight, gain, hidden, grad_out, *grads)
+        compiler_params=params(60),
+    )(slots, pack, inv, logit, router_weight, gain, hidden, grad_out, *grads)
     return grad_hidden, router_grad
 
 

time: 198 us -> 176 us (0.89)
  blocking collectives: 27.1 us -> 44.2 us
  local copies, waits for them, and re-layouts: 32.1 us -> 15.5 us
  waiting for transfers between devices: 76.4 us -> 64.3 us
  starting transfers between devices: 38.3 us -> 32.5 us
  other arithmetic: 6.28 us -> 0.99 us
    all_to_all x0 -> x1, blocking collectives: none -> 19 us  [body(): partial = jnp.sum(lax.all_to_all(partial, 'seq', 0, 0, tiled=True), axis=0)]
    squeeze x5 -> x0, local copies, waits for them, and re-layouts: 11.6 us -> none  [pick(): return lax.dynamic_index_in_dim(v, i, axis, keepdims=False)]
    all_to_all x1 -> x0, waiting for transfers between devices: 11.3 us -> none  [body(): partial = jnp.sum(lax.all_to_all(partial, 'seq', 0, 0, tiled=True), axis=0)]
    all_to_all x1 -> x0, starting transfers between devices: 7.75 us -> none  [body(): partial = jnp.sum(lax.all_to_all(partial, 'seq', 0, 0, tiled=True), axis=0)]
    concatenate x4 -> x1, other arithmetic: 5.49 us -> 0.27 us  [body(): ready = [jnp.concatenate([b, share], axis=0) for b in ready[:3]] + ready[3:]]
    unnamed x20 -> x26, local copies, waits for them, and re-layouts: 6.55 us -> 2.22 us
    ppermute x11 -> x14, waiting for transfers between devices: 55 us -> 54.1 us  [ring_permute(): return lax.ppermute(v, 'exp', perm)]
    dynamic_slice x7 -> x3, local copies, waits for them, and re-layouts: 11.5 us -> 12 us  [block(): lax.dynamic_slice(array, (0, 0, to * CAP, 0), (1, 2, CAP, D))]
  transfers between devices with their start and end apart: 21 -> 23, of which waited for: 13 -> 12; matrix products, arithmetic and copies ran while one was open for 14% -> 6% of each run, Pallas kernels for 4% -> 4%
where the time goes in v5:
time: 176 us; the launch traced here: 175 us
  waiting for transfers between devices  64.3 us (37%)
  blocking collectives  44.2 us (25%)
  starting transfers between devices  32.5 us (18%)
  Pallas kernels  16.9 us (10%)
  local copies, waits for them, and re-layouts  15.5 us (9%)
    ppermute x14, waiting for transfers between devices, ring_permute(): return lax.ppermute(v, 'exp', perm)  54.1 us
    all_gather x1, blocking collectives, body(): router_grad = lax.all_gather(partial, 'seq').reshape(EXPERTS, D)  25.3 us
    all_to_all x1, blocking collectives, body(): partial = jnp.sum(lax.all_to_all(partial, 'seq', 0, 0, tiled=True), axis=0)  19 us
    ppermute x14, starting transfers between devices, ring_permute(): return lax.ppermute(v, 'exp', perm)  16 us
    dynamic_slice x3, local copies, waits for them, and re-layouts, block(): lax.dynamic_slice(array, (0, 0, to * CAP, 0), (1, 2, CAP, D))  12 us
    ppermute x5, starting transfers between devices, body(): tally.append(tally[-1] + lax.ppermute(tally[-1], AXES, xor_perm(axis, d)))  10.5 us
    pallas_call x1, Pallas kernels, body(): pl.pallas_call(last_kernel, grid=(2, STEPS), out_shape=jax.ShapeDtypeStru...  10 us
    pallas_call x1, Pallas kernels, body(): pl.pallas_call(mid_kernel, grid=(2, STEPS), out_shape=(jax.ShapeDtypeStru...  6.56 us
  transfers between devices with their start and end apart: 23, of which 12 were waited for; matrix products, arithmetic and copies ran while one was open for 6% of the time, Pallas kernels for 4%

profile of v5, /device:TPU:0, one launch (start us, length us, event | category | flops | bytes accessed | tf_op | source)
XLA Modules:
  0.0 175.3 jit_solution(17780439425069025768)
XLA Ops:
  0.7 0.0 copy-start
  0.7 3.4 %constant_dynamic-slice_fusion.12 = (bf16[1,2,24,8192]{3,2,1,0:T(8,128)(2,1)S(1)}, bf16[1,2,24,8192]{3,2,1,0:T(8,128)(2,1)}, bf16[1,2,24,8192]{3,2,1,0:T(8,128)(2,1)}, bf16[1,2,24,8192]{3,2,1,0:T(8,128)(2,1)}) fusion(bf16[1,2,192,8192]{3,2,1,0:T(8,128)(2,1)} %param.15, s32[]{:T(128)S(6)} %select_n.35, s32[]{:T(128)S(6)} %select_n.34, s32[]{:T(128)S(6)} %select_n.33, ...), kind=kLoop, calls=%fused_computation.25 | loop fusion | bytes 6291472 | tf_op jit(solution)/shard_map/dynamic_slice | solution.py:250
  4.1 0.1 copy.10.ids_ref
  4.2 0.1 copy.11.logits_ref
  4.3 0.4 shard_map.95
  4.7 1.7 collective-permute-start
  6.5 1.5 collective-permute-start.5
  7.9 2.7 %collective-permute-start.7 = (bf16[48,8192]{1,0:T(8,128)(2,1)}, bf16[48,8192]{1,0:T(8,128)(2,1)}, u32[]{:S(2)}, u32[]{:S(2)}) collective-permute-start(bf16[48,8192]{1,0:T(8,128)(2,1)} %bitcast.35), channel_id=1, source_target_pairs={{0,4},{1,5},{2,6},{3,7},{4,0},{5,1},{6,2},{7,3},{8,12},{9,13},{10,... | collective-permute-start | bytes 2359304 | tf_op jit(solution)/shard_map/ppermute | solution.py:50
  10.7 1.4 collective-permute-start.6
  12.1 0.1 stack.35
  12.2 0.5 multiply_reduce_fusion
  12.7 0.1 iota_add_fusion
  12.8 0.0 collective-permute-done
  12.8 2.9 %collective-permute-start.1 = (f32[8,16]{1,0:T(8,128)S(1)}, f32[8,16]{1,0:T(8,128)S(1)}, u32[]{:S(2)}, u32[]{:S(2)}) collective-permute-start(f32[8,16]{1,0:T(8,128)S(1)} %add.195), channel_id=1, source_target_pairs={{0,64},{1,65},{2,66},{3,67},{4,68},{5,69},{6,70},{7,71},{8,72},{9,... | collective-permute-start | bytes 1544 | tf_op jit(solution)/shard_map/ppermute | solution.py:271
  15.7 2.2 %collective-permute-done.1 = f32[8,16]{1,0:T(8,128)S(1)} collective-permute-done((f32[8,16]{1,0:T(8,128)S(1)}, f32[8,16]{1,0:T(8,128)S(1)}, u32[]{:S(2)}, u32[]{:S(2)}) %collective-permute-start.1) | collective-permute-done | bytes 544 | tf_op jit(solution)/shard_map/ppermute | solution.py:271
  17.9 1.9 %collective-permute-start.2 = (f32[8,16]{1,0:T(8,128)S(1)}, f32[8,16]{1,0:T(8,128)S(1)}, u32[]{:S(2)}, u32[]{:S(2)}) collective-permute-start(f32[8,16]{1,0:T(8,128)S(1)} %add.196), channel_id=1, source_target_pairs={{0,8},{1,9},{2,10},{3,11},{4,12},{5,13},{6,14},{7,15},{8,0},{9,1},... | collective-permute-start | bytes 1544 | tf_op jit(solution)/shard_map/ppermute | solution.py:271
  19.9 0.1 copy.13.ids_ref
  20.0 0.1 add.183.slots_ref
  20.0 0.1 copy.14.inv_ref
  20.2 1.4 collective-permute-done.2
  21.5 3.9 %collective-permute-start.3 = (f32[8,16]{1,0:T(8,128)S(1)}, f32[8,16]{1,0:T(8,128)S(1)}, u32[]{:S(2)}, u32[]{:S(2)}) collective-permute-start(f32[8,16]{1,0:T(8,128)S(1)} %add.197), channel_id=1, source_target_pairs={{0,16},{1,17},{2,18},{3,19},{4,20},{5,21},{6,22},{7,23},{8,24},{9,... | collective-permute-start | bytes 1544 | tf_op jit(solution)/shard_map/ppermute | solution.py:271
  25.4 1.6 collective-permute-done.3
  27.0 0.0 collective-permute-start.4
  27.0 4.9 %constant_dynamic-slice_fusion = (bf16[1,2,24,8192]{3,2,1,0:T(8,128)(2,1)}, bf16[1,2,24,8192]{3,2,1,0:T(8,128)(2,1)}, bf16[1,2,24,8192]{3,2,1,0:T(8,128)(2,1)}, ...) fusion(bf16[1,2,192,8192]{3,2,1,0:T(8,128)(2,1)} %param.14, ...), kind=kLoop, calls=%fused_computation.13 | loop fusion | bytes 12582928 | tf_op jit(solution)/shard_map/dynamic_slice | solution.py:250
  32.0 0.0 collective-permute-done.4
  32.0 0.1 fusion.5
  32.1 0.3 pad_maximum_fusion
  32.3 0.2 collective-permute-start.9
  32.5 0.0 collective-permute-done.5.refs_1_
  32.5 1.6 collective-permute-start.8
  34.2 12.2 %collective-permute-done.7.refs_3_ = bf16[48,8192]{1,0:T(8,128)(2,1)} collective-permute-done((bf16[48,8192]{1,0:T(8,128)(2,1)}, bf16[48,8192]{1,0:T(8,128)(2,1)}, u32[]{:S(2)}, u32[]{:S(2)}) %collective-permute-start.7) | collective-permute-done | bytes 786464 | tf_op jit(solution)/shard_map/ppermute | solution.py:50
  46.3 0.9 collective-permute-start.11
  47.3 3.6 %constant_dynamic-slice_fusion.4 = (bf16[1,2,24,8192]{3,2,1,0:T(8,128)(2,1)}, bf16[1,2,24,8192]{3,2,1,0:T(8,128)(2,1)}, bf16[1,2,24,8192]{3,2,1,0:T(8,128)(2,1)}, bf16[1,2,24,8192]{3,2,1,0:T(8,128)(2,1)}) fusion(bf16[1,2,192,8192]{3,2,1,0:T(8,128)(2,1)} %param.14, s32[]{:T(128)S(6)} %select_n.35, s32[]{:T(128)S(6)} %select_n.34, s32[]{:T(128)S(6)} %select_n.32, ...), kind=kLoop, calls=%fused_computation.17 | loop fusion | bytes 6291472 | tf_op jit(solution)/shard_map/dynamic_slice | solution.py:250
  50.8 13.7 %collective-permute-done.9.refs_5_ = bf16[56,8192]{1,0:T(8,128)(2,1)S(1)} collective-permute-done((bf16[56,8192]{1,0:T(8,128)(2,1)S(1)}, bf16[56,8192]{1,0:T(8,128)(2,1)S(1)}, u32[]{:S(2)}, u32[]{:S(2)}) %collective-permute-start.9) | collective-permute-done | bytes 917536 | tf_op jit(solution)/shard_map/ppermute | solution.py:50
  64.5 1.6 collective-permute-start.15
  66.2 0.0 collective-permute-done.8.refs_4_
  66.2 2.0 %collective-permute-start.14 = (bf16[48,8192]{1,0:T(8,128)(2,1)}, bf16[48,8192]{1,0:T(8,128)(2,1)}, u32[]{:S(2)}, u32[]{:S(2)}) collective-permute-start(bf16[48,8192]{1,0:T(8,128)(2,1)} %bitcast.17), channel_id=1, source_target_pairs={{0,6},{1,7},{2,0},{3,1},{4,2},{5,3},{6,4},{7,5},{8,14},{9,15},{10,... | collective-permute-start | bytes 2359304 | tf_op jit(solution)/shard_map/ppermute | solution.py:50
  68.2 0.9 collective-permute-start.13
  69.1 0.0 collective-permute-done.11.refs_7_
  69.1 13.6 %collective-permute-done.10.refs_6_ = bf16[56,8192]{1,0:T(8,128)(2,1)S(1)} collective-permute-done((bf16[56,8192]{1,0:T(8,128)(2,1)S(1)}, bf16[56,8192]{1,0:T(8,128)(2,1)S(1)}, u32[]{:S(2)}, u32[]{:S(2)}) %collective-permute-start.10) | collective-permute-done | bytes 917536 | tf_op jit(solution)/shard_map/ppermute | solution.py:50
  82.7 6.6 %shard_map.96 = (f32[128,16]{1,0:T(8,128)S(1)}, f32[16,8,1024]{2,1,0:T(8,128)S(1)}) custom-call(f32[1,384]{1,0:T(1,128)S(1)} %add.183.slots_ref, f32[128,8]{1,0:T(8,128)S(1)} %get-tuple-element.36.pack_ref, f32[128,1]{1,0:T(8,128)S(1)} %copy.14.inv_ref, s32[128,2]{1,0:T(8,128)S(1)} %copy.13.ids_ref, f32[128,16]{1,0:T(8,128)S(1)} %get-tuple-element.37.probs_ref, ...), custom_call_target="tpu_custom_call" | custom-call | flops 20000000000 | bytes 60000000 | tf_op jit(solution)/shard_map/pallas_call | solution.py:294
  89.3 0.6 copy-done.4
  89.9 19.0 %all_to_all.5 = f32[16,8,1024]{2,1,0:T(8,128)S(1)} all-to-all(f32[16,8,1024]{2,1,0:T(8,128)S(1)} %get-tuple-element.54), channel_id=1, replica_groups=mesh['seq'=16,'exp'=8] {'seq'}, dimensions={0} | all-to-all | bytes 1048576 | tf_op jit(solution)/shard_map/all_to_all | solution.py:325
  108.9 1.4 collective-permute-start.12
  110.3 0.9 collective-permute-done.12
  111.2 6.4 %collective-permute-done.14.refs_2_ = bf16[48,8192]{1,0:T(8,128)(2,1)} collective-permute-done((bf16[48,8192]{1,0:T(8,128)(2,1)}, bf16[48,8192]{1,0:T(8,128)(2,1)}, u32[]{:S(2)}, u32[]{:S(2)}) %collective-permute-start.14) | collective-permute-done | bytes 786464 | tf_op jit(solution)/shard_map/ppermute | solution.py:50
  117.5 0.4 collective-permute-done.13.refs_1_
  117.9 2.0 %collective-permute-start.16 = (f32[8,1024]{1,0:T(8,128)S(1)}, f32[8,1024]{1,0:T(8,128)S(1)}, u32[]{:S(2)}, u32[]{:S(2)}) collective-permute-start(f32[8,1024]{1,0:T(8,128)S(1)} %add.208), channel_id=1, source_target_pairs={{0,2},{1,3},{2,0},{3,1},{4,6},{5,7},{6,4},{7,5},{8,10},{9,11},{10,... | collective-permute-start | bytes 98312 | tf_op jit(solution)/shard_map/ppermute | solution.py:236
  119.9 1.7 collective-permute-start.17
  121.6 1.0 collective-permute-start.18
  122.6 0.0 collective-permute-done.16
  122.6 2.8 %collective-permute-done.17 = f32[8,1024]{1,0:T(8,128)S(1)} collective-permute-done((f32[8,1024]{1,0:T(8,128)S(1)}, f32[8,1024]{1,0:T(8,128)S(1)}, u32[]{:S(2)}, u32[]{:S(2)}) %collective-permute-start.17) | collective-permute-done | bytes 32800 | tf_op jit(solution)/shard_map/ppermute | solution.py:236
  125.4 1.4 collective-permute-done.18
  126.8 0.1 collective-permute-start.19
  126.8 2.9 %collective-permute-start.20 = (bf16[48,8192]{1,0:T(8,128)(2,1)}, bf16[48,8192]{1,0:T(8,128)(2,1)S(1)}, u32[]{:S(2)}, u32[]{:S(2)}) collective-permute-start(bf16[48,8192]{1,0:T(8,128)(2,1)} %bitcast.39), channel_id=1, source_target_pairs={{0,7},{1,6},{2,1},{3,0},{4,3},{5,2},{6,5},{7,4},{8,15},{9,14},{10,... | collective-permute-start | bytes 2359304 | tf_op jit(solution)/shard_map/ppermute | solution.py:50
  129.8 0.0 collective-permute-start.21
  129.8 25.3 %all-gather = f32[128,1024]{1,0:T(8,128)S(1)} all-gather(f32[8,1024]{1,0:T(8,128)S(1)} %add_add_fusion), channel_id=2, replica_groups=mesh['seq'=16,'exp'=8] {'seq'}, dimensions={0}, use_global_device_ids=true | all-gather | bytes 557056 | tf_op jit(solution)/shard_map/all_gather | solution.py:331
  155.0 0.9 reshape.185
  155.9 7.9 %collective-permute-done.19.refs_4_ = bf16[48,8192]{1,0:T(8,128)(2,1)S(1)} collective-permute-done((bf16[48,8192]{1,0:T(8,128)(2,1)}, bf16[48,8192]{1,0:T(8,128)(2,1)S(1)}, u32[]{:S(2)}, u32[]{:S(2)}) %collective-permute-start.19) | collective-permute-done | bytes 786464 | tf_op jit(solution)/shard_map/ppermute | solution.py:50
  163.9 0.0 collective-permute-done.21.refs_6_
  163.9 0.8 copy-done.7
  164.8 0.3 copy-done.8
  165.1 0.2 copy-done.9
  165.3 10.0 %shard_map.97 = bf16[128,8192]{1,0:T(8,128)(2,1)} custom-call(f32[1,384]{1,0:T(1,128)} %copy-done.6, f32[128,8]{1,0:T(8,128)} %copy-done.3, f32[128,1]{1,0:T(8,128)} %copy-done.2, f32[128,16]{1,0:T(8,128)} %copy-done.4, f32[16,8192]{1,0:T(8,128)} %weight_ref.1, f32[1,8192]{1,0:T(1,128)} %bitcast.28, bf16[128,8192]{1,0:T(8,128)(2,1)} %hidden_ref.3, ...), custom_call_target="tpu_custom_call" | custom-call | tf_op jit(solution)/shard_map/pallas_call | solution.py:333
  (37 shorter events, 0.1 us)
Async XLA Ops:
  0.7 3.5 %copy-start.11 = (s32[128,2]{0,1:T(2,128)S(1)}, s32[128,2]{0,1:T(2,128)}, u32[]{:S(2)}) copy-start(s32[128,2]{0,1:T(2,128)} %param.13) | copy-start | bytes 3076
  0.7 3.6 %copy-start.10 = (f32[128,16]{0,1:T(8,128)S(1)}, f32[128,16]{0,1:T(8,128)}, u32[]{:S(2)}) copy-start(f32[128,16]{0,1:T(8,128)} %param.11) | copy-start | bytes 24580
  0.7 11.5 %copy-start = (bf16[128,8192]{1,0:T(8,128)(2,1)S(1)}, bf16[128,8192]{1,0:T(8,128)(2,1)}, u32[]{:S(2)}) copy-start(bf16[128,8192]{1,0:T(8,128)(2,1)} %hidden_ref.3) | copy-start | bytes 6291460
  4.7 78.0 %copy-start.3 = (f32[128,8]{1,0:T(8,128)}, f32[128,8]{1,0:T(8,128)S(1)}, u32[]{:S(2)}) copy-start(f32[128,8]{1,0:T(8,128)S(1)} %get-tuple-element.36.pack_ref) | copy-start | bytes 12292
  4.7 8.1 %collective-permute-start = (f32[8,16]{1,0:T(8,128)S(1)}, f32[8,16]{1,0:T(8,128)S(1)}, u32[]{:S(2)}, u32[]{:S(2)}) collective-permute-start(f32[8,16]{1,0:T(8,128)S(1)} %get-tuple-element.38), channel_id=1, source_target_pairs={{0,32},{1,33},{2,34},{3,35},{4,36},{5,37},{6,38},{7,39},{8,40},{9,... | collective-permute-start | bytes 1544 | tf_op jit(solution)/shard_map/ppermute | solution.py:271
  6.5 26.1 %collective-permute-start.5 = (bf16[48,8192]{1,0:T(8,128)(2,1)}, bf16[48,8192]{1,0:T(8,128)(2,1)}, u32[]{:S(2)}, u32[]{:S(2)}) collective-permute-start(bf16[48,8192]{1,0:T(8,128)(2,1)} %bitcast.36), channel_id=1, source_target_pairs={{0,2},{1,3},{2,4},{3,5},{4,6},{5,7},{6,0},{7,1},{8,10},{9,11},{10,... | collective-permute-start | bytes 2359304 | tf_op jit(solution)/shard_map/ppermute | solution.py:50
  7.9 38.4 %collective-permute-start.7 = (bf16[48,8192]{1,0:T(8,128)(2,1)}, bf16[48,8192]{1,0:T(8,128)(2,1)}, u32[]{:S(2)}, u32[]{:S(2)}) collective-permute-start(bf16[48,8192]{1,0:T(8,128)(2,1)} %bitcast.35), channel_id=1, source_target_pairs={{0,4},{1,5},{2,6},{3,7},{4,0},{5,1},{6,2},{7,3},{8,12},{9,13},{10,... | collective-permute-start | bytes 2359304 | tf_op jit(solution)/shard_map/ppermute | solution.py:50
  10.7 57.5 %collective-permute-start.6 = (bf16[48,8192]{1,0:T(8,128)(2,1)}, bf16[48,8192]{1,0:T(8,128)(2,1)}, u32[]{:S(2)}, u32[]{:S(2)}) collective-permute-start(bf16[48,8192]{1,0:T(8,128)(2,1)} %bitcast.34), channel_id=1, source_target_pairs={{0,6},{1,7},{2,0},{3,1},{4,2},{5,3},{6,4},{7,5},{8,14},{9,15},{10,... | collective-permute-start | bytes 2359304 | tf_op jit(solution)/shard_map/ppermute | solution.py:50
  12.8 5.2 %collective-permute-start.1 = (f32[8,16]{1,0:T(8,128)S(1)}, f32[8,16]{1,0:T(8,128)S(1)}, u32[]{:S(2)}, u32[]{:S(2)}) collective-permute-start(f32[8,16]{1,0:T(8,128)S(1)} %add.195), channel_id=1, source_target_pairs={{0,64},{1,65},{2,66},{3,67},{4,68},{5,69},{6,70},{7,71},{8,72},{9,... | collective-permute-start | bytes 1544 | tf_op jit(solution)/shard_map/ppermute | solution.py:271
  17.9 3.6 %collective-permute-start.2 = (f32[8,16]{1,0:T(8,128)S(1)}, f32[8,16]{1,0:T(8,128)S(1)}, u32[]{:S(2)}, u32[]{:S(2)}) collective-permute-start(f32[8,16]{1,0:T(8,128)S(1)} %add.196), channel_id=1, source_target_pairs={{0,8},{1,9},{2,10},{3,11},{4,12},{5,13},{6,14},{7,15},{8,0},{9,1},... | collective-permute-start | bytes 1544 | tf_op jit(solution)/shard_map/ppermute | solution.py:271
  20.0 62.7 %copy-start.6 = (f32[1,384]{1,0:T(1,128)}, f32[1,384]{1,0:T(1,128)S(1)}, u32[]{:S(2)}) copy-start(f32[1,384]{1,0:T(1,128)S(1)} %add.183.slots_ref) | copy-start | bytes 4612
  20.2 62.6 %copy-start.2 = (f32[128,1]{1,0:T(8,128)}, f32[128,1]{1,0:T(8,128)S(1)}, u32[]{:S(2)}) copy-start(f32[128,1]{1,0:T(8,128)S(1)} %copy.14.inv_ref) | copy-start | bytes 1540
  21.5 5.5 %collective-permute-start.3 = (f32[8,16]{1,0:T(8,128)S(1)}, f32[8,16]{1,0:T(8,128)S(1)}, u32[]{:S(2)}, u32[]{:S(2)}) collective-permute-start(f32[8,16]{1,0:T(8,128)S(1)} %add.197), channel_id=1, source_target_pairs={{0,16},{1,17},{2,18},{3,19},{4,20},{5,21},{6,22},{7,23},{8,24},{9,... | collective-permute-start | bytes 1544 | tf_op jit(solution)/shard_map/ppermute | solution.py:271
  27.0 4.9 %collective-permute-start.4 = (f32[8,16]{1,0:T(8,128)S(1)}, f32[8,16]{1,0:T(8,128)S(1)}, u32[]{:S(2)}, u32[]{:S(2)}) collective-permute-start(f32[8,16]{1,0:T(8,128)S(1)} %add.198), channel_id=1, source_target_pairs={{0,1},{1,0},{2,3},{3,2},{4,5},{5,4},{6,7},{7,6},{8,9},{9,8},{10,11... | collective-permute-start | bytes 1544 | tf_op jit(solution)/shard_map/ppermute | solution.py:271
  32.3 32.2 %collective-permute-start.9 = (bf16[56,8192]{1,0:T(8,128)(2,1)S(1)}, bf16[56,8192]{1,0:T(8,128)(2,1)S(1)}, u32[]{:S(2)}, u32[]{:S(2)}) collective-permute-start(bf16[56,8192]{1,0:T(8,128)(2,1)S(1)} %get-tuple-element.84), channel_id=1, source_target_pairs={{0,7},{1,6},{2,1},{3,0},{4,3},{5,2},{6,5},{7,4},{8,15},{9,14},{10,... | collective-permute-start | bytes 2752520 | tf_op jit(solution)/shard_map/ppermute | solution.py:50
  32.5 33.6 %collective-permute-start.8 = (bf16[56,8192]{1,0:T(8,128)(2,1)S(1)}, bf16[56,8192]{1,0:T(8,128)(2,1)S(1)}, u32[]{:S(2)}, u32[]{:S(2)}) collective-permute-start(bf16[56,8192]{1,0:T(8,128)(2,1)S(1)} %get-tuple-element.47), channel_id=1, source_target_pairs={{0,3},{1,2},{2,5},{3,4},{4,7},{5,6},{6,1},{7,0},{8,11},{9,10},{10,... | collective-permute-start | bytes 2752520 | tf_op jit(solution)/shard_map/ppermute | solution.py:50
  46.3 36.4 %collective-permute-start.10 = (bf16[56,8192]{1,0:T(8,128)(2,1)S(1)}, bf16[56,8192]{1,0:T(8,128)(2,1)S(1)}, u32[]{:S(2)}, u32[]{:S(2)}) collective-permute-start(bf16[56,8192]{1,0:T(8,128)(2,1)S(1)} %get-tuple-element.51), channel_id=1, source_target_pairs={{0,5},{1,4},{2,7},{3,6},{4,1},{5,0},{6,3},{7,2},{8,13},{9,12},{10,... | collective-permute-start | bytes 2752520 | tf_op jit(solution)/shard_map/ppermute | solution.py:50
  46.3 36.4 %copy-start.1 = (bf16[128,8192]{1,0:T(8,128)(2,1)S(1)}, bf16[128,8192]{1,0:T(8,128)(2,1)}, u32[]{:S(2)}) copy-start(bf16[128,8192]{1,0:T(8,128)(2,1)} %grad_ref.3) | copy-start | bytes 6291460
  46.3 36.4 %copy-start.5 = (f32[8192]{0:T(1024)S(1)}, f32[8192]{0:T(1024)}, u32[]{:S(2)}) copy-start(f32[8192]{0:T(1024)} %param.10) | copy-start | bytes 98308
  46.3 22.8 %collective-permute-start.11 = (bf16[48,8192]{1,0:T(8,128)(2,1)S(1)}, bf16[48,8192]{1,0:T(8,128)(2,1)S(1)}, u32[]{:S(2)}, u32[]{:S(2)}) collective-permute-start(bf16[48,8192]{1,0:T(8,128)(2,1)S(1)} %bitcast.41), channel_id=1, source_target_pairs={{0,1},{1,0},{2,3},{3,2},{4,5},{5,4},{6,7},{7,6},{8,9},{9,8},{10,11... | collective-permute-start | bytes 2359304 | tf_op jit(solution)/shard_map/ppermute | solution.py:50
  64.5 46.6 %collective-permute-start.15 = (bf16[48,8192]{1,0:T(8,128)(2,1)}, bf16[48,8192]{1,0:T(8,128)(2,1)}, u32[]{:S(2)}, u32[]{:S(2)}) collective-permute-start(bf16[48,8192]{1,0:T(8,128)(2,1)} %bitcast.19), channel_id=1, source_target_pairs={{0,4},{1,5},{2,6},{3,7},{4,0},{5,1},{6,2},{7,3},{8,12},{9,13},{10,... | collective-permute-start | bytes 2359304 | tf_op jit(solution)/shard_map/ppermute | solution.py:50
  66.2 51.4 %collective-permute-start.14 = (bf16[48,8192]{1,0:T(8,128)(2,1)}, bf16[48,8192]{1,0:T(8,128)(2,1)}, u32[]{:S(2)}, u32[]{:S(2)}) collective-permute-start(bf16[48,8192]{1,0:T(8,128)(2,1)} %bitcast.17), channel_id=1, source_target_pairs={{0,6},{1,7},{2,0},{3,1},{4,2},{5,3},{6,4},{7,5},{8,14},{9,15},{10,... | collective-permute-start | bytes 2359304 | tf_op jit(solution)/shard_map/ppermute | solution.py:50
  68.2 49.7 %collective-permute-start.13 = (bf16[48,8192]{1,0:T(8,128)(2,1)}, bf16[48,8192]{1,0:T(8,128)(2,1)}, u32[]{:S(2)}, u32[]{:S(2)}) collective-permute-start(bf16[48,8192]{1,0:T(8,128)(2,1)} %bitcast.18), channel_id=1, source_target_pairs={{0,2},{1,3},{2,4},{3,5},{4,6},{5,7},{6,0},{7,1},{8,10},{9,11},{10,... | collective-permute-start | bytes 2359304 | tf_op jit(solution)/shard_map/ppermute | solution.py:50
  89.3 0.6 copy-start.4
  108.9 2.2 %collective-permute-start.12 = (f32[8,1024]{1,0:T(8,128)S(1)}, f32[8,1024]{1,0:T(8,128)S(1)}, u32[]{:S(2)}, u32[]{:S(2)}) collective-permute-start(f32[8,1024]{1,0:T(8,128)S(1)} %reduce_sum.19), channel_id=1, source_target_pairs={{0,1},{1,0},{2,3},{3,2},{4,5},{5,4},{6,7},{7,6},{8,9},{9,8},{10,11... | collective-permute-start | bytes 98312 | tf_op jit(solution)/shard_map/ppermute | solution.py:326
  117.9 4.7 %collective-permute-start.16 = (f32[8,1024]{1,0:T(8,128)S(1)}, f32[8,1024]{1,0:T(8,128)S(1)}, u32[]{:S(2)}, u32[]{:S(2)}) collective-permute-start(f32[8,1024]{1,0:T(8,128)S(1)} %add.208), channel_id=1, source_target_pairs={{0,2},{1,3},{2,0},{3,1},{4,6},{5,7},{6,4},{7,5},{8,10},{9,11},{10,... | collective-permute-start | bytes 98312 | tf_op jit(solution)/shard_map/ppermute | solution.py:236
  119.9 5.5 %collective-permute-start.17 = (f32[8,1024]{1,0:T(8,128)S(1)}, f32[8,1024]{1,0:T(8,128)S(1)}, u32[]{:S(2)}, u32[]{:S(2)}) collective-permute-start(f32[8,1024]{1,0:T(8,128)S(1)} %add.208), channel_id=1, source_target_pairs={{0,4},{1,5},{2,6},{3,7},{4,0},{5,1},{6,2},{7,3},{8,12},{9,13},{10,... | collective-permute-start | bytes 98312 | tf_op jit(solution)/shard_map/ppermute | solution.py:236
  121.6 5.1 %collective-permute-start.18 = (f32[8,1024]{1,0:T(8,128)S(1)}, f32[8,1024]{1,0:T(8,128)S(1)}, u32[]{:S(2)}, u32[]{:S(2)}) collective-permute-start(f32[8,1024]{1,0:T(8,128)S(1)} %add.208), channel_id=1, source_target_pairs={{0,6},{1,7},{2,4},{3,5},{4,2},{5,3},{6,0},{7,1},{8,14},{9,15},{10,... | collective-permute-start | bytes 98312 | tf_op jit(solution)/shard_map/ppermute | solution.py:236
  126.8 37.1 %collective-permute-start.19 = (bf16[48,8192]{1,0:T(8,128)(2,1)}, bf16[48,8192]{1,0:T(8,128)(2,1)S(1)}, u32[]{:S(2)}, u32[]{:S(2)}) collective-permute-start(bf16[48,8192]{1,0:T(8,128)(2,1)} %bitcast.40), channel_id=1, source_target_pairs={{0,3},{1,2},{2,5},{3,4},{4,7},{5,6},{6,1},{7,0},{8,11},{9,10},{10,... | collective-permute-start | bytes 2359304 | tf_op jit(solution)/shard_map/ppermute | solution.py:50
  126.8 37.0 %collective-permute-start.20 = (bf16[48,8192]{1,0:T(8,128)(2,1)}, bf16[48,8192]{1,0:T(8,128)(2,1)S(1)}, u32[]{:S(2)}, u32[]{:S(2)}) collective-permute-start(bf16[48,8192]{1,0:T(8,128)(2,1)} %bitcast.39), channel_id=1, source_target_pairs={{0,7},{1,6},{2,1},{3,0},{4,3},{5,2},{6,5},{7,4},{8,15},{9,14},{10,... | collective-permute-start | bytes 2359304 | tf_op jit(solution)/shard_map/ppermute | solution.py:50
  129.8 34.1 %collective-permute-start.21 = (bf16[48,8192]{1,0:T(8,128)(2,1)}, bf16[48,8192]{1,0:T(8,128)(2,1)S(1)}, u32[]{:S(2)}, u32[]{:S(2)}) collective-permute-start(bf16[48,8192]{1,0:T(8,128)(2,1)} %bitcast.38), channel_id=1, source_target_pairs={{0,5},{1,4},{2,7},{3,6},{4,1},{5,0},{6,3},{7,2},{8,13},{9,12},{10,... | collective-permute-start | bytes 2359304 | tf_op jit(solution)/shard_map/ppermute | solution.py:50
  129.8 34.1 %collective-permute-start.22 = (bf16[48,8192]{1,0:T(8,128)(2,1)}, bf16[48,8192]{1,0:T(8,128)(2,1)}, u32[]{:S(2)}, u32[]{:S(2)}) collective-permute-start(bf16[48,8192]{1,0:T(8,128)(2,1)} %bitcast.37), channel_id=1, source_target_pairs={{0,1},{1,0},{2,3},{3,2},{4,5},{5,4},{6,7},{7,6},{8,9},{9,8},{10,11... | collective-permute-start | bytes 2359304 | tf_op jit(solution)/shard_map/ppermute | solution.py:50
  163.9 0.9 copy-start.7
  163.9 1.2 copy-start.8
  163.9 1.4 copy-start.9

commit v6 on v5

--- a/solution.py
+++ b/solution.py
@@ -17,7 +17,7 @@
 BF16 = jnp.bfloat16
 VMEM = pl.BlockSpec(memory_space=pltpu.VMEM)
 
-ROUTES = ((0, 0), (1, 0), (3, 0), (2, 0), (1, 1), (3, 1), (2, 1), (0, 1))
+ROUTES = ((0, 0), (2, 0), (1, 0), (3, 0), (2, 1), (1, 1), (3, 1), (0, 1))
 
 
 def coords():
@@ -158,8 +158,8 @@
             left_ref[...], hidden_ref[...], (((0,), (0,)), ((), ())), preferred_element_type=F32
         )
         p = (p[0:16] + p[16:32] + p[32:48]) * (gain_ref[...] * (1.0 / 128.0))
-        for j in range(WIDE // 1024):
-            partial_ref[:, c * (WIDE // 1024) + j, :] = p[:, j * 1024 : (j + 1) * 1024]
+        for j in range(WIDE // 512):
+            partial_ref[c // 2, :, (c % 2) * 4 + j, :] = p[:, j * 512 : (j + 1) * 512]
 
 
 def last_kernel(
@@ -250,7 +250,7 @@
         return lax.dynamic_slice(array, (0, 0, to * CAP, 0), (1, 2, CAP, D)).reshape(ROWS, D)
 
     ready = [block(expert_out, s, m) for s, m in ROUTES[1:4]]
-    ids, *ready = after(expert_ids, *ready)
+    ids, ready[0] = after(expert_ids, ready[0])
     outs = [ring_permute(b, s, m) for b, (s, m) in zip(ready, ROUTES[1:4])]
 
     pack, probs, counts = pl.pallas_call(
@@ -277,14 +277,14 @@
     ready = [block(source, s, m) for s, m in ROUTES[4:]]
     ready = [jnp.concatenate([b, share], axis=0) for b in ready[:3]] + ready[3:]
     for n, (b, (s, m)) in enumerate(zip(ready, ROUTES[4:])):
-        if n != 1:
+        if n > 0:
             b, outs[n % 3] = after(b, outs[n % 3])
         outs.append(ring_permute(b, s, m))
     own_out = block(expert_out, 0, 0)
 
     source, tally[2] = after(expert_grad, tally[2])
     grads = [block(source, 0, 0)]
-    for n, (s, m) in zip((3, 3, 4), ROUTES[1:4]):
+    for n, (s, m) in zip((4, 5, 5), ROUTES[1:4]):
         b, outs[n] = after(block(source, s, m), outs[n])
         grads.append(ring_permute(b, s, m))
     source, tally[3] = after(expert_grad, tally[3])
@@ -296,7 +296,7 @@
         grid=(2, STEPS),
         out_shape=(
             jax.ShapeDtypeStruct((TOK, EXPERTS), F32),
-            jax.ShapeDtypeStruct((EXPERTS, 8, 1024), F32),
+            jax.ShapeDtypeStruct((2, EXPERTS, 8, 512), F32),
         ),
         in_specs=[
             small(1, 8 * ROWS),
@@ -312,7 +312,7 @@
         + [first(b.shape[0]) for b in (own_out, *outs)],
         out_specs=(
             small(TOK, EXPERTS),
-            small(EXPERTS, 8, 1024),
+            small(2, EXPERTS, 8, 512),
         ),
         scratch_shapes=[
             pltpu.VMEM((TOK, 8 * ROWS), F32),
@@ -322,13 +322,18 @@
         cost_estimate=pl.CostEstimate(flops=20_000_000_000, bytes_accessed=60_000_000, transcendentals=0),
         compiler_params=params(20),
     )(slots, pack, inv, expert_ids, probs, tally[5], gain, hidden, grad_out, own_out, *outs)
+    mine, other = [lax.dynamic_index_in_dim(partial, at["c"] ^ i, 0, False) for i in range(2)]
+    partial = mine + lax.ppermute(other, AXES, xor_perm("c", 1))
     partial = jnp.sum(lax.all_to_all(partial, "seq", 0, 0, tiled=True), axis=0)
-    partial = partial + lax.ppermute(partial, AXES, xor_perm("c", 1))
     partial, *grads[1:4] = after(partial, *grads[1:4])
     partial = sum_x(partial)
     *rest, partial = after(*rest, partial)
     grads += [ring_permute(b, s, m) for b, (s, m) in zip(rest, ROUTES[4:])]
-    router_grad = lax.all_gather(partial, "seq").reshape(EXPERTS, D)
+    mine = lax.all_gather(partial, "seq").reshape(EXPERTS, D // 2)
+    mine, *grads[4:] = after(mine, *grads[4:])
+    other = lax.ppermute(mine, AXES, xor_perm("c", 1))
+    low = at["c"] == 0
+    router_grad = jnp.concatenate([jnp.where(low, mine, other), jnp.where(low, other, mine)], axis=1)
 
     grad_hidden = pl.pallas_call(
         last_kernel,

time: 176 us -> 185 us (1.051)
  waiting for transfers between devices: 64.3 us -> 80 us
  starting transfers between devices: 32.5 us -> 27.9 us
  blocking collectives: 44.2 us -> 41.3 us
    ppermute x14, waiting for transfers between devices: 54.1 us -> 70.8 us  [ring_permute(): return lax.ppermute(v, 'exp', perm)]
    ppermute x14, starting transfers between devices: 16 us -> 12.5 us  [ring_permute(): return lax.ppermute(v, 'exp', perm)]
    all_to_all x1, blocking collectives: 19 us -> 16.4 us  [body(): partial = jnp.sum(lax.all_to_all(partial, 'seq', 0, 0, tiled=True), axis=0)]
  transfers between devices with their start and end apart: 23 -> 24, of which waited for: 12 -> 12; matrix products, arithmetic and copies ran while one was open for 6% -> 6% of each run, Pallas kernels for 4% -> 9%
where the time goes in v6:
time: 185 us; the launch traced here: 183 us
  waiting for transfers between devices  80 us (43%)
  blocking collectives  41.3 us (22%)
  starting transfers between devices  27.9 us (15%)
  Pallas kernels  16.9 us (9%)
  local copies, waits for them, and re-layouts  14 us (8%)
    ppermute x14, waiting for transfers between devices, ring_permute(): return lax.ppermute(v, 'exp', perm)  70.8 us
    all_gather x1, blocking collectives, body(): mine = lax.all_gather(partial, 'seq').reshape(EXPERTS, D // 2)  24.9 us
    all_to_all x1, blocking collectives, body(): partial = jnp.sum(lax.all_to_all(partial, 'seq', 0, 0, tiled=True), axis=0)  16.4 us
    ppermute x14, starting transfers between devices, ring_permute(): return lax.ppermute(v, 'exp', perm)  12.5 us
    dynamic_slice x3, local copies, waits for them, and re-layouts, block(): lax.dynamic_slice(array, (0, 0, to * CAP, 0), (1, 2, CAP, D))  12.1 us
    ppermute x5, starting transfers between devices, body(): tally.append(tally[-1] + lax.ppermute(tally[-1], AXES, xor_perm(axis, d)))  10.5 us
    pallas_call x1, Pallas kernels, body(): pl.pallas_call(last_kernel, grid=(2, STEPS), out_shape=jax.ShapeDtypeStru...  10 us
    pallas_call x1, Pallas kernels, body(): pl.pallas_call(mid_kernel, grid=(2, STEPS), out_shape=(jax.ShapeDtypeStru...  6.54 us
  transfers between devices with their start and end apart: 24, of which 12 were waited for; matrix products, arithmetic and copies ran while one was open for 6% of the time, Pallas kernels for 9%

profile of v6, /device:TPU:0, one launch (start us, length us, event | category | flops | bytes accessed | tf_op | source)
XLA Modules:
  0.0 183.0 jit_solution(12336874816190017862)
XLA Ops:
  0.7 0.0 copy-start
  0.7 3.5 %constant_dynamic-slice_fusion.9 = (bf16[1,2,24,8192]{3,2,1,0:T(8,128)(2,1)}, bf16[1,2,24,8192]{3,2,1,0:T(8,128)(2,1)S(1)}, bf16[1,2,24,8192]{3,2,1,0:T(8,128)(2,1)}, bf16[1,2,24,8192]{3,2,1,0:T(8,128)(2,1)}) fusion(bf16[1,2,192,8192]{3,2,1,0:T(8,128)(2,1)} %param.15, s32[]{:T(128)S(6)} %select_n.57, s32[]{:T(128)S(6)} %select_n.52, s32[]{:T(128)S(6)} %select_n.51, ...), kind=kLoop, calls=%fused_computation.27 | loop fusion | bytes 6291472 | tf_op jit(solution)/shard_map/dynamic_slice | solution.py:250
  4.1 0.1 copy.10.ids_ref
  4.3 0.1 copy.11.logits_ref
  4.4 0.4 shard_map.95
  4.7 0.0 copy-start.3
  4.7 1.7 collective-permute-start
  6.5 2.8 %collective-permute-start.7 = (bf16[48,8192]{1,0:T(8,128)(2,1)}, bf16[48,8192]{1,0:T(8,128)(2,1)}, u32[]{:S(2)}, u32[]{:S(2)}) collective-permute-start(bf16[48,8192]{1,0:T(8,128)(2,1)} %bitcast.40), channel_id=1, source_target_pairs={{0,6},{1,7},{2,0},{3,1},{4,2},{5,3},{6,4},{7,5},{8,14},{9,15},{10,... | collective-permute-start | bytes 2359304 | tf_op jit(solution)/shard_map/ppermute | solution.py:50
  9.2 0.0 collective-permute-start.6
  9.2 2.3 %collective-permute-start.5 = (bf16[48,8192]{1,0:T(8,128)(2,1)}, bf16[48,8192]{1,0:T(8,128)(2,1)}, u32[]{:S(2)}, u32[]{:S(2)}) collective-permute-start(bf16[48,8192]{1,0:T(8,128)(2,1)} %bitcast.38), channel_id=1, source_target_pairs={{0,4},{1,5},{2,6},{3,7},{4,0},{5,1},{6,2},{7,3},{8,12},{9,13},{10,... | collective-permute-start | bytes 2359304 | tf_op jit(solution)/shard_map/ppermute | solution.py:50
  11.5 0.1 stack.35
  11.6 0.1 iota_add_fusion
  11.7 0.5 multiply_reduce_fusion
  12.2 0.0 collective-permute-done
  12.2 3.0 %collective-permute-start.1 = (f32[8,16]{1,0:T(8,128)S(1)}, f32[8,16]{1,0:T(8,128)S(1)}, u32[]{:S(2)}, u32[]{:S(2)}) collective-permute-start(f32[8,16]{1,0:T(8,128)S(1)} %add.196), channel_id=1, source_target_pairs={{0,64},{1,65},{2,66},{3,67},{4,68},{5,69},{6,70},{7,71},{8,72},{9,... | collective-permute-start | bytes 1544 | tf_op jit(solution)/shard_map/ppermute | solution.py:271
  15.2 2.2 %collective-permute-done.1 = f32[8,16]{1,0:T(8,128)S(1)} collective-permute-done((f32[8,16]{1,0:T(8,128)S(1)}, f32[8,16]{1,0:T(8,128)S(1)}, u32[]{:S(2)}, u32[]{:S(2)}) %collective-permute-start.1) | collective-permute-done | bytes 544 | tf_op jit(solution)/shard_map/ppermute | solution.py:271
  17.4 1.9 %collective-permute-start.2 = (f32[8,16]{1,0:T(8,128)S(1)}, f32[8,16]{1,0:T(8,128)S(1)}, u32[]{:S(2)}, u32[]{:S(2)}) collective-permute-start(f32[8,16]{1,0:T(8,128)S(1)} %add.197), channel_id=1, source_target_pairs={{0,8},{1,9},{2,10},{3,11},{4,12},{5,13},{6,14},{7,15},{8,0},{9,1},... | collective-permute-start | bytes 1544 | tf_op jit(solution)/shard_map/ppermute | solution.py:271
  19.3 0.7 copy.13.ids_ref
  20.1 0.1 add.190.slots_ref
  20.2 0.1 copy.14.inv_ref
  20.3 0.7 collective-permute-done.2
  21.0 3.9 %collective-permute-start.3 = (f32[8,16]{1,0:T(8,128)S(1)}, f32[8,16]{1,0:T(8,128)S(1)}, u32[]{:S(2)}, u32[]{:S(2)}) collective-permute-start(f32[8,16]{1,0:T(8,128)S(1)} %add.198), channel_id=1, source_target_pairs={{0,16},{1,17},{2,18},{3,19},{4,20},{5,21},{6,22},{7,23},{8,24},{9,... | collective-permute-start | bytes 1544 | tf_op jit(solution)/shard_map/ppermute | solution.py:271
  24.9 1.6 collective-permute-done.3
  26.5 0.0 collective-permute-start.4
  26.5 4.9 %constant_dynamic-slice_fusion = (bf16[1,2,24,8192]{3,2,1,0:T(8,128)(2,1)}, bf16[1,2,24,8192]{3,2,1,0:T(8,128)(2,1)}, bf16[1,2,24,8192]{3,2,1,0:T(8,128)(2,1)}, ...) fusion(bf16[1,2,192,8192]{3,2,1,0:T(8,128)(2,1)} %param.14, ...), kind=kLoop, calls=%fused_computation.18 | loop fusion | bytes 12582928 | tf_op jit(solution)/shard_map/dynamic_slice | solution.py:250
  31.4 0.0 collective-permute-done.4
  31.4 0.1 fusion.5
  31.5 0.2 pad_maximum_fusion
  31.7 1.4 collective-permute-start.8
  33.2 29.5 %collective-permute-done.7.refs_3_ = bf16[48,8192]{1,0:T(8,128)(2,1)} collective-permute-done((bf16[48,8192]{1,0:T(8,128)(2,1)}, bf16[48,8192]{1,0:T(8,128)(2,1)}, u32[]{:S(2)}, u32[]{:S(2)}) %collective-permute-start.7) | collective-permute-done | bytes 786464 | tf_op jit(solution)/shard_map/ppermute | solution.py:50
  62.6 0.0 collective-permute-start.10
  62.6 3.4 %collective-permute-done.6.refs_2_ = bf16[48,8192]{1,0:T(8,128)(2,1)} collective-permute-done((bf16[48,8192]{1,0:T(8,128)(2,1)}, bf16[48,8192]{1,0:T(8,128)(2,1)}, u32[]{:S(2)}, u32[]{:S(2)}) %collective-permute-start.6) | collective-permute-done | bytes 786464 | tf_op jit(solution)/shard_map/ppermute | solution.py:50
  66.0 0.0 copy-start.6
  66.0 0.5 collective-permute-start.11
  66.5 3.7 %constant_dynamic-slice_fusion.4 = (bf16[1,2,24,8192]{3,2,1,0:T(8,128)(2,1)}, bf16[1,2,24,8192]{3,2,1,0:T(8,128)(2,1)}, bf16[1,2,24,8192]{3,2,1,0:T(8,128)(2,1)}, bf16[1,2,24,8192]{3,2,1,0:T(8,128)(2,1)}) fusion(bf16[1,2,192,8192]{3,2,1,0:T(8,128)(2,1)} %param.14, s32[]{:T(128)S(6)} %select_n.52, s32[]{:T(128)S(6)} %select_n.55, s32[]{:T(128)S(6)} %select_n.57, ...), kind=kLoop, calls=%fused_computation.22 | loop fusion | bytes 6291472 | tf_op jit(solution)/shard_map/dynamic_slice | solution.py:250
  70.3 11.6 %collective-permute-done.10.refs_6_ = bf16[56,8192]{1,0:T(8,128)(2,1)S(1)} collective-permute-done((bf16[56,8192]{1,0:T(8,128)(2,1)S(1)}, bf16[56,8192]{1,0:T(8,128)(2,1)S(1)}, u32[]{:S(2)}, u32[]{:S(2)}) %collective-permute-start.10) | collective-permute-done | bytes 917536 | tf_op jit(solution)/shard_map/ppermute | solution.py:50
  81.9 7.4 %collective-permute-done.9.refs_5_ = bf16[56,8192]{1,0:T(8,128)(2,1)S(1)} collective-permute-done((bf16[56,8192]{1,0:T(8,128)(2,1)S(1)}, bf16[56,8192]{1,0:T(8,128)(2,1)S(1)}, u32[]{:S(2)}, u32[]{:S(2)}) %collective-permute-start.9) | collective-permute-done | bytes 917536 | tf_op jit(solution)/shard_map/ppermute | solution.py:50
  89.3 0.1 collective-permute-start.15
  89.4 1.9 %collective-permute-start.14 = (bf16[48,8192]{1,0:T(8,128)(2,1)}, bf16[48,8192]{1,0:T(8,128)(2,1)}, u32[]{:S(2)}, u32[]{:S(2)}) collective-permute-start(bf16[48,8192]{1,0:T(8,128)(2,1)} %bitcast.20), channel_id=1, source_target_pairs={{0,2},{1,3},{2,4},{3,5},{4,6},{5,7},{6,0},{7,1},{8,10},{9,11},{10,... | collective-permute-start | bytes 2359304 | tf_op jit(solution)/shard_map/ppermute | solution.py:50
  91.4 6.5 %shard_map.96 = (f32[128,16]{1,0:T(8,128)S(1)}, f32[2,16,8,512]{3,2,1,0:T(8,128)S(1)}) custom-call(f32[1,384]{1,0:T(1,128)S(1)} %add.190.slots_ref, f32[128,8]{1,0:T(8,128)S(1)} %get-tuple-element.39.pack_ref, f32[128,1]{1,0:T(8,128)S(1)} %copy.14.inv_ref, s32[128,2]{1,0:T(8,128)S(1)} %copy-done.5, f32[128,16]{1,0:T(8,128)S(1)} %copy-done.9, ...), custom_call_target="tpu_custom_call" | custom-call | flops 20000000000 | bytes 60000000 | tf_op jit(solution)/shard_map/pallas_call | solution.py:294
  98.0 0.6 copy-done.4
  98.6 0.1 collective-permute-start.12
  98.7 1.5 collective-permute-done.12
  100.3 16.4 %all_to_all.5 = f32[16,8,512]{2,1,0:T(8,128)S(1)} all-to-all(f32[16,8,512]{2,1,0:T(8,128)S(1)} %bitcast_add_fusion), channel_id=1, replica_groups=mesh['seq'=16,'exp'=8] {'seq'}, dimensions={0} | all-to-all | bytes 524288 | tf_op jit(solution)/shard_map/all_to_all | solution.py:327
  116.7 10.8 %collective-permute-done.14.refs_2_ = bf16[48,8192]{1,0:T(8,128)(2,1)} collective-permute-done((bf16[48,8192]{1,0:T(8,128)(2,1)}, bf16[48,8192]{1,0:T(8,128)(2,1)}, u32[]{:S(2)}, u32[]{:S(2)}) %collective-permute-start.14) | collective-permute-done | bytes 786464 | tf_op jit(solution)/shard_map/ppermute | solution.py:50
  127.5 0.0 collective-permute-done.13.refs_1_
  127.5 2.9 %collective-permute-start.17 = (f32[8,512]{1,0:T(8,128)S(1)}, f32[8,512]{1,0:T(8,128)S(1)}, u32[]{:S(2)}, u32[]{:S(2)}) collective-permute-start(f32[8,512]{1,0:T(8,128)S(1)} %reduce_sum.19), channel_id=1, source_target_pairs={{0,4},{1,5},{2,6},{3,7},{4,0},{5,1},{6,2},{7,3},{8,12},{9,13},{10,... | collective-permute-start | bytes 49160 | tf_op jit(solution)/shard_map/ppermute | solution.py:236
  130.4 1.8 collective-permute-start.18
  132.2 0.0 collective-permute-done.16
  132.2 0.5 collective-permute-done.17
  132.8 2.6 %collective-permute-done.18 = f32[8,512]{1,0:T(8,128)S(1)} collective-permute-done((f32[8,512]{1,0:T(8,128)S(1)}, f32[8,512]{1,0:T(8,128)S(1)}, u32[]{:S(2)}, u32[]{:S(2)}) %collective-permute-start.18) | collective-permute-done | bytes 16416 | tf_op jit(solution)/shard_map/ppermute | solution.py:236
  135.4 0.1 collective-permute-start.19
  135.5 2.3 %collective-permute-start.20 = (bf16[48,8192]{1,0:T(8,128)(2,1)}, bf16[48,8192]{1,0:T(8,128)(2,1)}, u32[]{:S(2)}, u32[]{:S(2)}) collective-permute-start(bf16[48,8192]{1,0:T(8,128)(2,1)} %bitcast.43), channel_id=1, source_target_pairs={{0,3},{1,2},{2,5},{3,4},{4,7},{5,6},{6,1},{7,0},{8,11},{9,10},{10,... | collective-permute-start | bytes 2359304 | tf_op jit(solution)/shard_map/ppermute | solution.py:50
  137.8 0.7 collective-permute-start.21
  138.5 0.3 collective-permute-start.22
  138.9 24.9 %all-gather = f32[128,512]{1,0:T(8,128)S(1)} all-gather(f32[8,512]{1,0:T(8,128)S(1)} %add_add_fusion), channel_id=2, replica_groups=mesh['seq'=16,'exp'=8] {'seq'}, dimensions={0}, use_global_device_ids=true | all-gather | bytes 278528 | tf_op jit(solution)/shard_map/all_gather | solution.py:332
  163.8 0.1 reshape.185
  163.8 0.0 collective-permute-done.19.refs_4_
  163.9 8.1 %collective-permute-done.20.refs_5_ = bf16[48,8192]{1,0:T(8,128)(2,1)} collective-permute-done((bf16[48,8192]{1,0:T(8,128)(2,1)}, bf16[48,8192]{1,0:T(8,128)(2,1)}, u32[]{:S(2)}, u32[]{:S(2)}) %collective-permute-start.20) | collective-permute-done | bytes 786464 | tf_op jit(solution)/shard_map/ppermute | solution.py:50
  172.0 0.0 collective-permute-done.21.refs_6_
  172.0 0.0 collective-permute-done.22.refs_7_
  172.0 0.1 collective-permute-start.23
  172.1 10.0 %shard_map.97 = bf16[128,8192]{1,0:T(8,128)(2,1)} custom-call(f32[1,384]{1,0:T(1,128)} %copy-done.7, f32[128,8]{1,0:T(8,128)} %copy-done.3, f32[128,1]{1,0:T(8,128)} %copy-done.2, f32[128,16]{1,0:T(8,128)} %copy-done.4, f32[16,8192]{1,0:T(8,128)} %weight_ref.1, f32[1,8192]{1,0:T(1,128)} %bitcast.32, bf16[128,8192]{1,0:T(8,128)(2,1)} %hidden_ref.3, ...), custom_call_target="tpu_custom_call" | custom-call | tf_op jit(solution)/shard_map/pallas_call | solution.py:338
  182.2 0.8 pad_maximum_fusion.3
  (48 shorter events, 0.2 us)
Async XLA Ops:
  0.7 3.5 %copy-start.14 = (s32[128,2]{0,1:T(2,128)S(1)}, s32[128,2]{0,1:T(2,128)}, u32[]{:S(2)}) copy-start(s32[128,2]{0,1:T(2,128)} %param.13) | copy-start | bytes 3076
  0.7 3.6 %copy-start.13 = (f32[128,16]{0,1:T(8,128)S(1)}, f32[128,16]{0,1:T(8,128)}, u32[]{:S(2)}) copy-start(f32[128,16]{0,1:T(8,128)} %param.11) | copy-start | bytes 24580
  0.7 11.0 %copy-start = (bf16[128,8192]{1,0:T(8,128)(2,1)S(1)}, bf16[128,8192]{1,0:T(8,128)(2,1)}, u32[]{:S(2)}) copy-start(bf16[128,8192]{1,0:T(8,128)(2,1)} %hidden_ref.3) | copy-start | bytes 6291460
  4.7 26.7 %copy-start.8 = (f32[128,16]{1,0:T(8,128)}, f32[128,16]{1,0:T(8,128)S(1)}, u32[]{:S(2)}) copy-start(f32[128,16]{1,0:T(8,128)S(1)} %get-tuple-element.40.probs_ref) | copy-start | bytes 24580
  4.7 86.6 %copy-start.3 = (f32[128,8]{1,0:T(8,128)}, f32[128,8]{1,0:T(8,128)S(1)}, u32[]{:S(2)}) copy-start(f32[128,8]{1,0:T(8,128)S(1)} %get-tuple-element.39.pack_ref) | copy-start | bytes 12292
  4.7 7.5 %collective-permute-start = (f32[8,16]{1,0:T(8,128)S(1)}, f32[8,16]{1,0:T(8,128)S(1)}, u32[]{:S(2)}, u32[]{:S(2)}) collective-permute-start(f32[8,16]{1,0:T(8,128)S(1)} %get-tuple-element.41), channel_id=1, source_target_pairs={{0,32},{1,33},{2,34},{3,35},{4,36},{5,37},{6,38},{7,39},{8,40},{9,... | collective-permute-start | bytes 1544 | tf_op jit(solution)/shard_map/ppermute | solution.py:271
  6.5 56.1 %collective-permute-start.7 = (bf16[48,8192]{1,0:T(8,128)(2,1)}, bf16[48,8192]{1,0:T(8,128)(2,1)}, u32[]{:S(2)}, u32[]{:S(2)}) collective-permute-start(bf16[48,8192]{1,0:T(8,128)(2,1)} %bitcast.40), channel_id=1, source_target_pairs={{0,6},{1,7},{2,0},{3,1},{4,2},{5,3},{6,4},{7,5},{8,14},{9,15},{10,... | collective-permute-start | bytes 2359304 | tf_op jit(solution)/shard_map/ppermute | solution.py:50
  9.2 56.8 %collective-permute-start.6 = (bf16[48,8192]{1,0:T(8,128)(2,1)}, bf16[48,8192]{1,0:T(8,128)(2,1)}, u32[]{:S(2)}, u32[]{:S(2)}) collective-permute-start(bf16[48,8192]{1,0:T(8,128)(2,1)} %bitcast.39), channel_id=1, source_target_pairs={{0,2},{1,3},{2,4},{3,5},{4,6},{5,7},{6,0},{7,1},{8,10},{9,11},{10,... | collective-permute-start | bytes 2359304 | tf_op jit(solution)/shard_map/ppermute | solution.py:50
  9.2 56.8 %collective-permute-start.5 = (bf16[48,8192]{1,0:T(8,128)(2,1)}, bf16[48,8192]{1,0:T(8,128)(2,1)}, u32[]{:S(2)}, u32[]{:S(2)}) collective-permute-start(bf16[48,8192]{1,0:T(8,128)(2,1)} %bitcast.38), channel_id=1, source_target_pairs={{0,4},{1,5},{2,6},{3,7},{4,0},{5,1},{6,2},{7,3},{8,12},{9,13},{10,... | collective-permute-start | bytes 2359304 | tf_op jit(solution)/shard_map/ppermute | solution.py:50
  12.2 5.2 %collective-permute-start.1 = (f32[8,16]{1,0:T(8,128)S(1)}, f32[8,16]{1,0:T(8,128)S(1)}, u32[]{:S(2)}, u32[]{:S(2)}) collective-permute-start(f32[8,16]{1,0:T(8,128)S(1)} %add.196), channel_id=1, source_target_pairs={{0,64},{1,65},{2,66},{3,67},{4,68},{5,69},{6,70},{7,71},{8,72},{9,... | collective-permute-start | bytes 1544 | tf_op jit(solution)/shard_map/ppermute | solution.py:271
  17.4 3.6 %collective-permute-start.2 = (f32[8,16]{1,0:T(8,128)S(1)}, f32[8,16]{1,0:T(8,128)S(1)}, u32[]{:S(2)}, u32[]{:S(2)}) collective-permute-start(f32[8,16]{1,0:T(8,128)S(1)} %add.197), channel_id=1, source_target_pairs={{0,8},{1,9},{2,10},{3,11},{4,12},{5,13},{6,14},{7,15},{8,0},{9,1},... | collective-permute-start | bytes 1544 | tf_op jit(solution)/shard_map/ppermute | solution.py:271
  20.2 71.2 %copy-start.7 = (f32[1,384]{1,0:T(1,128)}, f32[1,384]{1,0:T(1,128)S(1)}, u32[]{:S(2)}) copy-start(f32[1,384]{1,0:T(1,128)S(1)} %add.190.slots_ref) | copy-start | bytes 4612
  20.3 71.1 %copy-start.2 = (f32[128,1]{1,0:T(8,128)}, f32[128,1]{1,0:T(8,128)S(1)}, u32[]{:S(2)}) copy-start(f32[128,1]{1,0:T(8,128)S(1)} %copy.14.inv_ref) | copy-start | bytes 1540
  21.0 5.5 %collective-permute-start.3 = (f32[8,16]{1,0:T(8,128)S(1)}, f32[8,16]{1,0:T(8,128)S(1)}, u32[]{:S(2)}, u32[]{:S(2)}) collective-permute-start(f32[8,16]{1,0:T(8,128)S(1)} %add.198), channel_id=1, source_target_pairs={{0,16},{1,17},{2,18},{3,19},{4,20},{5,21},{6,22},{7,23},{8,24},{9,... | collective-permute-start | bytes 1544 | tf_op jit(solution)/shard_map/ppermute | solution.py:271
  26.5 4.9 %collective-permute-start.4 = (f32[8,16]{1,0:T(8,128)S(1)}, f32[8,16]{1,0:T(8,128)S(1)}, u32[]{:S(2)}, u32[]{:S(2)}) collective-permute-start(f32[8,16]{1,0:T(8,128)S(1)} %add.199), channel_id=1, source_target_pairs={{0,1},{1,0},{2,3},{3,2},{4,5},{5,4},{6,7},{7,6},{8,9},{9,8},{10,11... | collective-permute-start | bytes 1544 | tf_op jit(solution)/shard_map/ppermute | solution.py:271
  31.7 59.6 %collective-permute-start.8 = (bf16[56,8192]{1,0:T(8,128)(2,1)S(1)}, bf16[56,8192]{1,0:T(8,128)(2,1)S(1)}, u32[]{:S(2)}, u32[]{:S(2)}) collective-permute-start(bf16[56,8192]{1,0:T(8,128)(2,1)S(1)} %get-tuple-element.92), channel_id=1, source_target_pairs={{0,5},{1,4},{2,7},{3,6},{4,1},{5,0},{6,3},{7,2},{8,13},{9,12},{10,... | collective-permute-start | bytes 2752520 | tf_op jit(solution)/shard_map/ppermute | solution.py:50
  62.6 19.3 %collective-permute-start.10 = (bf16[56,8192]{1,0:T(8,128)(2,1)S(1)}, bf16[56,8192]{1,0:T(8,128)(2,1)S(1)}, u32[]{:S(2)}, u32[]{:S(2)}) collective-permute-start(bf16[56,8192]{1,0:T(8,128)(2,1)S(1)} %get-tuple-element.50), channel_id=1, source_target_pairs={{0,7},{1,6},{2,1},{3,0},{4,3},{5,2},{6,5},{7,4},{8,15},{9,14},{10,... | collective-permute-start | bytes 2752520 | tf_op jit(solution)/shard_map/ppermute | solution.py:50
  66.0 23.3 %collective-permute-start.9 = (bf16[56,8192]{1,0:T(8,128)(2,1)S(1)}, bf16[56,8192]{1,0:T(8,128)(2,1)S(1)}, u32[]{:S(2)}, u32[]{:S(2)}) collective-permute-start(bf16[56,8192]{1,0:T(8,128)(2,1)S(1)} %get-tuple-element.48), channel_id=1, source_target_pairs={{0,3},{1,2},{2,5},{3,4},{4,7},{5,6},{6,1},{7,0},{8,11},{9,10},{10,... | collective-permute-start | bytes 2752520 | tf_op jit(solution)/shard_map/ppermute | solution.py:50
  66.0 25.4 %copy-start.1 = (bf16[128,8192]{1,0:T(8,128)(2,1)S(1)}, bf16[128,8192]{1,0:T(8,128)(2,1)}, u32[]{:S(2)}) copy-start(bf16[128,8192]{1,0:T(8,128)(2,1)} %grad_ref.3) | copy-start | bytes 6291460
  66.0 25.4 %copy-start.5 = (s32[128,2]{1,0:T(8,128)S(1)}, s32[128,2]{1,0:T(8,128)}, u32[]{:S(2)}) copy-start(s32[128,2]{1,0:T(8,128)} %copy.13.ids_ref) | copy-start | bytes 3076
  66.0 25.4 %copy-start.6 = (f32[8192]{0:T(1024)S(1)}, f32[8192]{0:T(1024)}, u32[]{:S(2)}) copy-start(f32[8192]{0:T(1024)} %param.10) | copy-start | bytes 98308
  66.0 25.4 %copy-start.9 = (f32[128,16]{1,0:T(8,128)S(1)}, f32[128,16]{1,0:T(8,128)}, u32[]{:S(2)}) copy-start(f32[128,16]{1,0:T(8,128)} %copy-done.8) | copy-start | bytes 24580
  66.0 25.3 %collective-permute-start.11 = (bf16[48,8192]{1,0:T(8,128)(2,1)S(1)}, bf16[48,8192]{1,0:T(8,128)(2,1)S(1)}, u32[]{:S(2)}, u32[]{:S(2)}) collective-permute-start(bf16[48,8192]{1,0:T(8,128)(2,1)S(1)} %bitcast.45), channel_id=1, source_target_pairs={{0,1},{1,0},{2,3},{3,2},{4,5},{5,4},{6,7},{7,6},{8,9},{9,8},{10,11... | collective-permute-start | bytes 2359304 | tf_op jit(solution)/shard_map/ppermute | solution.py:50
  89.3 27.4 %collective-permute-start.15 = (bf16[48,8192]{1,0:T(8,128)(2,1)}, bf16[48,8192]{1,0:T(8,128)(2,1)}, u32[]{:S(2)}, u32[]{:S(2)}) collective-permute-start(bf16[48,8192]{1,0:T(8,128)(2,1)} %bitcast.19), channel_id=1, source_target_pairs={{0,6},{1,7},{2,0},{3,1},{4,2},{5,3},{6,4},{7,5},{8,14},{9,15},{10,... | collective-permute-start | bytes 2359304 | tf_op jit(solution)/shard_map/ppermute | solution.py:50
  89.4 38.1 %collective-permute-start.14 = (bf16[48,8192]{1,0:T(8,128)(2,1)}, bf16[48,8192]{1,0:T(8,128)(2,1)}, u32[]{:S(2)}, u32[]{:S(2)}) collective-permute-start(bf16[48,8192]{1,0:T(8,128)(2,1)} %bitcast.20), channel_id=1, source_target_pairs={{0,2},{1,3},{2,4},{3,5},{4,6},{5,7},{6,0},{7,1},{8,10},{9,11},{10,... | collective-permute-start | bytes 2359304 | tf_op jit(solution)/shard_map/ppermute | solution.py:50
  91.4 36.2 %collective-permute-start.13 = (bf16[48,8192]{1,0:T(8,128)(2,1)}, bf16[48,8192]{1,0:T(8,128)(2,1)}, u32[]{:S(2)}, u32[]{:S(2)}) collective-permute-start(bf16[48,8192]{1,0:T(8,128)(2,1)} %bitcast.18), channel_id=1, source_target_pairs={{0,4},{1,5},{2,6},{3,7},{4,0},{5,1},{6,2},{7,3},{8,12},{9,13},{10,... | collective-permute-start | bytes 2359304 | tf_op jit(solution)/shard_map/ppermute | solution.py:50
  98.0 0.6 copy-start.4
  98.6 39.2 %copy-start.11 = (bf16[1,2,24,8192]{3,2,1,0:T(8,128)(2,1)S(1)}, bf16[1,2,24,8192]{3,2,1,0:T(8,128)(2,1)}, u32[]{:S(2)}) copy-start(bf16[1,2,24,8192]{3,2,1,0:T(8,128)(2,1)} %get-tuple-element.75) | copy-start | bytes 2359300
  98.6 39.9 %copy-start.10 = (bf16[1,2,24,8192]{3,2,1,0:T(8,128)(2,1)S(1)}, bf16[1,2,24,8192]{3,2,1,0:T(8,128)(2,1)}, u32[]{:S(2)}) copy-start(bf16[1,2,24,8192]{3,2,1,0:T(8,128)(2,1)} %get-tuple-element.74) | copy-start | bytes 2359300
  98.6 1.6 collective-permute-start.12
  127.5 4.7 %collective-permute-start.16 = (f32[8,512]{1,0:T(8,128)S(1)}, f32[8,512]{1,0:T(8,128)S(1)}, u32[]{:S(2)}, u32[]{:S(2)}) collective-permute-start(f32[8,512]{1,0:T(8,128)S(1)} %reduce_sum.19), channel_id=1, source_target_pairs={{0,2},{1,3},{2,0},{3,1},{4,6},{5,7},{6,4},{7,5},{8,10},{9,11},{10,... | collective-permute-start | bytes 49160 | tf_op jit(solution)/shard_map/ppermute | solution.py:236
  127.5 5.2 %collective-permute-start.17 = (f32[8,512]{1,0:T(8,128)S(1)}, f32[8,512]{1,0:T(8,128)S(1)}, u32[]{:S(2)}, u32[]{:S(2)}) collective-permute-start(f32[8,512]{1,0:T(8,128)S(1)} %reduce_sum.19), channel_id=1, source_target_pairs={{0,4},{1,5},{2,6},{3,7},{4,0},{5,1},{6,2},{7,3},{8,12},{9,13},{10,... | collective-permute-start | bytes 49160 | tf_op jit(solution)/shard_map/ppermute | solution.py:236
  130.4 4.9 %collective-permute-start.18 = (f32[8,512]{1,0:T(8,128)S(1)}, f32[8,512]{1,0:T(8,128)S(1)}, u32[]{:S(2)}, u32[]{:S(2)}) collective-permute-start(f32[8,512]{1,0:T(8,128)S(1)} %reduce_sum.19), channel_id=1, source_target_pairs={{0,6},{1,7},{2,4},{3,5},{4,2},{5,3},{6,0},{7,1},{8,14},{9,15},{10,... | collective-permute-start | bytes 49160 | tf_op jit(solution)/shard_map/ppermute | solution.py:236
  135.4 28.5 %collective-permute-start.19 = (bf16[48,8192]{1,0:T(8,128)(2,1)}, bf16[48,8192]{1,0:T(8,128)(2,1)S(1)}, u32[]{:S(2)}, u32[]{:S(2)}) collective-permute-start(bf16[48,8192]{1,0:T(8,128)(2,1)} %bitcast.44), channel_id=1, source_target_pairs={{0,5},{1,4},{2,7},{3,6},{4,1},{5,0},{6,3},{7,2},{8,13},{9,12},{10,... | collective-permute-start | bytes 2359304 | tf_op jit(solution)/shard_map/ppermute | solution.py:50
  135.5 36.5 %collective-permute-start.20 = (bf16[48,8192]{1,0:T(8,128)(2,1)}, bf16[48,8192]{1,0:T(8,128)(2,1)}, u32[]{:S(2)}, u32[]{:S(2)}) collective-permute-start(bf16[48,8192]{1,0:T(8,128)(2,1)} %bitcast.43), channel_id=1, source_target_pairs={{0,3},{1,2},{2,5},{3,4},{4,7},{5,6},{6,1},{7,0},{8,11},{9,10},{10,... | collective-permute-start | bytes 2359304 | tf_op jit(solution)/shard_map/ppermute | solution.py:50
  137.8 34.1 %collective-permute-start.21 = (bf16[48,8192]{1,0:T(8,128)(2,1)S(1)}, bf16[48,8192]{1,0:T(8,128)(2,1)}, u32[]{:S(2)}, u32[]{:S(2)}) collective-permute-start(bf16[48,8192]{1,0:T(8,128)(2,1)S(1)} %bitcast.42), channel_id=1, source_target_pairs={{0,7},{1,6},{2,1},{3,0},{4,3},{5,2},{6,5},{7,4},{8,15},{9,14},{10,... | collective-permute-start | bytes 2359304 | tf_op jit(solution)/shard_map/ppermute | solution.py:50
  138.5 33.5 %collective-permute-start.22 = (bf16[48,8192]{1,0:T(8,128)(2,1)S(1)}, bf16[48,8192]{1,0:T(8,128)(2,1)}, u32[]{:S(2)}, u32[]{:S(2)}) collective-permute-start(bf16[48,8192]{1,0:T(8,128)(2,1)S(1)} %bitcast.41), channel_id=1, source_target_pairs={{0,1},{1,0},{2,3},{3,2},{4,5},{5,4},{6,7},{7,6},{8,9},{9,8},{10,11... | collective-permute-start | bytes 2359304 | tf_op jit(solution)/shard_map/ppermute | solution.py:50
  163.9 8.2 %copy-start.12 = (bf16[48,8192]{1,0:T(8,128)(2,1)}, bf16[48,8192]{1,0:T(8,128)(2,1)S(1)}, u32[]{:S(2)}) copy-start(bf16[48,8192]{1,0:T(8,128)(2,1)S(1)} %collective-permute-done.19.refs_4_) | copy-start | bytes 2359300
  172.0 10.1 %collective-permute-start.23 = (f32[16,4096]{1,0:T(8,128)S(1)}, f32[16,4096]{1,0:T(8,128)S(1)}, u32[]{:S(2)}, u32[]{:S(2)}) collective-permute-start(f32[16,4096]{1,0:T(8,128)S(1)} %reshape.185), channel_id=1, source_target_pairs={{0,1},{1,0},{2,3},{3,2},{4,5},{5,4},{6,7},{7,6},{8,9},{9,8},{10,11... | collective-permute-start | bytes 786440 | tf_op jit(solution)/shard_map/ppermute | solution.py:334

commit v7 on v5

--- a/solution.py
+++ b/solution.py
@@ -103,12 +103,13 @@
     grad_ref,
     *refs,
 ):
-    blocks, (logit_ref, partial_ref, dots_ref, left_ref, total_ref) = refs[:8], refs[8:]
+    blocks, shares = refs[:8], refs[8:11]
+    logit_ref, partial_ref, dots_ref, left_ref, total_ref = refs[11:]
     stage, c = pl.program_id(0), pl.program_id(1)
 
     @pl.when(stage == 0)
     def _():
-        picked = jnp.concatenate([b[:ROWS] for b in blocks], axis=0)
+        picked = jnp.concatenate([b[...] for b in blocks], axis=0)
         d = lax.dot_general(
             grad_ref[...], picked, (((1,), (1,)), ((), ())), preferred_element_type=F32
         )
@@ -117,9 +118,9 @@
         def _():
             dots_ref[...] = d
             total = counts_ref[...]
-            for b in blocks[4:7]:
-                other = b[ROWS : ROWS + 8, 0 : 2 * EXPERTS].astype(F32)
-                total = total + other[:, :EXPERTS] + other[:, EXPERTS:]
+            for b in shares:
+                other = b[...].astype(F32)[0:8]
+                total = total + other[:, :EXPERTS] + other[:, EXPERTS : 2 * EXPERTS]
             total_ref[...] = total
 
         @pl.when(c > 0)
@@ -162,20 +163,29 @@
             partial_ref[:, c * (WIDE // 1024) + j, :] = p[:, j * 1024 : (j + 1) * 1024]
 
 
-def last_kernel(
-    slots_ref, pack_ref, inv_ref, logit_ref, weight_ref, gain_ref, hidden_ref, grad_ref, *refs
+def weights(slots, pack):
+    w = jnp.where(slots == pack[:, 2:3], pack[:, 0:1], 0.0)
+    w = w + jnp.where(slots == pack[:, 3:4], pack[:, 1:2], 0.0)
+    return split3(w)[:2]
+
+
+def row_sums(scaled, hidden):
+    prod = scaled * hidden.astype(F32)
+    total = prod[:, 0:128]
+    for j in range(1, WIDE // 128):
+        total = total + prod[:, j * 128 : (j + 1) * 128]
+    return total
+
+
+def half_kernel(
+    slots_ref, pack_ref, logit_ref, weight_ref, gain_ref, hidden_ref, *refs
 ):
-    blocks, (out_ref, scaled_ref, normed_ref, left_ref, acc_ref, factor_ref) = refs[:-6], refs[-6:]
-    stage, c = pl.program_id(0), pl.program_id(1)
-    cols = pl.ds(pl.multiple_of(c * WIDE, WIDE), WIDE)
-
-    @pl.when((stage == 0) & (c == 0))
-    def _():
-        pack = pack_ref[...]
-        slots = slots_ref[...]
-        w = jnp.where(slots == pack[:, 2:3], pack[:, 0:1], 0.0)
-        w = w + jnp.where(slots == pack[:, 3:4], pack[:, 1:2], 0.0)
-        w_hi, w_lo, _ = split3(w)
+    blocks, (part_ref, sums_ref, left_ref) = refs[:-3], refs[-3:]
+    c = pl.program_id(0)
+
+    @pl.when(c == 0)
+    def _():
+        w_hi, w_lo = weights(slots_ref[...], pack_ref[...])
         l0, l1, l2 = split3(logit_ref[...])
         zero = jnp.zeros_like(l0)
         left_ref[...] = jnp.concatenate(
@@ -185,22 +195,37 @@
             ],
             axis=0,
         )
-        acc_ref[...] = jnp.zeros_like(acc_ref)
+        sums_ref[...] = jnp.zeros_like(sums_ref)
+
+    r0, r1, r2 = split3(weight_ref[...])
+    right = jnp.concatenate([b[...] for b in blocks] + [r0, r1, r2, r0], axis=0)
+    both = jnp.dot(left_ref[...], right, preferred_element_type=F32)
+    part = (both[:TOK] + both[TOK:]) * gain_ref[...]
+    part_ref[...] = part
+    sums_ref[...] += row_sums(part, hidden_ref[...])
+
+
+def last_kernel(
+    slots_ref, pack_ref, inv_ref, sums_ref, gain_ref, part_ref, hidden_ref, grad_ref, *refs
+):
+    blocks, (out_ref, scaled_ref, normed_ref, left_ref, acc_ref, factor_ref) = refs[:-6], refs[-6:]
+    stage, c = pl.program_id(0), pl.program_id(1)
+    cols = pl.ds(pl.multiple_of(c * WIDE, WIDE), WIDE)
+
+    @pl.when((stage == 0) & (c == 0))
+    def _():
+        left_ref[...] = jnp.concatenate(weights(slots_ref[...], pack_ref[...]), axis=0)
+        acc_ref[...] = sums_ref[...]
 
     @pl.when(stage == 0)
     def _():
-        r0, r1, r2 = split3(weight_ref[...])
-        right = jnp.concatenate([b[...] for b in blocks] + [r0, r1, r2, r0], axis=0)
+        right = jnp.concatenate([b[...] for b in blocks], axis=0)
         both = jnp.dot(left_ref[...], right, preferred_element_type=F32)
-        scaled = (both[:TOK] + both[TOK:]) * gain_ref[...]
-        scaled_ref[:, cols] = scaled
+        more = (both[:TOK] + both[TOK:]) * gain_ref[...]
+        scaled_ref[:, cols] = part_ref[...] + more
         hidden = hidden_ref[...]
         normed_ref[:, cols] = hidden
-        prod = scaled * hidden.astype(F32)
-        acc = acc_ref[...]
-        for j in range(WIDE // 128):
-            acc = acc + prod[:, j * 128 : (j + 1) * 128]
-        acc_ref[...] = acc
+        acc_ref[...] += row_sums(more, hidden)
 
     @pl.when((stage == 1) & (c == 0))
     def _():
@@ -230,11 +255,6 @@
 
 def params(mib):
     return pltpu.CompilerParams(vmem_limit_bytes=mib * 1024 * 1024)
-
-
-def sum_x(v):
-    a, b, c = [lax.ppermute(v, AXES, xor_perm("x", d)) for d in (1, 2, 3)]
-    return (v + a) + (b + c)
 
 
 def body(
@@ -271,11 +291,11 @@
         tally.append(tally[-1] + lax.ppermute(tally[-1], AXES, xor_perm(axis, d)))
     share = tally[5][0:1].astype(BF16)
     share = jnp.concatenate([share, (tally[5][0:1] - share.astype(F32)).astype(BF16)], axis=1)
-    share = jnp.pad(share, ((0, 7), (0, D - 2 * EXPERTS)))
+    share = jnp.broadcast_to(jnp.pad(share, ((0, 0), (0, 128 - 2 * EXPERTS))), (ROWS, 128))
 
     source, tally[1] = after(expert_out, tally[1])
     ready = [block(source, s, m) for s, m in ROUTES[4:]]
-    ready = [jnp.concatenate([b, share], axis=0) for b in ready[:3]] + ready[3:]
+    ready = [jnp.concatenate([b, share], axis=1) for b in ready[:3]] + ready[3:]
     for n, (b, (s, m)) in enumerate(zip(ready, ROUTES[4:])):
         if n != 1:
             b, outs[n % 3] = after(b, outs[n % 3])
@@ -309,7 +329,8 @@
             second(TOK),
             first(TOK),
         ]
-        + [first(b.shape[0]) for b in (own_out, *outs)],
+        + [first(ROWS)] * 8
+        + [pl.BlockSpec((ROWS, 128), lambda p, c: (0, D // 128))] * 3,
         out_specs=(
             small(TOK, EXPERTS),
             small(EXPERTS, 8, 1024),
@@ -321,13 +342,40 @@
         ],
         cost_estimate=pl.CostEstimate(flops=20_000_000_000, bytes_accessed=60_000_000, transcendentals=0),
         compiler_params=params(20),
-    )(slots, pack, inv, expert_ids, probs, tally[5], gain, hidden, grad_out, own_out, *outs)
+    )(slots, pack, inv, expert_ids, probs, tally[5], gain, hidden, grad_out, own_out, *outs, *outs[3:6])
     partial = jnp.sum(lax.all_to_all(partial, "seq", 0, 0, tiled=True), axis=0)
     partial = partial + lax.ppermute(partial, AXES, xor_perm("c", 1))
+    near = [lax.ppermute(partial, AXES, xor_perm("x", d)) for d in (1, 2)]
     partial, *grads[1:4] = after(partial, *grads[1:4])
-    partial = sum_x(partial)
-    *rest, partial = after(*rest, partial)
+    partial = (partial + near[0]) + (near[1] + lax.ppermute(partial, AXES, xor_perm("x", 3)))
+    partial, *rest = after(partial, *rest)
     grads += [ring_permute(b, s, m) for b, (s, m) in zip(rest, ROUTES[4:])]
+    once = lambda rows: pl.BlockSpec((rows, WIDE), lambda c: (0, c))
+    fixed = lambda *shape: pl.BlockSpec(shape, lambda c: (0,) * len(shape))
+    half = 4 * ROWS
+    begin, partial = after(pack, partial)
+    part, sums = pl.pallas_call(
+        half_kernel,
+        grid=(STEPS,),
+        out_shape=(
+            jax.ShapeDtypeStruct((TOK, D), F32),
+            jax.ShapeDtypeStruct((TOK, 128), F32),
+        ),
+        in_specs=[
+            fixed(1, half),
+            fixed(TOK, 8),
+            fixed(TOK, EXPERTS),
+            once(EXPERTS),
+            once(1),
+            once(TOK),
+        ]
+        + [once(ROWS)] * 4,
+        out_specs=(once(TOK), fixed(TOK, 128)),
+        scratch_shapes=[pltpu.VMEM((2 * TOK, half + 4 * EXPERTS), BF16)],
+        compiler_params=params(24),
+        cost_estimate=pl.CostEstimate(flops=10_000_000_000, bytes_accessed=30_000_000, transcendentals=0),
+    )(slots[:, :half], begin, logit, router_weight, gain, hidden, *grads[:4])
+    partial, sums = after(partial, sums)
     router_grad = lax.all_gather(partial, "seq").reshape(EXPERTS, D)
 
     grad_hidden = pl.pallas_call(
@@ -335,26 +383,26 @@
         grid=(2, STEPS),
         out_shape=jax.ShapeDtypeStruct((TOK, D), BF16),
         in_specs=[
-            small(1, 8 * ROWS),
+            small(1, half),
             small(TOK, 8),
             small(TOK, 1),
-            small(TOK, EXPERTS),
-            first(EXPERTS),
+            small(TOK, 128),
             first(1),
+            first(TOK),
             first(TOK),
             second(TOK),
         ]
-        + [first(g.shape[0]) for g in grads],
+        + [first(ROWS)] * 4,
         out_specs=second(TOK),
         scratch_shapes=[
             pltpu.VMEM((TOK, D), F32),
             pltpu.VMEM((TOK, D), BF16),
-            pltpu.VMEM((2 * TOK, 8 * ROWS + 4 * EXPERTS), BF16),
+            pltpu.VMEM((2 * TOK, half), BF16),
             pltpu.VMEM((TOK, 128), F32),
             pltpu.VMEM((TOK, 128), F32),
         ],
         compiler_params=params(60),
-    )(slots, pack, inv, logit, router_weight, gain, hidden, grad_out, *grads)
+    )(slots[:, half:], pack, inv, sums, gain, part, hidden, grad_out, *grads[4:])
     return grad_hidden, router_grad
 
 

time: 176 us -> 167 us (0.949)
  waiting for transfers between devices: 64.3 us -> 44.6 us
  Pallas kernels: 16.9 us -> 21 us
  starting transfers between devices: 32.5 us -> 36.2 us
  local copies, waits for them, and re-layouts: 15.5 us -> 18.9 us
    ppermute x14, waiting for transfers between devices: 54.1 us -> 36.3 us  [ring_permute(): return lax.ppermute(v, 'exp', perm)]
    pallas_call x0 -> x1, Pallas kernels: none -> 4.28 us  [body(): pl.pallas_call(half_kernel, grid=(STEPS,), out_shape=(jax.ShapeDtypeStruc...]
    ppermute x3, starting transfers between devices: 4.7 us -> 7.68 us  [the longest x2 5.41 us: body(): near = [lax.ppermute(partial, AXES, xor_perm('x', d)) for d in (1, 2)]]
    unnamed x26 -> x24, local copies, waits for them, and re-layouts: 2.22 us -> 5.09 us
    ppermute x3, waiting for transfers between devices: 4.15 us -> 2.24 us  [the longest x1 2.24 us: body(): lax.ppermute(partial, AXES, xor_perm('x', 3))]
  transfers between devices with their start and end apart: 23 -> 23, of which waited for: 12 -> 9; matrix products, arithmetic and copies ran while one was open for 6% -> 7% of each run, Pallas kernels for 4% -> 7%
where the time goes in v7:
time: 167 us
  waiting for transfers between devices  44.6 us (27%)
  blocking collectives  44.3 us (27%)
  starting transfers between devices  36.2 us (22%)
  Pallas kernels  21 us (13%)
  local copies, waits for them, and re-layouts  18.9 us (11%)
    ppermute x14, waiting for transfers between devices, ring_permute(): return lax.ppermute(v, 'exp', perm)  36.3 us
    all_gather x1, blocking collectives, body(): router_grad = lax.all_gather(partial, 'seq').reshape(EXPERTS, D)  25.3 us
    all_to_all x1, blocking collectives, body(): partial = jnp.sum(lax.all_to_all(partial, 'seq', 0, 0, tiled=True), axis=0)  19 us
    ppermute x14, starting transfers between devices, ring_permute(): return lax.ppermute(v, 'exp', perm)  16.7 us
    dynamic_slice x3, local copies, waits for them, and re-layouts, block(): lax.dynamic_slice(array, (0, 0, to * CAP, 0), (1, 2, CAP, D))  11.9 us
    ppermute x5, starting transfers between devices, body(): tally.append(tally[-1] + lax.ppermute(tally[-1], AXES, xor_perm(axis, d)))  10.5 us
    pallas_call x1, Pallas kernels, body(): pl.pallas_call(last_kernel, grid=(2, STEPS), out_shape=jax.ShapeDtypeStru...  9.54 us
    pallas_call x1, Pallas kernels, body(): pl.pallas_call(mid_kernel, grid=(2, STEPS), out_shape=(jax.ShapeDtypeStru...  6.81 us
  transfers between devices with their start and end apart: 23, of which 9 were waited for; matrix products, arithmetic and copies ran while one was open for 7% of the time, Pallas kernels for 7%

profile of v7, /device:TPU:0, one launch (start us, length us, event | category | flops | bytes accessed | tf_op | source)
XLA Modules:
  0.0 167.0 jit_solution(14425905464260050503)
XLA Ops:
  0.7 0.0 copy-start
  0.7 3.5 %constant_dynamic-slice_fusion.12 = (bf16[1,2,24,8192]{3,2,1,0:T(8,128)(2,1)S(1)}, bf16[1,2,24,8192]{3,2,1,0:T(8,128)(2,1)}, bf16[1,2,24,8192]{3,2,1,0:T(8,128)(2,1)}, bf16[1,2,24,8192]{3,2,1,0:T(8,128)(2,1)}) fusion(bf16[1,2,192,8192]{3,2,1,0:T(8,128)(2,1)} %param.15, s32[]{:T(128)S(6)} %select_n.35, s32[]{:T(128)S(6)} %select_n.34, s32[]{:T(128)S(6)} %select_n.33, ...), kind=kLoop, calls=%fused_computation.17 | loop fusion | bytes 6291472 | tf_op jit(solution)/shard_map/dynamic_slice | solution.py:270
  4.1 0.1 copy.10.ids_ref
  4.3 0.1 copy.11.logits_ref
  4.4 0.4 shard_map.95
  4.7 1.7 %collective-permute-start = (f32[8,16]{1,0:T(8,128)S(1)}, f32[8,16]{1,0:T(8,128)S(1)}, u32[]{:S(2)}, u32[]{:S(2)}) collective-permute-start(f32[8,16]{1,0:T(8,128)S(1)} %get-tuple-element.44), channel_id=1, source_target_pairs={{0,32},{1,33},{2,34},{3,35},{4,36},{5,37},{6,38},{7,39},{8,40},{9,... | collective-permute-start | bytes 1544 | tf_op jit(solution)/shard_map/ppermute | solution.py:291
  6.5 1.5 collective-permute-start.5
  8.0 2.7 %collective-permute-start.7 = (bf16[48,8192]{1,0:T(8,128)(2,1)}, bf16[48,8192]{1,0:T(8,128)(2,1)}, u32[]{:S(2)}, u32[]{:S(2)}) collective-permute-start(bf16[48,8192]{1,0:T(8,128)(2,1)} %bitcast.38), channel_id=1, source_target_pairs={{0,4},{1,5},{2,6},{3,7},{4,0},{5,1},{6,2},{7,3},{8,12},{9,13},{10,... | collective-permute-start | bytes 2359304 | tf_op jit(solution)/shard_map/ppermute | solution.py:50
  10.7 1.4 collective-permute-start.6
  12.1 0.1 stack.35
  12.2 0.5 multiply_reduce_fusion
  12.7 0.1 iota_add_fusion
  12.8 0.0 collective-permute-done
  12.8 2.9 %collective-permute-start.1 = (f32[8,16]{1,0:T(8,128)S(1)}, f32[8,16]{1,0:T(8,128)S(1)}, u32[]{:S(2)}, u32[]{:S(2)}) collective-permute-start(f32[8,16]{1,0:T(8,128)S(1)} %add.195), channel_id=1, source_target_pairs={{0,64},{1,65},{2,66},{3,67},{4,68},{5,69},{6,70},{7,71},{8,72},{9,... | collective-permute-start | bytes 1544 | tf_op jit(solution)/shard_map/ppermute | solution.py:291
  15.7 2.2 %collective-permute-done.1 = f32[8,16]{1,0:T(8,128)S(1)} collective-permute-done((f32[8,16]{1,0:T(8,128)S(1)}, f32[8,16]{1,0:T(8,128)S(1)}, u32[]{:S(2)}, u32[]{:S(2)}) %collective-permute-start.1) | collective-permute-done | bytes 544 | tf_op jit(solution)/shard_map/ppermute | solution.py:291
  17.9 1.9 %collective-permute-start.2 = (f32[8,16]{1,0:T(8,128)S(1)}, f32[8,16]{1,0:T(8,128)S(1)}, u32[]{:S(2)}, u32[]{:S(2)}) collective-permute-start(f32[8,16]{1,0:T(8,128)S(1)} %add.196), channel_id=1, source_target_pairs={{0,8},{1,9},{2,10},{3,11},{4,12},{5,13},{6,14},{7,15},{8,0},{9,1},... | collective-permute-start | bytes 1544 | tf_op jit(solution)/shard_map/ppermute | solution.py:291
  19.9 0.1 copy.13.ids_ref
  20.0 0.1 add.183.slots_ref
  20.1 0.1 copy.14.inv_ref
  20.2 1.4 collective-permute-done.2
  21.6 3.9 %collective-permute-start.3 = (f32[8,16]{1,0:T(8,128)S(1)}, f32[8,16]{1,0:T(8,128)S(1)}, u32[]{:S(2)}, u32[]{:S(2)}) collective-permute-start(f32[8,16]{1,0:T(8,128)S(1)} %add.197), channel_id=1, source_target_pairs={{0,16},{1,17},{2,18},{3,19},{4,20},{5,21},{6,22},{7,23},{8,24},{9,... | collective-permute-start | bytes 1544 | tf_op jit(solution)/shard_map/ppermute | solution.py:291
  25.4 1.6 collective-permute-done.3
  27.0 0.0 collective-permute-start.4
  27.0 4.9 %constant_dynamic-slice_fusion.1 = (bf16[1,2,24,8192]{3,2,1,0:T(8,128)(2,1)}, bf16[1,2,24,8192]{3,2,1,0:T(8,128)(2,1)}, bf16[1,2,24,8192]{3,2,1,0:T(8,128)(2,1)}...) fusion(bf16[1,2,192,8192]{3,2,1,0:T(8,128)(2,1)} %param.14, ...), kind=kLoop, calls=%fused_computation.6 | loop fusion | bytes 12582928 | tf_op jit(solution)/shard_map/dynamic_slice | solution.py:270
  32.0 0.1 fusion.1
  32.0 0.4 pad_maximum_fusion.2
  32.4 0.2 collective-permute-start.9
  32.6 0.0 collective-permute-done.5.refs_1_
  32.6 1.6 collective-permute-start.8
  34.3 12.1 %collective-permute-done.7.refs_3_ = bf16[48,8192]{1,0:T(8,128)(2,1)} collective-permute-done((bf16[48,8192]{1,0:T(8,128)(2,1)}, bf16[48,8192]{1,0:T(8,128)(2,1)}, u32[]{:S(2)}, u32[]{:S(2)}) %collective-permute-start.7) | collective-permute-done | bytes 786464 | tf_op jit(solution)/shard_map/ppermute | solution.py:50
  46.3 0.9 collective-permute-start.11
  47.3 3.6 %constant_dynamic-slice_fusion = (bf16[1,2,24,8192]{3,2,1,0:T(8,128)(2,1)}, bf16[1,2,24,8192]{3,2,1,0:T(8,128)(2,1)}, bf16[1,2,24,8192]{3,2,1,0:T(8,128)(2,1)}, bf16[1,2,24,8192]{3,2,1,0:T(8,128)(2,1)}) fusion(bf16[1,2,192,8192]{3,2,1,0:T(8,128)(2,1)} %param.14, s32[]{:T(128)S(6)} %select_n.35, s32[]{:T(128)S(6)} %select_n.34, s32[]{:T(128)S(6)} %select_n.32, ...), kind=kLoop, calls=%fused_computation.5 | loop fusion | bytes 6291472 | tf_op jit(solution)/shard_map/dynamic_slice | solution.py:270
  50.8 11.2 %collective-permute-done.9.refs_5_.refs_9_ = bf16[48,8320]{1,0:T(8,128)(2,1)S(1)} collective-permute-done((bf16[48,8320]{1,0:T(8,128)(2,1)S(1)}, bf16[48,8320]{1,0:T(8,128)(2,1)S(1)}, u32[]{:S(2)}, u32[]{:S(2)}) %collective-permute-start.9) | collective-permute-done | bytes 798752 | tf_op jit(solution)/shard_map/ppermute | solution.py:50
  62.0 1.6 collective-permute-start.15
  63.6 0.0 collective-permute-done.8.refs_4_.refs_8_
  63.6 2.0 %collective-permute-start.14 = (bf16[48,8192]{1,0:T(8,128)(2,1)}, bf16[48,8192]{1,0:T(8,128)(2,1)}, u32[]{:S(2)}, u32[]{:S(2)}) collective-permute-start(bf16[48,8192]{1,0:T(8,128)(2,1)} %bitcast.18), channel_id=1, source_target_pairs={{0,6},{1,7},{2,0},{3,1},{4,2},{5,3},{6,4},{7,5},{8,14},{9,15},{10,... | collective-permute-start | bytes 2359304 | tf_op jit(solution)/shard_map/ppermute | solution.py:50
  65.6 0.0 collective-permute-done.6.refs_2_
  65.6 0.9 collective-permute-start.13
  66.6 11.1 %collective-permute-done.10.refs_6_.refs_10_ = bf16[48,8320]{1,0:T(8,128)(2,1)S(1)} collective-permute-done((bf16[48,8320]{1,0:T(8,128)(2,1)S(1)}, bf16[48,8320]{1,0:T(8,128)(2,1)S(1)}, u32[]{:S(2)}, u32[]{:S(2)}) %collective-permute-start.10) | collective-permute-done | bytes 798752 | tf_op jit(solution)/shard_map/ppermute | solution.py:50
  77.6 6.8 %shard_map.96 = (f32[128,16]{1,0:T(8,128)S(1)}, f32[16,8,1024]{2,1,0:T(8,128)S(1)}) custom-call(f32[1,384]{1,0:T(1,128)S(1)} %add.183.slots_ref, f32[128,8]{1,0:T(8,128)S(1)} %get-tuple-element.67.pack_ref, f32[128,1]{1,0:T(8,128)S(1)} %copy.14.inv_ref, s32[128,2]{1,0:T(8,128)S(1)} %copy.13.ids_ref, f32[128,16]{1,0:T(8,128)S(1)} %get-tuple-element.43.probs_ref, ...), custom_call_target="tpu_custom_call" | custom-call | flops 20000000000 | bytes 60000000 | tf_op jit(solution)/shard_map/pallas_call | solution.py:314
  84.5 19.0 %all_to_all.5 = f32[16,8,1024]{2,1,0:T(8,128)S(1)} all-to-all(f32[16,8,1024]{2,1,0:T(8,128)S(1)} %get-tuple-element.59), channel_id=1, replica_groups=mesh['seq'=16,'exp'=8] {'seq'}, dimensions={0} | all-to-all | bytes 1048576 | tf_op jit(solution)/shard_map/all_to_all | solution.py:346
  103.5 1.4 collective-permute-start.12
  104.9 0.9 collective-permute-done.12
  105.7 2.3 %collective-permute-start.16 = (f32[8,1024]{1,0:T(8,128)S(1)}, f32[8,1024]{1,0:T(8,128)S(1)}, u32[]{:S(2)}, u32[]{:S(2)}) collective-permute-start(f32[8,1024]{1,0:T(8,128)S(1)} %add.208), channel_id=1, source_target_pairs={{0,2},{1,3},{2,0},{3,1},{4,6},{5,7},{6,4},{7,5},{8,10},{9,11},{10,... | collective-permute-start | bytes 98312 | tf_op jit(solution)/shard_map/ppermute | solution.py:348
  108.0 3.1 %collective-permute-start.17 = (f32[8,1024]{1,0:T(8,128)S(1)}, f32[8,1024]{1,0:T(8,128)S(1)}, u32[]{:S(2)}, u32[]{:S(2)}) collective-permute-start(f32[8,1024]{1,0:T(8,128)S(1)} %add.208), channel_id=1, source_target_pairs={{0,4},{1,5},{2,6},{3,7},{4,0},{5,1},{6,2},{7,3},{8,12},{9,13},{10,... | collective-permute-start | bytes 98312 | tf_op jit(solution)/shard_map/ppermute | solution.py:348
  111.1 0.0 collective-permute-done.15.refs_3_
  111.1 2.0 %collective-permute-done.14.refs_2_ = bf16[48,8192]{1,0:T(8,128)(2,1)} collective-permute-done((bf16[48,8192]{1,0:T(8,128)(2,1)}, bf16[48,8192]{1,0:T(8,128)(2,1)}, u32[]{:S(2)}, u32[]{:S(2)}) %collective-permute-start.14) | collective-permute-done | bytes 786464 | tf_op jit(solution)/shard_map/ppermute | solution.py:50
  113.2 2.3 %collective-permute-start.18 = (f32[8,1024]{1,0:T(8,128)S(1)}, f32[8,1024]{1,0:T(8,128)S(1)}, u32[]{:S(2)}, u32[]{:S(2)}) collective-permute-start(f32[8,1024]{1,0:T(8,128)S(1)} %add.208), channel_id=1, source_target_pairs={{0,6},{1,7},{2,4},{3,5},{4,2},{5,3},{6,0},{7,1},{8,14},{9,15},{10,... | collective-permute-start | bytes 98312 | tf_op jit(solution)/shard_map/ppermute | solution.py:350
  115.4 0.6 fusion.2
  116.0 0.0 collective-permute-done.17
  116.0 2.2 %collective-permute-done.18 = f32[8,1024]{1,0:T(8,128)S(1)} collective-permute-done((f32[8,1024]{1,0:T(8,128)S(1)}, f32[8,1024]{1,0:T(8,128)S(1)}, u32[]{:S(2)}, u32[]{:S(2)}) %collective-permute-start.18) | collective-permute-done | bytes 32800 | tf_op jit(solution)/shard_map/ppermute | solution.py:350
  118.3 0.1 collective-permute-start.19
  118.4 2.9 %collective-permute-start.20 = (bf16[48,8192]{1,0:T(8,128)(2,1)}, bf16[48,8192]{1,0:T(8,128)(2,1)}, u32[]{:S(2)}, u32[]{:S(2)}) collective-permute-start(bf16[48,8192]{1,0:T(8,128)(2,1)} %bitcast.42), channel_id=1, source_target_pairs={{0,7},{1,6},{2,1},{3,0},{4,3},{5,2},{6,5},{7,4},{8,15},{9,14},{10,... | collective-permute-start | bytes 2359304 | tf_op jit(solution)/shard_map/ppermute | solution.py:50
  121.3 0.5 collective-permute-start.21
  121.8 0.2 collective-permute-start.22
  122.0 1.1 copy-done.3
  123.2 1.0 copy-done.8
  124.2 4.3 %shard_map.97 = (f32[128,8192]{1,0:T(8,128)S(1)}, f32[128,128]{1,0:T(8,128)S(1)}) custom-call(f32[1,192]{1,0:T(1,128)S(1)} %get-tuple-element.99.slots_ref, f32[128,8]{1,0:T(8,128)S(1)} %get-tuple-element.67.pack_ref, f32[128,16]{1,0:T(8,128)S(1)} %get-tuple-element.68.logit_ref, f32[16,8192]{1,0:T(8,128)S(1)} %copy-done.8, f32[1,8192]{1,0:T(1,128)S(1)} %bitcast.33, ...), custom_call_target="tpu_custom_call" | custom-call | flops 10000000000 | bytes 30000000 | tf_op jit(solution)/shard_map/pallas_call | solution.py:357
  128.5 2.1 %copy-done.1 = f32[128,8192]{1,0:T(8,128)} copy-done((f32[128,8192]{1,0:T(8,128)}, f32[128,8192]{1,0:T(8,128)S(1)}, u32[]{:S(2)}) %copy-start.1) | copy-done | bytes 4194328
  130.6 0.6 copy-done.6
  131.2 25.3 %all-gather = f32[128,1024]{1,0:T(8,128)S(1)} all-gather(f32[8,1024]{1,0:T(8,128)S(1)} %add_add_fusion), channel_id=2, replica_groups=mesh['seq'=16,'exp'=8] {'seq'}, dimensions={0}, use_global_device_ids=true | all-gather | bytes 557056 | tf_op jit(solution)/shard_map/all_gather | solution.py:379
  156.5 0.9 reshape.185
  157.4 0.0 collective-permute-done.19.refs_0_
  157.4 9.5 %shard_map.98 = bf16[128,8192]{1,0:T(8,128)(2,1)} custom-call(f32[1,192]{1,0:T(1,128)} %get-tuple-element.100.slots_ref, f32[128,8]{1,0:T(8,128)} %copy-done.5, f32[128,1]{1,0:T(8,128)} %copy-done.4, f32[128,128]{1,0:T(8,128)} %copy-done.6, f32[1,8192]{1,0:T(1,128)} %bitcast.31, f32[128,8192]{1,0:T(8,128)} %copy-done.1, bf16[128,8192]{1,0:T(8,128)(2,1)} %hidden_ref.5, ...), custom_call_target="tpu_custom_call" | custom-call | tf_op jit(solution)/shard_map/pallas_call | solution.py:381
  (38 shorter events, 0.1 us)
Async XLA Ops:
  0.7 3.5 %copy-start.10 = (s32[128,2]{0,1:T(2,128)S(1)}, s32[128,2]{0,1:T(2,128)}, u32[]{:S(2)}) copy-start(s32[128,2]{0,1:T(2,128)} %param.13) | copy-start | bytes 3076
  0.7 3.6 %copy-start.9 = (f32[128,16]{0,1:T(8,128)S(1)}, f32[128,16]{0,1:T(8,128)}, u32[]{:S(2)}) copy-start(f32[128,16]{0,1:T(8,128)} %param.11) | copy-start | bytes 24580
  0.7 11.5 %copy-start = (bf16[128,8192]{1,0:T(8,128)(2,1)S(1)}, bf16[128,8192]{1,0:T(8,128)(2,1)}, u32[]{:S(2)}) copy-start(bf16[128,8192]{1,0:T(8,128)(2,1)} %hidden_ref.5) | copy-start | bytes 6291460
  4.7 117.3 %copy-start.5 = (f32[128,8]{1,0:T(8,128)}, f32[128,8]{1,0:T(8,128)S(1)}, u32[]{:S(2)}) copy-start(f32[128,8]{1,0:T(8,128)S(1)} %get-tuple-element.67.pack_ref) | copy-start | bytes 12292
  4.7 8.1 %collective-permute-start = (f32[8,16]{1,0:T(8,128)S(1)}, f32[8,16]{1,0:T(8,128)S(1)}, u32[]{:S(2)}, u32[]{:S(2)}) collective-permute-start(f32[8,16]{1,0:T(8,128)S(1)} %get-tuple-element.44), channel_id=1, source_target_pairs={{0,32},{1,33},{2,34},{3,35},{4,36},{5,37},{6,38},{7,39},{8,40},{9,... | collective-permute-start | bytes 1544 | tf_op jit(solution)/shard_map/ppermute | solution.py:291
  6.5 26.2 %collective-permute-start.5 = (bf16[48,8192]{1,0:T(8,128)(2,1)}, bf16[48,8192]{1,0:T(8,128)(2,1)}, u32[]{:S(2)}, u32[]{:S(2)}) collective-permute-start(bf16[48,8192]{1,0:T(8,128)(2,1)} %bitcast.39), channel_id=1, source_target_pairs={{0,2},{1,3},{2,4},{3,5},{4,6},{5,7},{6,0},{7,1},{8,10},{9,11},{10,... | collective-permute-start | bytes 2359304 | tf_op jit(solution)/shard_map/ppermute | solution.py:50
  8.0 38.4 %collective-permute-start.7 = (bf16[48,8192]{1,0:T(8,128)(2,1)}, bf16[48,8192]{1,0:T(8,128)(2,1)}, u32[]{:S(2)}, u32[]{:S(2)}) collective-permute-start(bf16[48,8192]{1,0:T(8,128)(2,1)} %bitcast.38), channel_id=1, source_target_pairs={{0,4},{1,5},{2,6},{3,7},{4,0},{5,1},{6,2},{7,3},{8,12},{9,13},{10,... | collective-permute-start | bytes 2359304 | tf_op jit(solution)/shard_map/ppermute | solution.py:50
  10.7 54.9 %collective-permute-start.6 = (bf16[48,8192]{1,0:T(8,128)(2,1)}, bf16[48,8192]{1,0:T(8,128)(2,1)}, u32[]{:S(2)}, u32[]{:S(2)}) collective-permute-start(bf16[48,8192]{1,0:T(8,128)(2,1)} %bitcast.37), channel_id=1, source_target_pairs={{0,6},{1,7},{2,0},{3,1},{4,2},{5,3},{6,4},{7,5},{8,14},{9,15},{10,... | collective-permute-start | bytes 2359304 | tf_op jit(solution)/shard_map/ppermute | solution.py:50
  12.8 5.2 %collective-permute-start.1 = (f32[8,16]{1,0:T(8,128)S(1)}, f32[8,16]{1,0:T(8,128)S(1)}, u32[]{:S(2)}, u32[]{:S(2)}) collective-permute-start(f32[8,16]{1,0:T(8,128)S(1)} %add.195), channel_id=1, source_target_pairs={{0,64},{1,65},{2,66},{3,67},{4,68},{5,69},{6,70},{7,71},{8,72},{9,... | collective-permute-start | bytes 1544 | tf_op jit(solution)/shard_map/ppermute | solution.py:291
  17.9 3.6 %collective-permute-start.2 = (f32[8,16]{1,0:T(8,128)S(1)}, f32[8,16]{1,0:T(8,128)S(1)}, u32[]{:S(2)}, u32[]{:S(2)}) collective-permute-start(f32[8,16]{1,0:T(8,128)S(1)} %add.196), channel_id=1, source_target_pairs={{0,8},{1,9},{2,10},{3,11},{4,12},{5,13},{6,14},{7,15},{8,0},{9,1},... | collective-permute-start | bytes 1544 | tf_op jit(solution)/shard_map/ppermute | solution.py:291
  20.2 57.5 %copy-start.4 = (f32[128,1]{1,0:T(8,128)}, f32[128,1]{1,0:T(8,128)S(1)}, u32[]{:S(2)}) copy-start(f32[128,1]{1,0:T(8,128)S(1)} %copy.14.inv_ref) | copy-start | bytes 1540
  21.6 5.5 %collective-permute-start.3 = (f32[8,16]{1,0:T(8,128)S(1)}, f32[8,16]{1,0:T(8,128)S(1)}, u32[]{:S(2)}, u32[]{:S(2)}) collective-permute-start(f32[8,16]{1,0:T(8,128)S(1)} %add.197), channel_id=1, source_target_pairs={{0,16},{1,17},{2,18},{3,19},{4,20},{5,21},{6,22},{7,23},{8,24},{9,... | collective-permute-start | bytes 1544 | tf_op jit(solution)/shard_map/ppermute | solution.py:291
  27.0 4.9 %collective-permute-start.4 = (f32[8,16]{1,0:T(8,128)S(1)}, f32[8,16]{1,0:T(8,128)S(1)}, u32[]{:S(2)}, u32[]{:S(2)}) collective-permute-start(f32[8,16]{1,0:T(8,128)S(1)} %add.198), channel_id=1, source_target_pairs={{0,1},{1,0},{2,3},{3,2},{4,5},{5,4},{6,7},{7,6},{8,9},{9,8},{10,11... | collective-permute-start | bytes 1544 | tf_op jit(solution)/shard_map/ppermute | solution.py:291
  32.4 29.5 %collective-permute-start.9 = (bf16[48,8320]{1,0:T(8,128)(2,1)S(1)}, bf16[48,8320]{1,0:T(8,128)(2,1)S(1)}, u32[]{:S(2)}, u32[]{:S(2)}) collective-permute-start(bf16[48,8320]{1,0:T(8,128)(2,1)S(1)} %get-tuple-element.96), channel_id=1, source_target_pairs={{0,7},{1,6},{2,1},{3,0},{4,3},{5,2},{6,5},{7,4},{8,15},{9,14},{10,... | collective-permute-start | bytes 2396168 | tf_op jit(solution)/shard_map/ppermute | solution.py:50
  32.6 31.0 %collective-permute-start.8 = (bf16[48,8320]{1,0:T(8,128)(2,1)S(1)}, bf16[48,8320]{1,0:T(8,128)(2,1)S(1)}, u32[]{:S(2)}, u32[]{:S(2)}) collective-permute-start(bf16[48,8320]{1,0:T(8,128)(2,1)S(1)} %get-tuple-element.53), channel_id=1, source_target_pairs={{0,3},{1,2},{2,5},{3,4},{4,7},{5,6},{6,1},{7,0},{8,11},{9,10},{10,... | collective-permute-start | bytes 2396168 | tf_op jit(solution)/shard_map/ppermute | solution.py:50
  46.3 31.3 %collective-permute-start.10 = (bf16[48,8320]{1,0:T(8,128)(2,1)S(1)}, bf16[48,8320]{1,0:T(8,128)(2,1)S(1)}, u32[]{:S(2)}, u32[]{:S(2)}) collective-permute-start(bf16[48,8320]{1,0:T(8,128)(2,1)S(1)} %get-tuple-element.57), channel_id=1, source_target_pairs={{0,5},{1,4},{2,7},{3,6},{4,1},{5,0},{6,3},{7,2},{8,13},{9,12},{10,... | collective-permute-start | bytes 2396168 | tf_op jit(solution)/shard_map/ppermute | solution.py:50
  46.3 31.3 %copy-start.2 = (bf16[128,8192]{1,0:T(8,128)(2,1)S(1)}, bf16[128,8192]{1,0:T(8,128)(2,1)}, u32[]{:S(2)}) copy-start(bf16[128,8192]{1,0:T(8,128)(2,1)} %grad_ref.3) | copy-start | bytes 6291460
  46.3 31.3 %copy-start.7 = (f32[8192]{0:T(1024)S(1)}, f32[8192]{0:T(1024)}, u32[]{:S(2)}) copy-start(f32[8192]{0:T(1024)} %param.10) | copy-start | bytes 98308
  46.3 20.2 %collective-permute-start.11 = (bf16[48,8192]{1,0:T(8,128)(2,1)S(1)}, bf16[48,8192]{1,0:T(8,128)(2,1)S(1)}, u32[]{:S(2)}, u32[]{:S(2)}) collective-permute-start(bf16[48,8192]{1,0:T(8,128)(2,1)S(1)} %bitcast.44), channel_id=1, source_target_pairs={{0,1},{1,0},{2,3},{3,2},{4,5},{5,4},{6,7},{7,6},{8,9},{9,8},{10,11... | collective-permute-start | bytes 2359304 | tf_op jit(solution)/shard_map/ppermute | solution.py:50
  62.0 49.1 %collective-permute-start.15 = (bf16[48,8192]{1,0:T(8,128)(2,1)}, bf16[48,8192]{1,0:T(8,128)(2,1)}, u32[]{:S(2)}, u32[]{:S(2)}) collective-permute-start(bf16[48,8192]{1,0:T(8,128)(2,1)} %bitcast.20), channel_id=1, source_target_pairs={{0,4},{1,5},{2,6},{3,7},{4,0},{5,1},{6,2},{7,3},{8,12},{9,13},{10,... | collective-permute-start | bytes 2359304 | tf_op jit(solution)/shard_map/ppermute | solution.py:50
  63.6 49.5 %collective-permute-start.14 = (bf16[48,8192]{1,0:T(8,128)(2,1)}, bf16[48,8192]{1,0:T(8,128)(2,1)}, u32[]{:S(2)}, u32[]{:S(2)}) collective-permute-start(bf16[48,8192]{1,0:T(8,128)(2,1)} %bitcast.18), channel_id=1, source_target_pairs={{0,6},{1,7},{2,0},{3,1},{4,2},{5,3},{6,4},{7,5},{8,14},{9,15},{10,... | collective-permute-start | bytes 2359304 | tf_op jit(solution)/shard_map/ppermute | solution.py:50
  65.6 47.5 %collective-permute-start.13 = (bf16[48,8192]{1,0:T(8,128)(2,1)}, bf16[48,8192]{1,0:T(8,128)(2,1)}, u32[]{:S(2)}, u32[]{:S(2)}) collective-permute-start(bf16[48,8192]{1,0:T(8,128)(2,1)} %bitcast.19), channel_id=1, source_target_pairs={{0,2},{1,3},{2,4},{3,5},{4,6},{5,7},{6,0},{7,1},{8,10},{9,11},{10,... | collective-permute-start | bytes 2359304 | tf_op jit(solution)/shard_map/ppermute | solution.py:50
  103.5 2.2 %collective-permute-start.12 = (f32[8,1024]{1,0:T(8,128)S(1)}, f32[8,1024]{1,0:T(8,128)S(1)}, u32[]{:S(2)}, u32[]{:S(2)}) collective-permute-start(f32[8,1024]{1,0:T(8,128)S(1)} %reduce_sum.19), channel_id=1, source_target_pairs={{0,1},{1,0},{2,3},{3,2},{4,5},{5,4},{6,7},{7,6},{8,9},{9,8},{10,11... | collective-permute-start | bytes 98312 | tf_op jit(solution)/shard_map/ppermute | solution.py:347
  105.7 10.3 %collective-permute-start.16 = (f32[8,1024]{1,0:T(8,128)S(1)}, f32[8,1024]{1,0:T(8,128)S(1)}, u32[]{:S(2)}, u32[]{:S(2)}) collective-permute-start(f32[8,1024]{1,0:T(8,128)S(1)} %add.208), channel_id=1, source_target_pairs={{0,2},{1,3},{2,0},{3,1},{4,6},{5,7},{6,4},{7,5},{8,10},{9,11},{10,... | collective-permute-start | bytes 98312 | tf_op jit(solution)/shard_map/ppermute | solution.py:348
  108.0 8.0 %collective-permute-start.17 = (f32[8,1024]{1,0:T(8,128)S(1)}, f32[8,1024]{1,0:T(8,128)S(1)}, u32[]{:S(2)}, u32[]{:S(2)}) collective-permute-start(f32[8,1024]{1,0:T(8,128)S(1)} %add.208), channel_id=1, source_target_pairs={{0,4},{1,5},{2,6},{3,7},{4,0},{5,1},{6,2},{7,3},{8,12},{9,13},{10,... | collective-permute-start | bytes 98312 | tf_op jit(solution)/shard_map/ppermute | solution.py:348
  113.2 5.1 %collective-permute-start.18 = (f32[8,1024]{1,0:T(8,128)S(1)}, f32[8,1024]{1,0:T(8,128)S(1)}, u32[]{:S(2)}, u32[]{:S(2)}) collective-permute-start(f32[8,1024]{1,0:T(8,128)S(1)} %add.208), channel_id=1, source_target_pairs={{0,6},{1,7},{2,4},{3,5},{4,2},{5,3},{6,0},{7,1},{8,14},{9,15},{10,... | collective-permute-start | bytes 98312 | tf_op jit(solution)/shard_map/ppermute | solution.py:350
  118.3 39.1 %collective-permute-start.19 = (bf16[48,8192]{1,0:T(8,128)(2,1)}, bf16[48,8192]{1,0:T(8,128)(2,1)}, u32[]{:S(2)}, u32[]{:S(2)}) collective-permute-start(bf16[48,8192]{1,0:T(8,128)(2,1)} %bitcast.43), channel_id=1, source_target_pairs={{0,3},{1,2},{2,5},{3,4},{4,7},{5,6},{6,1},{7,0},{8,11},{9,10},{10,... | collective-permute-start | bytes 2359304 | tf_op jit(solution)/shard_map/ppermute | solution.py:50
  118.4 39.0 %collective-permute-start.20 = (bf16[48,8192]{1,0:T(8,128)(2,1)}, bf16[48,8192]{1,0:T(8,128)(2,1)}, u32[]{:S(2)}, u32[]{:S(2)}) collective-permute-start(bf16[48,8192]{1,0:T(8,128)(2,1)} %bitcast.42), channel_id=1, source_target_pairs={{0,7},{1,6},{2,1},{3,0},{4,3},{5,2},{6,5},{7,4},{8,15},{9,14},{10,... | collective-permute-start | bytes 2359304 | tf_op jit(solution)/shard_map/ppermute | solution.py:50
  121.3 36.1 %collective-permute-start.21 = (bf16[48,8192]{1,0:T(8,128)(2,1)}, bf16[48,8192]{1,0:T(8,128)(2,1)}, u32[]{:S(2)}, u32[]{:S(2)}) collective-permute-start(bf16[48,8192]{1,0:T(8,128)(2,1)} %bitcast.41), channel_id=1, source_target_pairs={{0,5},{1,4},{2,7},{3,6},{4,1},{5,0},{6,3},{7,2},{8,13},{9,12},{10,... | collective-permute-start | bytes 2359304 | tf_op jit(solution)/shard_map/ppermute | solution.py:50
  121.8 35.6 %collective-permute-start.22 = (bf16[48,8192]{1,0:T(8,128)(2,1)}, bf16[48,8192]{1,0:T(8,128)(2,1)}, u32[]{:S(2)}, u32[]{:S(2)}) collective-permute-start(bf16[48,8192]{1,0:T(8,128)(2,1)} %bitcast.40), channel_id=1, source_target_pairs={{0,1},{1,0},{2,3},{3,2},{4,5},{5,4},{6,7},{7,6},{8,9},{9,8},{10,11... | collective-permute-start | bytes 2359304 | tf_op jit(solution)/shard_map/ppermute | solution.py:50
  122.0 1.1 copy-start.3
  123.2 1.0 copy-start.8
  128.5 2.1 %copy-start.1 = (f32[128,8192]{1,0:T(8,128)}, f32[128,8192]{1,0:T(8,128)S(1)}, u32[]{:S(2)}) copy-start(f32[128,8192]{1,0:T(8,128)S(1)} %get-tuple-element.74.part_ref) | copy-start | bytes 12582916
  130.6 0.6 copy-start.6

commit v8 on v7

--- a/solution.py
+++ b/solution.py
@@ -150,8 +150,9 @@
         load = total_ref[0:1, :] * (EXPERTS / (2 * TOKENS))
         aux = probs * (load - jnp.sum(probs * load, axis=1, keepdims=True))
         logit = direct + aux
+        logit = logit * inv_ref[...]
         logit_ref[...] = logit
-        left_ref[...] = jnp.concatenate(split3(logit * inv_ref[...]), axis=1)
+        left_ref[...] = jnp.concatenate(split3(logit), axis=1)
 
     @pl.when(stage == 1)
     def _():
@@ -163,10 +164,10 @@
             partial_ref[:, c * (WIDE // 1024) + j, :] = p[:, j * 1024 : (j + 1) * 1024]
 
 
-def weights(slots, pack):
+def weights(slots, pack, inv):
     w = jnp.where(slots == pack[:, 2:3], pack[:, 0:1], 0.0)
     w = w + jnp.where(slots == pack[:, 3:4], pack[:, 1:2], 0.0)
-    return split3(w)[:2]
+    return split3(w * inv)[:2]
 
 
 def row_sums(scaled, hidden):
@@ -178,67 +179,58 @@
 
 
 def half_kernel(
-    slots_ref, pack_ref, logit_ref, weight_ref, gain_ref, hidden_ref, *refs
+    slots_ref, pack_ref, inv_ref, logit_ref, weight_ref, gain_ref, hidden_ref, grad_ref, *refs
 ):
     blocks, (part_ref, sums_ref, left_ref) = refs[:-3], refs[-3:]
     c = pl.program_id(0)
 
     @pl.when(c == 0)
     def _():
-        w_hi, w_lo = weights(slots_ref[...], pack_ref[...])
+        w_hi, w_lo = weights(slots_ref[...], pack_ref[...], inv_ref[...])
         l0, l1, l2 = split3(logit_ref[...])
-        zero = jnp.zeros_like(l0)
-        left_ref[...] = jnp.concatenate(
-            [
-                jnp.concatenate([w_hi, l0, l0, l0, l2], axis=1),
-                jnp.concatenate([w_lo, l1, l1, zero, zero], axis=1),
-            ],
-            axis=0,
-        )
+        left_ref[...] = jnp.concatenate([w_hi, w_lo, l0, l0, l0, l1, l1, l2], axis=1)
         sums_ref[...] = jnp.zeros_like(sums_ref)
 
     r0, r1, r2 = split3(weight_ref[...])
-    right = jnp.concatenate([b[...] for b in blocks] + [r0, r1, r2, r0], axis=0)
-    both = jnp.dot(left_ref[...], right, preferred_element_type=F32)
-    part = (both[:TOK] + both[TOK:]) * gain_ref[...]
-    part_ref[...] = part
-    sums_ref[...] += row_sums(part, hidden_ref[...])
+    rows = [b[...] for b in blocks]
+    right = jnp.concatenate(rows + rows + [r0, r1, r2, r0, r1, r0], axis=0)
+    scaled = jnp.dot(left_ref[...], right, preferred_element_type=F32) * gain_ref[...]
+    part_ref[...] = grad_ref[...].astype(F32) + scaled
+    sums_ref[...] += row_sums(scaled, hidden_ref[...])
 
 
 def last_kernel(
-    slots_ref, pack_ref, inv_ref, sums_ref, gain_ref, part_ref, hidden_ref, grad_ref, *refs
+    slots_ref, pack_ref, inv_ref, sums_ref, gain_ref, part_ref, hidden_ref, *refs
 ):
-    blocks, (out_ref, scaled_ref, normed_ref, left_ref, acc_ref, factor_ref) = refs[:-6], refs[-6:]
+    blocks, (out_ref, part_scr, left_ref, acc_ref, factor_ref) = refs[:-5], refs[-5:]
     stage, c = pl.program_id(0), pl.program_id(1)
     cols = pl.ds(pl.multiple_of(c * WIDE, WIDE), WIDE)
 
     @pl.when((stage == 0) & (c == 0))
     def _():
-        left_ref[...] = jnp.concatenate(weights(slots_ref[...], pack_ref[...]), axis=0)
+        left_ref[...] = jnp.concatenate(
+            weights(slots_ref[...], pack_ref[...], inv_ref[...]), axis=1
+        )
         acc_ref[...] = sums_ref[...]
 
     @pl.when(stage == 0)
     def _():
-        right = jnp.concatenate([b[...] for b in blocks], axis=0)
-        both = jnp.dot(left_ref[...], right, preferred_element_type=F32)
-        more = (both[:TOK] + both[TOK:]) * gain_ref[...]
-        scaled_ref[:, cols] = part_ref[...] + more
-        hidden = hidden_ref[...]
-        normed_ref[:, cols] = hidden
-        acc_ref[...] += row_sums(more, hidden)
+        rows = [b[...] for b in blocks]
+        right = jnp.concatenate(rows + rows, axis=0)
+        scaled = jnp.dot(left_ref[...], right, preferred_element_type=F32) * gain_ref[...]
+        part_scr[:, cols] = part_ref[...] + scaled
+        acc_ref[...] += row_sums(scaled, hidden_ref[...])
 
     @pl.when((stage == 1) & (c == 0))
     def _():
         inv = inv_ref[...]
-        mean = jnp.sum(acc_ref[...], axis=1, keepdims=True) * inv / D
-        factor_ref[...] = jnp.broadcast_to(inv * mean, (TOK, 128))
+        mean = jnp.sum(acc_ref[...], axis=1, keepdims=True) / D
+        factor_ref[...] = jnp.broadcast_to(inv * inv * mean, (TOK, 128))
 
     @pl.when(stage == 1)
     def _():
-        inv = inv_ref[...]
-        factor = factor_ref[:, 0:1]
-        back = inv * (scaled_ref[:, cols] - normed_ref[:, cols].astype(F32) * factor)
-        out_ref[...] = (grad_ref[...].astype(F32) + back).astype(BF16)
+        normed = hidden_ref[...].astype(F32) * factor_ref[:, 0:1]
+        out_ref[...] = (part_scr[:, cols] - normed).astype(BF16)
 
 
 STEPS = 4
@@ -247,6 +239,10 @@
 
 def first(rows):
     return pl.BlockSpec((rows, WIDE), lambda p, c: (0, jnp.where(p == 0, c, STEPS - 1)))
+
+
+def twice(rows):
+    return pl.BlockSpec((rows, WIDE), lambda p, c: (0, c))
 
 
 def second(rows):
@@ -364,17 +360,21 @@
         in_specs=[
             fixed(1, half),
             fixed(TOK, 8),
+            fixed(TOK, 1),
             fixed(TOK, EXPERTS),
             once(EXPERTS),
             once(1),
             once(TOK),
+            once(TOK),
         ]
         + [once(ROWS)] * 4,
         out_specs=(once(TOK), fixed(TOK, 128)),
-        scratch_shapes=[pltpu.VMEM((2 * TOK, half + 4 * EXPERTS), BF16)],
+        scratch_shapes=[pltpu.VMEM((TOK, 2 * half + 6 * EXPERTS), BF16)],
         compiler_params=params(24),
-        cost_estimate=pl.CostEstimate(flops=10_000_000_000, bytes_accessed=30_000_000, transcendentals=0),
-    )(slots[:, :half], begin, logit, router_weight, gain, hidden, *grads[:4])
+        cost_estimate=pl.CostEstimate(
+            flops=10_000_000_000, bytes_accessed=30_000_000, transcendentals=0
+        ),
+    )(slots[:, :half], begin, inv, logit, router_weight, gain, hidden, grad_out, *grads[:4])
     partial, sums = after(partial, sums)
     router_grad = lax.all_gather(partial, "seq").reshape(EXPERTS, D)
 
@@ -389,20 +389,18 @@
             small(TOK, 128),
             first(1),
             first(TOK),
-            first(TOK),
-            second(TOK),
+            twice(TOK),
         ]
         + [first(ROWS)] * 4,
         out_specs=second(TOK),
         scratch_shapes=[
             pltpu.VMEM((TOK, D), F32),
-            pltpu.VMEM((TOK, D), BF16),
-            pltpu.VMEM((2 * TOK, half), BF16),
+            pltpu.VMEM((TOK, 2 * half), BF16),
             pltpu.VMEM((TOK, 128), F32),
             pltpu.VMEM((TOK, 128), F32),
         ],
-        compiler_params=params(60),
-    )(slots[:, half:], pack, inv, sums, gain, part, hidden, grad_out, *grads[4:])
+        compiler_params=params(24),
+    )(slots[:, half:], pack, inv, sums, gain, part, hidden, *grads[4:])
     return grad_hidden, router_grad
 
 

time: 167 us -> 171 us (1.024)
  local copies, waits for them, and re-layouts: 18.9 us -> 22.4 us
  Pallas kernels: 21 us -> 18.8 us
  blocking collectives: 44.3 us -> 46.2 us
    unnamed x24 -> x22, local copies, waits for them, and re-layouts: 5.09 us -> 8.14 us
    pallas_call x1, Pallas kernels: 9.54 us -> 7.04 us  [body(): pl.pallas_call(last_kernel, grid=(2, STEPS), out_shape=jax.ShapeDtypeStru...]
    all_gather x1, blocking collectives: 25.3 us -> 27.2 us  [body(): router_grad = lax.all_gather(partial, 'seq').reshape(EXPERTS, D)]
where the time goes in v8:
time: 171 us
  blocking collectives  46.2 us (27%)
  waiting for transfers between devices  45.3 us (26%)
  starting transfers between devices  36.2 us (21%)
  local copies, waits for them, and re-layouts  22.4 us (13%)
  Pallas kernels  18.8 us (11%)
    ppermute x14, waiting for transfers between devices, ring_permute(): return lax.ppermute(v, 'exp', perm)  36.5 us
    all_gather x1, blocking collectives, body(): router_grad = lax.all_gather(partial, 'seq').reshape(EXPERTS, D)  27.2 us
    all_to_all x1, blocking collectives, body(): partial = jnp.sum(lax.all_to_all(partial, 'seq', 0, 0, tiled=True), axis=0)  19 us
    ppermute x14, starting transfers between devices, ring_permute(): return lax.ppermute(v, 'exp', perm)  16.7 us
    dynamic_slice x3, local copies, waits for them, and re-layouts, block(): lax.dynamic_slice(array, (0, 0, to * CAP, 0), (1, 2, CAP, D))  11.8 us
    ppermute x5, starting transfers between devices, body(): tally.append(tally[-1] + lax.ppermute(tally[-1], AXES, xor_perm(axis, d)))  10.5 us
    unnamed x22, local copies, waits for them, and re-layouts  8.14 us
    pallas_call x1, Pallas kernels, body(): pl.pallas_call(last_kernel, grid=(2, STEPS), out_shape=jax.ShapeDtypeStru...  7.04 us
  transfers between devices with their start and end apart: 23, of which 9 were waited for; matrix products, arithmetic and copies ran while one was open for 7% of the time, Pallas kernels for 7%

profile of v8, /device:TPU:0, one launch (start us, length us, event | category | flops | bytes accessed | tf_op | source)
XLA Modules:
  0.0 170.8 jit_solution(16732794887474760344)
XLA Ops:
  0.7 3.5 %constant_dynamic-slice_fusion.12 = (bf16[1,2,24,8192]{3,2,1,0:T(8,128)(2,1)S(1)}, bf16[1,2,24,8192]{3,2,1,0:T(8,128)(2,1)}, bf16[1,2,24,8192]{3,2,1,0:T(8,128)(2,1)}, bf16[1,2,24,8192]{3,2,1,0:T(8,128)(2,1)}) fusion(bf16[1,2,192,8192]{3,2,1,0:T(8,128)(2,1)} %param.15, s32[]{:T(128)S(6)} %select_n.35, s32[]{:T(128)S(6)} %select_n.34, s32[]{:T(128)S(6)} %select_n.33, ...), kind=kLoop, calls=%fused_computation.17 | loop fusion | bytes 6291472 | tf_op jit(solution)/shard_map/dynamic_slice | solution.py:266
  4.1 0.1 copy.10.ids_ref
  4.3 0.1 copy.11.logits_ref
  4.4 0.4 shard_map.95
  4.7 1.7 %collective-permute-start = (f32[8,16]{1,0:T(8,128)S(1)}, f32[8,16]{1,0:T(8,128)S(1)}, u32[]{:S(2)}, u32[]{:S(2)}) collective-permute-start(f32[8,16]{1,0:T(8,128)S(1)} %get-tuple-element.44), channel_id=1, source_target_pairs={{0,32},{1,33},{2,34},{3,35},{4,36},{5,37},{6,38},{7,39},{8,40},{9,... | collective-permute-start | bytes 1544 | tf_op jit(solution)/shard_map/ppermute | solution.py:287
  6.5 1.5 collective-permute-start.5
  7.9 2.7 %collective-permute-start.7 = (bf16[48,8192]{1,0:T(8,128)(2,1)}, bf16[48,8192]{1,0:T(8,128)(2,1)}, u32[]{:S(2)}, u32[]{:S(2)}) collective-permute-start(bf16[48,8192]{1,0:T(8,128)(2,1)} %bitcast.38), channel_id=1, source_target_pairs={{0,4},{1,5},{2,6},{3,7},{4,0},{5,1},{6,2},{7,3},{8,12},{9,13},{10,... | collective-permute-start | bytes 2359304 | tf_op jit(solution)/shard_map/ppermute | solution.py:50
  10.7 1.4 collective-permute-start.6
  12.1 0.1 stack.35
  12.2 0.5 multiply_reduce_fusion
  12.7 0.1 iota_add_fusion
  12.8 2.9 %collective-permute-start.1 = (f32[8,16]{1,0:T(8,128)S(1)}, f32[8,16]{1,0:T(8,128)S(1)}, u32[]{:S(2)}, u32[]{:S(2)}) collective-permute-start(f32[8,16]{1,0:T(8,128)S(1)} %add.195), channel_id=1, source_target_pairs={{0,64},{1,65},{2,66},{3,67},{4,68},{5,69},{6,70},{7,71},{8,72},{9,... | collective-permute-start | bytes 1544 | tf_op jit(solution)/shard_map/ppermute | solution.py:287
  15.7 2.2 %collective-permute-done.1 = f32[8,16]{1,0:T(8,128)S(1)} collective-permute-done((f32[8,16]{1,0:T(8,128)S(1)}, f32[8,16]{1,0:T(8,128)S(1)}, u32[]{:S(2)}, u32[]{:S(2)}) %collective-permute-start.1) | collective-permute-done | bytes 544 | tf_op jit(solution)/shard_map/ppermute | solution.py:287
  17.9 1.9 %collective-permute-start.2 = (f32[8,16]{1,0:T(8,128)S(1)}, f32[8,16]{1,0:T(8,128)S(1)}, u32[]{:S(2)}, u32[]{:S(2)}) collective-permute-start(f32[8,16]{1,0:T(8,128)S(1)} %add.196), channel_id=1, source_target_pairs={{0,8},{1,9},{2,10},{3,11},{4,12},{5,13},{6,14},{7,15},{8,0},{9,1},... | collective-permute-start | bytes 1544 | tf_op jit(solution)/shard_map/ppermute | solution.py:287
  19.9 0.1 copy.13.ids_ref
  20.0 0.1 add.183.slots_ref
  20.0 0.1 copy.15.inv_ref
  20.2 1.4 collective-permute-done.2
  21.5 3.9 %collective-permute-start.3 = (f32[8,16]{1,0:T(8,128)S(1)}, f32[8,16]{1,0:T(8,128)S(1)}, u32[]{:S(2)}, u32[]{:S(2)}) collective-permute-start(f32[8,16]{1,0:T(8,128)S(1)} %add.197), channel_id=1, source_target_pairs={{0,16},{1,17},{2,18},{3,19},{4,20},{5,21},{6,22},{7,23},{8,24},{9,... | collective-permute-start | bytes 1544 | tf_op jit(solution)/shard_map/ppermute | solution.py:287
  25.4 1.6 collective-permute-done.3
  27.0 4.8 %constant_dynamic-slice_fusion.1 = (bf16[1,2,24,8192]{3,2,1,0:T(8,128)(2,1)}, bf16[1,2,24,8192]{3,2,1,0:T(8,128)(2,1)}, bf16[1,2,24,8192]{3,2,1,0:T(8,128)(2,1)}...) fusion(bf16[1,2,192,8192]{3,2,1,0:T(8,128)(2,1)} %param.14, ...), kind=kLoop, calls=%fused_computation.6 | loop fusion | bytes 12582928 | tf_op jit(solution)/shard_map/dynamic_slice | solution.py:266
  31.8 0.0 collective-permute-done.4
  31.9 0.1 fusion.1
  32.0 0.4 pad_maximum_fusion.2
  32.4 0.2 collective-permute-start.9
  32.5 0.0 collective-permute-done.5.refs_1_
  32.5 1.6 collective-permute-start.8
  34.2 12.1 %collective-permute-done.7.refs_3_ = bf16[48,8192]{1,0:T(8,128)(2,1)} collective-permute-done((bf16[48,8192]{1,0:T(8,128)(2,1)}, bf16[48,8192]{1,0:T(8,128)(2,1)}, u32[]{:S(2)}, u32[]{:S(2)}) %collective-permute-start.7) | collective-permute-done | bytes 786464 | tf_op jit(solution)/shard_map/ppermute | solution.py:50
  46.3 0.0 collective-permute-start.10
  46.3 0.9 collective-permute-start.11
  47.3 3.6 %constant_dynamic-slice_fusion = (bf16[1,2,24,8192]{3,2,1,0:T(8,128)(2,1)}, bf16[1,2,24,8192]{3,2,1,0:T(8,128)(2,1)}, bf16[1,2,24,8192]{3,2,1,0:T(8,128)(2,1)}, bf16[1,2,24,8192]{3,2,1,0:T(8,128)(2,1)}) fusion(bf16[1,2,192,8192]{3,2,1,0:T(8,128)(2,1)} %param.14, s32[]{:T(128)S(6)} %select_n.35, s32[]{:T(128)S(6)} %select_n.34, s32[]{:T(128)S(6)} %select_n.32, ...), kind=kLoop, calls=%fused_computation.5 | loop fusion | bytes 6291472 | tf_op jit(solution)/shard_map/dynamic_slice | solution.py:266
  50.8 11.2 %collective-permute-done.9.refs_5_.refs_9_ = bf16[48,8320]{1,0:T(8,128)(2,1)S(1)} collective-permute-done((bf16[48,8320]{1,0:T(8,128)(2,1)S(1)}, bf16[48,8320]{1,0:T(8,128)(2,1)S(1)}, u32[]{:S(2)}, u32[]{:S(2)}) %collective-permute-start.9) | collective-permute-done | bytes 798752 | tf_op jit(solution)/shard_map/ppermute | solution.py:50
  62.0 1.6 collective-permute-start.15
  63.6 2.0 %collective-permute-start.14 = (bf16[48,8192]{1,0:T(8,128)(2,1)}, bf16[48,8192]{1,0:T(8,128)(2,1)}, u32[]{:S(2)}, u32[]{:S(2)}) collective-permute-start(bf16[48,8192]{1,0:T(8,128)(2,1)} %bitcast.18), channel_id=1, source_target_pairs={{0,6},{1,7},{2,0},{3,1},{4,2},{5,3},{6,4},{7,5},{8,14},{9,15},{10,... | collective-permute-start | bytes 2359304 | tf_op jit(solution)/shard_map/ppermute | solution.py:50
  65.6 0.0 collective-permute-done.6.refs_2_
  65.6 0.9 collective-permute-start.13
  66.6 11.1 %collective-permute-done.10.refs_6_.refs_10_ = bf16[48,8320]{1,0:T(8,128)(2,1)S(1)} collective-permute-done((bf16[48,8320]{1,0:T(8,128)(2,1)S(1)}, bf16[48,8320]{1,0:T(8,128)(2,1)S(1)}, u32[]{:S(2)}, u32[]{:S(2)}) %collective-permute-start.10) | collective-permute-done | bytes 798752 | tf_op jit(solution)/shard_map/ppermute | solution.py:50
  77.6 6.8 %shard_map.96 = (f32[128,16]{1,0:T(8,128)S(1)}, f32[16,8,1024]{2,1,0:T(8,128)S(1)}) custom-call(f32[1,384]{1,0:T(1,128)S(1)} %add.183.slots_ref, f32[128,8]{1,0:T(8,128)S(1)} %get-tuple-element.67.pack_ref, f32[128,1]{1,0:T(8,128)S(1)} %copy.15.inv_ref, s32[128,2]{1,0:T(8,128)S(1)} %copy.13.ids_ref, f32[128,16]{1,0:T(8,128)S(1)} %get-tuple-element.43.probs_ref, ...), custom_call_target="tpu_custom_call" | custom-call | flops 20000000000 | bytes 60000000 | tf_op jit(solution)/shard_map/pallas_call | solution.py:310
  84.4 19.0 %all_to_all.5 = f32[16,8,1024]{2,1,0:T(8,128)S(1)} all-to-all(f32[16,8,1024]{2,1,0:T(8,128)S(1)} %get-tuple-element.59), channel_id=1, replica_groups=mesh['seq'=16,'exp'=8] {'seq'}, dimensions={0} | all-to-all | bytes 1048576 | tf_op jit(solution)/shard_map/all_to_all | solution.py:342
  103.4 1.4 collective-permute-start.12
  104.8 0.9 collective-permute-done.12
  105.7 2.3 %collective-permute-start.16 = (f32[8,1024]{1,0:T(8,128)S(1)}, f32[8,1024]{1,0:T(8,128)S(1)}, u32[]{:S(2)}, u32[]{:S(2)}) collective-permute-start(f32[8,1024]{1,0:T(8,128)S(1)} %add.208), channel_id=1, source_target_pairs={{0,2},{1,3},{2,0},{3,1},{4,6},{5,7},{6,4},{7,5},{8,10},{9,11},{10,... | collective-permute-start | bytes 98312 | tf_op jit(solution)/shard_map/ppermute | solution.py:344
  108.0 3.1 %collective-permute-start.17 = (f32[8,1024]{1,0:T(8,128)S(1)}, f32[8,1024]{1,0:T(8,128)S(1)}, u32[]{:S(2)}, u32[]{:S(2)}) collective-permute-start(f32[8,1024]{1,0:T(8,128)S(1)} %add.208), channel_id=1, source_target_pairs={{0,4},{1,5},{2,6},{3,7},{4,0},{5,1},{6,2},{7,3},{8,12},{9,13},{10,... | collective-permute-start | bytes 98312 | tf_op jit(solution)/shard_map/ppermute | solution.py:344
  111.1 0.0 collective-permute-done.15.refs_3_
  111.1 2.1 %collective-permute-done.14.refs_2_ = bf16[48,8192]{1,0:T(8,128)(2,1)} collective-permute-done((bf16[48,8192]{1,0:T(8,128)(2,1)}, bf16[48,8192]{1,0:T(8,128)(2,1)}, u32[]{:S(2)}, u32[]{:S(2)}) %collective-permute-start.14) | collective-permute-done | bytes 786464 | tf_op jit(solution)/shard_map/ppermute | solution.py:50
  113.1 0.0 collective-permute-done.13.refs_1_
  113.1 2.3 %collective-permute-start.18 = (f32[8,1024]{1,0:T(8,128)S(1)}, f32[8,1024]{1,0:T(8,128)S(1)}, u32[]{:S(2)}, u32[]{:S(2)}) collective-permute-start(f32[8,1024]{1,0:T(8,128)S(1)} %add.208), channel_id=1, source_target_pairs={{0,6},{1,7},{2,4},{3,5},{4,2},{5,3},{6,0},{7,1},{8,14},{9,15},{10,... | collective-permute-start | bytes 98312 | tf_op jit(solution)/shard_map/ppermute | solution.py:346
  115.4 0.1 fusion.2
  115.5 2.8 %collective-permute-done.18 = f32[8,1024]{1,0:T(8,128)S(1)} collective-permute-done((f32[8,1024]{1,0:T(8,128)S(1)}, f32[8,1024]{1,0:T(8,128)S(1)}, u32[]{:S(2)}, u32[]{:S(2)}) %collective-permute-start.18) | collective-permute-done | bytes 32800 | tf_op jit(solution)/shard_map/ppermute | solution.py:346
  118.3 0.1 collective-permute-start.19
  118.4 2.9 %collective-permute-start.20 = (bf16[48,8192]{1,0:T(8,128)(2,1)}, bf16[48,8192]{1,0:T(8,128)(2,1)}, u32[]{:S(2)}, u32[]{:S(2)}) collective-permute-start(bf16[48,8192]{1,0:T(8,128)(2,1)} %bitcast.42), channel_id=1, source_target_pairs={{0,7},{1,6},{2,1},{3,0},{4,3},{5,2},{6,5},{7,4},{8,15},{9,14},{10,... | collective-permute-start | bytes 2359304 | tf_op jit(solution)/shard_map/ppermute | solution.py:50
  121.3 0.5 collective-permute-start.21
  121.8 0.2 collective-permute-start.22
  122.0 1.1 copy-done.3
  123.2 1.6 copy-done.6
  124.8 1.0 copy-done.7
  125.8 4.6 %shard_map.97 = (f32[128,8192]{1,0:T(8,128)S(1)}, f32[128,128]{1,0:T(8,128)S(1)}) custom-call(f32[1,192]{1,0:T(1,128)S(1)} %get-tuple-element.99.slots_ref, f32[128,8]{1,0:T(8,128)S(1)} %get-tuple-element.67.pack_ref, f32[128,1]{1,0:T(8,128)S(1)} %copy.15.inv_ref, f32[128,16]{1,0:T(8,128)S(1)} %get-tuple-element.68.logit_ref, f32[16,8192]{1,0:T(8,128)S(1)} %copy-done.7, ...), custom_call_target="tpu_custom_call" | custom-call | flops 10000000000 | bytes 30000000 | tf_op jit(solution)/shard_map/pallas_call | solution.py:353
  130.4 2.0 %copy-done.1 = f32[128,8192]{1,0:T(8,128)} copy-done((f32[128,8192]{1,0:T(8,128)}, f32[128,8192]{1,0:T(8,128)S(1)}, u32[]{:S(2)}) %copy-start.1) | copy-done | bytes 4194328
  132.4 27.2 %all-gather = f32[128,1024]{1,0:T(8,128)} all-gather(f32[8,1024]{1,0:T(8,128)S(1)} %add_add_fusion), channel_id=2, replica_groups=mesh['seq'=16,'exp'=8] {'seq'}, dimensions={0}, use_global_device_ids=true | all-gather | bytes 557056 | tf_op jit(solution)/shard_map/all_gather | solution.py:379
  159.6 1.9 %reshape.185 = f32[16,8192]{1,0:T(8,128)} reshape(f32[128,1024]{1,0:T(8,128)} %all-gather) | data formatting | bytes 1048576 | tf_op jit(solution)/shard_map/reshape | solution.py:379
  161.5 0.0 collective-permute-done.20.refs_1_
  161.5 0.0 collective-permute-done.21.refs_2_
  161.6 2.2 %copy-done.2 = f32[128,8192]{1,0:T(8,128)S(1)} copy-done((f32[128,8192]{1,0:T(8,128)S(1)}, f32[128,8192]{1,0:T(8,128)}, u32[]{:S(2)}) %copy-start.2) | copy-done | bytes 4194328
  163.7 7.0 %shard_map.98 = bf16[128,8192]{1,0:T(8,128)(2,1)} custom-call(f32[1,192]{1,0:T(1,128)S(1)} %get-tuple-element.100.slots_ref, f32[128,8]{1,0:T(8,128)S(1)} %get-tuple-element.67.pack_ref, f32[128,1]{1,0:T(8,128)S(1)} %copy.15.inv_ref, f32[128,128]{1,0:T(8,128)S(1)} %get-tuple-element.73.sums_ref, f32[1,8192]{1,0:T(1,128)S(1)} %bitcast.33, ...), custom_call_target="tpu_custom_call" | custom-call | tf_op jit(solution)/shard_map/pallas_call | solution.py:381
  (36 shorter events, 0.1 us)
Async XLA Ops:
  0.7 3.5 %copy-start.9 = (s32[128,2]{0,1:T(2,128)S(1)}, s32[128,2]{0,1:T(2,128)}, u32[]{:S(2)}) copy-start(s32[128,2]{0,1:T(2,128)} %param.13) | copy-start | bytes 3076
  0.7 3.6 %copy-start.8 = (f32[128,16]{0,1:T(8,128)S(1)}, f32[128,16]{0,1:T(8,128)}, u32[]{:S(2)}) copy-start(f32[128,16]{0,1:T(8,128)} %param.11) | copy-start | bytes 24580
  0.7 11.5 %copy-start = (bf16[128,8192]{1,0:T(8,128)(2,1)S(1)}, bf16[128,8192]{1,0:T(8,128)(2,1)}, u32[]{:S(2)}) copy-start(bf16[128,8192]{1,0:T(8,128)(2,1)} %hidden_ref.5) | copy-start | bytes 6291460
  4.7 8.1 %collective-permute-start = (f32[8,16]{1,0:T(8,128)S(1)}, f32[8,16]{1,0:T(8,128)S(1)}, u32[]{:S(2)}, u32[]{:S(2)}) collective-permute-start(f32[8,16]{1,0:T(8,128)S(1)} %get-tuple-element.44), channel_id=1, source_target_pairs={{0,32},{1,33},{2,34},{3,35},{4,36},{5,37},{6,38},{7,39},{8,40},{9,... | collective-permute-start | bytes 1544 | tf_op jit(solution)/shard_map/ppermute | solution.py:287
  6.5 26.1 %collective-permute-start.5 = (bf16[48,8192]{1,0:T(8,128)(2,1)}, bf16[48,8192]{1,0:T(8,128)(2,1)}, u32[]{:S(2)}, u32[]{:S(2)}) collective-permute-start(bf16[48,8192]{1,0:T(8,128)(2,1)} %bitcast.39), channel_id=1, source_target_pairs={{0,2},{1,3},{2,4},{3,5},{4,6},{5,7},{6,0},{7,1},{8,10},{9,11},{10,... | collective-permute-start | bytes 2359304 | tf_op jit(solution)/shard_map/ppermute | solution.py:50
  7.9 38.4 %collective-permute-start.7 = (bf16[48,8192]{1,0:T(8,128)(2,1)}, bf16[48,8192]{1,0:T(8,128)(2,1)}, u32[]{:S(2)}, u32[]{:S(2)}) collective-permute-start(bf16[48,8192]{1,0:T(8,128)(2,1)} %bitcast.38), channel_id=1, source_target_pairs={{0,4},{1,5},{2,6},{3,7},{4,0},{5,1},{6,2},{7,3},{8,12},{9,13},{10,... | collective-permute-start | bytes 2359304 | tf_op jit(solution)/shard_map/ppermute | solution.py:50
  10.7 55.0 %collective-permute-start.6 = (bf16[48,8192]{1,0:T(8,128)(2,1)}, bf16[48,8192]{1,0:T(8,128)(2,1)}, u32[]{:S(2)}, u32[]{:S(2)}) collective-permute-start(bf16[48,8192]{1,0:T(8,128)(2,1)} %bitcast.37), channel_id=1, source_target_pairs={{0,6},{1,7},{2,0},{3,1},{4,2},{5,3},{6,4},{7,5},{8,14},{9,15},{10,... | collective-permute-start | bytes 2359304 | tf_op jit(solution)/shard_map/ppermute | solution.py:50
  12.8 5.2 %collective-permute-start.1 = (f32[8,16]{1,0:T(8,128)S(1)}, f32[8,16]{1,0:T(8,128)S(1)}, u32[]{:S(2)}, u32[]{:S(2)}) collective-permute-start(f32[8,16]{1,0:T(8,128)S(1)} %add.195), channel_id=1, source_target_pairs={{0,64},{1,65},{2,66},{3,67},{4,68},{5,69},{6,70},{7,71},{8,72},{9,... | collective-permute-start | bytes 1544 | tf_op jit(solution)/shard_map/ppermute | solution.py:287
  17.9 3.6 %collective-permute-start.2 = (f32[8,16]{1,0:T(8,128)S(1)}, f32[8,16]{1,0:T(8,128)S(1)}, u32[]{:S(2)}, u32[]{:S(2)}) collective-permute-start(f32[8,16]{1,0:T(8,128)S(1)} %add.196), channel_id=1, source_target_pairs={{0,8},{1,9},{2,10},{3,11},{4,12},{5,13},{6,14},{7,15},{8,0},{9,1},... | collective-permute-start | bytes 1544 | tf_op jit(solution)/shard_map/ppermute | solution.py:287
  21.5 5.5 %collective-permute-start.3 = (f32[8,16]{1,0:T(8,128)S(1)}, f32[8,16]{1,0:T(8,128)S(1)}, u32[]{:S(2)}, u32[]{:S(2)}) collective-permute-start(f32[8,16]{1,0:T(8,128)S(1)} %add.197), channel_id=1, source_target_pairs={{0,16},{1,17},{2,18},{3,19},{4,20},{5,21},{6,22},{7,23},{8,24},{9,... | collective-permute-start | bytes 1544 | tf_op jit(solution)/shard_map/ppermute | solution.py:287
  27.0 4.8 %collective-permute-start.4 = (f32[8,16]{1,0:T(8,128)S(1)}, f32[8,16]{1,0:T(8,128)S(1)}, u32[]{:S(2)}, u32[]{:S(2)}) collective-permute-start(f32[8,16]{1,0:T(8,128)S(1)} %add.198), channel_id=1, source_target_pairs={{0,1},{1,0},{2,3},{3,2},{4,5},{5,4},{6,7},{7,6},{8,9},{9,8},{10,11... | collective-permute-start | bytes 1544 | tf_op jit(solution)/shard_map/ppermute | solution.py:287
  32.4 29.6 %collective-permute-start.9 = (bf16[48,8320]{1,0:T(8,128)(2,1)S(1)}, bf16[48,8320]{1,0:T(8,128)(2,1)S(1)}, u32[]{:S(2)}, u32[]{:S(2)}) collective-permute-start(bf16[48,8320]{1,0:T(8,128)(2,1)S(1)} %get-tuple-element.96), channel_id=1, source_target_pairs={{0,7},{1,6},{2,1},{3,0},{4,3},{5,2},{6,5},{7,4},{8,15},{9,14},{10,... | collective-permute-start | bytes 2396168 | tf_op jit(solution)/shard_map/ppermute | solution.py:50
  32.5 31.1 %collective-permute-start.8 = (bf16[48,8320]{1,0:T(8,128)(2,1)S(1)}, bf16[48,8320]{1,0:T(8,128)(2,1)S(1)}, u32[]{:S(2)}, u32[]{:S(2)}) collective-permute-start(bf16[48,8320]{1,0:T(8,128)(2,1)S(1)} %get-tuple-element.53), channel_id=1, source_target_pairs={{0,3},{1,2},{2,5},{3,4},{4,7},{5,6},{6,1},{7,0},{8,11},{9,10},{10,... | collective-permute-start | bytes 2396168 | tf_op jit(solution)/shard_map/ppermute | solution.py:50
  46.3 31.3 %collective-permute-start.10 = (bf16[48,8320]{1,0:T(8,128)(2,1)S(1)}, bf16[48,8320]{1,0:T(8,128)(2,1)S(1)}, u32[]{:S(2)}, u32[]{:S(2)}) collective-permute-start(bf16[48,8320]{1,0:T(8,128)(2,1)S(1)} %get-tuple-element.57), channel_id=1, source_target_pairs={{0,5},{1,4},{2,7},{3,6},{4,1},{5,0},{6,3},{7,2},{8,13},{9,12},{10,... | collective-permute-start | bytes 2396168 | tf_op jit(solution)/shard_map/ppermute | solution.py:50
  46.3 31.3 %copy-start.4 = (f32[8192]{0:T(1024)S(1)}, f32[8192]{0:T(1024)}, u32[]{:S(2)}) copy-start(f32[8192]{0:T(1024)} %param.10) | copy-start | bytes 98308
  46.3 31.3 %copy-start.5 = (bf16[128,8192]{1,0:T(8,128)(2,1)S(1)}, bf16[128,8192]{1,0:T(8,128)(2,1)}, u32[]{:S(2)}) copy-start(bf16[128,8192]{1,0:T(8,128)(2,1)} %grad_ref.3) | copy-start | bytes 6291460
  46.3 20.2 %collective-permute-start.11 = (bf16[48,8192]{1,0:T(8,128)(2,1)S(1)}, bf16[48,8192]{1,0:T(8,128)(2,1)S(1)}, u32[]{:S(2)}, u32[]{:S(2)}) collective-permute-start(bf16[48,8192]{1,0:T(8,128)(2,1)S(1)} %bitcast.44), channel_id=1, source_target_pairs={{0,1},{1,0},{2,3},{3,2},{4,5},{5,4},{6,7},{7,6},{8,9},{9,8},{10,11... | collective-permute-start | bytes 2359304 | tf_op jit(solution)/shard_map/ppermute | solution.py:50
  62.0 49.1 %collective-permute-start.15 = (bf16[48,8192]{1,0:T(8,128)(2,1)}, bf16[48,8192]{1,0:T(8,128)(2,1)}, u32[]{:S(2)}, u32[]{:S(2)}) collective-permute-start(bf16[48,8192]{1,0:T(8,128)(2,1)} %bitcast.20), channel_id=1, source_target_pairs={{0,4},{1,5},{2,6},{3,7},{4,0},{5,1},{6,2},{7,3},{8,12},{9,13},{10,... | collective-permute-start | bytes 2359304 | tf_op jit(solution)/shard_map/ppermute | solution.py:50
  63.6 49.5 %collective-permute-start.14 = (bf16[48,8192]{1,0:T(8,128)(2,1)}, bf16[48,8192]{1,0:T(8,128)(2,1)}, u32[]{:S(2)}, u32[]{:S(2)}) collective-permute-start(bf16[48,8192]{1,0:T(8,128)(2,1)} %bitcast.18), channel_id=1, source_target_pairs={{0,6},{1,7},{2,0},{3,1},{4,2},{5,3},{6,4},{7,5},{8,14},{9,15},{10,... | collective-permute-start | bytes 2359304 | tf_op jit(solution)/shard_map/ppermute | solution.py:50
  65.6 47.5 %collective-permute-start.13 = (bf16[48,8192]{1,0:T(8,128)(2,1)}, bf16[48,8192]{1,0:T(8,128)(2,1)}, u32[]{:S(2)}, u32[]{:S(2)}) collective-permute-start(bf16[48,8192]{1,0:T(8,128)(2,1)} %bitcast.19), channel_id=1, source_target_pairs={{0,2},{1,3},{2,4},{3,5},{4,6},{5,7},{6,0},{7,1},{8,10},{9,11},{10,... | collective-permute-start | bytes 2359304 | tf_op jit(solution)/shard_map/ppermute | solution.py:50
  103.4 2.2 %collective-permute-start.12 = (f32[8,1024]{1,0:T(8,128)S(1)}, f32[8,1024]{1,0:T(8,128)S(1)}, u32[]{:S(2)}, u32[]{:S(2)}) collective-permute-start(f32[8,1024]{1,0:T(8,128)S(1)} %reduce_sum.19), channel_id=1, source_target_pairs={{0,1},{1,0},{2,3},{3,2},{4,5},{5,4},{6,7},{7,6},{8,9},{9,8},{10,11... | collective-permute-start | bytes 98312 | tf_op jit(solution)/shard_map/ppermute | solution.py:343
  105.7 9.8 %collective-permute-start.16 = (f32[8,1024]{1,0:T(8,128)S(1)}, f32[8,1024]{1,0:T(8,128)S(1)}, u32[]{:S(2)}, u32[]{:S(2)}) collective-permute-start(f32[8,1024]{1,0:T(8,128)S(1)} %add.208), channel_id=1, source_target_pairs={{0,2},{1,3},{2,0},{3,1},{4,6},{5,7},{6,4},{7,5},{8,10},{9,11},{10,... | collective-permute-start | bytes 98312 | tf_op jit(solution)/shard_map/ppermute | solution.py:344
  108.0 7.5 %collective-permute-start.17 = (f32[8,1024]{1,0:T(8,128)S(1)}, f32[8,1024]{1,0:T(8,128)S(1)}, u32[]{:S(2)}, u32[]{:S(2)}) collective-permute-start(f32[8,1024]{1,0:T(8,128)S(1)} %add.208), channel_id=1, source_target_pairs={{0,4},{1,5},{2,6},{3,7},{4,0},{5,1},{6,2},{7,3},{8,12},{9,13},{10,... | collective-permute-start | bytes 98312 | tf_op jit(solution)/shard_map/ppermute | solution.py:344
  113.1 5.1 %collective-permute-start.18 = (f32[8,1024]{1,0:T(8,128)S(1)}, f32[8,1024]{1,0:T(8,128)S(1)}, u32[]{:S(2)}, u32[]{:S(2)}) collective-permute-start(f32[8,1024]{1,0:T(8,128)S(1)} %add.208), channel_id=1, source_target_pairs={{0,6},{1,7},{2,4},{3,5},{4,2},{5,3},{6,0},{7,1},{8,14},{9,15},{10,... | collective-permute-start | bytes 98312 | tf_op jit(solution)/shard_map/ppermute | solution.py:346
  118.3 43.3 %collective-permute-start.19 = (bf16[48,8192]{1,0:T(8,128)(2,1)}, bf16[48,8192]{1,0:T(8,128)(2,1)S(1)}, u32[]{:S(2)}, u32[]{:S(2)}) collective-permute-start(bf16[48,8192]{1,0:T(8,128)(2,1)} %bitcast.43), channel_id=1, source_target_pairs={{0,3},{1,2},{2,5},{3,4},{4,7},{5,6},{6,1},{7,0},{8,11},{9,10},{10,... | collective-permute-start | bytes 2359304 | tf_op jit(solution)/shard_map/ppermute | solution.py:50
  118.4 43.2 %collective-permute-start.20 = (bf16[48,8192]{1,0:T(8,128)(2,1)}, bf16[48,8192]{1,0:T(8,128)(2,1)}, u32[]{:S(2)}, u32[]{:S(2)}) collective-permute-start(bf16[48,8192]{1,0:T(8,128)(2,1)} %bitcast.42), channel_id=1, source_target_pairs={{0,7},{1,6},{2,1},{3,0},{4,3},{5,2},{6,5},{7,4},{8,15},{9,14},{10,... | collective-permute-start | bytes 2359304 | tf_op jit(solution)/shard_map/ppermute | solution.py:50
  121.3 40.2 %collective-permute-start.21 = (bf16[48,8192]{1,0:T(8,128)(2,1)}, bf16[48,8192]{1,0:T(8,128)(2,1)}, u32[]{:S(2)}, u32[]{:S(2)}) collective-permute-start(bf16[48,8192]{1,0:T(8,128)(2,1)} %bitcast.41), channel_id=1, source_target_pairs={{0,5},{1,4},{2,7},{3,6},{4,1},{5,0},{6,3},{7,2},{8,13},{9,12},{10,... | collective-permute-start | bytes 2359304 | tf_op jit(solution)/shard_map/ppermute | solution.py:50
  121.8 39.7 %collective-permute-start.22 = (bf16[48,8192]{1,0:T(8,128)(2,1)}, bf16[48,8192]{1,0:T(8,128)(2,1)}, u32[]{:S(2)}, u32[]{:S(2)}) collective-permute-start(bf16[48,8192]{1,0:T(8,128)(2,1)} %bitcast.40), channel_id=1, source_target_pairs={{0,1},{1,0},{2,3},{3,2},{4,5},{5,4},{6,7},{7,6},{8,9},{9,8},{10,11... | collective-permute-start | bytes 2359304 | tf_op jit(solution)/shard_map/ppermute | solution.py:50
  122.0 1.1 copy-start.3
  123.2 1.6 copy-start.6
  124.8 1.0 copy-start.7
  130.4 2.0 %copy-start.1 = (f32[128,8192]{1,0:T(8,128)}, f32[128,8192]{1,0:T(8,128)S(1)}, u32[]{:S(2)}) copy-start(f32[128,8192]{1,0:T(8,128)S(1)} %get-tuple-element.74.part_ref) | copy-start | bytes 12582916
  161.6 2.2 %copy-start.2 = (f32[128,8192]{1,0:T(8,128)S(1)}, f32[128,8192]{1,0:T(8,128)}, u32[]{:S(2)}) copy-start(f32[128,8192]{1,0:T(8,128)} %copy-done.1) | copy-start | bytes 12582916

commit v9 on v8

--- a/solution.py
+++ b/solution.py
@@ -370,13 +370,16 @@
         + [once(ROWS)] * 4,
         out_specs=(once(TOK), fixed(TOK, 128)),
         scratch_shapes=[pltpu.VMEM((TOK, 2 * half + 6 * EXPERTS), BF16)],
-        compiler_params=params(24),
+        compiler_params=params(60),
         cost_estimate=pl.CostEstimate(
             flops=10_000_000_000, bytes_accessed=30_000_000, transcendentals=0
         ),
     )(slots[:, :half], begin, inv, logit, router_weight, gain, hidden, grad_out, *grads[:4])
     partial, sums = after(partial, sums)
-    router_grad = lax.all_gather(partial, "seq").reshape(EXPERTS, D)
+    along_z = [[4 * y + z for z in range(4)] for y in range(4)]
+    along_y = [[4 * y + z for y in range(4)] for z in range(4)]
+    partial = lax.all_gather(partial, "seq", axis_index_groups=along_z)
+    router_grad = lax.all_gather(partial, "seq", axis_index_groups=along_y).reshape(EXPERTS, D)
 
     grad_hidden = pl.pallas_call(
         last_kernel,
@@ -399,7 +402,7 @@
             pltpu.VMEM((TOK, 128), F32),
             pltpu.VMEM((TOK, 128), F32),
         ],
-        compiler_params=params(24),
+        compiler_params=params(60),
     )(slots[:, half:], pack, inv, sums, gain, part, hidden, *grads[4:])
     return grad_hidden, router_grad
 

time: 171 us -> 168 us (0.982)
  local copies, waits for them, and re-layouts: 22.4 us -> 16.4 us
  Pallas kernels: 18.8 us -> 23.5 us
    unnamed x22 -> x27, local copies, waits for them, and re-layouts: 8.14 us -> 3.54 us
    pallas_call x1, Pallas kernels: 4.62 us -> 6.97 us  [body(): pl.pallas_call(half_kernel, grid=(STEPS,), out_shape=(jax.ShapeDtypeStruc...]
    pallas_call x1, Pallas kernels: 7.04 us -> 9.34 us  [body(): pl.pallas_call(last_kernel, grid=(2, STEPS), out_shape=jax.ShapeDtypeStru...]
    reshape x1 -> x0, local copies, waits for them, and re-layouts: 1.93 us -> none  [body(): router_grad = lax.all_gather(partial, 'seq').reshape(EXPERTS, D)]
    all_gather x1 -> x2, blocking collectives: 27.2 us -> 26.8 us  [the longest x1 13.6 us: body(): lax.all_gather(partial, 'seq', axis_index_groups=along_y)]
  transfers between devices with their start and end apart: 23 -> 23, of which waited for: 9 -> 9; matrix products, arithmetic and copies ran while one was open for 7% -> 7% of each run, Pallas kernels for 7% -> 8%
where the time goes in v9:
time: 168 us
  blocking collectives  45.8 us (27%)
  waiting for transfers between devices  44.1 us (26%)
  starting transfers between devices  36.1 us (21%)
  Pallas kernels  23.5 us (14%)
  local copies, waits for them, and re-layouts  16.4 us (10%)
    ppermute x14, waiting for transfers between devices, ring_permute(): return lax.ppermute(v, 'exp', perm)  35.7 us
    all_to_all x1, blocking collectives, body(): partial = jnp.sum(lax.all_to_all(partial, 'seq', 0, 0, tiled=True), axis=0)  19 us
    ppermute x14, starting transfers between devices, ring_permute(): return lax.ppermute(v, 'exp', perm)  16.7 us
    all_gather x1, blocking collectives, body(): lax.all_gather(partial, 'seq', axis_index_groups=along_y)  13.6 us
    all_gather x1, blocking collectives, body(): partial = lax.all_gather(partial, 'seq', axis_index_groups=along_z)  13.2 us
    dynamic_slice x3, local copies, waits for them, and re-layouts, block(): lax.dynamic_slice(array, (0, 0, to * CAP, 0), (1, 2, CAP, D))  11.8 us
    ppermute x5, starting transfers between devices, body(): tally.append(tally[-1] + lax.ppermute(tally[-1], AXES, xor_perm(axis, d)))  10.5 us
    pallas_call x1, Pallas kernels, body(): pl.pallas_call(last_kernel, grid=(2, STEPS), out_shape=jax.ShapeDtypeStru...  9.34 us
  transfers between devices with their start and end apart: 23, of which 9 were waited for; matrix products, arithmetic and copies ran while one was open for 7% of the time, Pallas kernels for 8%

profile of v9, /device:TPU:0, one launch (start us, length us, event | category | flops | bytes accessed | tf_op | source)
XLA Modules:
  0.0 167.9 jit_solution(11400417302537411299)
XLA Ops:
  0.7 0.0 copy-start
  0.7 3.5 %constant_dynamic-slice_fusion.12 = (bf16[1,2,24,8192]{3,2,1,0:T(8,128)(2,1)S(1)}, bf16[1,2,24,8192]{3,2,1,0:T(8,128)(2,1)}, bf16[1,2,24,8192]{3,2,1,0:T(8,128)(2,1)}, bf16[1,2,24,8192]{3,2,1,0:T(8,128)(2,1)}) fusion(bf16[1,2,192,8192]{3,2,1,0:T(8,128)(2,1)} %param.15, s32[]{:T(128)S(6)} %select_n.35, s32[]{:T(128)S(6)} %select_n.34, s32[]{:T(128)S(6)} %select_n.33, ...), kind=kLoop, calls=%fused_computation.17 | loop fusion | bytes 6291472 | tf_op jit(solution)/shard_map/dynamic_slice | solution.py:266
  4.1 0.1 copy.16.ids_ref
  4.3 0.1 copy.17.logits_ref
  4.4 0.4 shard_map.95
  4.7 1.7 %collective-permute-start = (f32[8,16]{1,0:T(8,128)S(1)}, f32[8,16]{1,0:T(8,128)S(1)}, u32[]{:S(2)}, u32[]{:S(2)}) collective-permute-start(f32[8,16]{1,0:T(8,128)S(1)} %get-tuple-element.44), channel_id=1, source_target_pairs={{0,32},{1,33},{2,34},{3,35},{4,36},{5,37},{6,38},{7,39},{8,40},{9,... | collective-permute-start | bytes 1544 | tf_op jit(solution)/shard_map/ppermute | solution.py:287
  6.5 1.5 collective-permute-start.5
  8.0 2.7 %collective-permute-start.7 = (bf16[48,8192]{1,0:T(8,128)(2,1)}, bf16[48,8192]{1,0:T(8,128)(2,1)}, u32[]{:S(2)}, u32[]{:S(2)}) collective-permute-start(bf16[48,8192]{1,0:T(8,128)(2,1)} %bitcast.41), channel_id=1, source_target_pairs={{0,4},{1,5},{2,6},{3,7},{4,0},{5,1},{6,2},{7,3},{8,12},{9,13},{10,... | collective-permute-start | bytes 2359304 | tf_op jit(solution)/shard_map/ppermute | solution.py:50
  10.7 1.4 collective-permute-start.6
  12.1 0.1 stack.35
  12.2 0.5 multiply_reduce_fusion
  12.7 0.1 iota_add_fusion
  12.8 0.0 collective-permute-done
  12.8 2.9 %collective-permute-start.1 = (f32[8,16]{1,0:T(8,128)S(1)}, f32[8,16]{1,0:T(8,128)S(1)}, u32[]{:S(2)}, u32[]{:S(2)}) collective-permute-start(f32[8,16]{1,0:T(8,128)S(1)} %add.195), channel_id=1, source_target_pairs={{0,64},{1,65},{2,66},{3,67},{4,68},{5,69},{6,70},{7,71},{8,72},{9,... | collective-permute-start | bytes 1544 | tf_op jit(solution)/shard_map/ppermute | solution.py:287
  15.7 2.2 %collective-permute-done.1 = f32[8,16]{1,0:T(8,128)S(1)} collective-permute-done((f32[8,16]{1,0:T(8,128)S(1)}, f32[8,16]{1,0:T(8,128)S(1)}, u32[]{:S(2)}, u32[]{:S(2)}) %collective-permute-start.1) | collective-permute-done | bytes 544 | tf_op jit(solution)/shard_map/ppermute | solution.py:287
  17.9 1.9 %collective-permute-start.2 = (f32[8,16]{1,0:T(8,128)S(1)}, f32[8,16]{1,0:T(8,128)S(1)}, u32[]{:S(2)}, u32[]{:S(2)}) collective-permute-start(f32[8,16]{1,0:T(8,128)S(1)} %add.196), channel_id=1, source_target_pairs={{0,8},{1,9},{2,10},{3,11},{4,12},{5,13},{6,14},{7,15},{8,0},{9,1},... | collective-permute-start | bytes 1544 | tf_op jit(solution)/shard_map/ppermute | solution.py:287
  19.9 0.1 copy.19.ids_ref
  20.0 0.1 add.183.slots_ref
  20.1 0.1 copy.21.inv_ref
  20.2 1.4 collective-permute-done.2
  21.6 3.9 %collective-permute-start.3 = (f32[8,16]{1,0:T(8,128)S(1)}, f32[8,16]{1,0:T(8,128)S(1)}, u32[]{:S(2)}, u32[]{:S(2)}) collective-permute-start(f32[8,16]{1,0:T(8,128)S(1)} %add.197), channel_id=1, source_target_pairs={{0,16},{1,17},{2,18},{3,19},{4,20},{5,21},{6,22},{7,23},{8,24},{9,... | collective-permute-start | bytes 1544 | tf_op jit(solution)/shard_map/ppermute | solution.py:287
  25.4 1.6 collective-permute-done.3
  27.0 4.8 %constant_dynamic-slice_fusion.1 = (bf16[1,2,24,8192]{3,2,1,0:T(8,128)(2,1)}, bf16[1,2,24,8192]{3,2,1,0:T(8,128)(2,1)}, bf16[1,2,24,8192]{3,2,1,0:T(8,128)(2,1)}...) fusion(bf16[1,2,192,8192]{3,2,1,0:T(8,128)(2,1)} %param.14, ...), kind=kLoop, calls=%fused_computation.6 | loop fusion | bytes 12582928 | tf_op jit(solution)/shard_map/dynamic_slice | solution.py:266
  31.9 0.0 collective-permute-done.4
  31.9 0.1 fusion.1
  32.0 0.4 pad_maximum_fusion.2
  32.4 0.2 collective-permute-start.9
  32.6 0.0 collective-permute-done.5.refs_1_
  32.6 1.6 collective-permute-start.8
  34.2 12.1 %collective-permute-done.7.refs_3_ = bf16[48,8192]{1,0:T(8,128)(2,1)} collective-permute-done((bf16[48,8192]{1,0:T(8,128)(2,1)}, bf16[48,8192]{1,0:T(8,128)(2,1)}, u32[]{:S(2)}, u32[]{:S(2)}) %collective-permute-start.7) | collective-permute-done | bytes 786464 | tf_op jit(solution)/shard_map/ppermute | solution.py:50
  46.3 0.9 collective-permute-start.11
  47.3 3.6 %constant_dynamic-slice_fusion = (bf16[1,2,24,8192]{3,2,1,0:T(8,128)(2,1)}, bf16[1,2,24,8192]{3,2,1,0:T(8,128)(2,1)}, bf16[1,2,24,8192]{3,2,1,0:T(8,128)(2,1)}, bf16[1,2,24,8192]{3,2,1,0:T(8,128)(2,1)}) fusion(bf16[1,2,192,8192]{3,2,1,0:T(8,128)(2,1)} %param.14, s32[]{:T(128)S(6)} %select_n.35, s32[]{:T(128)S(6)} %select_n.34, s32[]{:T(128)S(6)} %select_n.32, ...), kind=kLoop, calls=%fused_computation.5 | loop fusion | bytes 6291472 | tf_op jit(solution)/shard_map/dynamic_slice | solution.py:266
  50.8 11.2 %collective-permute-done.9.refs_5_.refs_9_ = bf16[48,8320]{1,0:T(8,128)(2,1)S(1)} collective-permute-done((bf16[48,8320]{1,0:T(8,128)(2,1)S(1)}, bf16[48,8320]{1,0:T(8,128)(2,1)S(1)}, u32[]{:S(2)}, u32[]{:S(2)}) %collective-permute-start.9) | collective-permute-done | bytes 798752 | tf_op jit(solution)/shard_map/ppermute | solution.py:50
  62.0 1.6 collective-permute-start.15
  63.6 0.0 collective-permute-done.8.refs_4_.refs_8_
  63.6 2.0 %collective-permute-start.14 = (bf16[48,8192]{1,0:T(8,128)(2,1)}, bf16[48,8192]{1,0:T(8,128)(2,1)}, u32[]{:S(2)}, u32[]{:S(2)}) collective-permute-start(bf16[48,8192]{1,0:T(8,128)(2,1)} %bitcast.18), channel_id=1, source_target_pairs={{0,6},{1,7},{2,0},{3,1},{4,2},{5,3},{6,4},{7,5},{8,14},{9,15},{10,... | collective-permute-start | bytes 2359304 | tf_op jit(solution)/shard_map/ppermute | solution.py:50
  65.6 0.9 collective-permute-start.13
  66.6 0.0 collective-permute-done.11.refs_7_
  66.6 11.1 %collective-permute-done.10.refs_6_.refs_10_ = bf16[48,8320]{1,0:T(8,128)(2,1)S(1)} collective-permute-done((bf16[48,8320]{1,0:T(8,128)(2,1)S(1)}, bf16[48,8320]{1,0:T(8,128)(2,1)S(1)}, u32[]{:S(2)}, u32[]{:S(2)}) %collective-permute-start.10) | collective-permute-done | bytes 798752 | tf_op jit(solution)/shard_map/ppermute | solution.py:50
  77.6 6.8 %shard_map.96 = (f32[128,16]{1,0:T(8,128)S(1)}, f32[16,8,1024]{2,1,0:T(8,128)S(1)}) custom-call(f32[1,384]{1,0:T(1,128)S(1)} %add.183.slots_ref, f32[128,8]{1,0:T(8,128)S(1)} %get-tuple-element.67.pack_ref, f32[128,1]{1,0:T(8,128)S(1)} %copy.21.inv_ref, s32[128,2]{1,0:T(8,128)S(1)} %copy.19.ids_ref, f32[128,16]{1,0:T(8,128)S(1)} %get-tuple-element.43.probs_ref, ...), custom_call_target="tpu_custom_call" | custom-call | flops 20000000000 | bytes 60000000 | tf_op jit(solution)/shard_map/pallas_call | solution.py:310
  84.5 0.0 copy-start.5
  84.5 0.6 copy-done.5
  85.1 19.0 %all_to_all.5 = f32[16,8,1024]{2,1,0:T(8,128)S(1)} all-to-all(f32[16,8,1024]{2,1,0:T(8,128)S(1)} %get-tuple-element.59), channel_id=1, replica_groups=mesh['seq'=16,'exp'=8] {'seq'}, dimensions={0} | all-to-all | bytes 1048576 | tf_op jit(solution)/shard_map/all_to_all | solution.py:342
  104.1 1.4 collective-permute-start.12
  105.5 0.9 collective-permute-done.12
  106.3 2.3 %collective-permute-start.16 = (f32[8,1024]{1,0:T(8,128)S(1)}, f32[8,1024]{1,0:T(8,128)S(1)}, u32[]{:S(2)}, u32[]{:S(2)}) collective-permute-start(f32[8,1024]{1,0:T(8,128)S(1)} %add.208), channel_id=1, source_target_pairs={{0,2},{1,3},{2,0},{3,1},{4,6},{5,7},{6,4},{7,5},{8,10},{9,11},{10,... | collective-permute-start | bytes 98312 | tf_op jit(solution)/shard_map/ppermute | solution.py:344
  108.7 3.2 %collective-permute-start.17 = (f32[8,1024]{1,0:T(8,128)S(1)}, f32[8,1024]{1,0:T(8,128)S(1)}, u32[]{:S(2)}, u32[]{:S(2)}) collective-permute-start(f32[8,1024]{1,0:T(8,128)S(1)} %add.208), channel_id=1, source_target_pairs={{0,4},{1,5},{2,6},{3,7},{4,0},{5,1},{6,2},{7,3},{8,12},{9,13},{10,... | collective-permute-start | bytes 98312 | tf_op jit(solution)/shard_map/ppermute | solution.py:344
  111.8 1.3 collective-permute-done.14.refs_2_
  113.2 2.1 %collective-permute-start.18 = (f32[8,1024]{1,0:T(8,128)S(1)}, f32[8,1024]{1,0:T(8,128)S(1)}, u32[]{:S(2)}, u32[]{:S(2)}) collective-permute-start(f32[8,1024]{1,0:T(8,128)S(1)} %add.208), channel_id=1, source_target_pairs={{0,6},{1,7},{2,4},{3,5},{4,2},{5,3},{6,0},{7,1},{8,14},{9,15},{10,... | collective-permute-start | bytes 98312 | tf_op jit(solution)/shard_map/ppermute | solution.py:346
  115.3 0.7 fusion.2
  115.9 2.4 %collective-permute-done.18 = f32[8,1024]{1,0:T(8,128)S(1)} collective-permute-done((f32[8,1024]{1,0:T(8,128)S(1)}, f32[8,1024]{1,0:T(8,128)S(1)}, u32[]{:S(2)}, u32[]{:S(2)}) %collective-permute-start.18) | collective-permute-done | bytes 32800 | tf_op jit(solution)/shard_map/ppermute | solution.py:346
  118.3 0.1 collective-permute-start.19
  118.4 2.9 %collective-permute-start.20 = (bf16[48,8192]{1,0:T(8,128)(2,1)}, bf16[48,8192]{1,0:T(8,128)(2,1)S(1)}, u32[]{:S(2)}, u32[]{:S(2)}) collective-permute-start(bf16[48,8192]{1,0:T(8,128)(2,1)} %bitcast.46), channel_id=1, source_target_pairs={{0,7},{1,6},{2,1},{3,0},{4,3},{5,2},{6,5},{7,4},{8,15},{9,14},{10,... | collective-permute-start | bytes 2359304 | tf_op jit(solution)/shard_map/ppermute | solution.py:50
  121.3 0.3 collective-permute-start.21
  121.7 0.4 collective-permute-start.22
  122.0 7.0 %shard_map.97 = (f32[128,8192]{1,0:T(8,128)}, f32[128,128]{1,0:T(8,128)}) custom-call(f32[1,192]{1,0:T(1,128)} %get-tuple-element.99.slots_ref, f32[128,8]{1,0:T(8,128)} %copy-done.2, f32[128,1]{1,0:T(8,128)} %copy-done.1, f32[128,16]{1,0:T(8,128)} %copy-done.5, f32[16,8192]{1,0:T(8,128)} %weight_ref.1, f32[1,8192]{1,0:T(1,128)} %bitcast.33, ...), custom_call_target="tpu_custom_call" | custom-call | flops 10000000000 | bytes 30000000 | tf_op jit(solution)/shard_map/pallas_call | solution.py:353
  129.0 13.2 %all-gather = f32[32,1024]{1,0:T(8,128)S(1)} all-gather(f32[8,1024]{1,0:T(8,128)S(1)} %add_add_fusion), channel_id=2, replica_groups={{0,8,16,24},{32,40,48,56},{64,72,80,88},{96,104,112,120},{1,9,17,25},{3..., dimensions={0}, use_global_device_ids=true | all-gather | bytes 163840 | tf_op jit(solution)/shard_map/all_gather | solution.py:381
  142.2 13.6 %all-gather.1 = f32[16,8,1024]{2,1,0:T(8,128)S(1)} all-gather(f32[4,8,1024]{2,1,0:T(8,128)S(1)} %bitcast.49), channel_id=3, replica_groups={{0,32,64,96},{8,40,72,104},{16,48,80,112},{24,56,88,120},{1,33,65,97},{..., dimensions={0}, use_global_device_ids=true | all-gather | bytes 655360 | tf_op jit(solution)/shard_map/all_gather | solution.py:382
  155.9 1.1 copy.22
  157.0 0.8 copy-done.6
  157.8 0.3 copy-done.7
  158.1 0.3 copy-done.8
  158.4 0.2 copy-done.9
  158.6 9.3 %shard_map.98 = bf16[128,8192]{1,0:T(8,128)(2,1)} custom-call(f32[1,192]{1,0:T(1,128)} %get-tuple-element.100.slots_ref, f32[128,8]{1,0:T(8,128)} %copy-done.2, f32[128,1]{1,0:T(8,128)} %copy-done.1, f32[128,128]{1,0:T(8,128)} %get-tuple-element.73.sums_ref, f32[1,8192]{1,0:T(1,128)} %bitcast.34, f32[128,8192]{1,0:T(8,128)} %get-tuple-element.74.part_ref, ...), custom_call_target="tpu_custom_call" | custom-call | tf_op jit(solution)/shard_map/pallas_call | solution.py:384
  (41 shorter events, 0.2 us)
Async XLA Ops:
  0.7 3.5 %copy-start.11 = (s32[128,2]{0,1:T(2,128)S(1)}, s32[128,2]{0,1:T(2,128)}, u32[]{:S(2)}) copy-start(s32[128,2]{0,1:T(2,128)} %param.13) | copy-start | bytes 3076
  0.7 3.6 %copy-start.10 = (f32[128,16]{0,1:T(8,128)S(1)}, f32[128,16]{0,1:T(8,128)}, u32[]{:S(2)}) copy-start(f32[128,16]{0,1:T(8,128)} %param.11) | copy-start | bytes 24580
  0.7 11.5 %copy-start = (bf16[128,8192]{1,0:T(8,128)(2,1)S(1)}, bf16[128,8192]{1,0:T(8,128)(2,1)}, u32[]{:S(2)}) copy-start(bf16[128,8192]{1,0:T(8,128)(2,1)} %hidden_ref.5) | copy-start | bytes 6291460
  4.7 72.9 %copy-start.2 = (f32[128,8]{1,0:T(8,128)}, f32[128,8]{1,0:T(8,128)S(1)}, u32[]{:S(2)}) copy-start(f32[128,8]{1,0:T(8,128)S(1)} %get-tuple-element.67.pack_ref) | copy-start | bytes 12292
  4.7 8.1 %collective-permute-start = (f32[8,16]{1,0:T(8,128)S(1)}, f32[8,16]{1,0:T(8,128)S(1)}, u32[]{:S(2)}, u32[]{:S(2)}) collective-permute-start(f32[8,16]{1,0:T(8,128)S(1)} %get-tuple-element.44), channel_id=1, source_target_pairs={{0,32},{1,33},{2,34},{3,35},{4,36},{5,37},{6,38},{7,39},{8,40},{9,... | collective-permute-start | bytes 1544 | tf_op jit(solution)/shard_map/ppermute | solution.py:287
  6.5 26.1 %collective-permute-start.5 = (bf16[48,8192]{1,0:T(8,128)(2,1)}, bf16[48,8192]{1,0:T(8,128)(2,1)}, u32[]{:S(2)}, u32[]{:S(2)}) collective-permute-start(bf16[48,8192]{1,0:T(8,128)(2,1)} %bitcast.42), channel_id=1, source_target_pairs={{0,2},{1,3},{2,4},{3,5},{4,6},{5,7},{6,0},{7,1},{8,10},{9,11},{10,... | collective-permute-start | bytes 2359304 | tf_op jit(solution)/shard_map/ppermute | solution.py:50
  8.0 38.4 %collective-permute-start.7 = (bf16[48,8192]{1,0:T(8,128)(2,1)}, bf16[48,8192]{1,0:T(8,128)(2,1)}, u32[]{:S(2)}, u32[]{:S(2)}) collective-permute-start(bf16[48,8192]{1,0:T(8,128)(2,1)} %bitcast.41), channel_id=1, source_target_pairs={{0,4},{1,5},{2,6},{3,7},{4,0},{5,1},{6,2},{7,3},{8,12},{9,13},{10,... | collective-permute-start | bytes 2359304 | tf_op jit(solution)/shard_map/ppermute | solution.py:50
  10.7 55.0 %collective-permute-start.6 = (bf16[48,8192]{1,0:T(8,128)(2,1)}, bf16[48,8192]{1,0:T(8,128)(2,1)}, u32[]{:S(2)}, u32[]{:S(2)}) collective-permute-start(bf16[48,8192]{1,0:T(8,128)(2,1)} %bitcast.40), channel_id=1, source_target_pairs={{0,6},{1,7},{2,0},{3,1},{4,2},{5,3},{6,4},{7,5},{8,14},{9,15},{10,... | collective-permute-start | bytes 2359304 | tf_op jit(solution)/shard_map/ppermute | solution.py:50
  12.8 5.2 %collective-permute-start.1 = (f32[8,16]{1,0:T(8,128)S(1)}, f32[8,16]{1,0:T(8,128)S(1)}, u32[]{:S(2)}, u32[]{:S(2)}) collective-permute-start(f32[8,16]{1,0:T(8,128)S(1)} %add.195), channel_id=1, source_target_pairs={{0,64},{1,65},{2,66},{3,67},{4,68},{5,69},{6,70},{7,71},{8,72},{9,... | collective-permute-start | bytes 1544 | tf_op jit(solution)/shard_map/ppermute | solution.py:287
  17.9 3.6 %collective-permute-start.2 = (f32[8,16]{1,0:T(8,128)S(1)}, f32[8,16]{1,0:T(8,128)S(1)}, u32[]{:S(2)}, u32[]{:S(2)}) collective-permute-start(f32[8,16]{1,0:T(8,128)S(1)} %add.196), channel_id=1, source_target_pairs={{0,8},{1,9},{2,10},{3,11},{4,12},{5,13},{6,14},{7,15},{8,0},{9,1},... | collective-permute-start | bytes 1544 | tf_op jit(solution)/shard_map/ppermute | solution.py:287
  20.2 57.5 %copy-start.1 = (f32[128,1]{1,0:T(8,128)}, f32[128,1]{1,0:T(8,128)S(1)}, u32[]{:S(2)}) copy-start(f32[128,1]{1,0:T(8,128)S(1)} %copy.21.inv_ref) | copy-start | bytes 1540
  21.6 5.5 %collective-permute-start.3 = (f32[8,16]{1,0:T(8,128)S(1)}, f32[8,16]{1,0:T(8,128)S(1)}, u32[]{:S(2)}, u32[]{:S(2)}) collective-permute-start(f32[8,16]{1,0:T(8,128)S(1)} %add.197), channel_id=1, source_target_pairs={{0,16},{1,17},{2,18},{3,19},{4,20},{5,21},{6,22},{7,23},{8,24},{9,... | collective-permute-start | bytes 1544 | tf_op jit(solution)/shard_map/ppermute | solution.py:287
  27.0 4.8 %collective-permute-start.4 = (f32[8,16]{1,0:T(8,128)S(1)}, f32[8,16]{1,0:T(8,128)S(1)}, u32[]{:S(2)}, u32[]{:S(2)}) collective-permute-start(f32[8,16]{1,0:T(8,128)S(1)} %add.198), channel_id=1, source_target_pairs={{0,1},{1,0},{2,3},{3,2},{4,5},{5,4},{6,7},{7,6},{8,9},{9,8},{10,11... | collective-permute-start | bytes 1544 | tf_op jit(solution)/shard_map/ppermute | solution.py:287
  32.4 29.6 %collective-permute-start.9 = (bf16[48,8320]{1,0:T(8,128)(2,1)S(1)}, bf16[48,8320]{1,0:T(8,128)(2,1)S(1)}, u32[]{:S(2)}, u32[]{:S(2)}) collective-permute-start(bf16[48,8320]{1,0:T(8,128)(2,1)S(1)} %get-tuple-element.96), channel_id=1, source_target_pairs={{0,7},{1,6},{2,1},{3,0},{4,3},{5,2},{6,5},{7,4},{8,15},{9,14},{10,... | collective-permute-start | bytes 2396168 | tf_op jit(solution)/shard_map/ppermute | solution.py:50
  32.6 31.0 %collective-permute-start.8 = (bf16[48,8320]{1,0:T(8,128)(2,1)S(1)}, bf16[48,8320]{1,0:T(8,128)(2,1)S(1)}, u32[]{:S(2)}, u32[]{:S(2)}) collective-permute-start(bf16[48,8320]{1,0:T(8,128)(2,1)S(1)} %get-tuple-element.53), channel_id=1, source_target_pairs={{0,3},{1,2},{2,5},{3,4},{4,7},{5,6},{6,1},{7,0},{8,11},{9,10},{10,... | collective-permute-start | bytes 2396168 | tf_op jit(solution)/shard_map/ppermute | solution.py:50
  46.3 31.3 %collective-permute-start.10 = (bf16[48,8320]{1,0:T(8,128)(2,1)S(1)}, bf16[48,8320]{1,0:T(8,128)(2,1)S(1)}, u32[]{:S(2)}, u32[]{:S(2)}) collective-permute-start(bf16[48,8320]{1,0:T(8,128)(2,1)S(1)} %get-tuple-element.57), channel_id=1, source_target_pairs={{0,5},{1,4},{2,7},{3,6},{4,1},{5,0},{6,3},{7,2},{8,13},{9,12},{10,... | collective-permute-start | bytes 2396168 | tf_op jit(solution)/shard_map/ppermute | solution.py:50
  46.3 31.3 %copy-start.3 = (f32[8192]{0:T(1024)S(1)}, f32[8192]{0:T(1024)}, u32[]{:S(2)}) copy-start(f32[8192]{0:T(1024)} %param.10) | copy-start | bytes 98308
  46.3 31.3 %copy-start.4 = (bf16[128,8192]{1,0:T(8,128)(2,1)S(1)}, bf16[128,8192]{1,0:T(8,128)(2,1)}, u32[]{:S(2)}) copy-start(bf16[128,8192]{1,0:T(8,128)(2,1)} %grad_ref.3) | copy-start | bytes 6291460
  46.3 20.2 %collective-permute-start.11 = (bf16[48,8192]{1,0:T(8,128)(2,1)S(1)}, bf16[48,8192]{1,0:T(8,128)(2,1)S(1)}, u32[]{:S(2)}, u32[]{:S(2)}) collective-permute-start(bf16[48,8192]{1,0:T(8,128)(2,1)S(1)} %bitcast.48), channel_id=1, source_target_pairs={{0,1},{1,0},{2,3},{3,2},{4,5},{5,4},{6,7},{7,6},{8,9},{9,8},{10,11... | collective-permute-start | bytes 2359304 | tf_op jit(solution)/shard_map/ppermute | solution.py:50
  62.0 49.8 %collective-permute-start.15 = (bf16[48,8192]{1,0:T(8,128)(2,1)}, bf16[48,8192]{1,0:T(8,128)(2,1)}, u32[]{:S(2)}, u32[]{:S(2)}) collective-permute-start(bf16[48,8192]{1,0:T(8,128)(2,1)} %bitcast.20), channel_id=1, source_target_pairs={{0,4},{1,5},{2,6},{3,7},{4,0},{5,1},{6,2},{7,3},{8,12},{9,13},{10,... | collective-permute-start | bytes 2359304 | tf_op jit(solution)/shard_map/ppermute | solution.py:50
  63.6 49.5 %collective-permute-start.14 = (bf16[48,8192]{1,0:T(8,128)(2,1)}, bf16[48,8192]{1,0:T(8,128)(2,1)}, u32[]{:S(2)}, u32[]{:S(2)}) collective-permute-start(bf16[48,8192]{1,0:T(8,128)(2,1)} %bitcast.18), channel_id=1, source_target_pairs={{0,6},{1,7},{2,0},{3,1},{4,2},{5,3},{6,4},{7,5},{8,14},{9,15},{10,... | collective-permute-start | bytes 2359304 | tf_op jit(solution)/shard_map/ppermute | solution.py:50
  65.6 47.5 %collective-permute-start.13 = (bf16[48,8192]{1,0:T(8,128)(2,1)}, bf16[48,8192]{1,0:T(8,128)(2,1)}, u32[]{:S(2)}, u32[]{:S(2)}) collective-permute-start(bf16[48,8192]{1,0:T(8,128)(2,1)} %bitcast.19), channel_id=1, source_target_pairs={{0,2},{1,3},{2,4},{3,5},{4,6},{5,7},{6,0},{7,1},{8,10},{9,11},{10,... | collective-permute-start | bytes 2359304 | tf_op jit(solution)/shard_map/ppermute | solution.py:50
  84.5 0.6 copy-start.5
  104.1 2.2 %collective-permute-start.12 = (f32[8,1024]{1,0:T(8,128)S(1)}, f32[8,1024]{1,0:T(8,128)S(1)}, u32[]{:S(2)}, u32[]{:S(2)}) collective-permute-start(f32[8,1024]{1,0:T(8,128)S(1)} %reduce_sum.19), channel_id=1, source_target_pairs={{0,1},{1,0},{2,3},{3,2},{4,5},{5,4},{6,7},{7,6},{8,9},{9,8},{10,11... | collective-permute-start | bytes 98312 | tf_op jit(solution)/shard_map/ppermute | solution.py:343
  106.3 9.6 %collective-permute-start.16 = (f32[8,1024]{1,0:T(8,128)S(1)}, f32[8,1024]{1,0:T(8,128)S(1)}, u32[]{:S(2)}, u32[]{:S(2)}) collective-permute-start(f32[8,1024]{1,0:T(8,128)S(1)} %add.208), channel_id=1, source_target_pairs={{0,2},{1,3},{2,0},{3,1},{4,6},{5,7},{6,4},{7,5},{8,10},{9,11},{10,... | collective-permute-start | bytes 98312 | tf_op jit(solution)/shard_map/ppermute | solution.py:344
  108.7 7.3 %collective-permute-start.17 = (f32[8,1024]{1,0:T(8,128)S(1)}, f32[8,1024]{1,0:T(8,128)S(1)}, u32[]{:S(2)}, u32[]{:S(2)}) collective-permute-start(f32[8,1024]{1,0:T(8,128)S(1)} %add.208), channel_id=1, source_target_pairs={{0,4},{1,5},{2,6},{3,7},{4,0},{5,1},{6,2},{7,3},{8,12},{9,13},{10,... | collective-permute-start | bytes 98312 | tf_op jit(solution)/shard_map/ppermute | solution.py:344
  113.2 5.1 %collective-permute-start.18 = (f32[8,1024]{1,0:T(8,128)S(1)}, f32[8,1024]{1,0:T(8,128)S(1)}, u32[]{:S(2)}, u32[]{:S(2)}) collective-permute-start(f32[8,1024]{1,0:T(8,128)S(1)} %add.208), channel_id=1, source_target_pairs={{0,6},{1,7},{2,4},{3,5},{4,2},{5,3},{6,0},{7,1},{8,14},{9,15},{10,... | collective-permute-start | bytes 98312 | tf_op jit(solution)/shard_map/ppermute | solution.py:346
  118.3 38.7 %collective-permute-start.19 = (bf16[48,8192]{1,0:T(8,128)(2,1)}, bf16[48,8192]{1,0:T(8,128)(2,1)S(1)}, u32[]{:S(2)}, u32[]{:S(2)}) collective-permute-start(bf16[48,8192]{1,0:T(8,128)(2,1)} %bitcast.47), channel_id=1, source_target_pairs={{0,3},{1,2},{2,5},{3,4},{4,7},{5,6},{6,1},{7,0},{8,11},{9,10},{10,... | collective-permute-start | bytes 2359304 | tf_op jit(solution)/shard_map/ppermute | solution.py:50
  118.4 38.6 %collective-permute-start.20 = (bf16[48,8192]{1,0:T(8,128)(2,1)}, bf16[48,8192]{1,0:T(8,128)(2,1)S(1)}, u32[]{:S(2)}, u32[]{:S(2)}) collective-permute-start(bf16[48,8192]{1,0:T(8,128)(2,1)} %bitcast.46), channel_id=1, source_target_pairs={{0,7},{1,6},{2,1},{3,0},{4,3},{5,2},{6,5},{7,4},{8,15},{9,14},{10,... | collective-permute-start | bytes 2359304 | tf_op jit(solution)/shard_map/ppermute | solution.py:50
  121.3 35.7 %collective-permute-start.21 = (bf16[48,8192]{1,0:T(8,128)(2,1)}, bf16[48,8192]{1,0:T(8,128)(2,1)S(1)}, u32[]{:S(2)}, u32[]{:S(2)}) collective-permute-start(bf16[48,8192]{1,0:T(8,128)(2,1)} %bitcast.45), channel_id=1, source_target_pairs={{0,5},{1,4},{2,7},{3,6},{4,1},{5,0},{6,3},{7,2},{8,13},{9,12},{10,... | collective-permute-start | bytes 2359304 | tf_op jit(solution)/shard_map/ppermute | solution.py:50
  121.7 35.3 %collective-permute-start.22 = (bf16[48,8192]{1,0:T(8,128)(2,1)}, bf16[48,8192]{1,0:T(8,128)(2,1)S(1)}, u32[]{:S(2)}, u32[]{:S(2)}) collective-permute-start(bf16[48,8192]{1,0:T(8,128)(2,1)} %bitcast.44), channel_id=1, source_target_pairs={{0,1},{1,0},{2,3},{3,2},{4,5},{5,4},{6,7},{7,6},{8,9},{9,8},{10,11... | collective-permute-start | bytes 2359304 | tf_op jit(solution)/shard_map/ppermute | solution.py:50
  157.0 0.9 copy-start.6
  157.0 1.1 copy-start.7
  157.0 1.4 copy-start.8
  157.0 1.6 copy-start.9

commit v10 on v8

--- a/solution.py
+++ b/solution.py
@@ -349,7 +349,8 @@
     once = lambda rows: pl.BlockSpec((rows, WIDE), lambda c: (0, c))
     fixed = lambda *shape: pl.BlockSpec(shape, lambda c: (0,) * len(shape))
     half = 4 * ROWS
-    begin, partial = after(pack, partial)
+    router_grad = lax.all_gather(partial, "seq").reshape(EXPERTS, D)
+    begin, router_grad = after(pack, router_grad)
     part, sums = pl.pallas_call(
         half_kernel,
         grid=(STEPS,),
@@ -371,12 +372,8 @@
         out_specs=(once(TOK), fixed(TOK, 128)),
         scratch_shapes=[pltpu.VMEM((TOK, 2 * half + 6 * EXPERTS), BF16)],
         compiler_params=params(24),
-        cost_estimate=pl.CostEstimate(
-            flops=10_000_000_000, bytes_accessed=30_000_000, transcendentals=0
-        ),
+        cost_estimate=pl.CostEstimate(flops=1_000, bytes_accessed=1_000, transcendentals=0),
     )(slots[:, :half], begin, inv, logit, router_weight, gain, hidden, grad_out, *grads[:4])
-    partial, sums = after(partial, sums)
-    router_grad = lax.all_gather(partial, "seq").reshape(EXPERTS, D)
 
     grad_hidden = pl.pallas_call(
         last_kernel,

time: 171 us -> 167 us (0.977)
  local copies, waits for them, and re-layouts: 22.4 us -> 18.4 us
  starting transfers between devices: 36.2 us -> 33.7 us
  other arithmetic: 1.11 us -> 3.53 us
    unnamed x22 -> x24, local copies, waits for them, and re-layouts: 8.14 us -> 4.05 us
    ppermute x14, waiting for transfers between devices: 36.5 us -> 34.6 us  [ring_permute(): return lax.ppermute(v, 'exp', perm)]
    ppermute x1, starting transfers between devices: 2.27 us -> 0.51 us  [body(): lax.ppermute(partial, AXES, xor_perm('x', 3))]
    ppermute x2, waiting for transfers between devices: 0.01 us -> 1.75 us  [body(): near = [lax.ppermute(partial, AXES, xor_perm('x', d)) for d in (1, 2)]]
  transfers between devices with their start and end apart: 23 -> 23, of which waited for: 9 -> 9; matrix products, arithmetic and copies ran while one was open for 7% -> 8% of each run, Pallas kernels for 7% -> 7%
where the time goes in v10:
time: 167 us
  blocking collectives  45.9 us (27%)
  waiting for transfers between devices  45.5 us (27%)
  starting transfers between devices  33.7 us (20%)
  Pallas kernels  19 us (11%)
  local copies, waits for them, and re-layouts  18.4 us (11%)
  other arithmetic  3.53 us (2%)
    ppermute x14, waiting for transfers between devices, ring_permute(): return lax.ppermute(v, 'exp', perm)  34.6 us
    all_gather x1, blocking collectives, body(): router_grad = lax.all_gather(partial, 'seq').reshape(EXPERTS, D)  26.7 us
    all_to_all x1, blocking collectives, body(): partial = jnp.sum(lax.all_to_all(partial, 'seq', 0, 0, tiled=True), axis=0)  19.2 us
    ppermute x14, starting transfers between devices, ring_permute(): return lax.ppermute(v, 'exp', perm)  16 us
    dynamic_slice x3, local copies, waits for them, and re-layouts, block(): lax.dynamic_slice(array, (0, 0, to * CAP, 0), (1, 2, CAP, D))  12 us
    ppermute x5, starting transfers between devices, body(): tally.append(tally[-1] + lax.ppermute(tally[-1], AXES, xor_perm(axis, d)))  10.5 us
    pallas_call x1, Pallas kernels, body(): pl.pallas_call(last_kernel, grid=(2, STEPS), out_shape=jax.ShapeDtypeStru...  7.19 us
    pallas_call x1, Pallas kernels, body(): pl.pallas_call(mid_kernel, grid=(2, STEPS), out_shape=(jax.ShapeDtypeStru...  6.81 us
  transfers between devices with their start and end apart: 23, of which 9 were waited for; matrix products, arithmetic and copies ran while one was open for 8% of the time, Pallas kernels for 7%

profile of v10, /device:TPU:0, one launch (start us, length us, event | category | flops | bytes accessed | tf_op | source)
XLA Modules:
  0.0 166.8 jit_solution(1902064563833211516)
XLA Ops:
  0.7 3.8 %constant_dynamic-slice_fusion.12 = (bf16[1,2,24,8192]{3,2,1,0:T(8,128)(2,1)}, bf16[1,2,24,8192]{3,2,1,0:T(8,128)(2,1)}, bf16[1,2,24,8192]{3,2,1,0:T(8,128)(2,1)}, bf16[1,2,24,8192]{3,2,1,0:T(8,128)(2,1)}) fusion(bf16[1,2,192,8192]{3,2,1,0:T(8,128)(2,1)} %param.15, s32[]{:T(128)S(6)} %select_n.35, s32[]{:T(128)S(6)} %select_n.34, s32[]{:T(128)S(6)} %select_n.33, ...), kind=kLoop, calls=%fused_computation.17 | loop fusion | bytes 6291472 | tf_op jit(solution)/shard_map/dynamic_slice | solution.py:266
  4.4 0.1 copy.10.ids_ref
  4.6 0.1 copy.11.logits_ref
  4.7 0.4 shard_map.95
  5.0 1.7 %collective-permute-start = (f32[8,16]{1,0:T(8,128)S(1)}, f32[8,16]{1,0:T(8,128)S(1)}, u32[]{:S(2)}, u32[]{:S(2)}) collective-permute-start(f32[8,16]{1,0:T(8,128)S(1)} %get-tuple-element.42), channel_id=1, source_target_pairs={{0,32},{1,33},{2,34},{3,35},{4,36},{5,37},{6,38},{7,39},{8,40},{9,... | collective-permute-start | bytes 1544 | tf_op jit(solution)/shard_map/ppermute | solution.py:287
  6.8 1.5 collective-permute-start.5
  8.2 2.7 %collective-permute-start.7 = (bf16[48,8192]{1,0:T(8,128)(2,1)}, bf16[48,8192]{1,0:T(8,128)(2,1)}, u32[]{:S(2)}, u32[]{:S(2)}) collective-permute-start(bf16[48,8192]{1,0:T(8,128)(2,1)} %bitcast.10), channel_id=1, source_target_pairs={{0,4},{1,5},{2,6},{3,7},{4,0},{5,1},{6,2},{7,3},{8,12},{9,13},{10,... | collective-permute-start | bytes 2359304 | tf_op jit(solution)/shard_map/ppermute | solution.py:50
  11.0 1.4 collective-permute-start.6
  12.4 0.1 stack.35
  12.5 0.5 multiply_reduce_fusion
  13.0 0.1 iota_add_fusion
  13.1 0.0 collective-permute-done
  13.1 2.9 %collective-permute-start.1 = (f32[8,16]{1,0:T(8,128)S(1)}, f32[8,16]{1,0:T(8,128)S(1)}, u32[]{:S(2)}, u32[]{:S(2)}) collective-permute-start(f32[8,16]{1,0:T(8,128)S(1)} %add.195), channel_id=1, source_target_pairs={{0,64},{1,65},{2,66},{3,67},{4,68},{5,69},{6,70},{7,71},{8,72},{9,... | collective-permute-start | bytes 1544 | tf_op jit(solution)/shard_map/ppermute | solution.py:287
  16.0 2.2 %collective-permute-done.1 = f32[8,16]{1,0:T(8,128)S(1)} collective-permute-done((f32[8,16]{1,0:T(8,128)S(1)}, f32[8,16]{1,0:T(8,128)S(1)}, u32[]{:S(2)}, u32[]{:S(2)}) %collective-permute-start.1) | collective-permute-done | bytes 544 | tf_op jit(solution)/shard_map/ppermute | solution.py:287
  18.2 1.9 %collective-permute-start.2 = (f32[8,16]{1,0:T(8,128)S(1)}, f32[8,16]{1,0:T(8,128)S(1)}, u32[]{:S(2)}, u32[]{:S(2)}) collective-permute-start(f32[8,16]{1,0:T(8,128)S(1)} %add.196), channel_id=1, source_target_pairs={{0,8},{1,9},{2,10},{3,11},{4,12},{5,13},{6,14},{7,15},{8,0},{9,1},... | collective-permute-start | bytes 1544 | tf_op jit(solution)/shard_map/ppermute | solution.py:287
  20.2 0.1 copy.13.ids_ref
  20.3 0.1 add.183.slots_ref
  20.3 0.1 copy.15.inv_ref
  20.5 1.4 collective-permute-done.2
  21.8 3.9 %collective-permute-start.3 = (f32[8,16]{1,0:T(8,128)S(1)}, f32[8,16]{1,0:T(8,128)S(1)}, u32[]{:S(2)}, u32[]{:S(2)}) collective-permute-start(f32[8,16]{1,0:T(8,128)S(1)} %add.197), channel_id=1, source_target_pairs={{0,16},{1,17},{2,18},{3,19},{4,20},{5,21},{6,22},{7,23},{8,24},{9,... | collective-permute-start | bytes 1544 | tf_op jit(solution)/shard_map/ppermute | solution.py:287
  25.7 1.6 collective-permute-done.3
  27.3 4.9 %constant_dynamic-slice_fusion.1 = (bf16[1,2,24,8192]{3,2,1,0:T(8,128)(2,1)}, bf16[1,2,24,8192]{3,2,1,0:T(8,128)(2,1)}, bf16[1,2,24,8192]{3,2,1,0:T(8,128)(2,1)}...) fusion(bf16[1,2,192,8192]{3,2,1,0:T(8,128)(2,1)} %param.14, ...), kind=kLoop, calls=%fused_computation.6 | loop fusion | bytes 12582928 | tf_op jit(solution)/shard_map/dynamic_slice | solution.py:266
  32.2 0.0 collective-permute-done.4
  32.2 0.1 fusion.1
  32.3 0.4 pad_maximum_fusion.2
  32.7 0.2 collective-permute-start.9
  32.9 0.0 collective-permute-done.5.refs_1_
  32.9 1.6 collective-permute-start.8
  34.5 12.1 %collective-permute-done.7.refs_3_ = bf16[48,8192]{1,0:T(8,128)(2,1)} collective-permute-done((bf16[48,8192]{1,0:T(8,128)(2,1)}, bf16[48,8192]{1,0:T(8,128)(2,1)}, u32[]{:S(2)}, u32[]{:S(2)}) %collective-permute-start.7) | collective-permute-done | bytes 786464 | tf_op jit(solution)/shard_map/ppermute | solution.py:50
  46.6 0.9 collective-permute-start.11
  47.5 3.4 %constant_dynamic-slice_fusion = (bf16[1,2,24,8192]{3,2,1,0:T(8,128)(2,1)S(1)}, bf16[1,2,24,8192]{3,2,1,0:T(8,128)(2,1)}, bf16[1,2,24,8192]{3,2,1,0:T(8,128)(2,1)}, bf16[1,2,24,8192]{3,2,1,0:T(8,128)(2,1)}) fusion(bf16[1,2,192,8192]{3,2,1,0:T(8,128)(2,1)} %param.14, s32[]{:T(128)S(6)} %select_n.35, s32[]{:T(128)S(6)} %select_n.34, s32[]{:T(128)S(6)} %select_n.32, ...), kind=kLoop, calls=%fused_computation.5 | loop fusion | bytes 6291472 | tf_op jit(solution)/shard_map/dynamic_slice | solution.py:266
  50.9 11.4 %collective-permute-done.9.refs_5_.refs_9_ = bf16[48,8320]{1,0:T(8,128)(2,1)S(1)} collective-permute-done((bf16[48,8320]{1,0:T(8,128)(2,1)S(1)}, bf16[48,8320]{1,0:T(8,128)(2,1)S(1)}, u32[]{:S(2)}, u32[]{:S(2)}) %collective-permute-start.9) | collective-permute-done | bytes 798752 | tf_op jit(solution)/shard_map/ppermute | solution.py:50
  62.3 1.6 collective-permute-start.15
  63.9 0.0 collective-permute-done.8.refs_4_.refs_8_
  63.9 2.0 %collective-permute-start.14 = (bf16[48,8192]{1,0:T(8,128)(2,1)}, bf16[48,8192]{1,0:T(8,128)(2,1)}, u32[]{:S(2)}, u32[]{:S(2)}) collective-permute-start(bf16[48,8192]{1,0:T(8,128)(2,1)} %bitcast.18), channel_id=1, source_target_pairs={{0,6},{1,7},{2,0},{3,1},{4,2},{5,3},{6,4},{7,5},{8,14},{9,15},{10,... | collective-permute-start | bytes 2359304 | tf_op jit(solution)/shard_map/ppermute | solution.py:50
  65.9 0.0 collective-permute-done.6.refs_2_
  65.9 0.9 collective-permute-start.13
  66.9 11.1 %collective-permute-done.10.refs_6_.refs_10_ = bf16[48,8320]{1,0:T(8,128)(2,1)S(1)} collective-permute-done((bf16[48,8320]{1,0:T(8,128)(2,1)S(1)}, bf16[48,8320]{1,0:T(8,128)(2,1)S(1)}, u32[]{:S(2)}, u32[]{:S(2)}) %collective-permute-start.10) | collective-permute-done | bytes 798752 | tf_op jit(solution)/shard_map/ppermute | solution.py:50
  77.9 6.8 %shard_map.96 = (f32[128,16]{1,0:T(8,128)S(1)}, f32[16,8,1024]{2,1,0:T(8,128)S(1)}) custom-call(f32[1,384]{1,0:T(1,128)S(1)} %add.183.slots_ref, f32[128,8]{1,0:T(8,128)S(1)} %get-tuple-element.64.pack_ref, f32[128,1]{1,0:T(8,128)S(1)} %copy.15.inv_ref, s32[128,2]{1,0:T(8,128)S(1)} %copy.13.ids_ref, f32[128,16]{1,0:T(8,128)S(1)} %get-tuple-element.41.probs_ref, ...), custom_call_target="tpu_custom_call" | custom-call | flops 20000000000 | bytes 60000000 | tf_op jit(solution)/shard_map/pallas_call | solution.py:310
  84.7 0.0 copy-start.7
  84.8 0.6 copy-done.7
  85.4 19.2 %all_to_all.5 = f32[16,8,1024]{2,1,0:T(8,128)} all-to-all(f32[16,8,1024]{2,1,0:T(8,128)S(1)} %get-tuple-element.57), channel_id=1, replica_groups=mesh['seq'=16,'exp'=8] {'seq'}, dimensions={0} | all-to-all | bytes 1048576 | tf_op jit(solution)/shard_map/all_to_all | solution.py:342
  104.6 1.7 %reduce_sum.19 = f32[8,1024]{1,0:T(8,128)} reduce(f32[16,8,1024]{2,1,0:T(8,128)} %all_to_all.5, f32[]{:T(128)} %constant.29.clone.1), dimensions={0}, to_apply=%region_1.2 | reduce | flops 122880 | bytes 557060 | tf_op jit(solution)/shard_map/reduce_sum | solution.py:342
  106.3 1.3 collective-permute-start.12
  107.6 1.1 collective-permute-done.12
  108.6 0.8 add.208
  109.4 2.3 %collective-permute-start.16 = (f32[8,1024]{1,0:T(8,128)S(1)}, f32[8,1024]{1,0:T(8,128)S(1)}, u32[]{:S(2)}, u32[]{:S(2)}) collective-permute-start(f32[8,1024]{1,0:T(8,128)S(1)} %add.208), channel_id=1, source_target_pairs={{0,2},{1,3},{2,0},{3,1},{4,6},{5,7},{6,4},{7,5},{8,10},{9,11},{10,... | collective-permute-start | bytes 98312 | tf_op jit(solution)/shard_map/ppermute | solution.py:344
  111.7 3.1 %collective-permute-start.17 = (f32[8,1024]{1,0:T(8,128)S(1)}, f32[8,1024]{1,0:T(8,128)S(1)}, u32[]{:S(2)}, u32[]{:S(2)}) collective-permute-start(f32[8,1024]{1,0:T(8,128)S(1)} %add.208), channel_id=1, source_target_pairs={{0,4},{1,5},{2,6},{3,7},{4,0},{5,1},{6,2},{7,3},{8,12},{9,13},{10,... | collective-permute-start | bytes 98312 | tf_op jit(solution)/shard_map/ppermute | solution.py:344
  114.8 0.0 collective-permute-done.15.refs_3_
  114.8 0.0 collective-permute-done.14.refs_2_
  114.8 0.0 collective-permute-done.13.refs_1_
  114.9 0.5 collective-permute-start.18
  115.4 1.7 %collective-permute-done.17 = f32[8,1024]{1,0:T(8,128)S(1)} collective-permute-done((f32[8,1024]{1,0:T(8,128)S(1)}, f32[8,1024]{1,0:T(8,128)S(1)}, u32[]{:S(2)}, u32[]{:S(2)}) %collective-permute-start.17) | collective-permute-done | bytes 32800 | tf_op jit(solution)/shard_map/ppermute | solution.py:344
  117.1 2.9 %collective-permute-done.18 = f32[8,1024]{1,0:T(8,128)S(1)} collective-permute-done((f32[8,1024]{1,0:T(8,128)S(1)}, f32[8,1024]{1,0:T(8,128)S(1)}, u32[]{:S(2)}, u32[]{:S(2)}) %collective-permute-start.18) | collective-permute-done | bytes 32800 | tf_op jit(solution)/shard_map/ppermute | solution.py:346
  120.1 0.1 collective-permute-start.19
  120.2 2.9 %collective-permute-start.20 = (bf16[48,8192]{1,0:T(8,128)(2,1)}, bf16[48,8192]{1,0:T(8,128)(2,1)}, u32[]{:S(2)}, u32[]{:S(2)}) collective-permute-start(bf16[48,8192]{1,0:T(8,128)(2,1)} %bitcast.39), channel_id=1, source_target_pairs={{0,7},{1,6},{2,1},{3,0},{4,3},{5,2},{6,5},{7,4},{8,15},{9,14},{10,... | collective-permute-start | bytes 2359304 | tf_op jit(solution)/shard_map/ppermute | solution.py:50
  123.1 0.1 fusion.2
  123.2 26.7 %all-gather = f32[128,1024]{1,0:T(8,128)} all-gather(f32[8,1024]{1,0:T(8,128)S(1)} %add_add_fusion), channel_id=2, replica_groups=mesh['seq'=16,'exp'=8] {'seq'}, dimensions={0}, use_global_device_ids=true | all-gather | bytes 557056 | tf_op jit(solution)/shard_map/all_gather | solution.py:352
  149.8 1.9 %reshape.184 = f32[16,8192]{1,0:T(8,128)} reshape(f32[128,1024]{1,0:T(8,128)} %all-gather) | data formatting | bytes 1048576 | tf_op jit(solution)/shard_map/reshape | solution.py:352
  151.8 1.6 copy-done.2
  153.4 0.8 copy-done.6
  154.1 0.8 copy-done.8
  155.0 4.6 %shard_map.97 = (f32[128,8192]{1,0:T(8,128)S(1)}, f32[128,128]{1,0:T(8,128)S(1)}) custom-call(f32[1,192]{1,0:T(1,128)S(1)} %get-tuple-element.95.slots_ref, f32[128,8]{1,0:T(8,128)S(1)} %get-tuple-element.64.pack_ref, f32[128,1]{1,0:T(8,128)S(1)} %copy.15.inv_ref, f32[128,16]{1,0:T(8,128)S(1)} %copy-done.8, f32[16,8192]{1,0:T(8,128)S(1)} %copy-done.4, ...), custom_call_target="tpu_custom_call" | custom-call | flops 1000 | bytes 1000 | tf_op jit(solution)/shard_map/pallas_call | solution.py:354
  159.6 7.2 %shard_map.98 = bf16[128,8192]{1,0:T(8,128)(2,1)} custom-call(f32[1,192]{1,0:T(1,128)S(1)} %get-tuple-element.96.slots_ref, f32[128,8]{1,0:T(8,128)S(1)} %get-tuple-element.64.pack_ref, f32[128,1]{1,0:T(8,128)S(1)} %copy.15.inv_ref, f32[128,128]{1,0:T(8,128)S(1)} %get-tuple-element.69.sums_ref, f32[1,8192]{1,0:T(1,128)S(1)} %bitcast.33, ...), custom_call_target="tpu_custom_call" | custom-call | tf_op jit(solution)/shard_map/pallas_call | solution.py:378
  (38 shorter events, 0.1 us)
Async XLA Ops:
  0.7 3.8 %copy-start.10 = (s32[128,2]{0,1:T(2,128)S(1)}, s32[128,2]{0,1:T(2,128)}, u32[]{:S(2)}) copy-start(s32[128,2]{0,1:T(2,128)} %param.13) | copy-start | bytes 3076
  0.7 3.9 %copy-start.9 = (f32[128,16]{0,1:T(8,128)S(1)}, f32[128,16]{0,1:T(8,128)}, u32[]{:S(2)}) copy-start(f32[128,16]{0,1:T(8,128)} %param.11) | copy-start | bytes 24580
  0.7 11.8 %copy-start = (bf16[128,8192]{1,0:T(8,128)(2,1)S(1)}, bf16[128,8192]{1,0:T(8,128)(2,1)}, u32[]{:S(2)}) copy-start(bf16[128,8192]{1,0:T(8,128)(2,1)} %hidden_ref.5) | copy-start | bytes 6291460
  5.0 8.1 %collective-permute-start = (f32[8,16]{1,0:T(8,128)S(1)}, f32[8,16]{1,0:T(8,128)S(1)}, u32[]{:S(2)}, u32[]{:S(2)}) collective-permute-start(f32[8,16]{1,0:T(8,128)S(1)} %get-tuple-element.42), channel_id=1, source_target_pairs={{0,32},{1,33},{2,34},{3,35},{4,36},{5,37},{6,38},{7,39},{8,40},{9,... | collective-permute-start | bytes 1544 | tf_op jit(solution)/shard_map/ppermute | solution.py:287
  6.8 26.1 %collective-permute-start.5 = (bf16[48,8192]{1,0:T(8,128)(2,1)}, bf16[48,8192]{1,0:T(8,128)(2,1)}, u32[]{:S(2)}, u32[]{:S(2)}) collective-permute-start(bf16[48,8192]{1,0:T(8,128)(2,1)} %bitcast.8), channel_id=1, source_target_pairs={{0,2},{1,3},{2,4},{3,5},{4,6},{5,7},{6,0},{7,1},{8,10},{9,11},{10,... | collective-permute-start | bytes 2359304 | tf_op jit(solution)/shard_map/ppermute | solution.py:50
  8.2 38.4 %collective-permute-start.7 = (bf16[48,8192]{1,0:T(8,128)(2,1)}, bf16[48,8192]{1,0:T(8,128)(2,1)}, u32[]{:S(2)}, u32[]{:S(2)}) collective-permute-start(bf16[48,8192]{1,0:T(8,128)(2,1)} %bitcast.10), channel_id=1, source_target_pairs={{0,4},{1,5},{2,6},{3,7},{4,0},{5,1},{6,2},{7,3},{8,12},{9,13},{10,... | collective-permute-start | bytes 2359304 | tf_op jit(solution)/shard_map/ppermute | solution.py:50
  11.0 54.9 %collective-permute-start.6 = (bf16[48,8192]{1,0:T(8,128)(2,1)}, bf16[48,8192]{1,0:T(8,128)(2,1)}, u32[]{:S(2)}, u32[]{:S(2)}) collective-permute-start(bf16[48,8192]{1,0:T(8,128)(2,1)} %bitcast.9), channel_id=1, source_target_pairs={{0,6},{1,7},{2,0},{3,1},{4,2},{5,3},{6,4},{7,5},{8,14},{9,15},{10,... | collective-permute-start | bytes 2359304 | tf_op jit(solution)/shard_map/ppermute | solution.py:50
  13.1 5.2 %collective-permute-start.1 = (f32[8,16]{1,0:T(8,128)S(1)}, f32[8,16]{1,0:T(8,128)S(1)}, u32[]{:S(2)}, u32[]{:S(2)}) collective-permute-start(f32[8,16]{1,0:T(8,128)S(1)} %add.195), channel_id=1, source_target_pairs={{0,64},{1,65},{2,66},{3,67},{4,68},{5,69},{6,70},{7,71},{8,72},{9,... | collective-permute-start | bytes 1544 | tf_op jit(solution)/shard_map/ppermute | solution.py:287
  18.2 3.6 %collective-permute-start.2 = (f32[8,16]{1,0:T(8,128)S(1)}, f32[8,16]{1,0:T(8,128)S(1)}, u32[]{:S(2)}, u32[]{:S(2)}) collective-permute-start(f32[8,16]{1,0:T(8,128)S(1)} %add.196), channel_id=1, source_target_pairs={{0,8},{1,9},{2,10},{3,11},{4,12},{5,13},{6,14},{7,15},{8,0},{9,1},... | collective-permute-start | bytes 1544 | tf_op jit(solution)/shard_map/ppermute | solution.py:287
  21.8 5.5 %collective-permute-start.3 = (f32[8,16]{1,0:T(8,128)S(1)}, f32[8,16]{1,0:T(8,128)S(1)}, u32[]{:S(2)}, u32[]{:S(2)}) collective-permute-start(f32[8,16]{1,0:T(8,128)S(1)} %add.197), channel_id=1, source_target_pairs={{0,16},{1,17},{2,18},{3,19},{4,20},{5,21},{6,22},{7,23},{8,24},{9,... | collective-permute-start | bytes 1544 | tf_op jit(solution)/shard_map/ppermute | solution.py:287
  27.3 4.9 %collective-permute-start.4 = (f32[8,16]{1,0:T(8,128)S(1)}, f32[8,16]{1,0:T(8,128)S(1)}, u32[]{:S(2)}, u32[]{:S(2)}) collective-permute-start(f32[8,16]{1,0:T(8,128)S(1)} %add.198), channel_id=1, source_target_pairs={{0,1},{1,0},{2,3},{3,2},{4,5},{5,4},{6,7},{7,6},{8,9},{9,8},{10,11... | collective-permute-start | bytes 1544 | tf_op jit(solution)/shard_map/ppermute | solution.py:287
  32.7 29.6 %collective-permute-start.9 = (bf16[48,8320]{1,0:T(8,128)(2,1)S(1)}, bf16[48,8320]{1,0:T(8,128)(2,1)S(1)}, u32[]{:S(2)}, u32[]{:S(2)}) collective-permute-start(bf16[48,8320]{1,0:T(8,128)(2,1)S(1)} %get-tuple-element.92), channel_id=1, source_target_pairs={{0,7},{1,6},{2,1},{3,0},{4,3},{5,2},{6,5},{7,4},{8,15},{9,14},{10,... | collective-permute-start | bytes 2396168 | tf_op jit(solution)/shard_map/ppermute | solution.py:50
  32.9 31.0 %collective-permute-start.8 = (bf16[48,8320]{1,0:T(8,128)(2,1)S(1)}, bf16[48,8320]{1,0:T(8,128)(2,1)S(1)}, u32[]{:S(2)}, u32[]{:S(2)}) collective-permute-start(bf16[48,8320]{1,0:T(8,128)(2,1)S(1)} %get-tuple-element.51), channel_id=1, source_target_pairs={{0,3},{1,2},{2,5},{3,4},{4,7},{5,6},{6,1},{7,0},{8,11},{9,10},{10,... | collective-permute-start | bytes 2396168 | tf_op jit(solution)/shard_map/ppermute | solution.py:50
  46.6 31.3 %collective-permute-start.10 = (bf16[48,8320]{1,0:T(8,128)(2,1)S(1)}, bf16[48,8320]{1,0:T(8,128)(2,1)S(1)}, u32[]{:S(2)}, u32[]{:S(2)}) collective-permute-start(bf16[48,8320]{1,0:T(8,128)(2,1)S(1)} %get-tuple-element.55), channel_id=1, source_target_pairs={{0,5},{1,4},{2,7},{3,6},{4,1},{5,0},{6,3},{7,2},{8,13},{9,12},{10,... | collective-permute-start | bytes 2396168 | tf_op jit(solution)/shard_map/ppermute | solution.py:50
  46.6 31.3 %copy-start.1 = (bf16[128,8192]{1,0:T(8,128)(2,1)S(1)}, bf16[128,8192]{1,0:T(8,128)(2,1)}, u32[]{:S(2)}) copy-start(bf16[128,8192]{1,0:T(8,128)(2,1)} %grad_ref.3) | copy-start | bytes 6291460
  46.6 31.3 %copy-start.3 = (bf16[1,2,24,8192]{3,2,1,0:T(8,128)(2,1)S(1)}, bf16[1,2,24,8192]{3,2,1,0:T(8,128)(2,1)}, u32[]{:S(2)}) copy-start(bf16[1,2,24,8192]{3,2,1,0:T(8,128)(2,1)} %get-tuple-element.88) | copy-start | bytes 2359300
  46.6 31.3 %copy-start.5 = (f32[8192]{0:T(1024)S(1)}, f32[8192]{0:T(1024)}, u32[]{:S(2)}) copy-start(f32[8192]{0:T(1024)} %param.10) | copy-start | bytes 98308
  46.6 20.2 %collective-permute-start.11 = (bf16[48,8192]{1,0:T(8,128)(2,1)S(1)}, bf16[48,8192]{1,0:T(8,128)(2,1)S(1)}, u32[]{:S(2)}, u32[]{:S(2)}) collective-permute-start(bf16[48,8192]{1,0:T(8,128)(2,1)S(1)} %bitcast.41), channel_id=1, source_target_pairs={{0,1},{1,0},{2,3},{3,2},{4,5},{5,4},{6,7},{7,6},{8,9},{9,8},{10,11... | collective-permute-start | bytes 2359304 | tf_op jit(solution)/shard_map/ppermute | solution.py:50
  62.3 52.6 %collective-permute-start.15 = (bf16[48,8192]{1,0:T(8,128)(2,1)}, bf16[48,8192]{1,0:T(8,128)(2,1)}, u32[]{:S(2)}, u32[]{:S(2)}) collective-permute-start(bf16[48,8192]{1,0:T(8,128)(2,1)} %bitcast.20), channel_id=1, source_target_pairs={{0,4},{1,5},{2,6},{3,7},{4,0},{5,1},{6,2},{7,3},{8,12},{9,13},{10,... | collective-permute-start | bytes 2359304 | tf_op jit(solution)/shard_map/ppermute | solution.py:50
  63.9 50.9 %collective-permute-start.14 = (bf16[48,8192]{1,0:T(8,128)(2,1)}, bf16[48,8192]{1,0:T(8,128)(2,1)}, u32[]{:S(2)}, u32[]{:S(2)}) collective-permute-start(bf16[48,8192]{1,0:T(8,128)(2,1)} %bitcast.18), channel_id=1, source_target_pairs={{0,6},{1,7},{2,0},{3,1},{4,2},{5,3},{6,4},{7,5},{8,14},{9,15},{10,... | collective-permute-start | bytes 2359304 | tf_op jit(solution)/shard_map/ppermute | solution.py:50
  65.9 48.9 %collective-permute-start.13 = (bf16[48,8192]{1,0:T(8,128)(2,1)}, bf16[48,8192]{1,0:T(8,128)(2,1)}, u32[]{:S(2)}, u32[]{:S(2)}) collective-permute-start(bf16[48,8192]{1,0:T(8,128)(2,1)} %bitcast.19), channel_id=1, source_target_pairs={{0,2},{1,3},{2,4},{3,5},{4,6},{5,7},{6,0},{7,1},{8,10},{9,11},{10,... | collective-permute-start | bytes 2359304 | tf_op jit(solution)/shard_map/ppermute | solution.py:50
  84.7 0.6 copy-start.7
  85.4 66.4 %copy-start.4 = (f32[16,8192]{1,0:T(8,128)S(1)}, f32[16,8192]{1,0:T(8,128)}, u32[]{:S(2)}) copy-start(f32[16,8192]{1,0:T(8,128)} %weight_ref.1) | copy-start | bytes 1572868
  106.3 2.4 %collective-permute-start.12 = (f32[8,1024]{1,0:T(8,128)}, f32[8,1024]{1,0:T(8,128)S(1)}, u32[]{:S(2)}, u32[]{:S(2)}) collective-permute-start(f32[8,1024]{1,0:T(8,128)} %reduce_sum.19), channel_id=1, source_target_pairs={{0,1},{1,0},{2,3},{3,2},{4,5},{5,4},{6,7},{7,6},{8,9},{9,8},{10,11... | collective-permute-start | bytes 98312 | tf_op jit(solution)/shard_map/ppermute | solution.py:343
  109.4 6.0 %collective-permute-start.16 = (f32[8,1024]{1,0:T(8,128)S(1)}, f32[8,1024]{1,0:T(8,128)S(1)}, u32[]{:S(2)}, u32[]{:S(2)}) collective-permute-start(f32[8,1024]{1,0:T(8,128)S(1)} %add.208), channel_id=1, source_target_pairs={{0,2},{1,3},{2,0},{3,1},{4,6},{5,7},{6,4},{7,5},{8,10},{9,11},{10,... | collective-permute-start | bytes 98312 | tf_op jit(solution)/shard_map/ppermute | solution.py:344
  111.7 5.4 %collective-permute-start.17 = (f32[8,1024]{1,0:T(8,128)S(1)}, f32[8,1024]{1,0:T(8,128)S(1)}, u32[]{:S(2)}, u32[]{:S(2)}) collective-permute-start(f32[8,1024]{1,0:T(8,128)S(1)} %add.208), channel_id=1, source_target_pairs={{0,4},{1,5},{2,6},{3,7},{4,0},{5,1},{6,2},{7,3},{8,12},{9,13},{10,... | collective-permute-start | bytes 98312 | tf_op jit(solution)/shard_map/ppermute | solution.py:344
  114.9 5.2 %collective-permute-start.18 = (f32[8,1024]{1,0:T(8,128)S(1)}, f32[8,1024]{1,0:T(8,128)S(1)}, u32[]{:S(2)}, u32[]{:S(2)}) collective-permute-start(f32[8,1024]{1,0:T(8,128)S(1)} %add.208), channel_id=1, source_target_pairs={{0,6},{1,7},{2,4},{3,5},{4,2},{5,3},{6,0},{7,1},{8,14},{9,15},{10,... | collective-permute-start | bytes 98312 | tf_op jit(solution)/shard_map/ppermute | solution.py:346
  120.1 39.5 %collective-permute-start.19 = (bf16[48,8192]{1,0:T(8,128)(2,1)}, bf16[48,8192]{1,0:T(8,128)(2,1)}, u32[]{:S(2)}, u32[]{:S(2)}) collective-permute-start(bf16[48,8192]{1,0:T(8,128)(2,1)} %bitcast.40), channel_id=1, source_target_pairs={{0,3},{1,2},{2,5},{3,4},{4,7},{5,6},{6,1},{7,0},{8,11},{9,10},{10,... | collective-permute-start | bytes 2359304 | tf_op jit(solution)/shard_map/ppermute | solution.py:50
  120.2 39.5 %collective-permute-start.20 = (bf16[48,8192]{1,0:T(8,128)(2,1)}, bf16[48,8192]{1,0:T(8,128)(2,1)}, u32[]{:S(2)}, u32[]{:S(2)}) collective-permute-start(bf16[48,8192]{1,0:T(8,128)(2,1)} %bitcast.39), channel_id=1, source_target_pairs={{0,7},{1,6},{2,1},{3,0},{4,3},{5,2},{6,5},{7,4},{8,15},{9,14},{10,... | collective-permute-start | bytes 2359304 | tf_op jit(solution)/shard_map/ppermute | solution.py:50
  123.1 36.5 %collective-permute-start.21 = (bf16[48,8192]{1,0:T(8,128)(2,1)}, bf16[48,8192]{1,0:T(8,128)(2,1)}, u32[]{:S(2)}, u32[]{:S(2)}) collective-permute-start(bf16[48,8192]{1,0:T(8,128)(2,1)} %bitcast.38), channel_id=1, source_target_pairs={{0,5},{1,4},{2,7},{3,6},{4,1},{5,0},{6,3},{7,2},{8,13},{9,12},{10,... | collective-permute-start | bytes 2359304 | tf_op jit(solution)/shard_map/ppermute | solution.py:50
  123.1 36.5 %collective-permute-start.22 = (bf16[48,8192]{1,0:T(8,128)(2,1)}, bf16[48,8192]{1,0:T(8,128)(2,1)}, u32[]{:S(2)}, u32[]{:S(2)}) collective-permute-start(bf16[48,8192]{1,0:T(8,128)(2,1)} %bitcast.37), channel_id=1, source_target_pairs={{0,1},{1,0},{2,3},{3,2},{4,5},{5,4},{6,7},{7,6},{8,9},{9,8},{10,11... | collective-permute-start | bytes 2359304 | tf_op jit(solution)/shard_map/ppermute | solution.py:50
  151.8 1.6 copy-start.2
  153.4 0.8 copy-start.6
  154.1 0.8 copy-start.8

commit v11 on v8

--- a/solution.py
+++ b/solution.py
@@ -52,7 +52,7 @@
 
 def slot_numbers(sources):
     base = jnp.stack(sources).astype(F32) * ROWS
-    return (base[:, None] + jnp.arange(ROWS, dtype=F32)[None, :]).reshape(1, 8 * ROWS)
+    return (base[:, None] + jnp.arange(ROWS, dtype=F32)[None, :]).reshape(1, len(sources) * ROWS)
 
 
 def split3(v):
@@ -202,7 +202,7 @@
 def last_kernel(
     slots_ref, pack_ref, inv_ref, sums_ref, gain_ref, part_ref, hidden_ref, *refs
 ):
-    blocks, (out_ref, part_scr, left_ref, acc_ref, factor_ref) = refs[:-5], refs[-5:]
+    blocks, (out_ref, part_scr, hidden_scr, left_ref, acc_ref, factor_ref) = refs[:-6], refs[-6:]
     stage, c = pl.program_id(0), pl.program_id(1)
     cols = pl.ds(pl.multiple_of(c * WIDE, WIDE), WIDE)
 
@@ -219,7 +219,9 @@
         right = jnp.concatenate(rows + rows, axis=0)
         scaled = jnp.dot(left_ref[...], right, preferred_element_type=F32) * gain_ref[...]
         part_scr[:, cols] = part_ref[...] + scaled
-        acc_ref[...] += row_sums(scaled, hidden_ref[...])
+        hidden = hidden_ref[...]
+        hidden_scr[:, cols] = hidden
+        acc_ref[...] += row_sums(scaled, hidden)
 
     @pl.when((stage == 1) & (c == 0))
     def _():
@@ -229,7 +231,7 @@
 
     @pl.when(stage == 1)
     def _():
-        normed = hidden_ref[...].astype(F32) * factor_ref[:, 0:1]
+        normed = hidden_scr[:, cols].astype(F32) * factor_ref[:, 0:1]
         out_ref[...] = (part_scr[:, cols] - normed).astype(BF16)
 
 
@@ -239,10 +241,6 @@
 
 def first(rows):
     return pl.BlockSpec((rows, WIDE), lambda p, c: (0, jnp.where(p == 0, c, STEPS - 1)))
-
-
-def twice(rows):
-    return pl.BlockSpec((rows, WIDE), lambda p, c: (0, c))
 
 
 def second(rows):
@@ -260,6 +258,7 @@
     gain = norm_gain.reshape(1, D)
     sources = [((at["x"] - s) & 3) * 2 + (at["c"] ^ m) for s, m in ROUTES]
     slots = slot_numbers(sources)
+    late_slots = slot_numbers([sources[i] for i in (6, 4, 5, 7)])
 
     def block(array, s, m):
         to = ((at["x"] + s) & 3) * 2 + (at["c"] ^ m)
@@ -304,7 +303,8 @@
         b, outs[n] = after(block(source, s, m), outs[n])
         grads.append(ring_permute(b, s, m))
     source, tally[3] = after(expert_grad, tally[3])
-    rest = [block(source, s, m) for s, m in ROUTES[4:]]
+    late = [ROUTES[i] for i in (6, 4, 5, 7)]
+    rest = [block(source, s, m) for s, m in late]
 
     small = lambda *shape: pl.BlockSpec(shape, lambda p, c: (0,) * len(shape))
     logit, partial = pl.pallas_call(
@@ -345,7 +345,7 @@
     partial, *grads[1:4] = after(partial, *grads[1:4])
     partial = (partial + near[0]) + (near[1] + lax.ppermute(partial, AXES, xor_perm("x", 3)))
     partial, *rest = after(partial, *rest)
-    grads += [ring_permute(b, s, m) for b, (s, m) in zip(rest, ROUTES[4:])]
+    grads += [ring_permute(b, s, m) for b, (s, m) in zip(rest, late)]
     once = lambda rows: pl.BlockSpec((rows, WIDE), lambda c: (0, c))
     fixed = lambda *shape: pl.BlockSpec(shape, lambda c: (0,) * len(shape))
     half = 4 * ROWS
@@ -370,7 +370,7 @@
         + [once(ROWS)] * 4,
         out_specs=(once(TOK), fixed(TOK, 128)),
         scratch_shapes=[pltpu.VMEM((TOK, 2 * half + 6 * EXPERTS), BF16)],
-        compiler_params=params(24),
+        compiler_params=params(60),
         cost_estimate=pl.CostEstimate(
             flops=10_000_000_000, bytes_accessed=30_000_000, transcendentals=0
         ),
@@ -389,18 +389,19 @@
             small(TOK, 128),
             first(1),
             first(TOK),
-            twice(TOK),
+            first(TOK),
         ]
         + [first(ROWS)] * 4,
         out_specs=second(TOK),
         scratch_shapes=[
             pltpu.VMEM((TOK, D), F32),
+            pltpu.VMEM((TOK, D), BF16),
             pltpu.VMEM((TOK, 2 * half), BF16),
             pltpu.VMEM((TOK, 128), F32),
             pltpu.VMEM((TOK, 128), F32),
         ],
-        compiler_params=params(24),
-    )(slots[:, half:], pack, inv, sums, gain, part, hidden, *grads[4:])
+        compiler_params=params(60),
+    )(late_slots, pack, inv, sums, gain, part, hidden, *grads[4:])
     return grad_hidden, router_grad
 
 

time: 171 us -> 166 us (0.971)
  local copies, waits for them, and re-layouts: 22.4 us -> 16.6 us
  Pallas kernels: 18.8 us -> 22.4 us
  blocking collectives: 46.2 us -> 44.3 us
  waiting for transfers between devices: 45.3 us -> 43.4 us
    unnamed x22 -> x24, local copies, waits for them, and re-layouts: 8.14 us -> 2.24 us
    pallas_call x1, Pallas kernels: 4.62 us -> 7 us  [body(): pl.pallas_call(half_kernel, grid=(STEPS,), out_shape=(jax.ShapeDtypeStruc...]
    all_gather x1, blocking collectives: 27.2 us -> 25.3 us  [body(): router_grad = lax.all_gather(partial, 'seq').reshape(EXPERTS, D)]
  transfers between devices with their start and end apart: 23 -> 23, of which waited for: 9 -> 9; matrix products, arithmetic and copies ran while one was open for 7% -> 7% of each run, Pallas kernels for 7% -> 8%
where the time goes in v11:
time: 166 us
  blocking collectives  44.3 us (27%)
  waiting for transfers between devices  43.4 us (26%)
  starting transfers between devices  37.4 us (23%)
  Pallas kernels  22.4 us (13%)
  local copies, waits for them, and re-layouts  16.6 us (10%)
    ppermute x14, waiting for transfers between devices, ring_permute(): return lax.ppermute(v, 'exp', perm)  35.7 us
    all_gather x1, blocking collectives, body(): router_grad = lax.all_gather(partial, 'seq').reshape(EXPERTS, D)  25.3 us
    all_to_all x1, blocking collectives, body(): partial = jnp.sum(lax.all_to_all(partial, 'seq', 0, 0, tiled=True), axis=0)  19 us
    ppermute x14, starting transfers between devices, ring_permute(): return lax.ppermute(v, 'exp', perm)  17.9 us
    dynamic_slice x3, local copies, waits for them, and re-layouts, block(): lax.dynamic_slice(array, (0, 0, to * CAP, 0), (1, 2, CAP, D))  11.8 us
    ppermute x5, starting transfers between devices, body(): tally.append(tally[-1] + lax.ppermute(tally[-1], AXES, xor_perm(axis, d)))  10.5 us
    pallas_call x1, Pallas kernels, body(): pl.pallas_call(last_kernel, grid=(2, STEPS), out_shape=jax.ShapeDtypeStru...  8.26 us
    pallas_call x1, Pallas kernels, body(): pl.pallas_call(half_kernel, grid=(STEPS,), out_shape=(jax.ShapeDtypeStruc...  7 us
  transfers between devices with their start and end apart: 23, of which 9 were waited for; matrix products, arithmetic and copies ran while one was open for 7% of the time, Pallas kernels for 8%

profile of v11, /device:TPU:0, one launch (start us, length us, event | category | flops | bytes accessed | tf_op | source)
XLA Modules:
  0.0 166.2 jit_solution(5142246329411044486)
XLA Ops:
  0.7 0.0 copy-start
  0.7 3.5 %constant_dynamic-slice_fusion.12 = (bf16[1,2,24,8192]{3,2,1,0:T(8,128)(2,1)S(1)}, bf16[1,2,24,8192]{3,2,1,0:T(8,128)(2,1)}, bf16[1,2,24,8192]{3,2,1,0:T(8,128)(2,1)}, bf16[1,2,24,8192]{3,2,1,0:T(8,128)(2,1)}) fusion(bf16[1,2,192,8192]{3,2,1,0:T(8,128)(2,1)} %param.15, s32[]{:T(128)S(6)} %select_n.35, s32[]{:T(128)S(6)} %select_n.34, s32[]{:T(128)S(6)} %select_n.33, ...), kind=kLoop, calls=%fused_computation.18 | loop fusion | bytes 6291472 | tf_op jit(solution)/shard_map/dynamic_slice | solution.py:265
  4.1 0.1 copy.10.ids_ref
  4.3 0.1 copy.11.logits_ref
  4.4 0.4 shard_map.95
  4.7 1.7 %collective-permute-start = (f32[8,16]{1,0:T(8,128)S(1)}, f32[8,16]{1,0:T(8,128)S(1)}, u32[]{:S(2)}, u32[]{:S(2)}) collective-permute-start(f32[8,16]{1,0:T(8,128)S(1)} %get-tuple-element.44), channel_id=1, source_target_pairs={{0,32},{1,33},{2,34},{3,35},{4,36},{5,37},{6,38},{7,39},{8,40},{9,... | collective-permute-start | bytes 1544 | tf_op jit(solution)/shard_map/ppermute | solution.py:286
  6.5 1.5 collective-permute-start.5
  8.0 2.7 %collective-permute-start.7 = (bf16[48,8192]{1,0:T(8,128)(2,1)}, bf16[48,8192]{1,0:T(8,128)(2,1)}, u32[]{:S(2)}, u32[]{:S(2)}) collective-permute-start(bf16[48,8192]{1,0:T(8,128)(2,1)} %bitcast.37), channel_id=1, source_target_pairs={{0,4},{1,5},{2,6},{3,7},{4,0},{5,1},{6,2},{7,3},{8,12},{9,13},{10,... | collective-permute-start | bytes 2359304 | tf_op jit(solution)/shard_map/ppermute | solution.py:50
  10.7 1.4 collective-permute-start.6
  12.1 0.1 stack.43
  12.2 0.5 multiply_reduce_fusion
  12.7 0.1 iota_add_fusion
  12.8 0.0 collective-permute-done
  12.8 2.9 %collective-permute-start.1 = (f32[8,16]{1,0:T(8,128)S(1)}, f32[8,16]{1,0:T(8,128)S(1)}, u32[]{:S(2)}, u32[]{:S(2)}) collective-permute-start(f32[8,16]{1,0:T(8,128)S(1)} %add.222), channel_id=1, source_target_pairs={{0,64},{1,65},{2,66},{3,67},{4,68},{5,69},{6,70},{7,71},{8,72},{9,... | collective-permute-start | bytes 1544 | tf_op jit(solution)/shard_map/ppermute | solution.py:286
  15.7 2.2 %collective-permute-done.1 = f32[8,16]{1,0:T(8,128)S(1)} collective-permute-done((f32[8,16]{1,0:T(8,128)S(1)}, f32[8,16]{1,0:T(8,128)S(1)}, u32[]{:S(2)}, u32[]{:S(2)}) %collective-permute-start.1) | collective-permute-done | bytes 544 | tf_op jit(solution)/shard_map/ppermute | solution.py:286
  17.9 1.9 %collective-permute-start.2 = (f32[8,16]{1,0:T(8,128)S(1)}, f32[8,16]{1,0:T(8,128)S(1)}, u32[]{:S(2)}, u32[]{:S(2)}) collective-permute-start(f32[8,16]{1,0:T(8,128)S(1)} %add.223), channel_id=1, source_target_pairs={{0,8},{1,9},{2,10},{3,11},{4,12},{5,13},{6,14},{7,15},{8,0},{9,1},... | collective-permute-start | bytes 1544 | tf_op jit(solution)/shard_map/ppermute | solution.py:286
  19.9 0.1 copy.13.ids_ref
  20.0 0.1 add.221.slots_ref
  20.1 0.1 copy.15.inv_ref
  20.2 1.4 collective-permute-done.2
  21.6 3.9 %collective-permute-start.3 = (f32[8,16]{1,0:T(8,128)S(1)}, f32[8,16]{1,0:T(8,128)S(1)}, u32[]{:S(2)}, u32[]{:S(2)}) collective-permute-start(f32[8,16]{1,0:T(8,128)S(1)} %add.224), channel_id=1, source_target_pairs={{0,16},{1,17},{2,18},{3,19},{4,20},{5,21},{6,22},{7,23},{8,24},{9,... | collective-permute-start | bytes 1544 | tf_op jit(solution)/shard_map/ppermute | solution.py:286
  25.4 1.6 collective-permute-done.3
  27.0 0.0 collective-permute-start.4
  27.0 4.8 %constant_dynamic-slice_fusion.1 = (bf16[1,2,24,8192]{3,2,1,0:T(8,128)(2,1)}, bf16[1,2,24,8192]{3,2,1,0:T(8,128)(2,1)}, bf16[1,2,24,8192]{3,2,1,0:T(8,128)(2,1)}...) fusion(bf16[1,2,192,8192]{3,2,1,0:T(8,128)(2,1)} %param.14, ...), kind=kLoop, calls=%fused_computation.7 | loop fusion | bytes 12582928 | tf_op jit(solution)/shard_map/dynamic_slice | solution.py:265
  31.9 0.1 fusion.2
  32.0 0.4 pad_maximum_fusion.2
  32.4 0.2 collective-permute-start.9
  32.6 0.0 collective-permute-done.5.refs_1_
  32.6 1.6 collective-permute-start.8
  34.2 12.1 %collective-permute-done.7.refs_3_ = bf16[48,8192]{1,0:T(8,128)(2,1)} collective-permute-done((bf16[48,8192]{1,0:T(8,128)(2,1)}, bf16[48,8192]{1,0:T(8,128)(2,1)}, u32[]{:S(2)}, u32[]{:S(2)}) %collective-permute-start.7) | collective-permute-done | bytes 786464 | tf_op jit(solution)/shard_map/ppermute | solution.py:50
  46.3 0.0 collective-permute-start.10
  46.3 0.9 collective-permute-start.11
  47.3 3.5 %constant_dynamic-slice_fusion = (bf16[1,2,24,8192]{3,2,1,0:T(8,128)(2,1)}, bf16[1,2,24,8192]{3,2,1,0:T(8,128)(2,1)}, bf16[1,2,24,8192]{3,2,1,0:T(8,128)(2,1)}, bf16[1,2,24,8192]{3,2,1,0:T(8,128)(2,1)}) fusion(bf16[1,2,192,8192]{3,2,1,0:T(8,128)(2,1)} %param.14, s32[]{:T(128)S(6)} %select_n.35, s32[]{:T(128)S(6)} %select_n.34, s32[]{:T(128)S(6)} %select_n.32, ...), kind=kLoop, calls=%fused_computation.6 | loop fusion | bytes 6291472 | tf_op jit(solution)/shard_map/dynamic_slice | solution.py:265
  50.8 11.2 %collective-permute-done.9.refs_5_.refs_9_ = bf16[48,8320]{1,0:T(8,128)(2,1)S(1)} collective-permute-done((bf16[48,8320]{1,0:T(8,128)(2,1)S(1)}, bf16[48,8320]{1,0:T(8,128)(2,1)S(1)}, u32[]{:S(2)}, u32[]{:S(2)}) %collective-permute-start.9) | collective-permute-done | bytes 798752 | tf_op jit(solution)/shard_map/ppermute | solution.py:50
  62.0 1.6 collective-permute-start.15
  63.6 2.0 %collective-permute-start.14 = (bf16[48,8192]{1,0:T(8,128)(2,1)}, bf16[48,8192]{1,0:T(8,128)(2,1)}, u32[]{:S(2)}, u32[]{:S(2)}) collective-permute-start(bf16[48,8192]{1,0:T(8,128)(2,1)} %bitcast.18), channel_id=1, source_target_pairs={{0,6},{1,7},{2,0},{3,1},{4,2},{5,3},{6,4},{7,5},{8,14},{9,15},{10,... | collective-permute-start | bytes 2359304 | tf_op jit(solution)/shard_map/ppermute | solution.py:50
  65.6 0.9 collective-permute-start.13
  66.6 11.1 %collective-permute-done.10.refs_6_.refs_10_ = bf16[48,8320]{1,0:T(8,128)(2,1)S(1)} collective-permute-done((bf16[48,8320]{1,0:T(8,128)(2,1)S(1)}, bf16[48,8320]{1,0:T(8,128)(2,1)S(1)}, u32[]{:S(2)}, u32[]{:S(2)}) %collective-permute-start.10) | collective-permute-done | bytes 798752 | tf_op jit(solution)/shard_map/ppermute | solution.py:50
  77.7 6.8 %shard_map.96 = (f32[128,16]{1,0:T(8,128)S(1)}, f32[16,8,1024]{2,1,0:T(8,128)S(1)}) custom-call(f32[1,384]{1,0:T(1,128)S(1)} %add.221.slots_ref, f32[128,8]{1,0:T(8,128)S(1)} %get-tuple-element.67.pack_ref, f32[128,1]{1,0:T(8,128)S(1)} %copy.15.inv_ref, s32[128,2]{1,0:T(8,128)S(1)} %copy.13.ids_ref, f32[128,16]{1,0:T(8,128)S(1)} %get-tuple-element.43.probs_ref, ...), custom_call_target="tpu_custom_call" | custom-call | flops 20000000000 | bytes 60000000 | tf_op jit(solution)/shard_map/pallas_call | solution.py:310
  84.5 0.0 copy-start.5
  84.5 0.6 copy-done.5
  85.1 19.0 %all_to_all.5 = f32[16,8,1024]{2,1,0:T(8,128)S(1)} all-to-all(f32[16,8,1024]{2,1,0:T(8,128)S(1)} %get-tuple-element.59), channel_id=1, replica_groups=mesh['seq'=16,'exp'=8] {'seq'}, dimensions={0} | all-to-all | bytes 1048576 | tf_op jit(solution)/shard_map/all_to_all | solution.py:342
  104.1 1.4 collective-permute-start.12
  105.5 0.1 fusion.1
  105.6 0.8 collective-permute-done.12
  106.3 2.3 %collective-permute-start.16 = (f32[8,1024]{1,0:T(8,128)S(1)}, f32[8,1024]{1,0:T(8,128)S(1)}, u32[]{:S(2)}, u32[]{:S(2)}) collective-permute-start(f32[8,1024]{1,0:T(8,128)S(1)} %add.235), channel_id=1, source_target_pairs={{0,2},{1,3},{2,0},{3,1},{4,6},{5,7},{6,4},{7,5},{8,10},{9,11},{10,... | collective-permute-start | bytes 98312 | tf_op jit(solution)/shard_map/ppermute | solution.py:344
  108.7 3.2 %collective-permute-start.17 = (f32[8,1024]{1,0:T(8,128)S(1)}, f32[8,1024]{1,0:T(8,128)S(1)}, u32[]{:S(2)}, u32[]{:S(2)}) collective-permute-start(f32[8,1024]{1,0:T(8,128)S(1)} %add.235), channel_id=1, source_target_pairs={{0,4},{1,5},{2,6},{3,7},{4,0},{5,1},{6,2},{7,3},{8,12},{9,13},{10,... | collective-permute-start | bytes 98312 | tf_op jit(solution)/shard_map/ppermute | solution.py:344
  111.8 1.3 collective-permute-done.14.refs_2_
  113.2 2.1 %collective-permute-start.18 = (f32[8,1024]{1,0:T(8,128)S(1)}, f32[8,1024]{1,0:T(8,128)S(1)}, u32[]{:S(2)}, u32[]{:S(2)}) collective-permute-start(f32[8,1024]{1,0:T(8,128)S(1)} %add.235), channel_id=1, source_target_pairs={{0,6},{1,7},{2,4},{3,5},{4,2},{5,3},{6,0},{7,1},{8,14},{9,15},{10,... | collective-permute-start | bytes 98312 | tf_op jit(solution)/shard_map/ppermute | solution.py:346
  115.3 0.1 iota_add_fusion.1
  115.3 0.6 slice.9.slots_ref
  115.9 0.7 add.202.slots_ref
  116.6 1.7 %collective-permute-done.18 = f32[8,1024]{1,0:T(8,128)S(1)} collective-permute-done((f32[8,1024]{1,0:T(8,128)S(1)}, f32[8,1024]{1,0:T(8,128)S(1)}, u32[]{:S(2)}, u32[]{:S(2)}) %collective-permute-start.18) | collective-permute-done | bytes 32800 | tf_op jit(solution)/shard_map/ppermute | solution.py:346
  118.3 0.1 collective-permute-start.19
  118.4 2.7 %collective-permute-start.20 = (bf16[48,8192]{1,0:T(8,128)(2,1)}, bf16[48,8192]{1,0:T(8,128)(2,1)S(1)}, u32[]{:S(2)}, u32[]{:S(2)}) collective-permute-start(bf16[48,8192]{1,0:T(8,128)(2,1)} %bitcast.42), channel_id=1, source_target_pairs={{0,3},{1,2},{2,5},{3,4},{4,7},{5,6},{6,1},{7,0},{8,11},{9,10},{10,... | collective-permute-start | bytes 2359304 | tf_op jit(solution)/shard_map/ppermute | solution.py:50
  121.1 0.5 collective-permute-start.21
  121.6 1.7 %collective-permute-start.22 = (bf16[48,8192]{1,0:T(8,128)(2,1)}, bf16[48,8192]{1,0:T(8,128)(2,1)}, u32[]{:S(2)}, u32[]{:S(2)}) collective-permute-start(bf16[48,8192]{1,0:T(8,128)(2,1)} %bitcast.40), channel_id=1, source_target_pairs={{0,1},{1,0},{2,3},{3,2},{4,5},{5,4},{6,7},{7,6},{8,9},{9,8},{10,11... | collective-permute-start | bytes 2359304 | tf_op jit(solution)/shard_map/ppermute | solution.py:50
  123.3 7.0 %shard_map.97 = (f32[128,8192]{1,0:T(8,128)}, f32[128,128]{1,0:T(8,128)}) custom-call(f32[1,192]{1,0:T(1,128)} %slice.9.slots_ref, f32[128,8]{1,0:T(8,128)} %copy-done.2, f32[128,1]{1,0:T(8,128)} %copy-done.1, f32[128,16]{1,0:T(8,128)} %copy-done.5, f32[16,8192]{1,0:T(8,128)} %weight_ref.1, f32[1,8192]{1,0:T(1,128)} %bitcast.30, ...), custom_call_target="tpu_custom_call" | custom-call | flops 10000000000 | bytes 30000000 | tf_op jit(solution)/shard_map/pallas_call | solution.py:353
  130.3 25.3 %all-gather = f32[128,1024]{1,0:T(8,128)S(1)} all-gather(f32[8,1024]{1,0:T(8,128)S(1)} %add_add_fusion), channel_id=2, replica_groups=mesh['seq'=16,'exp'=8] {'seq'}, dimensions={0}, use_global_device_ids=true | all-gather | bytes 557056 | tf_op jit(solution)/shard_map/all_gather | solution.py:379
  155.6 0.9 reshape.242
  156.5 0.8 copy-done.6
  157.4 0.3 copy-done.7
  157.6 0.3 copy-done.8
  157.9 8.3 %shard_map.98 = bf16[128,8192]{1,0:T(8,128)(2,1)} custom-call(f32[1,192]{1,0:T(1,128)} %add.202.slots_ref, f32[128,8]{1,0:T(8,128)} %copy-done.2, f32[128,1]{1,0:T(8,128)} %copy-done.1, f32[128,128]{1,0:T(8,128)} %get-tuple-element.73.sums_ref, f32[1,8192]{1,0:T(1,128)} %bitcast.31, f32[128,8192]{1,0:T(8,128)} %get-tuple-element.74.part_ref, ...), custom_call_target="tpu_custom_call" | custom-call | tf_op jit(solution)/shard_map/pallas_call | solution.py:381
  (41 shorter events, 0.2 us)
Async XLA Ops:
  0.7 3.5 %copy-start.10 = (s32[128,2]{0,1:T(2,128)S(1)}, s32[128,2]{0,1:T(2,128)}, u32[]{:S(2)}) copy-start(s32[128,2]{0,1:T(2,128)} %param.13) | copy-start | bytes 3076
  0.7 3.6 %copy-start.9 = (f32[128,16]{0,1:T(8,128)S(1)}, f32[128,16]{0,1:T(8,128)}, u32[]{:S(2)}) copy-start(f32[128,16]{0,1:T(8,128)} %param.11) | copy-start | bytes 24580
  0.7 11.5 %copy-start = (bf16[128,8192]{1,0:T(8,128)(2,1)S(1)}, bf16[128,8192]{1,0:T(8,128)(2,1)}, u32[]{:S(2)}) copy-start(bf16[128,8192]{1,0:T(8,128)(2,1)} %hidden_ref.5) | copy-start | bytes 6291460
  4.7 72.9 %copy-start.2 = (f32[128,8]{1,0:T(8,128)}, f32[128,8]{1,0:T(8,128)S(1)}, u32[]{:S(2)}) copy-start(f32[128,8]{1,0:T(8,128)S(1)} %get-tuple-element.67.pack_ref) | copy-start | bytes 12292
  4.7 8.1 %collective-permute-start = (f32[8,16]{1,0:T(8,128)S(1)}, f32[8,16]{1,0:T(8,128)S(1)}, u32[]{:S(2)}, u32[]{:S(2)}) collective-permute-start(f32[8,16]{1,0:T(8,128)S(1)} %get-tuple-element.44), channel_id=1, source_target_pairs={{0,32},{1,33},{2,34},{3,35},{4,36},{5,37},{6,38},{7,39},{8,40},{9,... | collective-permute-start | bytes 1544 | tf_op jit(solution)/shard_map/ppermute | solution.py:286
  6.5 26.1 %collective-permute-start.5 = (bf16[48,8192]{1,0:T(8,128)(2,1)}, bf16[48,8192]{1,0:T(8,128)(2,1)}, u32[]{:S(2)}, u32[]{:S(2)}) collective-permute-start(bf16[48,8192]{1,0:T(8,128)(2,1)} %bitcast.38), channel_id=1, source_target_pairs={{0,2},{1,3},{2,4},{3,5},{4,6},{5,7},{6,0},{7,1},{8,10},{9,11},{10,... | collective-permute-start | bytes 2359304 | tf_op jit(solution)/shard_map/ppermute | solution.py:50
  8.0 38.4 %collective-permute-start.7 = (bf16[48,8192]{1,0:T(8,128)(2,1)}, bf16[48,8192]{1,0:T(8,128)(2,1)}, u32[]{:S(2)}, u32[]{:S(2)}) collective-permute-start(bf16[48,8192]{1,0:T(8,128)(2,1)} %bitcast.37), channel_id=1, source_target_pairs={{0,4},{1,5},{2,6},{3,7},{4,0},{5,1},{6,2},{7,3},{8,12},{9,13},{10,... | collective-permute-start | bytes 2359304 | tf_op jit(solution)/shard_map/ppermute | solution.py:50
  10.7 55.0 %collective-permute-start.6 = (bf16[48,8192]{1,0:T(8,128)(2,1)}, bf16[48,8192]{1,0:T(8,128)(2,1)}, u32[]{:S(2)}, u32[]{:S(2)}) collective-permute-start(bf16[48,8192]{1,0:T(8,128)(2,1)} %bitcast.36), channel_id=1, source_target_pairs={{0,6},{1,7},{2,0},{3,1},{4,2},{5,3},{6,4},{7,5},{8,14},{9,15},{10,... | collective-permute-start | bytes 2359304 | tf_op jit(solution)/shard_map/ppermute | solution.py:50
  12.8 5.2 %collective-permute-start.1 = (f32[8,16]{1,0:T(8,128)S(1)}, f32[8,16]{1,0:T(8,128)S(1)}, u32[]{:S(2)}, u32[]{:S(2)}) collective-permute-start(f32[8,16]{1,0:T(8,128)S(1)} %add.222), channel_id=1, source_target_pairs={{0,64},{1,65},{2,66},{3,67},{4,68},{5,69},{6,70},{7,71},{8,72},{9,... | collective-permute-start | bytes 1544 | tf_op jit(solution)/shard_map/ppermute | solution.py:286
  17.9 3.6 %collective-permute-start.2 = (f32[8,16]{1,0:T(8,128)S(1)}, f32[8,16]{1,0:T(8,128)S(1)}, u32[]{:S(2)}, u32[]{:S(2)}) collective-permute-start(f32[8,16]{1,0:T(8,128)S(1)} %add.223), channel_id=1, source_target_pairs={{0,8},{1,9},{2,10},{3,11},{4,12},{5,13},{6,14},{7,15},{8,0},{9,1},... | collective-permute-start | bytes 1544 | tf_op jit(solution)/shard_map/ppermute | solution.py:286
  20.2 57.5 %copy-start.1 = (f32[128,1]{1,0:T(8,128)}, f32[128,1]{1,0:T(8,128)S(1)}, u32[]{:S(2)}) copy-start(f32[128,1]{1,0:T(8,128)S(1)} %copy.15.inv_ref) | copy-start | bytes 1540
  21.6 5.5 %collective-permute-start.3 = (f32[8,16]{1,0:T(8,128)S(1)}, f32[8,16]{1,0:T(8,128)S(1)}, u32[]{:S(2)}, u32[]{:S(2)}) collective-permute-start(f32[8,16]{1,0:T(8,128)S(1)} %add.224), channel_id=1, source_target_pairs={{0,16},{1,17},{2,18},{3,19},{4,20},{5,21},{6,22},{7,23},{8,24},{9,... | collective-permute-start | bytes 1544 | tf_op jit(solution)/shard_map/ppermute | solution.py:286
  27.0 4.8 %collective-permute-start.4 = (f32[8,16]{1,0:T(8,128)S(1)}, f32[8,16]{1,0:T(8,128)S(1)}, u32[]{:S(2)}, u32[]{:S(2)}) collective-permute-start(f32[8,16]{1,0:T(8,128)S(1)} %add.225), channel_id=1, source_target_pairs={{0,1},{1,0},{2,3},{3,2},{4,5},{5,4},{6,7},{7,6},{8,9},{9,8},{10,11... | collective-permute-start | bytes 1544 | tf_op jit(solution)/shard_map/ppermute | solution.py:286
  32.4 29.6 %collective-permute-start.9 = (bf16[48,8320]{1,0:T(8,128)(2,1)S(1)}, bf16[48,8320]{1,0:T(8,128)(2,1)S(1)}, u32[]{:S(2)}, u32[]{:S(2)}) collective-permute-start(bf16[48,8320]{1,0:T(8,128)(2,1)S(1)} %get-tuple-element.96), channel_id=1, source_target_pairs={{0,7},{1,6},{2,1},{3,0},{4,3},{5,2},{6,5},{7,4},{8,15},{9,14},{10,... | collective-permute-start | bytes 2396168 | tf_op jit(solution)/shard_map/ppermute | solution.py:50
  32.6 31.1 %collective-permute-start.8 = (bf16[48,8320]{1,0:T(8,128)(2,1)S(1)}, bf16[48,8320]{1,0:T(8,128)(2,1)S(1)}, u32[]{:S(2)}, u32[]{:S(2)}) collective-permute-start(bf16[48,8320]{1,0:T(8,128)(2,1)S(1)} %get-tuple-element.53), channel_id=1, source_target_pairs={{0,3},{1,2},{2,5},{3,4},{4,7},{5,6},{6,1},{7,0},{8,11},{9,10},{10,... | collective-permute-start | bytes 2396168 | tf_op jit(solution)/shard_map/ppermute | solution.py:50
  46.3 31.3 %collective-permute-start.10 = (bf16[48,8320]{1,0:T(8,128)(2,1)S(1)}, bf16[48,8320]{1,0:T(8,128)(2,1)S(1)}, u32[]{:S(2)}, u32[]{:S(2)}) collective-permute-start(bf16[48,8320]{1,0:T(8,128)(2,1)S(1)} %get-tuple-element.57), channel_id=1, source_target_pairs={{0,5},{1,4},{2,7},{3,6},{4,1},{5,0},{6,3},{7,2},{8,13},{9,12},{10,... | collective-permute-start | bytes 2396168 | tf_op jit(solution)/shard_map/ppermute | solution.py:50
  46.3 31.3 %copy-start.3 = (f32[8192]{0:T(1024)S(1)}, f32[8192]{0:T(1024)}, u32[]{:S(2)}) copy-start(f32[8192]{0:T(1024)} %param.10) | copy-start | bytes 98308
  46.3 31.3 %copy-start.4 = (bf16[128,8192]{1,0:T(8,128)(2,1)S(1)}, bf16[128,8192]{1,0:T(8,128)(2,1)}, u32[]{:S(2)}) copy-start(bf16[128,8192]{1,0:T(8,128)(2,1)} %grad_ref.3) | copy-start | bytes 6291460
  46.3 20.2 %collective-permute-start.11 = (bf16[48,8192]{1,0:T(8,128)(2,1)S(1)}, bf16[48,8192]{1,0:T(8,128)(2,1)S(1)}, u32[]{:S(2)}, u32[]{:S(2)}) collective-permute-start(bf16[48,8192]{1,0:T(8,128)(2,1)S(1)} %bitcast.44), channel_id=1, source_target_pairs={{0,1},{1,0},{2,3},{3,2},{4,5},{5,4},{6,7},{7,6},{8,9},{9,8},{10,11... | collective-permute-start | bytes 2359304 | tf_op jit(solution)/shard_map/ppermute | solution.py:50
  62.0 49.8 %collective-permute-start.15 = (bf16[48,8192]{1,0:T(8,128)(2,1)}, bf16[48,8192]{1,0:T(8,128)(2,1)}, u32[]{:S(2)}, u32[]{:S(2)}) collective-permute-start(bf16[48,8192]{1,0:T(8,128)(2,1)} %bitcast.20), channel_id=1, source_target_pairs={{0,4},{1,5},{2,6},{3,7},{4,0},{5,1},{6,2},{7,3},{8,12},{9,13},{10,... | collective-permute-start | bytes 2359304 | tf_op jit(solution)/shard_map/ppermute | solution.py:50
  63.6 49.5 %collective-permute-start.14 = (bf16[48,8192]{1,0:T(8,128)(2,1)}, bf16[48,8192]{1,0:T(8,128)(2,1)}, u32[]{:S(2)}, u32[]{:S(2)}) collective-permute-start(bf16[48,8192]{1,0:T(8,128)(2,1)} %bitcast.18), channel_id=1, source_target_pairs={{0,6},{1,7},{2,0},{3,1},{4,2},{5,3},{6,4},{7,5},{8,14},{9,15},{10,... | collective-permute-start | bytes 2359304 | tf_op jit(solution)/shard_map/ppermute | solution.py:50
  65.6 47.5 %collective-permute-start.13 = (bf16[48,8192]{1,0:T(8,128)(2,1)}, bf16[48,8192]{1,0:T(8,128)(2,1)}, u32[]{:S(2)}, u32[]{:S(2)}) collective-permute-start(bf16[48,8192]{1,0:T(8,128)(2,1)} %bitcast.19), channel_id=1, source_target_pairs={{0,2},{1,3},{2,4},{3,5},{4,6},{5,7},{6,0},{7,1},{8,10},{9,11},{10,... | collective-permute-start | bytes 2359304 | tf_op jit(solution)/shard_map/ppermute | solution.py:50
  84.5 0.6 copy-start.5
  104.1 2.2 %collective-permute-start.12 = (f32[8,1024]{1,0:T(8,128)S(1)}, f32[8,1024]{1,0:T(8,128)S(1)}, u32[]{:S(2)}, u32[]{:S(2)}) collective-permute-start(f32[8,1024]{1,0:T(8,128)S(1)} %reduce_sum.19), channel_id=1, source_target_pairs={{0,1},{1,0},{2,3},{3,2},{4,5},{5,4},{6,7},{7,6},{8,9},{9,8},{10,11... | collective-permute-start | bytes 98312 | tf_op jit(solution)/shard_map/ppermute | solution.py:343
  106.3 10.2 %collective-permute-start.16 = (f32[8,1024]{1,0:T(8,128)S(1)}, f32[8,1024]{1,0:T(8,128)S(1)}, u32[]{:S(2)}, u32[]{:S(2)}) collective-permute-start(f32[8,1024]{1,0:T(8,128)S(1)} %add.235), channel_id=1, source_target_pairs={{0,2},{1,3},{2,0},{3,1},{4,6},{5,7},{6,4},{7,5},{8,10},{9,11},{10,... | collective-permute-start | bytes 98312 | tf_op jit(solution)/shard_map/ppermute | solution.py:344
  108.7 7.9 %collective-permute-start.17 = (f32[8,1024]{1,0:T(8,128)S(1)}, f32[8,1024]{1,0:T(8,128)S(1)}, u32[]{:S(2)}, u32[]{:S(2)}) collective-permute-start(f32[8,1024]{1,0:T(8,128)S(1)} %add.235), channel_id=1, source_target_pairs={{0,4},{1,5},{2,6},{3,7},{4,0},{5,1},{6,2},{7,3},{8,12},{9,13},{10,... | collective-permute-start | bytes 98312 | tf_op jit(solution)/shard_map/ppermute | solution.py:344
  113.2 5.1 %collective-permute-start.18 = (f32[8,1024]{1,0:T(8,128)S(1)}, f32[8,1024]{1,0:T(8,128)S(1)}, u32[]{:S(2)}, u32[]{:S(2)}) collective-permute-start(f32[8,1024]{1,0:T(8,128)S(1)} %add.235), channel_id=1, source_target_pairs={{0,6},{1,7},{2,4},{3,5},{4,2},{5,3},{6,0},{7,1},{8,14},{9,15},{10,... | collective-permute-start | bytes 98312 | tf_op jit(solution)/shard_map/ppermute | solution.py:346
  118.3 38.2 %collective-permute-start.19 = (bf16[48,8192]{1,0:T(8,128)(2,1)}, bf16[48,8192]{1,0:T(8,128)(2,1)S(1)}, u32[]{:S(2)}, u32[]{:S(2)}) collective-permute-start(bf16[48,8192]{1,0:T(8,128)(2,1)} %bitcast.43), channel_id=1, source_target_pairs={{0,5},{1,4},{2,7},{3,6},{4,1},{5,0},{6,3},{7,2},{8,13},{9,12},{10,... | collective-permute-start | bytes 2359304 | tf_op jit(solution)/shard_map/ppermute | solution.py:50
  118.4 38.1 %collective-permute-start.20 = (bf16[48,8192]{1,0:T(8,128)(2,1)}, bf16[48,8192]{1,0:T(8,128)(2,1)S(1)}, u32[]{:S(2)}, u32[]{:S(2)}) collective-permute-start(bf16[48,8192]{1,0:T(8,128)(2,1)} %bitcast.42), channel_id=1, source_target_pairs={{0,3},{1,2},{2,5},{3,4},{4,7},{5,6},{6,1},{7,0},{8,11},{9,10},{10,... | collective-permute-start | bytes 2359304 | tf_op jit(solution)/shard_map/ppermute | solution.py:50
  121.1 35.4 %collective-permute-start.21 = (bf16[48,8192]{1,0:T(8,128)(2,1)}, bf16[48,8192]{1,0:T(8,128)(2,1)S(1)}, u32[]{:S(2)}, u32[]{:S(2)}) collective-permute-start(bf16[48,8192]{1,0:T(8,128)(2,1)} %bitcast.41), channel_id=1, source_target_pairs={{0,7},{1,6},{2,1},{3,0},{4,3},{5,2},{6,5},{7,4},{8,15},{9,14},{10,... | collective-permute-start | bytes 2359304 | tf_op jit(solution)/shard_map/ppermute | solution.py:50
  121.6 34.9 %collective-permute-start.22 = (bf16[48,8192]{1,0:T(8,128)(2,1)}, bf16[48,8192]{1,0:T(8,128)(2,1)}, u32[]{:S(2)}, u32[]{:S(2)}) collective-permute-start(bf16[48,8192]{1,0:T(8,128)(2,1)} %bitcast.40), channel_id=1, source_target_pairs={{0,1},{1,0},{2,3},{3,2},{4,5},{5,4},{6,7},{7,6},{8,9},{9,8},{10,11... | collective-permute-start | bytes 2359304 | tf_op jit(solution)/shard_map/ppermute | solution.py:50
  156.5 0.9 copy-start.6
  156.5 1.1 copy-start.7
  156.5 1.4 copy-start.8

commit v12 on v11

--- a/solution.py
+++ b/solution.py
@@ -258,7 +258,8 @@
     gain = norm_gain.reshape(1, D)
     sources = [((at["x"] - s) & 3) * 2 + (at["c"] ^ m) for s, m in ROUTES]
     slots = slot_numbers(sources)
-    late_slots = slot_numbers([sources[i] for i in (6, 4, 5, 7)])
+    early_slots = slot_numbers([sources[i] for i in (0, 1, 2, 3, 7)])
+    late_slots = slot_numbers([sources[i] for i in (6, 4, 5)])
 
     def block(array, s, m):
         to = ((at["x"] + s) & 3) * 2 + (at["c"] ^ m)
@@ -299,11 +300,11 @@
 
     source, tally[2] = after(expert_grad, tally[2])
     grads = [block(source, 0, 0)]
-    for n, (s, m) in zip((3, 3, 4), ROUTES[1:4]):
+    for n, (s, m) in zip((3, 3, 4, 4), ROUTES[1:4] + ROUTES[7:]):
         b, outs[n] = after(block(source, s, m), outs[n])
         grads.append(ring_permute(b, s, m))
     source, tally[3] = after(expert_grad, tally[3])
-    late = [ROUTES[i] for i in (6, 4, 5, 7)]
+    late = [ROUTES[i] for i in (6, 4, 5)]
     rest = [block(source, s, m) for s, m in late]
 
     small = lambda *shape: pl.BlockSpec(shape, lambda p, c: (0,) * len(shape))
@@ -342,13 +343,13 @@
     partial = jnp.sum(lax.all_to_all(partial, "seq", 0, 0, tiled=True), axis=0)
     partial = partial + lax.ppermute(partial, AXES, xor_perm("c", 1))
     near = [lax.ppermute(partial, AXES, xor_perm("x", d)) for d in (1, 2)]
-    partial, *grads[1:4] = after(partial, *grads[1:4])
+    partial, *grads[1:5] = after(partial, *grads[1:5])
     partial = (partial + near[0]) + (near[1] + lax.ppermute(partial, AXES, xor_perm("x", 3)))
     partial, *rest = after(partial, *rest)
     grads += [ring_permute(b, s, m) for b, (s, m) in zip(rest, late)]
     once = lambda rows: pl.BlockSpec((rows, WIDE), lambda c: (0, c))
     fixed = lambda *shape: pl.BlockSpec(shape, lambda c: (0,) * len(shape))
-    half = 4 * ROWS
+    early, last = 5 * ROWS, 3 * ROWS
     begin, partial = after(pack, partial)
     part, sums = pl.pallas_call(
         half_kernel,
@@ -358,7 +359,7 @@
             jax.ShapeDtypeStruct((TOK, 128), F32),
         ),
         in_specs=[
-            fixed(1, half),
+            fixed(1, early),
             fixed(TOK, 8),
             fixed(TOK, 1),
             fixed(TOK, EXPERTS),
@@ -367,14 +368,14 @@
             once(TOK),
             once(TOK),
         ]
-        + [once(ROWS)] * 4,
+        + [once(ROWS)] * 5,
         out_specs=(once(TOK), fixed(TOK, 128)),
-        scratch_shapes=[pltpu.VMEM((TOK, 2 * half + 6 * EXPERTS), BF16)],
+        scratch_shapes=[pltpu.VMEM((TOK, 2 * early + 6 * EXPERTS), BF16)],
         compiler_params=params(60),
         cost_estimate=pl.CostEstimate(
             flops=10_000_000_000, bytes_accessed=30_000_000, transcendentals=0
         ),
-    )(slots[:, :half], begin, inv, logit, router_weight, gain, hidden, grad_out, *grads[:4])
+    )(early_slots, begin, inv, logit, router_weight, gain, hidden, grad_out, *grads[:5])
     partial, sums = after(partial, sums)
     router_grad = lax.all_gather(partial, "seq").reshape(EXPERTS, D)
 
@@ -383,7 +384,7 @@
         grid=(2, STEPS),
         out_shape=jax.ShapeDtypeStruct((TOK, D), BF16),
         in_specs=[
-            small(1, half),
+            small(1, last),
             small(TOK, 8),
             small(TOK, 1),
             small(TOK, 128),
@@ -391,17 +392,17 @@
             first(TOK),
             first(TOK),
         ]
-        + [first(ROWS)] * 4,
+        + [first(ROWS)] * 3,
         out_specs=second(TOK),
         scratch_shapes=[
             pltpu.VMEM((TOK, D), F32),
             pltpu.VMEM((TOK, D), BF16),
-            pltpu.VMEM((TOK, 2 * half), BF16),
+            pltpu.VMEM((TOK, 2 * last), BF16),
             pltpu.VMEM((TOK, 128), F32),
             pltpu.VMEM((TOK, 128), F32),
         ],
         compiler_params=params(60),
-    )(late_slots, pack, inv, sums, gain, part, hidden, *grads[4:])
+    )(late_slots, pack, inv, sums, gain, part, hidden, *grads[5:])
     return grad_hidden, router_grad
 
 

time: 166 us -> 166 us (level)
  blocking collectives: 44.3 us -> 25.3 us
  waiting for transfers between devices: 43.4 us -> 51.7 us
  starting transfers between devices: 37.4 us -> 45.6 us
    all_to_all x1 -> x0, blocking collectives: 19 us -> none  [body(): partial = jnp.sum(lax.all_to_all(partial, 'seq', 0, 0, tiled=True), axis=0)]
    all_to_all x0 -> x1, waiting for transfers between devices: none -> 11.3 us  [body(): partial = jnp.sum(lax.all_to_all(partial, 'seq', 0, 0, tiled=True), axis=0)]
    all_to_all x0 -> x1, starting transfers between devices: none -> 7.75 us  [body(): partial = jnp.sum(lax.all_to_all(partial, 'seq', 0, 0, tiled=True), axis=0)]
    ppermute x14, waiting for transfers between devices: 35.7 us -> 32.9 us  [ring_permute(): return lax.ppermute(v, 'exp', perm)]
  transfers between devices with their start and end apart: 23 -> 24, of which waited for: 9 -> 10; matrix products, arithmetic and copies ran while one was open for 7% -> 7% of each run, Pallas kernels for 8% -> 9%
where the time goes in v12:
time: 166 us; the launch traced here: 165 us
  waiting for transfers between devices  51.7 us (31%)
  starting transfers between devices  45.6 us (27%)
  blocking collectives  25.3 us (15%)
  Pallas kernels  23.4 us (14%)
  local copies, waits for them, and re-layouts  16.5 us (10%)
    ppermute x14, waiting for transfers between devices, ring_permute(): return lax.ppermute(v, 'exp', perm)  32.9 us
    all_gather x1, blocking collectives, body(): router_grad = lax.all_gather(partial, 'seq').reshape(EXPERTS, D)  25.3 us
    ppermute x14, starting transfers between devices, ring_permute(): return lax.ppermute(v, 'exp', perm)  18.3 us
    dynamic_slice x3, local copies, waits for them, and re-layouts, block(): lax.dynamic_slice(array, (0, 0, to * CAP, 0), (1, 2, CAP, D))  11.8 us
    all_to_all x1, waiting for transfers between devices, body(): partial = jnp.sum(lax.all_to_all(partial, 'seq', 0, 0, tiled=True), axis=0)  11.3 us
    ppermute x5, starting transfers between devices, body(): tally.append(tally[-1] + lax.ppermute(tally[-1], AXES, xor_perm(axis, d)))  10.5 us
    pallas_call x1, Pallas kernels, body(): pl.pallas_call(last_kernel, grid=(2, STEPS), out_shape=jax.ShapeDtypeStru...  7.99 us
    all_to_all x1, starting transfers between devices, body(): partial = jnp.sum(lax.all_to_all(partial, 'seq', 0, 0, tiled=True), axis=0)  7.75 us
  transfers between devices with their start and end apart: 24, of which 10 were waited for; matrix products, arithmetic and copies ran while one was open for 7% of the time, Pallas kernels for 9%

profile of v12, /device:TPU:0, one launch (start us, length us, event | category | flops | bytes accessed | tf_op | source)
XLA Modules:
  0.0 164.7 jit_solution(5086785091833315624)
XLA Ops:
  0.7 0.0 copy-start
  0.7 3.5 %constant_dynamic-slice_fusion.12 = (bf16[1,2,24,8192]{3,2,1,0:T(8,128)(2,1)S(1)}, bf16[1,2,24,8192]{3,2,1,0:T(8,128)(2,1)}, bf16[1,2,24,8192]{3,2,1,0:T(8,128)(2,1)}, bf16[1,2,24,8192]{3,2,1,0:T(8,128)(2,1)}) fusion(bf16[1,2,192,8192]{3,2,1,0:T(8,128)(2,1)} %param.15, s32[]{:T(128)S(6)} %select_n.35, s32[]{:T(128)S(6)} %select_n.34, s32[]{:T(128)S(6)} %select_n.33, ...), kind=kLoop, calls=%fused_computation.19 | loop fusion | bytes 6291472 | tf_op jit(solution)/shard_map/dynamic_slice | solution.py:266
  4.1 0.1 copy.10.ids_ref
  4.3 0.1 copy.11.logits_ref
  4.4 0.4 shard_map.95
  4.7 1.7 %collective-permute-start = (f32[8,16]{1,0:T(8,128)S(1)}, f32[8,16]{1,0:T(8,128)S(1)}, u32[]{:S(2)}, u32[]{:S(2)}) collective-permute-start(f32[8,16]{1,0:T(8,128)S(1)} %get-tuple-element.46), channel_id=1, source_target_pairs={{0,32},{1,33},{2,34},{3,35},{4,36},{5,37},{6,38},{7,39},{8,40},{9,... | collective-permute-start | bytes 1544 | tf_op jit(solution)/shard_map/ppermute | solution.py:287
  6.5 1.5 collective-permute-start.5
  8.0 2.7 %collective-permute-start.7 = (bf16[48,8192]{1,0:T(8,128)(2,1)}, bf16[48,8192]{1,0:T(8,128)(2,1)}, u32[]{:S(2)}, u32[]{:S(2)}) collective-permute-start(bf16[48,8192]{1,0:T(8,128)(2,1)} %bitcast.42), channel_id=1, source_target_pairs={{0,4},{1,5},{2,6},{3,7},{4,0},{5,1},{6,2},{7,3},{8,12},{9,13},{10,... | collective-permute-start | bytes 2359304 | tf_op jit(solution)/shard_map/ppermute | solution.py:50
  10.7 1.4 collective-permute-start.6
  12.1 0.1 stack.50
  12.2 0.5 multiply_reduce_fusion
  12.7 0.1 iota_add_fusion.1
  12.8 2.9 %collective-permute-start.1 = (f32[8,16]{1,0:T(8,128)S(1)}, f32[8,16]{1,0:T(8,128)S(1)}, u32[]{:S(2)}, u32[]{:S(2)}) collective-permute-start(f32[8,16]{1,0:T(8,128)S(1)} %add.245), channel_id=1, source_target_pairs={{0,64},{1,65},{2,66},{3,67},{4,68},{5,69},{6,70},{7,71},{8,72},{9,... | collective-permute-start | bytes 1544 | tf_op jit(solution)/shard_map/ppermute | solution.py:287
  15.7 2.2 %collective-permute-done.1 = f32[8,16]{1,0:T(8,128)S(1)} collective-permute-done((f32[8,16]{1,0:T(8,128)S(1)}, f32[8,16]{1,0:T(8,128)S(1)}, u32[]{:S(2)}, u32[]{:S(2)}) %collective-permute-start.1) | collective-permute-done | bytes 544 | tf_op jit(solution)/shard_map/ppermute | solution.py:287
  17.9 1.9 %collective-permute-start.2 = (f32[8,16]{1,0:T(8,128)S(1)}, f32[8,16]{1,0:T(8,128)S(1)}, u32[]{:S(2)}, u32[]{:S(2)}) collective-permute-start(f32[8,16]{1,0:T(8,128)S(1)} %add.246), channel_id=1, source_target_pairs={{0,8},{1,9},{2,10},{3,11},{4,12},{5,13},{6,14},{7,15},{8,0},{9,1},... | collective-permute-start | bytes 1544 | tf_op jit(solution)/shard_map/ppermute | solution.py:287
  19.9 0.1 copy.13.ids_ref
  20.0 0.1 add.244.slots_ref
  20.1 0.1 copy.15.inv_ref
  20.2 1.4 collective-permute-done.2
  21.6 3.9 %collective-permute-start.3 = (f32[8,16]{1,0:T(8,128)S(1)}, f32[8,16]{1,0:T(8,128)S(1)}, u32[]{:S(2)}, u32[]{:S(2)}) collective-permute-start(f32[8,16]{1,0:T(8,128)S(1)} %add.247), channel_id=1, source_target_pairs={{0,16},{1,17},{2,18},{3,19},{4,20},{5,21},{6,22},{7,23},{8,24},{9,... | collective-permute-start | bytes 1544 | tf_op jit(solution)/shard_map/ppermute | solution.py:287
  25.4 1.6 collective-permute-done.3
  27.0 0.0 collective-permute-start.4
  27.0 4.2 %constant_dynamic-slice_fusion.1 = (bf16[1,2,24,8192]{3,2,1,0:T(8,128)(2,1)}, bf16[1,2,24,8192]{3,2,1,0:T(8,128)(2,1)}, bf16[1,2,24,8192]{3,2,1,0:T(8,128)(2,1)}...) fusion(bf16[1,2,192,8192]{3,2,1,0:T(8,128)(2,1)} %param.14, ...), kind=kLoop, calls=%fused_computation.8 | loop fusion | bytes 11010064 | tf_op jit(solution)/shard_map/dynamic_slice | solution.py:266
  31.3 0.0 collective-permute-done.4
  31.3 0.1 fusion.2
  31.4 0.4 pad_maximum_fusion.2
  31.8 0.2 collective-permute-start.9
  32.0 1.6 collective-permute-start.8
  33.6 12.7 %collective-permute-done.7.refs_3_ = bf16[48,8192]{1,0:T(8,128)(2,1)} collective-permute-done((bf16[48,8192]{1,0:T(8,128)(2,1)}, bf16[48,8192]{1,0:T(8,128)(2,1)}, u32[]{:S(2)}, u32[]{:S(2)}) %collective-permute-start.7) | collective-permute-done | bytes 786464 | tf_op jit(solution)/shard_map/ppermute | solution.py:50
  46.3 0.9 collective-permute-start.11
  47.3 4.1 %constant_dynamic-slice_fusion = (bf16[1,2,24,8192]{3,2,1,0:T(8,128)(2,1)}, bf16[1,2,24,8192]{3,2,1,0:T(8,128)(2,1)}, bf16[1,2,24,8192]{3,2,1,0:T(8,128)(2,1)}, ...) fusion(bf16[1,2,192,8192]{3,2,1,0:T(8,128)(2,1)} %param.14, s32[]{:T(128)S(6)} %select_n.35, s32[]{:T(128)S(6)} %select_n.34, ...), kind=kLoop, calls=%fused_computation.7 | loop fusion | bytes 7864340 | tf_op jit(solution)/shard_map/dynamic_slice | solution.py:266
  51.3 10.7 %collective-permute-done.9.refs_5_.refs_9_ = bf16[48,8320]{1,0:T(8,128)(2,1)S(1)} collective-permute-done((bf16[48,8320]{1,0:T(8,128)(2,1)S(1)}, bf16[48,8320]{1,0:T(8,128)(2,1)S(1)}, u32[]{:S(2)}, u32[]{:S(2)}) %collective-permute-start.9) | collective-permute-done | bytes 798752 | tf_op jit(solution)/shard_map/ppermute | solution.py:50
  62.0 1.4 collective-permute-start.16
  63.4 3.0 %collective-permute-start.15 = (bf16[48,8192]{1,0:T(8,128)(2,1)}, bf16[48,8192]{1,0:T(8,128)(2,1)}, u32[]{:S(2)}, u32[]{:S(2)}) collective-permute-start(bf16[48,8192]{1,0:T(8,128)(2,1)} %bitcast.21), channel_id=1, source_target_pairs={{0,4},{1,5},{2,6},{3,7},{4,0},{5,1},{6,2},{7,3},{8,12},{9,13},{10,... | collective-permute-start | bytes 2359304 | tf_op jit(solution)/shard_map/ppermute | solution.py:50
  66.3 0.6 collective-permute-start.14
  67.0 1.4 collective-permute-start.13
  68.4 9.3 %collective-permute-done.10.refs_6_.refs_10_ = bf16[48,8320]{1,0:T(8,128)(2,1)S(1)} collective-permute-done((bf16[48,8320]{1,0:T(8,128)(2,1)S(1)}, bf16[48,8320]{1,0:T(8,128)(2,1)S(1)}, u32[]{:S(2)}, u32[]{:S(2)}) %collective-permute-start.10) | collective-permute-done | bytes 798752 | tf_op jit(solution)/shard_map/ppermute | solution.py:50
  77.6 7.6 %shard_map.96 = (f32[128,16]{1,0:T(8,128)S(1)}, f32[16,8,1024]{2,1,0:T(8,128)}) custom-call(f32[1,384]{1,0:T(1,128)S(1)} %add.244.slots_ref, f32[128,8]{1,0:T(8,128)S(1)} %get-tuple-element.71.pack_ref, f32[128,1]{1,0:T(8,128)S(1)} %copy.15.inv_ref, s32[128,2]{1,0:T(8,128)S(1)} %copy.13.ids_ref, f32[128,16]{1,0:T(8,128)S(1)} %get-tuple-element.45.probs_ref, ...), custom_call_target="tpu_custom_call" | custom-call | flops 20000000000 | bytes 60000000 | tf_op jit(solution)/shard_map/pallas_call | solution.py:311
  85.2 0.6 copy-done.5
  85.9 7.7 %all-to-all-start = ((f32[16,8,1024]{2,1,0:T(8,128)}), f32[16,8,1024]{2,1,0:T(8,128)S(1)}, u32[]{:S(2)}, u32[]{:S(2)}) async-start(f32[16,8,1024]{2,1,0:T(8,128)} %get-tuple-element.62), calls=%async_computation | async-start | bytes 1048576 | tf_op jit(solution)/shard_map/all_to_all | solution.py:343
  93.6 0.1 stack.51
  93.7 0.1 iota_add_fusion
  93.8 11.3 %all-to-all-done = f32[16,8,1024]{2,1,0:T(8,128)S(1)} async-done(((f32[16,8,1024]{2,1,0:T(8,128)}), f32[16,8,1024]{2,1,0:T(8,128)S(1)}, u32[]{:S(2)}, u32[]{:S(2)}) %all-to-all-start) | async-done | bytes 524320 | tf_op jit(solution)/shard_map/all_to_all | solution.py:343
  105.1 1.4 collective-permute-start.12
  106.5 0.1 fusion.1
  106.5 0.8 collective-permute-done.12
  107.3 2.3 %collective-permute-start.17 = (f32[8,1024]{1,0:T(8,128)S(1)}, f32[8,1024]{1,0:T(8,128)S(1)}, u32[]{:S(2)}, u32[]{:S(2)}) collective-permute-start(f32[8,1024]{1,0:T(8,128)S(1)} %add.258), channel_id=1, source_target_pairs={{0,2},{1,3},{2,0},{3,1},{4,6},{5,7},{6,4},{7,5},{8,10},{9,11},{10,... | collective-permute-start | bytes 98312 | tf_op jit(solution)/shard_map/ppermute | solution.py:345
  109.6 3.2 %collective-permute-start.18 = (f32[8,1024]{1,0:T(8,128)S(1)}, f32[8,1024]{1,0:T(8,128)S(1)}, u32[]{:S(2)}, u32[]{:S(2)}) collective-permute-start(f32[8,1024]{1,0:T(8,128)S(1)} %add.258), channel_id=1, source_target_pairs={{0,4},{1,5},{2,6},{3,7},{4,0},{5,1},{6,2},{7,3},{8,12},{9,13},{10,... | collective-permute-start | bytes 98312 | tf_op jit(solution)/shard_map/ppermute | solution.py:345
  112.8 2.3 %collective-permute-start.19 = (f32[8,1024]{1,0:T(8,128)S(1)}, f32[8,1024]{1,0:T(8,128)S(1)}, u32[]{:S(2)}, u32[]{:S(2)}) collective-permute-start(f32[8,1024]{1,0:T(8,128)S(1)} %add.258), channel_id=1, source_target_pairs={{0,6},{1,7},{2,4},{3,5},{4,2},{5,3},{6,0},{7,1},{8,14},{9,15},{10,... | collective-permute-start | bytes 98312 | tf_op jit(solution)/shard_map/ppermute | solution.py:347
  115.1 0.1 iota_add_fusion.2
  115.2 0.6 add.265.slots_ref
  115.8 0.7 add.224.slots_ref
  116.5 1.6 collective-permute-done.19
  118.0 0.1 collective-permute-start.20
  118.1 2.7 %collective-permute-start.21 = (bf16[48,8192]{1,0:T(8,128)(2,1)}, bf16[48,8192]{1,0:T(8,128)(2,1)S(1)}, u32[]{:S(2)}, u32[]{:S(2)}) collective-permute-start(bf16[48,8192]{1,0:T(8,128)(2,1)} %bitcast.37), channel_id=1, source_target_pairs={{0,3},{1,2},{2,5},{3,4},{4,7},{5,6},{6,1},{7,0},{8,11},{9,10},{10,... | collective-permute-start | bytes 2359304 | tf_op jit(solution)/shard_map/ppermute | solution.py:50
  120.9 0.7 collective-permute-start.22
  121.6 7.5 %shard_map.97 = (f32[128,8192]{1,0:T(8,128)}, f32[128,128]{1,0:T(8,128)}) custom-call(f32[1,240]{1,0:T(1,128)} %add.265.slots_ref, f32[128,8]{1,0:T(8,128)} %copy-done.2, f32[128,1]{1,0:T(8,128)} %copy-done.1, f32[128,16]{1,0:T(8,128)} %copy-done.5, f32[16,8192]{1,0:T(8,128)} %weight_ref.1, f32[1,8192]{1,0:T(1,128)} %bitcast.30, ...), custom_call_target="tpu_custom_call" | custom-call | flops 10000000000 | bytes 30000000 | tf_op jit(solution)/shard_map/pallas_call | solution.py:354
  129.1 25.3 %all-gather = f32[128,1024]{1,0:T(8,128)S(1)} all-gather(f32[8,1024]{1,0:T(8,128)S(1)} %add_add_fusion), channel_id=2, replica_groups=mesh['seq'=16,'exp'=8] {'seq'}, dimensions={0}, use_global_device_ids=true | all-gather | bytes 557056 | tf_op jit(solution)/shard_map/all_gather | solution.py:380
  154.4 0.9 reshape.299
  155.3 0.3 collective-permute-done.21.refs_1_
  155.6 0.6 copy-done.6
  156.1 0.3 copy-done.7
  156.4 0.3 copy-done.8
  156.7 8.0 %shard_map.98 = bf16[128,8192]{1,0:T(8,128)(2,1)} custom-call(f32[1,144]{1,0:T(1,128)} %add.224.slots_ref, f32[128,8]{1,0:T(8,128)} %copy-done.2, f32[128,1]{1,0:T(8,128)} %copy-done.1, f32[128,128]{1,0:T(8,128)} %get-tuple-element.78.sums_ref, f32[1,8192]{1,0:T(1,128)} %bitcast.31, f32[128,8192]{1,0:T(8,128)} %get-tuple-element.79.part_ref, ...), custom_call_target="tpu_custom_call" | custom-call | tf_op jit(solution)/shard_map/pallas_call | solution.py:382
  (45 shorter events, 0.2 us)
Async XLA Ops:
  0.7 3.5 %copy-start.10 = (s32[128,2]{0,1:T(2,128)S(1)}, s32[128,2]{0,1:T(2,128)}, u32[]{:S(2)}) copy-start(s32[128,2]{0,1:T(2,128)} %param.13) | copy-start | bytes 3076
  0.7 3.6 %copy-start.9 = (f32[128,16]{0,1:T(8,128)S(1)}, f32[128,16]{0,1:T(8,128)}, u32[]{:S(2)}) copy-start(f32[128,16]{0,1:T(8,128)} %param.11) | copy-start | bytes 24580
  0.7 11.5 %copy-start = (bf16[128,8192]{1,0:T(8,128)(2,1)S(1)}, bf16[128,8192]{1,0:T(8,128)(2,1)}, u32[]{:S(2)}) copy-start(bf16[128,8192]{1,0:T(8,128)(2,1)} %hidden_ref.5) | copy-start | bytes 6291460
  4.7 72.9 %copy-start.2 = (f32[128,8]{1,0:T(8,128)}, f32[128,8]{1,0:T(8,128)S(1)}, u32[]{:S(2)}) copy-start(f32[128,8]{1,0:T(8,128)S(1)} %get-tuple-element.71.pack_ref) | copy-start | bytes 12292
  4.7 8.1 %collective-permute-start = (f32[8,16]{1,0:T(8,128)S(1)}, f32[8,16]{1,0:T(8,128)S(1)}, u32[]{:S(2)}, u32[]{:S(2)}) collective-permute-start(f32[8,16]{1,0:T(8,128)S(1)} %get-tuple-element.46), channel_id=1, source_target_pairs={{0,32},{1,33},{2,34},{3,35},{4,36},{5,37},{6,38},{7,39},{8,40},{9,... | collective-permute-start | bytes 1544 | tf_op jit(solution)/shard_map/ppermute | solution.py:287
  6.5 25.5 %collective-permute-start.5 = (bf16[48,8192]{1,0:T(8,128)(2,1)}, bf16[48,8192]{1,0:T(8,128)(2,1)}, u32[]{:S(2)}, u32[]{:S(2)}) collective-permute-start(bf16[48,8192]{1,0:T(8,128)(2,1)} %bitcast.43), channel_id=1, source_target_pairs={{0,2},{1,3},{2,4},{3,5},{4,6},{5,7},{6,0},{7,1},{8,10},{9,11},{10,... | collective-permute-start | bytes 2359304 | tf_op jit(solution)/shard_map/ppermute | solution.py:50
  8.0 38.4 %collective-permute-start.7 = (bf16[48,8192]{1,0:T(8,128)(2,1)}, bf16[48,8192]{1,0:T(8,128)(2,1)}, u32[]{:S(2)}, u32[]{:S(2)}) collective-permute-start(bf16[48,8192]{1,0:T(8,128)(2,1)} %bitcast.42), channel_id=1, source_target_pairs={{0,4},{1,5},{2,6},{3,7},{4,0},{5,1},{6,2},{7,3},{8,12},{9,13},{10,... | collective-permute-start | bytes 2359304 | tf_op jit(solution)/shard_map/ppermute | solution.py:50
  10.7 55.7 %collective-permute-start.6 = (bf16[48,8192]{1,0:T(8,128)(2,1)}, bf16[48,8192]{1,0:T(8,128)(2,1)}, u32[]{:S(2)}, u32[]{:S(2)}) collective-permute-start(bf16[48,8192]{1,0:T(8,128)(2,1)} %bitcast.41), channel_id=1, source_target_pairs={{0,6},{1,7},{2,0},{3,1},{4,2},{5,3},{6,4},{7,5},{8,14},{9,15},{10,... | collective-permute-start | bytes 2359304 | tf_op jit(solution)/shard_map/ppermute | solution.py:50
  12.8 5.2 %collective-permute-start.1 = (f32[8,16]{1,0:T(8,128)S(1)}, f32[8,16]{1,0:T(8,128)S(1)}, u32[]{:S(2)}, u32[]{:S(2)}) collective-permute-start(f32[8,16]{1,0:T(8,128)S(1)} %add.245), channel_id=1, source_target_pairs={{0,64},{1,65},{2,66},{3,67},{4,68},{5,69},{6,70},{7,71},{8,72},{9,... | collective-permute-start | bytes 1544 | tf_op jit(solution)/shard_map/ppermute | solution.py:287
  17.9 3.6 %collective-permute-start.2 = (f32[8,16]{1,0:T(8,128)S(1)}, f32[8,16]{1,0:T(8,128)S(1)}, u32[]{:S(2)}, u32[]{:S(2)}) collective-permute-start(f32[8,16]{1,0:T(8,128)S(1)} %add.246), channel_id=1, source_target_pairs={{0,8},{1,9},{2,10},{3,11},{4,12},{5,13},{6,14},{7,15},{8,0},{9,1},... | collective-permute-start | bytes 1544 | tf_op jit(solution)/shard_map/ppermute | solution.py:287
  20.2 57.5 %copy-start.1 = (f32[128,1]{1,0:T(8,128)}, f32[128,1]{1,0:T(8,128)S(1)}, u32[]{:S(2)}) copy-start(f32[128,1]{1,0:T(8,128)S(1)} %copy.15.inv_ref) | copy-start | bytes 1540
  21.6 5.5 %collective-permute-start.3 = (f32[8,16]{1,0:T(8,128)S(1)}, f32[8,16]{1,0:T(8,128)S(1)}, u32[]{:S(2)}, u32[]{:S(2)}) collective-permute-start(f32[8,16]{1,0:T(8,128)S(1)} %add.247), channel_id=1, source_target_pairs={{0,16},{1,17},{2,18},{3,19},{4,20},{5,21},{6,22},{7,23},{8,24},{9,... | collective-permute-start | bytes 1544 | tf_op jit(solution)/shard_map/ppermute | solution.py:287
  27.0 4.3 %collective-permute-start.4 = (f32[8,16]{1,0:T(8,128)S(1)}, f32[8,16]{1,0:T(8,128)S(1)}, u32[]{:S(2)}, u32[]{:S(2)}) collective-permute-start(f32[8,16]{1,0:T(8,128)S(1)} %add.248), channel_id=1, source_target_pairs={{0,1},{1,0},{2,3},{3,2},{4,5},{5,4},{6,7},{7,6},{8,9},{9,8},{10,11... | collective-permute-start | bytes 1544 | tf_op jit(solution)/shard_map/ppermute | solution.py:287
  31.8 30.2 %collective-permute-start.9 = (bf16[48,8320]{1,0:T(8,128)(2,1)S(1)}, bf16[48,8320]{1,0:T(8,128)(2,1)S(1)}, u32[]{:S(2)}, u32[]{:S(2)}) collective-permute-start(bf16[48,8320]{1,0:T(8,128)(2,1)S(1)} %get-tuple-element.100), channel_id=1, source_target_pairs={{0,7},{1,6},{2,1},{3,0},{4,3},{5,2},{6,5},{7,4},{8,15},{9,14},{10,... | collective-permute-start | bytes 2396168 | tf_op jit(solution)/shard_map/ppermute | solution.py:50
  32.0 31.4 %collective-permute-start.8 = (bf16[48,8320]{1,0:T(8,128)(2,1)S(1)}, bf16[48,8320]{1,0:T(8,128)(2,1)S(1)}, u32[]{:S(2)}, u32[]{:S(2)}) collective-permute-start(bf16[48,8320]{1,0:T(8,128)(2,1)S(1)} %get-tuple-element.55), channel_id=1, source_target_pairs={{0,3},{1,2},{2,5},{3,4},{4,7},{5,6},{6,1},{7,0},{8,11},{9,10},{10,... | collective-permute-start | bytes 2396168 | tf_op jit(solution)/shard_map/ppermute | solution.py:50
  46.3 31.3 %collective-permute-start.10 = (bf16[48,8320]{1,0:T(8,128)(2,1)S(1)}, bf16[48,8320]{1,0:T(8,128)(2,1)S(1)}, u32[]{:S(2)}, u32[]{:S(2)}) collective-permute-start(bf16[48,8320]{1,0:T(8,128)(2,1)S(1)} %get-tuple-element.60), channel_id=1, source_target_pairs={{0,5},{1,4},{2,7},{3,6},{4,1},{5,0},{6,3},{7,2},{8,13},{9,12},{10,... | collective-permute-start | bytes 2396168 | tf_op jit(solution)/shard_map/ppermute | solution.py:50
  46.3 31.3 %copy-start.3 = (f32[8192]{0:T(1024)S(1)}, f32[8192]{0:T(1024)}, u32[]{:S(2)}) copy-start(f32[8192]{0:T(1024)} %param.10) | copy-start | bytes 98308
  46.3 31.3 %copy-start.4 = (bf16[128,8192]{1,0:T(8,128)(2,1)S(1)}, bf16[128,8192]{1,0:T(8,128)(2,1)}, u32[]{:S(2)}) copy-start(bf16[128,8192]{1,0:T(8,128)(2,1)} %grad_ref.3) | copy-start | bytes 6291460
  46.3 20.6 %collective-permute-start.11 = (bf16[48,8192]{1,0:T(8,128)(2,1)S(1)}, bf16[48,8192]{1,0:T(8,128)(2,1)S(1)}, u32[]{:S(2)}, u32[]{:S(2)}) collective-permute-start(bf16[48,8192]{1,0:T(8,128)(2,1)S(1)} %bitcast.40), channel_id=1, source_target_pairs={{0,1},{1,0},{2,3},{3,2},{4,5},{5,4},{6,7},{7,6},{8,9},{9,8},{10,11... | collective-permute-start | bytes 2359304 | tf_op jit(solution)/shard_map/ppermute | solution.py:50
  62.0 47.6 %collective-permute-start.16 = (bf16[48,8192]{1,0:T(8,128)(2,1)}, bf16[48,8192]{1,0:T(8,128)(2,1)}, u32[]{:S(2)}, u32[]{:S(2)}) collective-permute-start(bf16[48,8192]{1,0:T(8,128)(2,1)} %bitcast.20), channel_id=1, source_target_pairs={{0,1},{1,0},{2,3},{3,2},{4,5},{5,4},{6,7},{7,6},{8,9},{9,8},{10,11... | collective-permute-start | bytes 2359304 | tf_op jit(solution)/shard_map/ppermute | solution.py:50
  63.4 49.5 %collective-permute-start.15 = (bf16[48,8192]{1,0:T(8,128)(2,1)}, bf16[48,8192]{1,0:T(8,128)(2,1)}, u32[]{:S(2)}, u32[]{:S(2)}) collective-permute-start(bf16[48,8192]{1,0:T(8,128)(2,1)} %bitcast.21), channel_id=1, source_target_pairs={{0,4},{1,5},{2,6},{3,7},{4,0},{5,1},{6,2},{7,3},{8,12},{9,13},{10,... | collective-permute-start | bytes 2359304 | tf_op jit(solution)/shard_map/ppermute | solution.py:50
  66.3 46.5 %collective-permute-start.14 = (bf16[48,8192]{1,0:T(8,128)(2,1)}, bf16[48,8192]{1,0:T(8,128)(2,1)}, u32[]{:S(2)}, u32[]{:S(2)}) collective-permute-start(bf16[48,8192]{1,0:T(8,128)(2,1)} %bitcast.18), channel_id=1, source_target_pairs={{0,6},{1,7},{2,0},{3,1},{4,2},{5,3},{6,4},{7,5},{8,14},{9,15},{10,... | collective-permute-start | bytes 2359304 | tf_op jit(solution)/shard_map/ppermute | solution.py:50
  67.0 45.8 %collective-permute-start.13 = (bf16[48,8192]{1,0:T(8,128)(2,1)}, bf16[48,8192]{1,0:T(8,128)(2,1)}, u32[]{:S(2)}, u32[]{:S(2)}) collective-permute-start(bf16[48,8192]{1,0:T(8,128)(2,1)} %bitcast.19), channel_id=1, source_target_pairs={{0,2},{1,3},{2,4},{3,5},{4,6},{5,7},{6,0},{7,1},{8,10},{9,11},{10,... | collective-permute-start | bytes 2359304 | tf_op jit(solution)/shard_map/ppermute | solution.py:50
  85.2 0.6 copy-start.5
  85.9 19.2 %all-to-all-start = ((f32[16,8,1024]{2,1,0:T(8,128)}), f32[16,8,1024]{2,1,0:T(8,128)S(1)}, u32[]{:S(2)}, u32[]{:S(2)}) async-start(f32[16,8,1024]{2,1,0:T(8,128)} %get-tuple-element.62), calls=%async_computation | async-start | bytes 1048576 | tf_op jit(solution)/shard_map/all_to_all | solution.py:343
  105.1 2.2 %collective-permute-start.12 = (f32[8,1024]{1,0:T(8,128)S(1)}, f32[8,1024]{1,0:T(8,128)S(1)}, u32[]{:S(2)}, u32[]{:S(2)}) collective-permute-start(f32[8,1024]{1,0:T(8,128)S(1)} %reduce_sum.19), channel_id=1, source_target_pairs={{0,1},{1,0},{2,3},{3,2},{4,5},{5,4},{6,7},{7,6},{8,9},{9,8},{10,11... | collective-permute-start | bytes 98312 | tf_op jit(solution)/shard_map/ppermute | solution.py:344
  107.3 9.1 %collective-permute-start.17 = (f32[8,1024]{1,0:T(8,128)S(1)}, f32[8,1024]{1,0:T(8,128)S(1)}, u32[]{:S(2)}, u32[]{:S(2)}) collective-permute-start(f32[8,1024]{1,0:T(8,128)S(1)} %add.258), channel_id=1, source_target_pairs={{0,2},{1,3},{2,0},{3,1},{4,6},{5,7},{6,4},{7,5},{8,10},{9,11},{10,... | collective-permute-start | bytes 98312 | tf_op jit(solution)/shard_map/ppermute | solution.py:345
  109.6 6.8 %collective-permute-start.18 = (f32[8,1024]{1,0:T(8,128)S(1)}, f32[8,1024]{1,0:T(8,128)S(1)}, u32[]{:S(2)}, u32[]{:S(2)}) collective-permute-start(f32[8,1024]{1,0:T(8,128)S(1)} %add.258), channel_id=1, source_target_pairs={{0,4},{1,5},{2,6},{3,7},{4,0},{5,1},{6,2},{7,3},{8,12},{9,13},{10,... | collective-permute-start | bytes 98312 | tf_op jit(solution)/shard_map/ppermute | solution.py:345
  112.8 5.2 %collective-permute-start.19 = (f32[8,1024]{1,0:T(8,128)S(1)}, f32[8,1024]{1,0:T(8,128)S(1)}, u32[]{:S(2)}, u32[]{:S(2)}) collective-permute-start(f32[8,1024]{1,0:T(8,128)S(1)} %add.258), channel_id=1, source_target_pairs={{0,6},{1,7},{2,4},{3,5},{4,2},{5,3},{6,0},{7,1},{8,14},{9,15},{10,... | collective-permute-start | bytes 98312 | tf_op jit(solution)/shard_map/ppermute | solution.py:347
  118.0 37.2 %collective-permute-start.20 = (bf16[48,8192]{1,0:T(8,128)(2,1)}, bf16[48,8192]{1,0:T(8,128)(2,1)S(1)}, u32[]{:S(2)}, u32[]{:S(2)}) collective-permute-start(bf16[48,8192]{1,0:T(8,128)(2,1)} %bitcast.38), channel_id=1, source_target_pairs={{0,5},{1,4},{2,7},{3,6},{4,1},{5,0},{6,3},{7,2},{8,13},{9,12},{10,... | collective-permute-start | bytes 2359304 | tf_op jit(solution)/shard_map/ppermute | solution.py:50
  118.1 37.4 %collective-permute-start.21 = (bf16[48,8192]{1,0:T(8,128)(2,1)}, bf16[48,8192]{1,0:T(8,128)(2,1)S(1)}, u32[]{:S(2)}, u32[]{:S(2)}) collective-permute-start(bf16[48,8192]{1,0:T(8,128)(2,1)} %bitcast.37), channel_id=1, source_target_pairs={{0,3},{1,2},{2,5},{3,4},{4,7},{5,6},{6,1},{7,0},{8,11},{9,10},{10,... | collective-permute-start | bytes 2359304 | tf_op jit(solution)/shard_map/ppermute | solution.py:50
  120.9 34.7 %collective-permute-start.22 = (bf16[48,8192]{1,0:T(8,128)(2,1)}, bf16[48,8192]{1,0:T(8,128)(2,1)S(1)}, u32[]{:S(2)}, u32[]{:S(2)}) collective-permute-start(bf16[48,8192]{1,0:T(8,128)(2,1)} %bitcast.36), channel_id=1, source_target_pairs={{0,7},{1,6},{2,1},{3,0},{4,3},{5,2},{6,5},{7,4},{8,15},{9,14},{10,... | collective-permute-start | bytes 2359304 | tf_op jit(solution)/shard_map/ppermute | solution.py:50
  155.3 0.9 copy-start.6
  155.5 0.9 copy-start.7
  155.6 1.1 copy-start.8

commit v13 on v12

--- a/solution.py
+++ b/solution.py
@@ -293,8 +293,8 @@
     ready = [block(source, s, m) for s, m in ROUTES[4:]]
     ready = [jnp.concatenate([b, share], axis=1) for b in ready[:3]] + ready[3:]
     for n, (b, (s, m)) in enumerate(zip(ready, ROUTES[4:])):
-        if n != 1:
-            b, outs[n % 3] = after(b, outs[n % 3])
+        if n in (0, 3):
+            b, outs[n // 3 * 2] = after(b, outs[n // 3 * 2])
         outs.append(ring_permute(b, s, m))
     own_out = block(expert_out, 0, 0)
 

time: 166 us -> 170 us (1.024)
  waiting for transfers between devices: 51.7 us -> 62.4 us
  starting transfers between devices: 45.6 us -> 38.9 us
    ppermute x14, waiting for transfers between devices: 32.9 us -> 42.8 us  [ring_permute(): return lax.ppermute(v, 'exp', perm)]
    ppermute x14, starting transfers between devices: 18.3 us -> 15.5 us  [ring_permute(): return lax.ppermute(v, 'exp', perm)]
  transfers between devices with their start and end apart: 24 -> 24, of which waited for: 10 -> 12; matrix products, arithmetic and copies ran while one was open for 7% -> 7% of each run, Pallas kernels for 9% -> 9%
where the time goes in v13:
time: 170 us; the launch traced here: 169 us
  waiting for transfers between devices  62.4 us (37%)
  starting transfers between devices  38.9 us (23%)
  blocking collectives  25.5 us (15%)
  Pallas kernels  23.4 us (14%)
  local copies, waits for them, and re-layouts  16.6 us (10%)
    ppermute x14, waiting for transfers between devices, ring_permute(): return lax.ppermute(v, 'exp', perm)  42.8 us
    all_gather x1, blocking collectives, body(): router_grad = lax.all_gather(partial, 'seq').reshape(EXPERTS, D)  25.5 us
    ppermute x14, starting transfers between devices, ring_permute(): return lax.ppermute(v, 'exp', perm)  15.5 us
    dynamic_slice x3, local copies, waits for them, and re-layouts, block(): lax.dynamic_slice(array, (0, 0, to * CAP, 0), (1, 2, CAP, D))  11.9 us
    all_to_all x1, waiting for transfers between devices, body(): partial = jnp.sum(lax.all_to_all(partial, 'seq', 0, 0, tiled=True), axis=0)  10.8 us
    ppermute x5, starting transfers between devices, body(): tally.append(tally[-1] + lax.ppermute(tally[-1], AXES, xor_perm(axis, d)))  10.5 us
    pallas_call x1, Pallas kernels, body(): pl.pallas_call(last_kernel, grid=(2, STEPS), out_shape=jax.ShapeDtypeStru...  7.98 us
    all_to_all x1, starting transfers between devices, body(): partial = jnp.sum(lax.all_to_all(partial, 'seq', 0, 0, tiled=True), axis=0)  7.75 us
  transfers between devices with their start and end apart: 24, of which 12 were waited for; matrix products, arithmetic and copies ran while one was open for 7% of the time, Pallas kernels for 9%

profile of v13, /device:TPU:0, one launch (start us, length us, event | category | flops | bytes accessed | tf_op | source)
XLA Modules:
  0.0 169.0 jit_solution(10873740137524737210)
XLA Ops:
  0.7 0.0 copy-start
  0.7 3.5 %constant_dynamic-slice_fusion.12 = (bf16[1,2,24,8192]{3,2,1,0:T(8,128)(2,1)S(1)}, bf16[1,2,24,8192]{3,2,1,0:T(8,128)(2,1)}, bf16[1,2,24,8192]{3,2,1,0:T(8,128)(2,1)}, bf16[1,2,24,8192]{3,2,1,0:T(8,128)(2,1)}) fusion(bf16[1,2,192,8192]{3,2,1,0:T(8,128)(2,1)} %param.15, s32[]{:T(128)S(6)} %select_n.35, s32[]{:T(128)S(6)} %select_n.34, s32[]{:T(128)S(6)} %select_n.33, ...), kind=kLoop, calls=%fused_computation.19 | loop fusion | bytes 6291472 | tf_op jit(solution)/shard_map/dynamic_slice | solution.py:266
  4.1 0.1 copy.10.ids_ref
  4.3 0.1 copy.11.logits_ref
  4.4 0.4 shard_map.95
  4.7 1.7 %collective-permute-start = (f32[8,16]{1,0:T(8,128)S(1)}, f32[8,16]{1,0:T(8,128)S(1)}, u32[]{:S(2)}, u32[]{:S(2)}) collective-permute-start(f32[8,16]{1,0:T(8,128)S(1)} %get-tuple-element.44), channel_id=1, source_target_pairs={{0,32},{1,33},{2,34},{3,35},{4,36},{5,37},{6,38},{7,39},{8,40},{9,... | collective-permute-start | bytes 1544 | tf_op jit(solution)/shard_map/ppermute | solution.py:287
  6.5 1.5 collective-permute-start.5
  8.0 2.7 %collective-permute-start.7 = (bf16[48,8192]{1,0:T(8,128)(2,1)}, bf16[48,8192]{1,0:T(8,128)(2,1)}, u32[]{:S(2)}, u32[]{:S(2)}) collective-permute-start(bf16[48,8192]{1,0:T(8,128)(2,1)} %bitcast.42), channel_id=1, source_target_pairs={{0,4},{1,5},{2,6},{3,7},{4,0},{5,1},{6,2},{7,3},{8,12},{9,13},{10,... | collective-permute-start | bytes 2359304 | tf_op jit(solution)/shard_map/ppermute | solution.py:50
  10.7 1.4 collective-permute-start.6
  12.1 0.1 stack.50
  12.2 0.5 multiply_reduce_fusion
  12.7 0.1 iota_add_fusion.1
  12.8 2.9 %collective-permute-start.1 = (f32[8,16]{1,0:T(8,128)S(1)}, f32[8,16]{1,0:T(8,128)S(1)}, u32[]{:S(2)}, u32[]{:S(2)}) collective-permute-start(f32[8,16]{1,0:T(8,128)S(1)} %add.245), channel_id=1, source_target_pairs={{0,64},{1,65},{2,66},{3,67},{4,68},{5,69},{6,70},{7,71},{8,72},{9,... | collective-permute-start | bytes 1544 | tf_op jit(solution)/shard_map/ppermute | solution.py:287
  15.7 2.2 %collective-permute-done.1 = f32[8,16]{1,0:T(8,128)S(1)} collective-permute-done((f32[8,16]{1,0:T(8,128)S(1)}, f32[8,16]{1,0:T(8,128)S(1)}, u32[]{:S(2)}, u32[]{:S(2)}) %collective-permute-start.1) | collective-permute-done | bytes 544 | tf_op jit(solution)/shard_map/ppermute | solution.py:287
  17.9 1.9 %collective-permute-start.2 = (f32[8,16]{1,0:T(8,128)S(1)}, f32[8,16]{1,0:T(8,128)S(1)}, u32[]{:S(2)}, u32[]{:S(2)}) collective-permute-start(f32[8,16]{1,0:T(8,128)S(1)} %add.246), channel_id=1, source_target_pairs={{0,8},{1,9},{2,10},{3,11},{4,12},{5,13},{6,14},{7,15},{8,0},{9,1},... | collective-permute-start | bytes 1544 | tf_op jit(solution)/shard_map/ppermute | solution.py:287
  19.9 0.1 copy.13.ids_ref
  20.0 0.1 add.244.slots_ref
  20.1 0.1 copy.15.inv_ref
  20.2 1.4 collective-permute-done.2
  21.6 3.9 %collective-permute-start.3 = (f32[8,16]{1,0:T(8,128)S(1)}, f32[8,16]{1,0:T(8,128)S(1)}, u32[]{:S(2)}, u32[]{:S(2)}) collective-permute-start(f32[8,16]{1,0:T(8,128)S(1)} %add.247), channel_id=1, source_target_pairs={{0,16},{1,17},{2,18},{3,19},{4,20},{5,21},{6,22},{7,23},{8,24},{9,... | collective-permute-start | bytes 1544 | tf_op jit(solution)/shard_map/ppermute | solution.py:287
  25.4 1.6 collective-permute-done.3
  27.0 0.0 collective-permute-start.4
  27.0 4.2 %constant_dynamic-slice_fusion.1 = (bf16[1,2,24,8192]{3,2,1,0:T(8,128)(2,1)}, bf16[1,2,24,8192]{3,2,1,0:T(8,128)(2,1)}, bf16[1,2,24,8192]{3,2,1,0:T(8,128)(2,1)}...) fusion(bf16[1,2,192,8192]{3,2,1,0:T(8,128)(2,1)} %param.14, ...), kind=kLoop, calls=%fused_computation.8 | loop fusion | bytes 11010064 | tf_op jit(solution)/shard_map/dynamic_slice | solution.py:266
  31.3 0.1 fusion.2
  31.4 0.4 pad_maximum_fusion.2
  31.8 0.2 collective-permute-start.9
  32.0 2.3 %collective-permute-start.10 = (bf16[48,8320]{1,0:T(8,128)(2,1)S(1)}, bf16[48,8320]{1,0:T(8,128)(2,1)S(1)}, u32[]{:S(2)}, u32[]{:S(2)}) collective-permute-start(bf16[48,8320]{1,0:T(8,128)(2,1)S(1)} %get-tuple-element.96), channel_id=1, source_target_pairs={{0,5},{1,4},{2,7},{3,6},{4,1},{5,0},{6,3},{7,2},{8,13},{9,12},{10,... | collective-permute-start | bytes 2396168 | tf_op jit(solution)/shard_map/ppermute | solution.py:50
  34.3 12.1 %collective-permute-done.7.refs_3_ = bf16[48,8192]{1,0:T(8,128)(2,1)} collective-permute-done((bf16[48,8192]{1,0:T(8,128)(2,1)}, bf16[48,8192]{1,0:T(8,128)(2,1)}, u32[]{:S(2)}, u32[]{:S(2)}) %collective-permute-start.7) | collective-permute-done | bytes 786464 | tf_op jit(solution)/shard_map/ppermute | solution.py:50
  46.4 4.2 %constant_dynamic-slice_fusion = (bf16[1,2,24,8192]{3,2,1,0:T(8,128)(2,1)}, bf16[1,2,24,8192]{3,2,1,0:T(8,128)(2,1)}, bf16[1,2,24,8192]{3,2,1,0:T(8,128)(2,1)}, ...) fusion(bf16[1,2,192,8192]{3,2,1,0:T(8,128)(2,1)} %param.14, s32[]{:T(128)S(6)} %select_n.35, s32[]{:T(128)S(6)} %select_n.34, ...), kind=kLoop, calls=%fused_computation.7 | loop fusion | bytes 7864340 | tf_op jit(solution)/shard_map/dynamic_slice | solution.py:266
  50.6 11.3 %collective-permute-done.9.refs_5_.refs_9_ = bf16[48,8320]{1,0:T(8,128)(2,1)S(1)} collective-permute-done((bf16[48,8320]{1,0:T(8,128)(2,1)S(1)}, bf16[48,8320]{1,0:T(8,128)(2,1)S(1)}, u32[]{:S(2)}, u32[]{:S(2)}) %collective-permute-start.9) | collective-permute-done | bytes 798752 | tf_op jit(solution)/shard_map/ppermute | solution.py:50
  62.0 1.4 collective-permute-start.16
  63.4 15.5 %collective-permute-done.8.refs_4_.refs_8_ = bf16[48,8320]{1,0:T(8,128)(2,1)S(1)} collective-permute-done((bf16[48,8320]{1,0:T(8,128)(2,1)S(1)}, bf16[48,8320]{1,0:T(8,128)(2,1)S(1)}, u32[]{:S(2)}, u32[]{:S(2)}) %collective-permute-start.8) | collective-permute-done | bytes 798752 | tf_op jit(solution)/shard_map/ppermute | solution.py:50
  78.9 0.9 collective-permute-start.15
  79.8 0.2 collective-permute-start.14
  80.0 1.8 %collective-permute-start.13 = (bf16[48,8192]{1,0:T(8,128)(2,1)}, bf16[48,8192]{1,0:T(8,128)(2,1)}, u32[]{:S(2)}, u32[]{:S(2)}) collective-permute-start(bf16[48,8192]{1,0:T(8,128)(2,1)} %bitcast.18), channel_id=1, source_target_pairs={{0,2},{1,3},{2,4},{3,5},{4,6},{5,7},{6,0},{7,1},{8,10},{9,11},{10,... | collective-permute-start | bytes 2359304 | tf_op jit(solution)/shard_map/ppermute | solution.py:50
  81.8 7.6 %shard_map.96 = (f32[128,16]{1,0:T(8,128)S(1)}, f32[16,8,1024]{2,1,0:T(8,128)}) custom-call(f32[1,384]{1,0:T(1,128)S(1)} %add.244.slots_ref, f32[128,8]{1,0:T(8,128)S(1)} %get-tuple-element.67.pack_ref, f32[128,1]{1,0:T(8,128)S(1)} %copy.15.inv_ref, s32[128,2]{1,0:T(8,128)S(1)} %copy.13.ids_ref, f32[128,16]{1,0:T(8,128)S(1)} %get-tuple-element.43.probs_ref, ...), custom_call_target="tpu_custom_call" | custom-call | flops 20000000000 | bytes 60000000 | tf_op jit(solution)/shard_map/pallas_call | solution.py:311
  89.4 0.6 copy-done.5
  90.0 7.8 %all-to-all-start = ((f32[16,8,1024]{2,1,0:T(8,128)}), f32[16,8,1024]{2,1,0:T(8,128)S(1)}, u32[]{:S(2)}, u32[]{:S(2)}) async-start(f32[16,8,1024]{2,1,0:T(8,128)} %get-tuple-element.58), calls=%async_computation | async-start | bytes 1048576 | tf_op jit(solution)/shard_map/all_to_all | solution.py:343
  97.8 0.1 stack.51
  97.9 0.1 iota_add_fusion
  98.0 10.8 %all-to-all-done = f32[16,8,1024]{2,1,0:T(8,128)S(1)} async-done(((f32[16,8,1024]{2,1,0:T(8,128)}), f32[16,8,1024]{2,1,0:T(8,128)S(1)}, u32[]{:S(2)}, u32[]{:S(2)}) %all-to-all-start) | async-done | bytes 524320 | tf_op jit(solution)/shard_map/all_to_all | solution.py:343
  108.8 0.1 collective-permute-start.12
  108.9 0.1 fusion.1
  108.9 1.1 collective-permute-done.12
  110.1 0.9 collective-permute-start.17
  111.0 2.9 %collective-permute-start.18 = (f32[8,1024]{1,0:T(8,128)S(1)}, f32[8,1024]{1,0:T(8,128)S(1)}, u32[]{:S(2)}, u32[]{:S(2)}) collective-permute-start(f32[8,1024]{1,0:T(8,128)S(1)} %add.258), channel_id=1, source_target_pairs={{0,4},{1,5},{2,6},{3,7},{4,0},{5,1},{6,2},{7,3},{8,12},{9,13},{10,... | collective-permute-start | bytes 98312 | tf_op jit(solution)/shard_map/ppermute | solution.py:345
  113.9 0.9 collective-permute-done.14.refs_2_
  114.8 2.4 %collective-permute-done.13.refs_1_ = bf16[48,8192]{1,0:T(8,128)(2,1)} collective-permute-done((bf16[48,8192]{1,0:T(8,128)(2,1)}, bf16[48,8192]{1,0:T(8,128)(2,1)}, u32[]{:S(2)}, u32[]{:S(2)}) %collective-permute-start.13) | collective-permute-done | bytes 786464 | tf_op jit(solution)/shard_map/ppermute | solution.py:50
  117.2 1.2 collective-permute-start.19
  118.4 0.1 iota_add_fusion.2
  118.5 0.6 add.265.slots_ref
  119.1 0.7 add.224.slots_ref
  119.8 2.5 %collective-permute-done.19 = f32[8,1024]{1,0:T(8,128)S(1)} collective-permute-done((f32[8,1024]{1,0:T(8,128)S(1)}, f32[8,1024]{1,0:T(8,128)S(1)}, u32[]{:S(2)}, u32[]{:S(2)}) %collective-permute-start.19) | collective-permute-done | bytes 32800 | tf_op jit(solution)/shard_map/ppermute | solution.py:347
  122.3 0.1 collective-permute-start.20
  122.4 1.8 %collective-permute-start.21 = (bf16[48,8192]{1,0:T(8,128)(2,1)}, bf16[48,8192]{1,0:T(8,128)(2,1)S(1)}, u32[]{:S(2)}, u32[]{:S(2)}) collective-permute-start(bf16[48,8192]{1,0:T(8,128)(2,1)} %bitcast.37), channel_id=1, source_target_pairs={{0,3},{1,2},{2,5},{3,4},{4,7},{5,6},{6,1},{7,0},{8,11},{9,10},{10,... | collective-permute-start | bytes 2359304 | tf_op jit(solution)/shard_map/ppermute | solution.py:50
  124.2 1.2 collective-permute-start.22
  125.5 7.5 %shard_map.97 = (f32[128,8192]{1,0:T(8,128)}, f32[128,128]{1,0:T(8,128)}) custom-call(f32[1,240]{1,0:T(1,128)} %add.265.slots_ref, f32[128,8]{1,0:T(8,128)} %copy-done.2, f32[128,1]{1,0:T(8,128)} %copy-done.1, f32[128,16]{1,0:T(8,128)} %copy-done.5, f32[16,8192]{1,0:T(8,128)} %weight_ref.1, f32[1,8192]{1,0:T(1,128)} %bitcast.30, ...), custom_call_target="tpu_custom_call" | custom-call | flops 10000000000 | bytes 30000000 | tf_op jit(solution)/shard_map/pallas_call | solution.py:354
  133.0 25.5 %all-gather = f32[128,1024]{1,0:T(8,128)S(1)} all-gather(f32[8,1024]{1,0:T(8,128)S(1)} %add_add_fusion), channel_id=2, replica_groups=mesh['seq'=16,'exp'=8] {'seq'}, dimensions={0}, use_global_device_ids=true | all-gather | bytes 557056 | tf_op jit(solution)/shard_map/all_gather | solution.py:380
  158.5 0.9 reshape.299
  159.4 0.5 collective-permute-done.21.refs_1_
  159.9 0.3 copy-done.6
  160.2 0.6 copy-done.7
  160.8 0.3 copy-done.8
  161.0 8.0 %shard_map.98 = bf16[128,8192]{1,0:T(8,128)(2,1)} custom-call(f32[1,144]{1,0:T(1,128)} %add.224.slots_ref, f32[128,8]{1,0:T(8,128)} %copy-done.2, f32[128,1]{1,0:T(8,128)} %copy-done.1, f32[128,128]{1,0:T(8,128)} %get-tuple-element.74.sums_ref, f32[1,8192]{1,0:T(1,128)} %bitcast.31, f32[128,8192]{1,0:T(8,128)} %get-tuple-element.75.part_ref, ...), custom_call_target="tpu_custom_call" | custom-call | tf_op jit(solution)/shard_map/pallas_call | solution.py:382
  (45 shorter events, 0.2 us)
Async XLA Ops:
  0.7 3.5 %copy-start.10 = (s32[128,2]{0,1:T(2,128)S(1)}, s32[128,2]{0,1:T(2,128)}, u32[]{:S(2)}) copy-start(s32[128,2]{0,1:T(2,128)} %param.13) | copy-start | bytes 3076
  0.7 3.6 %copy-start.9 = (f32[128,16]{0,1:T(8,128)S(1)}, f32[128,16]{0,1:T(8,128)}, u32[]{:S(2)}) copy-start(f32[128,16]{0,1:T(8,128)} %param.11) | copy-start | bytes 24580
  0.7 11.5 %copy-start = (bf16[128,8192]{1,0:T(8,128)(2,1)S(1)}, bf16[128,8192]{1,0:T(8,128)(2,1)}, u32[]{:S(2)}) copy-start(bf16[128,8192]{1,0:T(8,128)(2,1)} %hidden_ref.5) | copy-start | bytes 6291460
  4.7 77.1 %copy-start.2 = (f32[128,8]{1,0:T(8,128)}, f32[128,8]{1,0:T(8,128)S(1)}, u32[]{:S(2)}) copy-start(f32[128,8]{1,0:T(8,128)S(1)} %get-tuple-element.67.pack_ref) | copy-start | bytes 12292
  4.7 8.1 %collective-permute-start = (f32[8,16]{1,0:T(8,128)S(1)}, f32[8,16]{1,0:T(8,128)S(1)}, u32[]{:S(2)}, u32[]{:S(2)}) collective-permute-start(f32[8,16]{1,0:T(8,128)S(1)} %get-tuple-element.44), channel_id=1, source_target_pairs={{0,32},{1,33},{2,34},{3,35},{4,36},{5,37},{6,38},{7,39},{8,40},{9,... | collective-permute-start | bytes 1544 | tf_op jit(solution)/shard_map/ppermute | solution.py:287
  6.5 27.8 %collective-permute-start.5 = (bf16[48,8192]{1,0:T(8,128)(2,1)}, bf16[48,8192]{1,0:T(8,128)(2,1)}, u32[]{:S(2)}, u32[]{:S(2)}) collective-permute-start(bf16[48,8192]{1,0:T(8,128)(2,1)} %bitcast.43), channel_id=1, source_target_pairs={{0,2},{1,3},{2,4},{3,5},{4,6},{5,7},{6,0},{7,1},{8,10},{9,11},{10,... | collective-permute-start | bytes 2359304 | tf_op jit(solution)/shard_map/ppermute | solution.py:50
  8.0 38.4 %collective-permute-start.7 = (bf16[48,8192]{1,0:T(8,128)(2,1)}, bf16[48,8192]{1,0:T(8,128)(2,1)}, u32[]{:S(2)}, u32[]{:S(2)}) collective-permute-start(bf16[48,8192]{1,0:T(8,128)(2,1)} %bitcast.42), channel_id=1, source_target_pairs={{0,4},{1,5},{2,6},{3,7},{4,0},{5,1},{6,2},{7,3},{8,12},{9,13},{10,... | collective-permute-start | bytes 2359304 | tf_op jit(solution)/shard_map/ppermute | solution.py:50
  10.7 69.1 %collective-permute-start.6 = (bf16[48,8192]{1,0:T(8,128)(2,1)}, bf16[48,8192]{1,0:T(8,128)(2,1)}, u32[]{:S(2)}, u32[]{:S(2)}) collective-permute-start(bf16[48,8192]{1,0:T(8,128)(2,1)} %bitcast.41), channel_id=1, source_target_pairs={{0,6},{1,7},{2,0},{3,1},{4,2},{5,3},{6,4},{7,5},{8,14},{9,15},{10,... | collective-permute-start | bytes 2359304 | tf_op jit(solution)/shard_map/ppermute | solution.py:50
  12.8 5.2 %collective-permute-start.1 = (f32[8,16]{1,0:T(8,128)S(1)}, f32[8,16]{1,0:T(8,128)S(1)}, u32[]{:S(2)}, u32[]{:S(2)}) collective-permute-start(f32[8,16]{1,0:T(8,128)S(1)} %add.245), channel_id=1, source_target_pairs={{0,64},{1,65},{2,66},{3,67},{4,68},{5,69},{6,70},{7,71},{8,72},{9,... | collective-permute-start | bytes 1544 | tf_op jit(solution)/shard_map/ppermute | solution.py:287
  17.9 3.6 %collective-permute-start.2 = (f32[8,16]{1,0:T(8,128)S(1)}, f32[8,16]{1,0:T(8,128)S(1)}, u32[]{:S(2)}, u32[]{:S(2)}) collective-permute-start(f32[8,16]{1,0:T(8,128)S(1)} %add.246), channel_id=1, source_target_pairs={{0,8},{1,9},{2,10},{3,11},{4,12},{5,13},{6,14},{7,15},{8,0},{9,1},... | collective-permute-start | bytes 1544 | tf_op jit(solution)/shard_map/ppermute | solution.py:287
  20.2 61.6 %copy-start.1 = (f32[128,1]{1,0:T(8,128)}, f32[128,1]{1,0:T(8,128)S(1)}, u32[]{:S(2)}) copy-start(f32[128,1]{1,0:T(8,128)S(1)} %copy.15.inv_ref) | copy-start | bytes 1540
  21.6 5.5 %collective-permute-start.3 = (f32[8,16]{1,0:T(8,128)S(1)}, f32[8,16]{1,0:T(8,128)S(1)}, u32[]{:S(2)}, u32[]{:S(2)}) collective-permute-start(f32[8,16]{1,0:T(8,128)S(1)} %add.247), channel_id=1, source_target_pairs={{0,16},{1,17},{2,18},{3,19},{4,20},{5,21},{6,22},{7,23},{8,24},{9,... | collective-permute-start | bytes 1544 | tf_op jit(solution)/shard_map/ppermute | solution.py:287
  27.0 4.3 %collective-permute-start.4 = (f32[8,16]{1,0:T(8,128)S(1)}, f32[8,16]{1,0:T(8,128)S(1)}, u32[]{:S(2)}, u32[]{:S(2)}) collective-permute-start(f32[8,16]{1,0:T(8,128)S(1)} %add.248), channel_id=1, source_target_pairs={{0,1},{1,0},{2,3},{3,2},{4,5},{5,4},{6,7},{7,6},{8,9},{9,8},{10,11... | collective-permute-start | bytes 1544 | tf_op jit(solution)/shard_map/ppermute | solution.py:287
  31.8 30.2 %collective-permute-start.9 = (bf16[48,8320]{1,0:T(8,128)(2,1)S(1)}, bf16[48,8320]{1,0:T(8,128)(2,1)S(1)}, u32[]{:S(2)}, u32[]{:S(2)}) collective-permute-start(bf16[48,8320]{1,0:T(8,128)(2,1)S(1)} %get-tuple-element.97), channel_id=1, source_target_pairs={{0,7},{1,6},{2,1},{3,0},{4,3},{5,2},{6,5},{7,4},{8,15},{9,14},{10,... | collective-permute-start | bytes 2396168 | tf_op jit(solution)/shard_map/ppermute | solution.py:50
  32.0 48.0 %collective-permute-start.10 = (bf16[48,8320]{1,0:T(8,128)(2,1)S(1)}, bf16[48,8320]{1,0:T(8,128)(2,1)S(1)}, u32[]{:S(2)}, u32[]{:S(2)}) collective-permute-start(bf16[48,8320]{1,0:T(8,128)(2,1)S(1)} %get-tuple-element.96), channel_id=1, source_target_pairs={{0,5},{1,4},{2,7},{3,6},{4,1},{5,0},{6,3},{7,2},{8,13},{9,12},{10,... | collective-permute-start | bytes 2396168 | tf_op jit(solution)/shard_map/ppermute | solution.py:50
  34.2 44.6 %collective-permute-start.8 = (bf16[48,8320]{1,0:T(8,128)(2,1)S(1)}, bf16[48,8320]{1,0:T(8,128)(2,1)S(1)}, u32[]{:S(2)}, u32[]{:S(2)}) collective-permute-start(bf16[48,8320]{1,0:T(8,128)(2,1)S(1)} %get-tuple-element.52), channel_id=1, source_target_pairs={{0,3},{1,2},{2,5},{3,4},{4,7},{5,6},{6,1},{7,0},{8,11},{9,10},{10,... | collective-permute-start | bytes 2396168 | tf_op jit(solution)/shard_map/ppermute | solution.py:50
  46.4 35.4 %copy-start.3 = (f32[8192]{0:T(1024)S(1)}, f32[8192]{0:T(1024)}, u32[]{:S(2)}) copy-start(f32[8192]{0:T(1024)} %param.10) | copy-start | bytes 98308
  46.4 35.4 %copy-start.4 = (bf16[128,8192]{1,0:T(8,128)(2,1)S(1)}, bf16[128,8192]{1,0:T(8,128)(2,1)}, u32[]{:S(2)}) copy-start(bf16[128,8192]{1,0:T(8,128)(2,1)} %grad_ref.3) | copy-start | bytes 6291460
  46.4 35.4 %collective-permute-start.11 = (bf16[48,8192]{1,0:T(8,128)(2,1)S(1)}, bf16[48,8192]{1,0:T(8,128)(2,1)S(1)}, u32[]{:S(2)}, u32[]{:S(2)}) collective-permute-start(bf16[48,8192]{1,0:T(8,128)(2,1)S(1)} %bitcast.40), channel_id=1, source_target_pairs={{0,1},{1,0},{2,3},{3,2},{4,5},{5,4},{6,7},{7,6},{8,9},{9,8},{10,11... | collective-permute-start | bytes 2359304 | tf_op jit(solution)/shard_map/ppermute | solution.py:50
  62.0 49.0 %collective-permute-start.16 = (bf16[48,8192]{1,0:T(8,128)(2,1)}, bf16[48,8192]{1,0:T(8,128)(2,1)}, u32[]{:S(2)}, u32[]{:S(2)}) collective-permute-start(bf16[48,8192]{1,0:T(8,128)(2,1)} %bitcast.19), channel_id=1, source_target_pairs={{0,1},{1,0},{2,3},{3,2},{4,5},{5,4},{6,7},{7,6},{8,9},{9,8},{10,11... | collective-permute-start | bytes 2359304 | tf_op jit(solution)/shard_map/ppermute | solution.py:50
  78.9 35.1 %collective-permute-start.15 = (bf16[48,8192]{1,0:T(8,128)(2,1)}, bf16[48,8192]{1,0:T(8,128)(2,1)}, u32[]{:S(2)}, u32[]{:S(2)}) collective-permute-start(bf16[48,8192]{1,0:T(8,128)(2,1)} %bitcast.20), channel_id=1, source_target_pairs={{0,4},{1,5},{2,6},{3,7},{4,0},{5,1},{6,2},{7,3},{8,12},{9,13},{10,... | collective-permute-start | bytes 2359304 | tf_op jit(solution)/shard_map/ppermute | solution.py:50
  79.8 35.1 %collective-permute-start.14 = (bf16[48,8192]{1,0:T(8,128)(2,1)}, bf16[48,8192]{1,0:T(8,128)(2,1)}, u32[]{:S(2)}, u32[]{:S(2)}) collective-permute-start(bf16[48,8192]{1,0:T(8,128)(2,1)} %bitcast.17), channel_id=1, source_target_pairs={{0,6},{1,7},{2,0},{3,1},{4,2},{5,3},{6,4},{7,5},{8,14},{9,15},{10,... | collective-permute-start | bytes 2359304 | tf_op jit(solution)/shard_map/ppermute | solution.py:50
  80.0 37.3 %collective-permute-start.13 = (bf16[48,8192]{1,0:T(8,128)(2,1)}, bf16[48,8192]{1,0:T(8,128)(2,1)}, u32[]{:S(2)}, u32[]{:S(2)}) collective-permute-start(bf16[48,8192]{1,0:T(8,128)(2,1)} %bitcast.18), channel_id=1, source_target_pairs={{0,2},{1,3},{2,4},{3,5},{4,6},{5,7},{6,0},{7,1},{8,10},{9,11},{10,... | collective-permute-start | bytes 2359304 | tf_op jit(solution)/shard_map/ppermute | solution.py:50
  89.4 0.6 copy-start.5
  90.0 18.7 %all-to-all-start = ((f32[16,8,1024]{2,1,0:T(8,128)}), f32[16,8,1024]{2,1,0:T(8,128)S(1)}, u32[]{:S(2)}, u32[]{:S(2)}) async-start(f32[16,8,1024]{2,1,0:T(8,128)} %get-tuple-element.58), calls=%async_computation | async-start | bytes 1048576 | tf_op jit(solution)/shard_map/all_to_all | solution.py:343
  108.8 1.3 collective-permute-start.12
  110.1 9.7 %collective-permute-start.17 = (f32[8,1024]{1,0:T(8,128)S(1)}, f32[8,1024]{1,0:T(8,128)S(1)}, u32[]{:S(2)}, u32[]{:S(2)}) collective-permute-start(f32[8,1024]{1,0:T(8,128)S(1)} %add.258), channel_id=1, source_target_pairs={{0,2},{1,3},{2,0},{3,1},{4,6},{5,7},{6,4},{7,5},{8,10},{9,11},{10,... | collective-permute-start | bytes 98312 | tf_op jit(solution)/shard_map/ppermute | solution.py:345
  111.0 8.8 %collective-permute-start.18 = (f32[8,1024]{1,0:T(8,128)S(1)}, f32[8,1024]{1,0:T(8,128)S(1)}, u32[]{:S(2)}, u32[]{:S(2)}) collective-permute-start(f32[8,1024]{1,0:T(8,128)S(1)} %add.258), channel_id=1, source_target_pairs={{0,4},{1,5},{2,6},{3,7},{4,0},{5,1},{6,2},{7,3},{8,12},{9,13},{10,... | collective-permute-start | bytes 98312 | tf_op jit(solution)/shard_map/ppermute | solution.py:345
  117.2 5.1 %collective-permute-start.19 = (f32[8,1024]{1,0:T(8,128)S(1)}, f32[8,1024]{1,0:T(8,128)S(1)}, u32[]{:S(2)}, u32[]{:S(2)}) collective-permute-start(f32[8,1024]{1,0:T(8,128)S(1)} %add.258), channel_id=1, source_target_pairs={{0,6},{1,7},{2,4},{3,5},{4,2},{5,3},{6,0},{7,1},{8,14},{9,15},{10,... | collective-permute-start | bytes 98312 | tf_op jit(solution)/shard_map/ppermute | solution.py:347
  122.3 37.0 %collective-permute-start.20 = (bf16[48,8192]{1,0:T(8,128)(2,1)}, bf16[48,8192]{1,0:T(8,128)(2,1)S(1)}, u32[]{:S(2)}, u32[]{:S(2)}) collective-permute-start(bf16[48,8192]{1,0:T(8,128)(2,1)} %bitcast.38), channel_id=1, source_target_pairs={{0,5},{1,4},{2,7},{3,6},{4,1},{5,0},{6,3},{7,2},{8,13},{9,12},{10,... | collective-permute-start | bytes 2359304 | tf_op jit(solution)/shard_map/ppermute | solution.py:50
  122.4 37.5 %collective-permute-start.21 = (bf16[48,8192]{1,0:T(8,128)(2,1)}, bf16[48,8192]{1,0:T(8,128)(2,1)S(1)}, u32[]{:S(2)}, u32[]{:S(2)}) collective-permute-start(bf16[48,8192]{1,0:T(8,128)(2,1)} %bitcast.37), channel_id=1, source_target_pairs={{0,3},{1,2},{2,5},{3,4},{4,7},{5,6},{6,1},{7,0},{8,11},{9,10},{10,... | collective-permute-start | bytes 2359304 | tf_op jit(solution)/shard_map/ppermute | solution.py:50
  124.2 35.7 %collective-permute-start.22 = (bf16[48,8192]{1,0:T(8,128)(2,1)}, bf16[48,8192]{1,0:T(8,128)(2,1)S(1)}, u32[]{:S(2)}, u32[]{:S(2)}) collective-permute-start(bf16[48,8192]{1,0:T(8,128)(2,1)} %bitcast.36), channel_id=1, source_target_pairs={{0,7},{1,6},{2,1},{3,0},{4,3},{5,2},{6,5},{7,4},{8,15},{9,14},{10,... | collective-permute-start | bytes 2359304 | tf_op jit(solution)/shard_map/ppermute | solution.py:50
  159.4 0.9 copy-start.6
  159.9 0.9 copy-start.7
  159.9 1.1 copy-start.8

commit v14 on v12

--- a/solution.py
+++ b/solution.py
@@ -235,7 +235,7 @@
         out_ref[...] = (part_scr[:, cols] - normed).astype(BF16)
 
 
-STEPS = 4
+STEPS = 8
 WIDE = D // STEPS
 
 

time: 166 us -> 172 us (1.036)
  Pallas kernels: 23.4 us -> 31.7 us
  waiting for transfers between devices: 51.7 us -> 54.5 us
  blocking collectives: 25.3 us -> 22.7 us
  starting transfers between devices: 45.6 us -> 43 us
    pallas_call x1, Pallas kernels: 7.99 us -> 11.1 us  [body(): pl.pallas_call(last_kernel, grid=(2, STEPS), out_shape=jax.ShapeDtypeStru...]
    pallas_call x1, Pallas kernels: 7.59 us -> 10.7 us  [body(): pl.pallas_call(mid_kernel, grid=(2, STEPS), out_shape=(jax.ShapeDtypeStru...]
    all_gather x1, blocking collectives: 25.3 us -> 22.7 us  [body(): router_grad = lax.all_gather(partial, 'seq').reshape(EXPERTS, D)]
    ppermute x1, starting transfers between devices: 2.26 us -> 0.09 us  [body(): lax.ppermute(partial, AXES, xor_perm('x', 3))]
    pallas_call x1, Pallas kernels: 7.49 us -> 9.53 us  [body(): pl.pallas_call(half_kernel, grid=(STEPS,), out_shape=(jax.ShapeDtypeStruc...]
  transfers between devices with their start and end apart: 24 -> 24, of which waited for: 10 -> 11; matrix products, arithmetic and copies ran while one was open for 7% -> 7% of each run, Pallas kernels for 9% -> 12%
where the time goes in v14:
time: 172 us; the launch traced here: 170 us
  waiting for transfers between devices  54.5 us (32%)
  starting transfers between devices  43 us (25%)
  Pallas kernels  31.7 us (18%)
  blocking collectives  22.7 us (13%)
  local copies, waits for them, and re-layouts  16.5 us (10%)
    ppermute x14, waiting for transfers between devices, ring_permute(): return lax.ppermute(v, 'exp', perm)  33.5 us
    all_gather x1, blocking collectives, body(): router_grad = lax.all_gather(partial, 'seq').reshape(EXPERTS, D)  22.7 us
    ppermute x14, starting transfers between devices, ring_permute(): return lax.ppermute(v, 'exp', perm)  17.9 us
    dynamic_slice x3, local copies, waits for them, and re-layouts, block(): lax.dynamic_slice(array, (0, 0, to * CAP, 0), (1, 2, CAP, D))  11.8 us
    all_to_all x1, waiting for transfers between devices, body(): partial = jnp.sum(lax.all_to_all(partial, 'seq', 0, 0, tiled=True), axis=0)  11.3 us
    pallas_call x1, Pallas kernels, body(): pl.pallas_call(last_kernel, grid=(2, STEPS), out_shape=jax.ShapeDtypeStru...  11.1 us
    pallas_call x1, Pallas kernels, body(): pl.pallas_call(mid_kernel, grid=(2, STEPS), out_shape=(jax.ShapeDtypeStru...  10.7 us
    ppermute x5, starting transfers between devices, body(): tally.append(tally[-1] + lax.ppermute(tally[-1], AXES, xor_perm(axis, d)))  10.5 us
  transfers between devices with their start and end apart: 24, of which 11 were waited for; matrix products, arithmetic and copies ran while one was open for 7% of the time, Pallas kernels for 12%

profile of v14, /device:TPU:0, one launch (start us, length us, event | category | flops | bytes accessed | tf_op | source)
XLA Modules:
  0.0 170.5 jit_solution(15988065825917583683)
XLA Ops:
  0.7 0.0 copy-start
  0.7 3.5 %constant_dynamic-slice_fusion.12 = (bf16[1,2,24,8192]{3,2,1,0:T(8,128)(2,1)S(1)}, bf16[1,2,24,8192]{3,2,1,0:T(8,128)(2,1)}, bf16[1,2,24,8192]{3,2,1,0:T(8,128)(2,1)}, bf16[1,2,24,8192]{3,2,1,0:T(8,128)(2,1)}) fusion(bf16[1,2,192,8192]{3,2,1,0:T(8,128)(2,1)} %param.15, s32[]{:T(128)S(6)} %select_n.35, s32[]{:T(128)S(6)} %select_n.34, s32[]{:T(128)S(6)} %select_n.33, ...), kind=kLoop, calls=%fused_computation.19 | loop fusion | bytes 6291472 | tf_op jit(solution)/shard_map/dynamic_slice | solution.py:266
  4.1 0.1 copy.10.ids_ref
  4.3 0.1 copy.11.logits_ref
  4.4 0.4 shard_map.95
  4.7 1.7 %collective-permute-start = (f32[8,16]{1,0:T(8,128)S(1)}, f32[8,16]{1,0:T(8,128)S(1)}, u32[]{:S(2)}, u32[]{:S(2)}) collective-permute-start(f32[8,16]{1,0:T(8,128)S(1)} %get-tuple-element.46), channel_id=1, source_target_pairs={{0,32},{1,33},{2,34},{3,35},{4,36},{5,37},{6,38},{7,39},{8,40},{9,... | collective-permute-start | bytes 1544 | tf_op jit(solution)/shard_map/ppermute | solution.py:287
  6.5 1.5 collective-permute-start.5
  8.0 2.7 %collective-permute-start.7 = (bf16[48,8192]{1,0:T(8,128)(2,1)}, bf16[48,8192]{1,0:T(8,128)(2,1)}, u32[]{:S(2)}, u32[]{:S(2)}) collective-permute-start(bf16[48,8192]{1,0:T(8,128)(2,1)} %bitcast.42), channel_id=1, source_target_pairs={{0,4},{1,5},{2,6},{3,7},{4,0},{5,1},{6,2},{7,3},{8,12},{9,13},{10,... | collective-permute-start | bytes 2359304 | tf_op jit(solution)/shard_map/ppermute | solution.py:50
  10.7 1.4 collective-permute-start.6
  12.1 0.1 stack.50
  12.2 0.5 multiply_reduce_fusion
  12.7 0.1 iota_add_fusion.1
  12.8 2.9 %collective-permute-start.1 = (f32[8,16]{1,0:T(8,128)S(1)}, f32[8,16]{1,0:T(8,128)S(1)}, u32[]{:S(2)}, u32[]{:S(2)}) collective-permute-start(f32[8,16]{1,0:T(8,128)S(1)} %add.245), channel_id=1, source_target_pairs={{0,64},{1,65},{2,66},{3,67},{4,68},{5,69},{6,70},{7,71},{8,72},{9,... | collective-permute-start | bytes 1544 | tf_op jit(solution)/shard_map/ppermute | solution.py:287
  15.7 2.2 %collective-permute-done.1 = f32[8,16]{1,0:T(8,128)S(1)} collective-permute-done((f32[8,16]{1,0:T(8,128)S(1)}, f32[8,16]{1,0:T(8,128)S(1)}, u32[]{:S(2)}, u32[]{:S(2)}) %collective-permute-start.1) | collective-permute-done | bytes 544 | tf_op jit(solution)/shard_map/ppermute | solution.py:287
  17.9 1.9 %collective-permute-start.2 = (f32[8,16]{1,0:T(8,128)S(1)}, f32[8,16]{1,0:T(8,128)S(1)}, u32[]{:S(2)}, u32[]{:S(2)}) collective-permute-start(f32[8,16]{1,0:T(8,128)S(1)} %add.246), channel_id=1, source_target_pairs={{0,8},{1,9},{2,10},{3,11},{4,12},{5,13},{6,14},{7,15},{8,0},{9,1},... | collective-permute-start | bytes 1544 | tf_op jit(solution)/shard_map/ppermute | solution.py:287
  19.9 0.1 copy.13.ids_ref
  20.0 0.1 add.244.slots_ref
  20.1 0.1 copy.15.inv_ref
  20.2 1.4 collective-permute-done.2
  21.6 3.9 %collective-permute-start.3 = (f32[8,16]{1,0:T(8,128)S(1)}, f32[8,16]{1,0:T(8,128)S(1)}, u32[]{:S(2)}, u32[]{:S(2)}) collective-permute-start(f32[8,16]{1,0:T(8,128)S(1)} %add.247), channel_id=1, source_target_pairs={{0,16},{1,17},{2,18},{3,19},{4,20},{5,21},{6,22},{7,23},{8,24},{9,... | collective-permute-start | bytes 1544 | tf_op jit(solution)/shard_map/ppermute | solution.py:287
  25.4 1.6 collective-permute-done.3
  27.0 0.0 collective-permute-start.4
  27.0 4.2 %constant_dynamic-slice_fusion.1 = (bf16[1,2,24,8192]{3,2,1,0:T(8,128)(2,1)}, bf16[1,2,24,8192]{3,2,1,0:T(8,128)(2,1)}, bf16[1,2,24,8192]{3,2,1,0:T(8,128)(2,1)}...) fusion(bf16[1,2,192,8192]{3,2,1,0:T(8,128)(2,1)} %param.14, ...), kind=kLoop, calls=%fused_computation.8 | loop fusion | bytes 11010064 | tf_op jit(solution)/shard_map/dynamic_slice | solution.py:266
  31.3 0.0 collective-permute-done.4
  31.3 0.1 fusion.2
  31.4 0.4 pad_maximum_fusion.2
  31.8 0.2 collective-permute-start.9
  32.0 1.6 collective-permute-start.8
  33.6 12.7 %collective-permute-done.7.refs_3_ = bf16[48,8192]{1,0:T(8,128)(2,1)} collective-permute-done((bf16[48,8192]{1,0:T(8,128)(2,1)}, bf16[48,8192]{1,0:T(8,128)(2,1)}, u32[]{:S(2)}, u32[]{:S(2)}) %collective-permute-start.7) | collective-permute-done | bytes 786464 | tf_op jit(solution)/shard_map/ppermute | solution.py:50
  46.3 0.9 collective-permute-start.11
  47.3 4.1 %constant_dynamic-slice_fusion = (bf16[1,2,24,8192]{3,2,1,0:T(8,128)(2,1)}, bf16[1,2,24,8192]{3,2,1,0:T(8,128)(2,1)}, bf16[1,2,24,8192]{3,2,1,0:T(8,128)(2,1)}, ...) fusion(bf16[1,2,192,8192]{3,2,1,0:T(8,128)(2,1)} %param.14, s32[]{:T(128)S(6)} %select_n.35, s32[]{:T(128)S(6)} %select_n.34, ...), kind=kLoop, calls=%fused_computation.7 | loop fusion | bytes 7864340 | tf_op jit(solution)/shard_map/dynamic_slice | solution.py:266
  51.3 10.7 %collective-permute-done.9.refs_5_.refs_9_ = bf16[48,8320]{1,0:T(8,128)(2,1)S(1)} collective-permute-done((bf16[48,8320]{1,0:T(8,128)(2,1)S(1)}, bf16[48,8320]{1,0:T(8,128)(2,1)S(1)}, u32[]{:S(2)}, u32[]{:S(2)}) %collective-permute-start.9) | collective-permute-done | bytes 798752 | tf_op jit(solution)/shard_map/ppermute | solution.py:50
  62.0 1.4 collective-permute-start.16
  63.4 3.0 %collective-permute-start.15 = (bf16[48,8192]{1,0:T(8,128)(2,1)}, bf16[48,8192]{1,0:T(8,128)(2,1)}, u32[]{:S(2)}, u32[]{:S(2)}) collective-permute-start(bf16[48,8192]{1,0:T(8,128)(2,1)} %bitcast.21), channel_id=1, source_target_pairs={{0,4},{1,5},{2,6},{3,7},{4,0},{5,1},{6,2},{7,3},{8,12},{9,13},{10,... | collective-permute-start | bytes 2359304 | tf_op jit(solution)/shard_map/ppermute | solution.py:50
  66.3 0.6 collective-permute-start.14
  67.0 1.4 collective-permute-start.13
  68.4 9.3 %collective-permute-done.10.refs_6_.refs_10_ = bf16[48,8320]{1,0:T(8,128)(2,1)S(1)} collective-permute-done((bf16[48,8320]{1,0:T(8,128)(2,1)S(1)}, bf16[48,8320]{1,0:T(8,128)(2,1)S(1)}, u32[]{:S(2)}, u32[]{:S(2)}) %collective-permute-start.10) | collective-permute-done | bytes 798752 | tf_op jit(solution)/shard_map/ppermute | solution.py:50
  77.6 10.7 %shard_map.96 = (f32[128,16]{1,0:T(8,128)S(1)}, f32[16,8,1024]{2,1,0:T(8,128)}) custom-call(f32[1,384]{1,0:T(1,128)S(1)} %add.244.slots_ref, f32[128,8]{1,0:T(8,128)S(1)} %get-tuple-element.71.pack_ref, f32[128,1]{1,0:T(8,128)S(1)} %copy.15.inv_ref, s32[128,2]{1,0:T(8,128)S(1)} %copy.13.ids_ref, f32[128,16]{1,0:T(8,128)S(1)} %get-tuple-element.45.probs_ref, ...), custom_call_target="tpu_custom_call" | custom-call | flops 20000000000 | bytes 60000000 | tf_op jit(solution)/shard_map/pallas_call | solution.py:311
  88.3 0.6 copy-done.5
  88.9 7.8 %all-to-all-start = ((f32[16,8,1024]{2,1,0:T(8,128)}), f32[16,8,1024]{2,1,0:T(8,128)S(1)}, u32[]{:S(2)}, u32[]{:S(2)}) async-start(f32[16,8,1024]{2,1,0:T(8,128)} %get-tuple-element.62), calls=%async_computation | async-start | bytes 1048576 | tf_op jit(solution)/shard_map/all_to_all | solution.py:343
  96.7 0.1 stack.51
  96.8 0.1 iota_add_fusion
  96.9 11.3 %all-to-all-done = f32[16,8,1024]{2,1,0:T(8,128)S(1)} async-done(((f32[16,8,1024]{2,1,0:T(8,128)}), f32[16,8,1024]{2,1,0:T(8,128)S(1)}, u32[]{:S(2)}, u32[]{:S(2)}) %all-to-all-start) | async-done | bytes 524320 | tf_op jit(solution)/shard_map/all_to_all | solution.py:343
  108.2 1.4 collective-permute-start.12
  109.5 0.1 fusion.1
  109.6 0.8 collective-permute-done.12
  110.4 2.3 %collective-permute-start.17 = (f32[8,1024]{1,0:T(8,128)S(1)}, f32[8,1024]{1,0:T(8,128)S(1)}, u32[]{:S(2)}, u32[]{:S(2)}) collective-permute-start(f32[8,1024]{1,0:T(8,128)S(1)} %add.258), channel_id=1, source_target_pairs={{0,2},{1,3},{2,0},{3,1},{4,6},{5,7},{6,4},{7,5},{8,10},{9,11},{10,... | collective-permute-start | bytes 98312 | tf_op jit(solution)/shard_map/ppermute | solution.py:345
  112.7 3.2 %collective-permute-start.18 = (f32[8,1024]{1,0:T(8,128)S(1)}, f32[8,1024]{1,0:T(8,128)S(1)}, u32[]{:S(2)}, u32[]{:S(2)}) collective-permute-start(f32[8,1024]{1,0:T(8,128)S(1)} %add.258), channel_id=1, source_target_pairs={{0,4},{1,5},{2,6},{3,7},{4,0},{5,1},{6,2},{7,3},{8,12},{9,13},{10,... | collective-permute-start | bytes 98312 | tf_op jit(solution)/shard_map/ppermute | solution.py:345
  115.9 0.1 collective-permute-start.19
  116.0 0.1 iota_add_fusion.2
  116.0 0.6 add.265.slots_ref
  116.7 0.7 add.224.slots_ref
  117.4 0.8 collective-permute-done.18
  118.1 3.0 %collective-permute-done.19 = f32[8,1024]{1,0:T(8,128)S(1)} collective-permute-done((f32[8,1024]{1,0:T(8,128)S(1)}, f32[8,1024]{1,0:T(8,128)S(1)}, u32[]{:S(2)}, u32[]{:S(2)}) %collective-permute-start.19) | collective-permute-done | bytes 32800 | tf_op jit(solution)/shard_map/ppermute | solution.py:347
  121.1 0.1 collective-permute-start.20
  121.2 0.6 collective-permute-start.21
  121.8 2.5 %collective-permute-start.22 = (bf16[48,8192]{1,0:T(8,128)(2,1)}, bf16[48,8192]{1,0:T(8,128)(2,1)S(1)}, u32[]{:S(2)}, u32[]{:S(2)}) collective-permute-start(bf16[48,8192]{1,0:T(8,128)(2,1)} %bitcast.36), channel_id=1, source_target_pairs={{0,7},{1,6},{2,1},{3,0},{4,3},{5,2},{6,5},{7,4},{8,15},{9,14},{10,... | collective-permute-start | bytes 2359304 | tf_op jit(solution)/shard_map/ppermute | solution.py:50
  124.2 9.5 %shard_map.97 = (f32[128,8192]{1,0:T(8,128)}, f32[128,128]{1,0:T(8,128)}) custom-call(f32[1,240]{1,0:T(1,128)} %add.265.slots_ref, f32[128,8]{1,0:T(8,128)} %copy-done.2, f32[128,1]{1,0:T(8,128)} %copy-done.1, f32[128,16]{1,0:T(8,128)} %copy-done.5, f32[16,8192]{1,0:T(8,128)} %weight_ref.1, f32[1,8192]{1,0:T(1,128)} %bitcast.30, ...), custom_call_target="tpu_custom_call" | custom-call | flops 10000000000 | bytes 30000000 | tf_op jit(solution)/shard_map/pallas_call | solution.py:354
  133.8 22.7 %all-gather = f32[128,1024]{1,0:T(8,128)S(1)} all-gather(f32[8,1024]{1,0:T(8,128)S(1)} %add_add_fusion), channel_id=2, replica_groups=mesh['seq'=16,'exp'=8] {'seq'}, dimensions={0}, use_global_device_ids=true | all-gather | bytes 557056 | tf_op jit(solution)/shard_map/all_gather | solution.py:380
  156.4 0.9 reshape.299
  157.3 0.9 collective-permute-done.21.refs_1_
  158.2 0.9 copy-done.7
  159.1 0.3 copy-done.8
  159.3 11.1 %shard_map.98 = bf16[128,8192]{1,0:T(8,128)(2,1)} custom-call(f32[1,144]{1,0:T(1,128)} %add.224.slots_ref, f32[128,8]{1,0:T(8,128)} %copy-done.2, f32[128,1]{1,0:T(8,128)} %copy-done.1, f32[128,128]{1,0:T(8,128)} %get-tuple-element.78.sums_ref, f32[1,8192]{1,0:T(1,128)} %bitcast.31, f32[128,8192]{1,0:T(8,128)} %get-tuple-element.79.part_ref, ...), custom_call_target="tpu_custom_call" | custom-call | tf_op jit(solution)/shard_map/pallas_call | solution.py:382
  (45 shorter events, 0.2 us)
Async XLA Ops:
  0.7 3.5 %copy-start.10 = (s32[128,2]{0,1:T(2,128)S(1)}, s32[128,2]{0,1:T(2,128)}, u32[]{:S(2)}) copy-start(s32[128,2]{0,1:T(2,128)} %param.13) | copy-start | bytes 3076
  0.7 3.6 %copy-start.9 = (f32[128,16]{0,1:T(8,128)S(1)}, f32[128,16]{0,1:T(8,128)}, u32[]{:S(2)}) copy-start(f32[128,16]{0,1:T(8,128)} %param.11) | copy-start | bytes 24580
  0.7 11.5 %copy-start = (bf16[128,8192]{1,0:T(8,128)(2,1)S(1)}, bf16[128,8192]{1,0:T(8,128)(2,1)}, u32[]{:S(2)}) copy-start(bf16[128,8192]{1,0:T(8,128)(2,1)} %hidden_ref.5) | copy-start | bytes 6291460
  4.7 72.9 %copy-start.2 = (f32[128,8]{1,0:T(8,128)}, f32[128,8]{1,0:T(8,128)S(1)}, u32[]{:S(2)}) copy-start(f32[128,8]{1,0:T(8,128)S(1)} %get-tuple-element.71.pack_ref) | copy-start | bytes 12292
  4.7 8.1 %collective-permute-start = (f32[8,16]{1,0:T(8,128)S(1)}, f32[8,16]{1,0:T(8,128)S(1)}, u32[]{:S(2)}, u32[]{:S(2)}) collective-permute-start(f32[8,16]{1,0:T(8,128)S(1)} %get-tuple-element.46), channel_id=1, source_target_pairs={{0,32},{1,33},{2,34},{3,35},{4,36},{5,37},{6,38},{7,39},{8,40},{9,... | collective-permute-start | bytes 1544 | tf_op jit(solution)/shard_map/ppermute | solution.py:287
  6.5 25.5 %collective-permute-start.5 = (bf16[48,8192]{1,0:T(8,128)(2,1)}, bf16[48,8192]{1,0:T(8,128)(2,1)}, u32[]{:S(2)}, u32[]{:S(2)}) collective-permute-start(bf16[48,8192]{1,0:T(8,128)(2,1)} %bitcast.43), channel_id=1, source_target_pairs={{0,2},{1,3},{2,4},{3,5},{4,6},{5,7},{6,0},{7,1},{8,10},{9,11},{10,... | collective-permute-start | bytes 2359304 | tf_op jit(solution)/shard_map/ppermute | solution.py:50
  8.0 38.4 %collective-permute-start.7 = (bf16[48,8192]{1,0:T(8,128)(2,1)}, bf16[48,8192]{1,0:T(8,128)(2,1)}, u32[]{:S(2)}, u32[]{:S(2)}) collective-permute-start(bf16[48,8192]{1,0:T(8,128)(2,1)} %bitcast.42), channel_id=1, source_target_pairs={{0,4},{1,5},{2,6},{3,7},{4,0},{5,1},{6,2},{7,3},{8,12},{9,13},{10,... | collective-permute-start | bytes 2359304 | tf_op jit(solution)/shard_map/ppermute | solution.py:50
  10.7 55.7 %collective-permute-start.6 = (bf16[48,8192]{1,0:T(8,128)(2,1)}, bf16[48,8192]{1,0:T(8,128)(2,1)}, u32[]{:S(2)}, u32[]{:S(2)}) collective-permute-start(bf16[48,8192]{1,0:T(8,128)(2,1)} %bitcast.41), channel_id=1, source_target_pairs={{0,6},{1,7},{2,0},{3,1},{4,2},{5,3},{6,4},{7,5},{8,14},{9,15},{10,... | collective-permute-start | bytes 2359304 | tf_op jit(solution)/shard_map/ppermute | solution.py:50
  12.8 5.2 %collective-permute-start.1 = (f32[8,16]{1,0:T(8,128)S(1)}, f32[8,16]{1,0:T(8,128)S(1)}, u32[]{:S(2)}, u32[]{:S(2)}) collective-permute-start(f32[8,16]{1,0:T(8,128)S(1)} %add.245), channel_id=1, source_target_pairs={{0,64},{1,65},{2,66},{3,67},{4,68},{5,69},{6,70},{7,71},{8,72},{9,... | collective-permute-start | bytes 1544 | tf_op jit(solution)/shard_map/ppermute | solution.py:287
  17.9 3.6 %collective-permute-start.2 = (f32[8,16]{1,0:T(8,128)S(1)}, f32[8,16]{1,0:T(8,128)S(1)}, u32[]{:S(2)}, u32[]{:S(2)}) collective-permute-start(f32[8,16]{1,0:T(8,128)S(1)} %add.246), channel_id=1, source_target_pairs={{0,8},{1,9},{2,10},{3,11},{4,12},{5,13},{6,14},{7,15},{8,0},{9,1},... | collective-permute-start | bytes 1544 | tf_op jit(solution)/shard_map/ppermute | solution.py:287
  20.2 57.5 %copy-start.1 = (f32[128,1]{1,0:T(8,128)}, f32[128,1]{1,0:T(8,128)S(1)}, u32[]{:S(2)}) copy-start(f32[128,1]{1,0:T(8,128)S(1)} %copy.15.inv_ref) | copy-start | bytes 1540
  21.6 5.5 %collective-permute-start.3 = (f32[8,16]{1,0:T(8,128)S(1)}, f32[8,16]{1,0:T(8,128)S(1)}, u32[]{:S(2)}, u32[]{:S(2)}) collective-permute-start(f32[8,16]{1,0:T(8,128)S(1)} %add.247), channel_id=1, source_target_pairs={{0,16},{1,17},{2,18},{3,19},{4,20},{5,21},{6,22},{7,23},{8,24},{9,... | collective-permute-start | bytes 1544 | tf_op jit(solution)/shard_map/ppermute | solution.py:287
  27.0 4.3 %collective-permute-start.4 = (f32[8,16]{1,0:T(8,128)S(1)}, f32[8,16]{1,0:T(8,128)S(1)}, u32[]{:S(2)}, u32[]{:S(2)}) collective-permute-start(f32[8,16]{1,0:T(8,128)S(1)} %add.248), channel_id=1, source_target_pairs={{0,1},{1,0},{2,3},{3,2},{4,5},{5,4},{6,7},{7,6},{8,9},{9,8},{10,11... | collective-permute-start | bytes 1544 | tf_op jit(solution)/shard_map/ppermute | solution.py:287
  31.8 30.2 %collective-permute-start.9 = (bf16[48,8320]{1,0:T(8,128)(2,1)S(1)}, bf16[48,8320]{1,0:T(8,128)(2,1)S(1)}, u32[]{:S(2)}, u32[]{:S(2)}) collective-permute-start(bf16[48,8320]{1,0:T(8,128)(2,1)S(1)} %get-tuple-element.100), channel_id=1, source_target_pairs={{0,7},{1,6},{2,1},{3,0},{4,3},{5,2},{6,5},{7,4},{8,15},{9,14},{10,... | collective-permute-start | bytes 2396168 | tf_op jit(solution)/shard_map/ppermute | solution.py:50
  32.0 31.4 %collective-permute-start.8 = (bf16[48,8320]{1,0:T(8,128)(2,1)S(1)}, bf16[48,8320]{1,0:T(8,128)(2,1)S(1)}, u32[]{:S(2)}, u32[]{:S(2)}) collective-permute-start(bf16[48,8320]{1,0:T(8,128)(2,1)S(1)} %get-tuple-element.55), channel_id=1, source_target_pairs={{0,3},{1,2},{2,5},{3,4},{4,7},{5,6},{6,1},{7,0},{8,11},{9,10},{10,... | collective-permute-start | bytes 2396168 | tf_op jit(solution)/shard_map/ppermute | solution.py:50
  46.3 31.3 %collective-permute-start.10 = (bf16[48,8320]{1,0:T(8,128)(2,1)S(1)}, bf16[48,8320]{1,0:T(8,128)(2,1)S(1)}, u32[]{:S(2)}, u32[]{:S(2)}) collective-permute-start(bf16[48,8320]{1,0:T(8,128)(2,1)S(1)} %get-tuple-element.60), channel_id=1, source_target_pairs={{0,5},{1,4},{2,7},{3,6},{4,1},{5,0},{6,3},{7,2},{8,13},{9,12},{10,... | collective-permute-start | bytes 2396168 | tf_op jit(solution)/shard_map/ppermute | solution.py:50
  46.3 31.3 %copy-start.3 = (f32[8192]{0:T(1024)S(1)}, f32[8192]{0:T(1024)}, u32[]{:S(2)}) copy-start(f32[8192]{0:T(1024)} %param.10) | copy-start | bytes 98308
  46.3 31.3 %copy-start.4 = (bf16[128,8192]{1,0:T(8,128)(2,1)S(1)}, bf16[128,8192]{1,0:T(8,128)(2,1)}, u32[]{:S(2)}) copy-start(bf16[128,8192]{1,0:T(8,128)(2,1)} %grad_ref.3) | copy-start | bytes 6291460
  46.3 20.6 %collective-permute-start.11 = (bf16[48,8192]{1,0:T(8,128)(2,1)S(1)}, bf16[48,8192]{1,0:T(8,128)(2,1)S(1)}, u32[]{:S(2)}, u32[]{:S(2)}) collective-permute-start(bf16[48,8192]{1,0:T(8,128)(2,1)S(1)} %bitcast.40), channel_id=1, source_target_pairs={{0,1},{1,0},{2,3},{3,2},{4,5},{5,4},{6,7},{7,6},{8,9},{9,8},{10,11... | collective-permute-start | bytes 2359304 | tf_op jit(solution)/shard_map/ppermute | solution.py:50
  62.0 50.7 %collective-permute-start.16 = (bf16[48,8192]{1,0:T(8,128)(2,1)}, bf16[48,8192]{1,0:T(8,128)(2,1)}, u32[]{:S(2)}, u32[]{:S(2)}) collective-permute-start(bf16[48,8192]{1,0:T(8,128)(2,1)} %bitcast.20), channel_id=1, source_target_pairs={{0,1},{1,0},{2,3},{3,2},{4,5},{5,4},{6,7},{7,6},{8,9},{9,8},{10,11... | collective-permute-start | bytes 2359304 | tf_op jit(solution)/shard_map/ppermute | solution.py:50
  63.4 52.5 %collective-permute-start.15 = (bf16[48,8192]{1,0:T(8,128)(2,1)}, bf16[48,8192]{1,0:T(8,128)(2,1)}, u32[]{:S(2)}, u32[]{:S(2)}) collective-permute-start(bf16[48,8192]{1,0:T(8,128)(2,1)} %bitcast.21), channel_id=1, source_target_pairs={{0,4},{1,5},{2,6},{3,7},{4,0},{5,1},{6,2},{7,3},{8,12},{9,13},{10,... | collective-permute-start | bytes 2359304 | tf_op jit(solution)/shard_map/ppermute | solution.py:50
  66.3 49.5 %collective-permute-start.14 = (bf16[48,8192]{1,0:T(8,128)(2,1)}, bf16[48,8192]{1,0:T(8,128)(2,1)}, u32[]{:S(2)}, u32[]{:S(2)}) collective-permute-start(bf16[48,8192]{1,0:T(8,128)(2,1)} %bitcast.18), channel_id=1, source_target_pairs={{0,6},{1,7},{2,0},{3,1},{4,2},{5,3},{6,4},{7,5},{8,14},{9,15},{10,... | collective-permute-start | bytes 2359304 | tf_op jit(solution)/shard_map/ppermute | solution.py:50
  67.0 48.9 %collective-permute-start.13 = (bf16[48,8192]{1,0:T(8,128)(2,1)}, bf16[48,8192]{1,0:T(8,128)(2,1)}, u32[]{:S(2)}, u32[]{:S(2)}) collective-permute-start(bf16[48,8192]{1,0:T(8,128)(2,1)} %bitcast.19), channel_id=1, source_target_pairs={{0,2},{1,3},{2,4},{3,5},{4,6},{5,7},{6,0},{7,1},{8,10},{9,11},{10,... | collective-permute-start | bytes 2359304 | tf_op jit(solution)/shard_map/ppermute | solution.py:50
  88.3 0.6 copy-start.5
  88.9 19.2 %all-to-all-start = ((f32[16,8,1024]{2,1,0:T(8,128)}), f32[16,8,1024]{2,1,0:T(8,128)S(1)}, u32[]{:S(2)}, u32[]{:S(2)}) async-start(f32[16,8,1024]{2,1,0:T(8,128)} %get-tuple-element.62), calls=%async_computation | async-start | bytes 1048576 | tf_op jit(solution)/shard_map/all_to_all | solution.py:343
  108.2 2.2 %collective-permute-start.12 = (f32[8,1024]{1,0:T(8,128)S(1)}, f32[8,1024]{1,0:T(8,128)S(1)}, u32[]{:S(2)}, u32[]{:S(2)}) collective-permute-start(f32[8,1024]{1,0:T(8,128)S(1)} %reduce_sum.19), channel_id=1, source_target_pairs={{0,1},{1,0},{2,3},{3,2},{4,5},{5,4},{6,7},{7,6},{8,9},{9,8},{10,11... | collective-permute-start | bytes 98312 | tf_op jit(solution)/shard_map/ppermute | solution.py:344
  110.4 6.9 %collective-permute-start.17 = (f32[8,1024]{1,0:T(8,128)S(1)}, f32[8,1024]{1,0:T(8,128)S(1)}, u32[]{:S(2)}, u32[]{:S(2)}) collective-permute-start(f32[8,1024]{1,0:T(8,128)S(1)} %add.258), channel_id=1, source_target_pairs={{0,2},{1,3},{2,0},{3,1},{4,6},{5,7},{6,4},{7,5},{8,10},{9,11},{10,... | collective-permute-start | bytes 98312 | tf_op jit(solution)/shard_map/ppermute | solution.py:345
  112.7 5.4 %collective-permute-start.18 = (f32[8,1024]{1,0:T(8,128)S(1)}, f32[8,1024]{1,0:T(8,128)S(1)}, u32[]{:S(2)}, u32[]{:S(2)}) collective-permute-start(f32[8,1024]{1,0:T(8,128)S(1)} %add.258), channel_id=1, source_target_pairs={{0,4},{1,5},{2,6},{3,7},{4,0},{5,1},{6,2},{7,3},{8,12},{9,13},{10,... | collective-permute-start | bytes 98312 | tf_op jit(solution)/shard_map/ppermute | solution.py:345
  115.9 5.2 %collective-permute-start.19 = (f32[8,1024]{1,0:T(8,128)S(1)}, f32[8,1024]{1,0:T(8,128)S(1)}, u32[]{:S(2)}, u32[]{:S(2)}) collective-permute-start(f32[8,1024]{1,0:T(8,128)S(1)} %add.258), channel_id=1, source_target_pairs={{0,6},{1,7},{2,4},{3,5},{4,2},{5,3},{6,0},{7,1},{8,14},{9,15},{10,... | collective-permute-start | bytes 98312 | tf_op jit(solution)/shard_map/ppermute | solution.py:347
  121.1 36.2 %collective-permute-start.20 = (bf16[48,8192]{1,0:T(8,128)(2,1)}, bf16[48,8192]{1,0:T(8,128)(2,1)S(1)}, u32[]{:S(2)}, u32[]{:S(2)}) collective-permute-start(bf16[48,8192]{1,0:T(8,128)(2,1)} %bitcast.38), channel_id=1, source_target_pairs={{0,5},{1,4},{2,7},{3,6},{4,1},{5,0},{6,3},{7,2},{8,13},{9,12},{10,... | collective-permute-start | bytes 2359304 | tf_op jit(solution)/shard_map/ppermute | solution.py:50
  121.2 37.0 %collective-permute-start.21 = (bf16[48,8192]{1,0:T(8,128)(2,1)}, bf16[48,8192]{1,0:T(8,128)(2,1)S(1)}, u32[]{:S(2)}, u32[]{:S(2)}) collective-permute-start(bf16[48,8192]{1,0:T(8,128)(2,1)} %bitcast.37), channel_id=1, source_target_pairs={{0,3},{1,2},{2,5},{3,4},{4,7},{5,6},{6,1},{7,0},{8,11},{9,10},{10,... | collective-permute-start | bytes 2359304 | tf_op jit(solution)/shard_map/ppermute | solution.py:50
  121.8 36.4 %collective-permute-start.22 = (bf16[48,8192]{1,0:T(8,128)(2,1)}, bf16[48,8192]{1,0:T(8,128)(2,1)S(1)}, u32[]{:S(2)}, u32[]{:S(2)}) collective-permute-start(bf16[48,8192]{1,0:T(8,128)(2,1)} %bitcast.36), channel_id=1, source_target_pairs={{0,7},{1,6},{2,1},{3,0},{4,3},{5,2},{6,5},{7,4},{8,15},{9,14},{10,... | collective-permute-start | bytes 2359304 | tf_op jit(solution)/shard_map/ppermute | solution.py:50
  157.3 0.9 copy-start.6
  158.2 0.9 copy-start.7
  158.2 1.1 copy-start.8
